TPU v7x, 32 devices: a whole 2x2x4 slice. The times are simulated.
32 devices in a mesh: date: 8 (over y, x, core), strip: 4 (over z).
Axes of the slice: x: 2, y: 2, z: 4, core: 2. Of those that a mesh axis runs over, the one named last changes fastest.
Arguments:
- slc: bfloat16 [2, 16, 128, 1024], P(None, 'date', 'strip')
- block_order: int32 [8], replicated, may hold values from 0 to 7, each once
- az_offset: int32 [32], P('strip'), may hold values from 0 to 3
- rg_offset: int32 [256], replicated, may hold values from 0 to 3
Outputs:
- coherence: float32 [2, 16, 16, 32, 256], P(None, 'date', None, 'strip')
Inputs may be any that keep to these rules, and one draw needn't show every extreme that they name: block_order is a permutation of the 8 chronological block numbers.
All inputs are finite; a program needn't handle non-finite values.
Results may differ from a plain program's by a relative error of at most 0.0003.
Values may be sent and summed in bfloat16 or wider, within the bound.
No kernel may reach another device: no remote copies, remote signals or barrier semaphores. Data moves between devices by JAX's collectives and lax.ppermute only.
A program may use at most 64 MiB of HBM per device.

v0:
```python
import jax
import jax.numpy as jnp
from jax import lax
from jax.sharding import PartitionSpec as P

RG_WIN = 5
STEP = 4
HALO = 5


epsilon = 1e-06


def with_halo(block, sides, width):
    for axis, dim in sides:
        count = lax.axis_size(axis)
        forward = [(i, i + 1) for i in range(count - 1)]
        backward = [(target, source) for source, target in forward]
        low = lax.ppermute(
            lax.slice_in_dim(block, block.shape[dim] - width, None, axis=dim), axis, forward
        )
        high = lax.ppermute(lax.slice_in_dim(block, 0, width, axis=dim), axis, backward)
        block = jnp.concatenate([low, block, high], axis=dim)
    return block


def window_sums(field, az_box, rg_box):
    along = jnp.einsum("ol,...lr->...or", az_box, field, precision=lax.Precision.HIGHEST)
    return jnp.einsum("...or,rc->...oc", along, rg_box, precision=lax.Precision.HIGHEST)


def power_scales(samples, az_box, rg_box):
    widened = samples.astype(jnp.float32)
    power = window_sums(widened[0] * widened[0] + widened[1] * widened[1], az_box, rg_box)
    return lax.rsqrt(power + epsilon)


def cross_block(mine, mine_scale, other, az_box, rg_box):
    other_scale = power_scales(other, az_box, rg_box)
    first = mine.astype(jnp.float32)[:, :, None]
    second = other.astype(jnp.float32)[:, None]
    real_part = first[0] * second[0] + first[1] * second[1]
    imag_part = first[1] * second[0] - first[0] * second[1]
    sums = window_sums(jnp.stack([real_part, imag_part]), az_box, rg_box)
    return sums * mine_scale[None, :, None] * other_scale[None, None, :]


def on_device(slc, block_order, az_offset, rg_offset):
    myself = lax.axis_index("date")
    blocks = lax.axis_size("date")
    per_block = slc.shape[1]
    date_count = blocks * per_block
    line_count = slc.shape[2]
    range_count = slc.shape[3]
    out_rows = line_count // STEP
    out_cols = range_count // STEP
    span_lines = line_count + 2 * HALO
    row_index = jnp.arange(out_rows, dtype=jnp.int32)[:, None]
    lower = STEP * row_index + az_offset[:, None]
    line_index = jnp.arange(span_lines, dtype=jnp.int32)[None]
    az_box = ((line_index >= lower) & (line_index <= lower + 2 * HALO)).astype(jnp.float32)
    centre = STEP * jnp.arange(out_cols, dtype=jnp.int32)[None] + rg_offset[None]
    sample = jnp.arange(range_count, dtype=jnp.int32)[:, None]
    rg_box = (jnp.abs(sample - centre) <= RG_WIN // 2).astype(jnp.float32)
    date_rank = (
        block_order[:, None] * per_block + jnp.arange(per_block, dtype=jnp.int32)[None]
    ).reshape(-1)
    positions = jnp.arange(blocks, dtype=jnp.int32)
    mine_ranks = lax.dynamic_slice_in_dim(date_rank, myself * per_block, per_block)
    haloed = with_halo(slc, (("strip", 2),), HALO)
    mine_scale = power_scales(haloed, az_box, rg_box)
    empty = jnp.zeros((2, per_block, date_count, out_rows, out_cols), jnp.float32)
    blank = jnp.zeros((2, per_block, per_block, out_rows, out_cols), jnp.float32)

    def rank_of(block):
        return jnp.sum(jnp.where(positions == block, block_order, 0))

    my_rank = rank_of(myself)

    def ranks_after(block):
        other_ranks = lax.dynamic_slice_in_dim(date_rank, block * per_block, per_block)
        return other_ranks[None, :] > mine_ranks[:, None]

    def compute(other):
        return cross_block(haloed, mine_scale, other, az_box, rg_box)

    def skipped(other):
        return blank

    portion = lax.all_gather(haloed, "date", axis=1, tiled=True)

    def one_shard(index, carried):
        other = lax.dynamic_slice_in_dim(portion, index * per_block, per_block, 1)
        column = index * per_block
        block = column // per_block
        coherent = lax.cond(rank_of(block) >= my_rank, compute, skipped, other)
        later = ranks_after(block)[None, :, :, None, None]
        return lax.dynamic_update_slice_in_dim(carried, jnp.where(later, coherent, 0.0), column, 2)

    return lax.fori_loop(0, portion.shape[1] // per_block, one_shard, empty)


def solution(mesh):
    placed = (P(None, "date", "strip", None), P(), P("strip"), P())
    return jax.shard_map(
        on_device,
        mesh=mesh,
        in_specs=placed,
        out_specs=P(None, "date", None, "strip", None),
        check_vma=False,
    )
```

profile of v0, /device:TPU:5, one launch (start us, length us, event | category | flops | bytes accessed | tf_op | source)
XLA Modules:
  0.0 115.5 jit_solution(15568098306904018081)
XLA Ops:
  6.5 0.9 fusion.43
  7.5 3.2 %collective-permute-start = (bf16[2,2,5,1024]{3,2,1,0:T(8,128)(2,1)S(1)}, bf16[2,2,5,1024]{3,2,1,0:T(8,128)(2,1)S(1)}, u32[]{:S(2)}, u32[]{:S(2)}) collective-permute-start(bf16[2,2,5,1024]{3,2,1,0:T(8,128)(2,1)S(1)} %get-tuple-element.400), channel_id=1, source_target_pairs={{0,1},{1,2},{2,3},{4,5},{5,6},{6,7},{8,9},{9,10},{10,11},{12,13},{... | collective-permute-start | bytes 122888 | tf_op jit(solution)/shard_map/ppermute | solution.py:19
  10.7 1.3 %collective-permute-start.1 = (bf16[2,2,5,1024]{3,2,1,0:T(8,128)(2,1)S(1)}, bf16[2,2,5,1024]{3,2,1,0:T(8,128)(2,1)S(1)}, u32[]{:S(2)}, u32[]{:S(2)}) collective-permute-start(bf16[2,2,5,1024]{3,2,1,0:T(8,128)(2,1)S(1)} %get-tuple-element.401), channel_id=1, source_target_pairs={{1,0},{2,1},{3,2},{5,4},{6,5},{7,6},{9,8},{10,9},{11,10},{13,12},{... | collective-permute-start | bytes 122888 | tf_op jit(solution)/shard_map/ppermute | solution.py:22
  12.0 3.7 %collective-permute-done.1 = bf16[2,2,5,1024]{3,2,1,0:T(8,128)(2,1)S(1)} collective-permute-done((bf16[2,2,5,1024]{3,2,1,0:T(8,128)(2,1)S(1)}, bf16[2,2,5,1024]{3,2,1,0:T(8,128)(2,1)S(1)}, u32[]{:S(2)}, u32[]{:S(2)}) %collective-permute-start.1) | collective-permute-done | bytes 40992 | tf_op jit(solution)/shard_map/ppermute | solution.py:22
  15.7 1.8 %fusion.42 = (f32[2,2,42,1024]{3,2,1,0:T(8,128)S(1)}, bf16[2,2,42,1024]{3,2,1,0:T(8,128)(2,1)}) fusion(bf16[2,2,5,1024]{3,2,1,0:T(8,128)(2,1)S(1)} %collective-permute-done.1, bf16[2,2,32,1024]{3,2,1,0:T(8,128)(2,1)} %param.8, bf16[2,2,5,1024]{3,2,1,0:T(8,128)(2,1)S(1)} %collective-permute-done), kind=kLoop, calls=%fused_computation.64 | loop fusion | flops 1204224 | bytes 1376256 | tf_op jit(solution)/shard_map/convert_element_type | solution.py:33
  19.4 32.6 %all-gather.2.cloned.1.call-done = bf16[2,16,42,1024]{3,2,1,0:T(8,128)(2,1)} async-done(((bf16[2,2,42,1024]{3,2,1,0:T(8,128)(2,1)}), bf16[2,16,42,1024]{3,2,1,0:T(8,128)(2,1)}) %all-gather.2.cloned.1.call-update) | async-done | bytes 2752528 | tf_op jit(solution)/shard_map/all_gather | solution.py:90
  52.0 55.9 %while.16 = (s32[]{:T(128)}, f32[2,2,16,8,256]{4,3,2,1,0:T(8,128)S(1)}, s32[16]{0:T(128)S(1)}, s32[2]{0:T(128)S(1)}, s32[8]{0:T(128)S(1)}, /*index=5*/s32[]{:T(1...) while((s32[]{:T(128)}, ...), condition=%wide.region_5.6_spmd.clone, body=%wide.region_1.5_spmd.clone.sunk | while | flops 296027488 | bytes 13686820 | solution.py:100
  54.5 4.5 %conditional.3 = (f32[2,2,2,8,256]{4,3,2,1,0:T(8,128)S(1)}) conditional(s32[]{:T(128)} %convert_element_type.49, () %tuple.62, (bf16[2,2,42,1024]{3,2,1,0:T(8,128)(2,1)S(1)}, bf16[2,16,42,1024]{3,2,1,0:T(8,128)(2,1)}, s32[]{:T(128)}, f32[8,42]{1,0:T(8,128)S(1)}, f32[1024,256]{1,0:T(8,128)S(1)}, /*index=5*/f32[2,8,256]{2,1,0:T(8,128)S(1)}) %tuple.63), branch_computations={%region_3.3_spmd, %region_4.4_spmd} | conditional | flops 294961152 | bytes 12503692 | solution.py:96
  54.6 1.1 dynamic-slice_convert_fusion
  57.1 1.2 %fusion.10 = f32[2,2,2,8,1024]{4,3,2,1,0:T(8,128)S(1)} fusion(f32[1,2,2,42,1024]{4,3,2,1,0:T(8,128)S(1)} %get-tuple-element.391, f32[1,2,2,42,1024]{4,3,2,1,0:T(8,128)S(1)} %get-tuple-element.390, f32[8,42]{1,0:T(8,128)S(1)} %get-tuple-element.317), kind=kOutput, calls=%fused_computation.7 | convolution fusion | flops 33374208 | bytes 1639744 | tf_op jit(solution)/shard_map/while/body/eval_jaxpr/cond/branch_1_fun/ol,...lr->...or/dot_general | solution.py:28
  61.4 4.5 %conditional.3 = (f32[2,2,2,8,256]{4,3,2,1,0:T(8,128)S(1)}) conditional(s32[]{:T(128)} %convert_element_type.49, () %tuple.62, (bf16[2,2,42,1024]{3,2,1,0:T(8,128)(2,1)S(1)}, bf16[2,16,42,1024]{3,2,1,0:T(8,128)(2,1)}, s32[]{:T(128)}, f32[8,42]{1,0:T(8,128)S(1)}, f32[1024,256]{1,0:T(8,128)S(1)}, /*index=5*/f32[2,8,256]{2,1,0:T(8,128)S(1)}) %tuple.63), branch_computations={%region_3.3_spmd, %region_4.4_spmd} | conditional | flops 294961152 | bytes 12503692 | solution.py:96
  61.5 1.1 dynamic-slice_convert_fusion
  64.1 1.2 %fusion.10 = f32[2,2,2,8,1024]{4,3,2,1,0:T(8,128)S(1)} fusion(f32[1,2,2,42,1024]{4,3,2,1,0:T(8,128)S(1)} %get-tuple-element.391, f32[1,2,2,42,1024]{4,3,2,1,0:T(8,128)S(1)} %get-tuple-element.390, f32[8,42]{1,0:T(8,128)S(1)} %get-tuple-element.317), kind=kOutput, calls=%fused_computation.7 | convolution fusion | flops 33374208 | bytes 1639744 | tf_op jit(solution)/shard_map/while/body/eval_jaxpr/cond/branch_1_fun/ol,...lr->...or/dot_general | solution.py:28
  68.4 4.5 %conditional.3 = (f32[2,2,2,8,256]{4,3,2,1,0:T(8,128)S(1)}) conditional(s32[]{:T(128)} %convert_element_type.49, () %tuple.62, (bf16[2,2,42,1024]{3,2,1,0:T(8,128)(2,1)S(1)}, bf16[2,16,42,1024]{3,2,1,0:T(8,128)(2,1)}, s32[]{:T(128)}, f32[8,42]{1,0:T(8,128)S(1)}, f32[1024,256]{1,0:T(8,128)S(1)}, /*index=5*/f32[2,8,256]{2,1,0:T(8,128)S(1)}) %tuple.63), branch_computations={%region_3.3_spmd, %region_4.4_spmd} | conditional | flops 294961152 | bytes 12503692 | solution.py:96
  68.5 1.1 dynamic-slice_convert_fusion
  71.0 1.2 %fusion.10 = f32[2,2,2,8,1024]{4,3,2,1,0:T(8,128)S(1)} fusion(f32[1,2,2,42,1024]{4,3,2,1,0:T(8,128)S(1)} %get-tuple-element.391, f32[1,2,2,42,1024]{4,3,2,1,0:T(8,128)S(1)} %get-tuple-element.390, f32[8,42]{1,0:T(8,128)S(1)} %get-tuple-element.317), kind=kOutput, calls=%fused_computation.7 | convolution fusion | flops 33374208 | bytes 1639744 | tf_op jit(solution)/shard_map/while/body/eval_jaxpr/cond/branch_1_fun/ol,...lr->...or/dot_general | solution.py:28
  75.4 4.5 %conditional.3 = (f32[2,2,2,8,256]{4,3,2,1,0:T(8,128)S(1)}) conditional(s32[]{:T(128)} %convert_element_type.49, () %tuple.62, (bf16[2,2,42,1024]{3,2,1,0:T(8,128)(2,1)S(1)}, bf16[2,16,42,1024]{3,2,1,0:T(8,128)(2,1)}, s32[]{:T(128)}, f32[8,42]{1,0:T(8,128)S(1)}, f32[1024,256]{1,0:T(8,128)S(1)}, /*index=5*/f32[2,8,256]{2,1,0:T(8,128)S(1)}) %tuple.63), branch_computations={%region_3.3_spmd, %region_4.4_spmd} | conditional | flops 294961152 | bytes 12503692 | solution.py:96
  75.5 1.1 dynamic-slice_convert_fusion
  78.0 1.2 %fusion.10 = f32[2,2,2,8,1024]{4,3,2,1,0:T(8,128)S(1)} fusion(f32[1,2,2,42,1024]{4,3,2,1,0:T(8,128)S(1)} %get-tuple-element.391, f32[1,2,2,42,1024]{4,3,2,1,0:T(8,128)S(1)} %get-tuple-element.390, f32[8,42]{1,0:T(8,128)S(1)} %get-tuple-element.317), kind=kOutput, calls=%fused_computation.7 | convolution fusion | flops 33374208 | bytes 1639744 | tf_op jit(solution)/shard_map/while/body/eval_jaxpr/cond/branch_1_fun/ol,...lr->...or/dot_general | solution.py:28
  82.4 4.5 %conditional.3 = (f32[2,2,2,8,256]{4,3,2,1,0:T(8,128)S(1)}) conditional(s32[]{:T(128)} %convert_element_type.49, () %tuple.62, (bf16[2,2,42,1024]{3,2,1,0:T(8,128)(2,1)S(1)}, bf16[2,16,42,1024]{3,2,1,0:T(8,128)(2,1)}, s32[]{:T(128)}, f32[8,42]{1,0:T(8,128)S(1)}, f32[1024,256]{1,0:T(8,128)S(1)}, /*index=5*/f32[2,8,256]{2,1,0:T(8,128)S(1)}) %tuple.63), branch_computations={%region_3.3_spmd, %region_4.4_spmd} | conditional | flops 294961152 | bytes 12503692 | solution.py:96
  82.5 1.1 dynamic-slice_convert_fusion
  85.0 1.2 %fusion.10 = f32[2,2,2,8,1024]{4,3,2,1,0:T(8,128)S(1)} fusion(f32[1,2,2,42,1024]{4,3,2,1,0:T(8,128)S(1)} %get-tuple-element.391, f32[1,2,2,42,1024]{4,3,2,1,0:T(8,128)S(1)} %get-tuple-element.390, f32[8,42]{1,0:T(8,128)S(1)} %get-tuple-element.317), kind=kOutput, calls=%fused_computation.7 | convolution fusion | flops 33374208 | bytes 1639744 | tf_op jit(solution)/shard_map/while/body/eval_jaxpr/cond/branch_1_fun/ol,...lr->...or/dot_general | solution.py:28
  89.3 4.5 %conditional.3 = (f32[2,2,2,8,256]{4,3,2,1,0:T(8,128)S(1)}) conditional(s32[]{:T(128)} %convert_element_type.49, () %tuple.62, (bf16[2,2,42,1024]{3,2,1,0:T(8,128)(2,1)S(1)}, bf16[2,16,42,1024]{3,2,1,0:T(8,128)(2,1)}, s32[]{:T(128)}, f32[8,42]{1,0:T(8,128)S(1)}, f32[1024,256]{1,0:T(8,128)S(1)}, /*index=5*/f32[2,8,256]{2,1,0:T(8,128)S(1)}) %tuple.63), branch_computations={%region_3.3_spmd, %region_4.4_spmd} | conditional | flops 294961152 | bytes 12503692 | solution.py:96
  89.5 1.1 dynamic-slice_convert_fusion
  92.0 1.2 %fusion.10 = f32[2,2,2,8,1024]{4,3,2,1,0:T(8,128)S(1)} fusion(f32[1,2,2,42,1024]{4,3,2,1,0:T(8,128)S(1)} %get-tuple-element.391, f32[1,2,2,42,1024]{4,3,2,1,0:T(8,128)S(1)} %get-tuple-element.390, f32[8,42]{1,0:T(8,128)S(1)} %get-tuple-element.317), kind=kOutput, calls=%fused_computation.7 | convolution fusion | flops 33374208 | bytes 1639744 | tf_op jit(solution)/shard_map/while/body/eval_jaxpr/cond/branch_1_fun/ol,...lr->...or/dot_general | solution.py:28
  96.3 4.5 %conditional.3 = (f32[2,2,2,8,256]{4,3,2,1,0:T(8,128)S(1)}) conditional(s32[]{:T(128)} %convert_element_type.49, () %tuple.62, (bf16[2,2,42,1024]{3,2,1,0:T(8,128)(2,1)S(1)}, bf16[2,16,42,1024]{3,2,1,0:T(8,128)(2,1)}, s32[]{:T(128)}, f32[8,42]{1,0:T(8,128)S(1)}, f32[1024,256]{1,0:T(8,128)S(1)}, /*index=5*/f32[2,8,256]{2,1,0:T(8,128)S(1)}) %tuple.63), branch_computations={%region_3.3_spmd, %region_4.4_spmd} | conditional | flops 294961152 | bytes 12503692 | solution.py:96
  96.4 1.1 dynamic-slice_convert_fusion
  98.9 1.2 %fusion.10 = f32[2,2,2,8,1024]{4,3,2,1,0:T(8,128)S(1)} fusion(f32[1,2,2,42,1024]{4,3,2,1,0:T(8,128)S(1)} %get-tuple-element.391, f32[1,2,2,42,1024]{4,3,2,1,0:T(8,128)S(1)} %get-tuple-element.390, f32[8,42]{1,0:T(8,128)S(1)} %get-tuple-element.317), kind=kOutput, calls=%fused_computation.7 | convolution fusion | flops 33374208 | bytes 1639744 | tf_op jit(solution)/shard_map/while/body/eval_jaxpr/cond/branch_1_fun/ol,...lr->...or/dot_general | solution.py:28
  103.3 4.5 %conditional.3 = (f32[2,2,2,8,256]{4,3,2,1,0:T(8,128)S(1)}) conditional(s32[]{:T(128)} %convert_element_type.49, () %tuple.62, (bf16[2,2,42,1024]{3,2,1,0:T(8,128)(2,1)S(1)}, bf16[2,16,42,1024]{3,2,1,0:T(8,128)(2,1)}, s32[]{:T(128)}, f32[8,42]{1,0:T(8,128)S(1)}, f32[1024,256]{1,0:T(8,128)S(1)}, /*index=5*/f32[2,8,256]{2,1,0:T(8,128)S(1)}) %tuple.63), branch_computations={%region_3.3_spmd, %region_4.4_spmd} | conditional | flops 294961152 | bytes 12503692 | solution.py:96
  103.4 1.1 dynamic-slice_convert_fusion
  105.9 1.2 %fusion.10 = f32[2,2,2,8,1024]{4,3,2,1,0:T(8,128)S(1)} fusion(f32[1,2,2,42,1024]{4,3,2,1,0:T(8,128)S(1)} %get-tuple-element.391, f32[1,2,2,42,1024]{4,3,2,1,0:T(8,128)S(1)} %get-tuple-element.390, f32[8,42]{1,0:T(8,128)S(1)} %get-tuple-element.317), kind=kOutput, calls=%fused_computation.7 | convolution fusion | flops 33374208 | bytes 1639744 | tf_op jit(solution)/shard_map/while/body/eval_jaxpr/cond/branch_1_fun/ol,...lr->...or/dot_general | solution.py:28
  107.9 0.8 copy-done.1
  (116 shorter events, 28.6 us)
Async XLA Ops:
  6.5 11.0 %copy-start.4 = (s32[8]{0:T(128)S(1)}, s32[8]{0:T(128)}, u32[]{:S(2)}) copy-start(s32[8]{0:T(128)} %param.9) | copy-start | bytes 100
  6.5 11.0 %copy-start.3 = (s32[8]{0:T(128)S(1)}, s32[8]{0:T(128)}, u32[]{:S(2)}) copy-start(s32[8]{0:T(128)} %param.10) | copy-start | bytes 100
  6.5 11.9 %copy-start.2 = (s32[256]{0:T(256)S(1)}, s32[256]{0:T(256)}, u32[]{:S(2)}) copy-start(s32[256]{0:T(256)} %param.11) | copy-start | bytes 3076
  6.5 45.4 %all-gather.2.cloned.1.call-start = ((), (), s32[]{:S(2)}) async-start(), calls=%async_computation | async-start | bytes 3538944 | tf_op jit(solution)/shard_map/all_gather | solution.py:90
  7.5 4.5 %collective-permute-start = (bf16[2,2,5,1024]{3,2,1,0:T(8,128)(2,1)S(1)}, bf16[2,2,5,1024]{3,2,1,0:T(8,128)(2,1)S(1)}, u32[]{:S(2)}, u32[]{:S(2)}) collective-permute-start(bf16[2,2,5,1024]{3,2,1,0:T(8,128)(2,1)S(1)} %get-tuple-element.400), channel_id=1, source_target_pairs={{0,1},{1,2},{2,3},{4,5},{5,6},{6,7},{8,9},{9,10},{10,11},{12,13},{... | collective-permute-start | bytes 122888 | tf_op jit(solution)/shard_map/ppermute | solution.py:19
  10.7 5.0 %collective-permute-start.1 = (bf16[2,2,5,1024]{3,2,1,0:T(8,128)(2,1)S(1)}, bf16[2,2,5,1024]{3,2,1,0:T(8,128)(2,1)S(1)}, u32[]{:S(2)}, u32[]{:S(2)}) collective-permute-start(bf16[2,2,5,1024]{3,2,1,0:T(8,128)(2,1)S(1)} %get-tuple-element.401), channel_id=1, source_target_pairs={{1,0},{2,1},{3,2},{5,4},{6,5},{7,6},{9,8},{10,9},{11,10},{13,12},{... | collective-permute-start | bytes 122888 | tf_op jit(solution)/shard_map/ppermute | solution.py:22
  17.5 34.5 %copy-start = (bf16[2,2,42,1024]{3,2,1,0:T(8,128)(2,1)S(1)}, bf16[2,2,42,1024]{3,2,1,0:T(8,128)(2,1)}, u32[]{:S(2)}) copy-start(bf16[2,2,42,1024]{3,2,1,0:T(8,128)(2,1)} %get-tuple-element.487) | copy-start | bytes 1032196
  107.9 0.8 copy-start.1
Sparse Core Ops, SparseCore 0:
  17.7 34.2 all-gather.1
where the time goes:
time: 117 us; the launch traced here: 116 us
  waiting for transfers between devices  36.3 us (31%)
  other arithmetic  23.4 us (20%)
  matrix products  23.2 us (20%)
  between operations  13.5 us (12%)
  loops' own time  10.7 us (9%)
  starting transfers between devices  4.5 us (4%)
  local copies, waits for them, and re-layouts  3.89 us (3%)
    all_gather x1, waiting for transfers between devices, on_device(): portion = lax.all_gather(haloed, 'date', axis=1, tiled=True)  32.6 us
    dot_general x17, matrix products, window_sums(): jnp.einsum('ol,...lr->...or', az_box, field, precision=lax.Precision.HIGH...  13.2 us
    another operation x1, loops' own time, on_device(): return lax.fori_loop(0, portion.shape[1] // per_block, one_shard, empty)  10.2 us
    dot_general x17, matrix products, window_sums(): jnp.einsum('...or,rc->...oc', along, rg_box, precision=lax.Precision.HIGH...  9.98 us
    convert_element_type x8, other arithmetic, cross_block(): second = other.astype(jnp.float32)[:, None]  8.65 us
    reduce_sum x9, other arithmetic, rank_of(): return jnp.sum(jnp.where(positions == block, block_order, 0))  6.18 us
    ppermute x1, waiting for transfers between devices, with_halo(): lax.ppermute(lax.slice_in_dim(block, 0, width, axis=dim), axis, backward)  3.7 us
    ppermute x1, starting transfers between devices, with_halo(): lax.ppermute(lax.slice_in_dim(block, block.shape[dim] - width, None, axis...  3.2 us
  transfers between devices with their start and end apart: 3, of which 2 were waited for; matrix products, arithmetic and copies ran while one was open for 2% of the time, Pallas kernels for 0%

commit v1 on v0

v1 whole, which is shorter than its diff:
```python
import functools

import jax
import jax.numpy as jnp
from jax import lax
from jax.experimental import pallas as pl
from jax.experimental.pallas import tpu as pltpu
from jax.sharding import PartitionSpec as P

STEP = 4
HALO = 5
REACH = 2
EDGE = 4
LANES = 128
VMEM = pl.BlockSpec(memory_space=pltpu.VMEM)
SMEM = pl.BlockSpec(memory_space=pltpu.SMEM)
PARAMS = pltpu.CompilerParams(vmem_limit_bytes=48 * 1024 * 1024)

epsilon = 1e-06


def iota(shape, dim):
    return lax.broadcasted_iota(jnp.int32, shape, dim)


def row_of(part, line, lines):
    if line < HALO:
        return 2 * lines + part * 2 * HALO + line
    if line < HALO + lines:
        return part * lines + line - HALO
    return 2 * lines + part * 2 * HALO + line - lines


def pack_kernel(blocks, per, lines, chunk, slc, low, high, send, stage, piece):
    rows = 2 * (lines + 2 * HALO)
    date_rows = rows + EDGE
    span = blocks * chunk
    for date in range(per):
        base = date * date_rows
        for part in range(2):
            edge = base + 2 * lines + part * 2 * HALO
            stage[base + part * lines : base + (part + 1) * lines, :] = slc[part, date].astype(jnp.float32)
            stage[edge : edge + HALO, :] = low[part, date].astype(jnp.float32)
            stage[edge + HALO : edge + 2 * HALO, :] = high[part, date].astype(jnp.float32)
        stage[base + rows : base + date_rows, :] = jnp.zeros((EDGE, span), jnp.float32)
    samples = stage[...].astype(jnp.bfloat16)
    shape = (EDGE * blocks, span)
    place = iota(shape, 0) % EDGE
    wanted = iota(shape, 0) // EDGE * chunk + jnp.where(place < REACH, place - REACH, place - REACH + chunk)
    picks = (iota(shape, 1) == wanted).astype(jnp.bfloat16)
    edges = lax.dot_general(picks, samples, (((1,), (1,)), ((), ())), preferred_element_type=jnp.float32)
    lane = iota((EDGE, LANES), 1)
    for block in range(blocks):
        if chunk == LANES:
            piece[...] = stage[:, block * chunk : (block + 1) * chunk]
        else:
            piece[...] = jnp.zeros(piece.shape, jnp.float32)
            piece[:, :chunk] = stage[:, block * chunk : (block + 1) * chunk]
        for date in range(per):
            base = date * date_rows
            mine = edges[block * EDGE : (block + 1) * EDGE, base : base + date_rows]
            piece[base + rows : base + date_rows, :] = jnp.zeros((EDGE, LANES), jnp.float32)
            piece[base + rows : base + date_rows, :date_rows] = mine
        send[block] = piece[...].astype(jnp.bfloat16)


def split(value):
    high = value.astype(jnp.bfloat16)
    return high, (value - high.astype(jnp.float32)).astype(jnp.bfloat16)


def pair_kernel(blocks, per, lines, chunk, group, recv, order, az, rg, tiled, send, x, left, weights, power):
    dates = blocks * per
    out_rows = lines // STEP
    cols = chunk // STEP
    wide = out_rows * cols
    rows = 2 * (lines + 2 * HALO)
    date_rows = rows + EDGE
    me = lax.axis_index("date")
    depth = out_rows * 2 * LANES

    for block in range(blocks):
        value = recv[block].astype(jnp.float32)
        for date in range(per):
            for tile in range(date_rows // 8):
                part = value[date * date_rows + 8 * tile : date * date_rows + 8 * tile + 8]
                x[pl.ds(8 * tile * dates + block * per + date, 8, stride=dates), :] = part

    shape = (LANES, wide)
    col = iota(shape, 1) % cols
    out_row = iota(shape, 1) // cols
    box = jnp.abs(iota(shape, 0) - STEP * col - tiled[...]) <= REACH
    for o in range(out_rows):
        mine = (box & (out_row == o)).astype(jnp.bfloat16)
        weights[2 * o * LANES : (2 * o + 1) * LANES, :] = mine
        weights[(2 * o + 1) * LANES : (2 * o + 2) * LANES, :] = mine
    at = iota(shape, 0)
    turn = jnp.where(at < 2 * lines, 0, (at - 2 * lines) % (2 * HALO))
    line = jnp.where(at < 2 * lines, at % lines + HALO, jnp.where(turn < HALO, turn, turn + lines))
    line = jnp.where(at < rows, line, -100)
    lower = jnp.zeros(shape, jnp.int32)
    for o in range(out_rows):
        lower = jnp.where(out_row == o, STEP * o + az[o], lower)
    window = (line >= lower) & (line <= lower + 2 * HALO)
    for side, edge_col in ((0, 0), (1, cols - 1)):
        mine = (window & (col == edge_col)).astype(jnp.bfloat16)
        for term in range(2):
            start = depth + (2 * side + term) * LANES
            weights[start : start + LANES, :] = mine
    first = rg[me * cols]
    last = rg[me * cols + cols - 1]
    edge_on = (first <= 0, first <= 1, last >= 2, last >= 3)

    lane = iota((16, LANES), 1)

    def swapped(value):
        up = jnp.where(lane < lines, pltpu.roll(value, LANES - lines, 1), pltpu.roll(value, LANES - 2 * HALO, 1))
        down = jnp.where(lane < 2 * lines, pltpu.roll(value, lines, 1), pltpu.roll(value, 2 * HALO, 1))
        real = (lane < lines) | ((lane >= 2 * lines) & (lane < 2 * lines + 2 * HALO))
        return jnp.where(real, up, -down)

    def one_date(first_date, step, carry):
        date = first_date + step
        target = (step // per * 2) * per + step % per
        for tile in range(dates // 16):

            def own(row):
                return x[pl.ds(row * dates + date, 1), :]

            def others(row):
                return x[row * dates + tile * 16 : row * dates + tile * 16 + 16, :]

            real, imag = [], []
            for line in range(lines + 2 * HALO):
                re_i, im_i = own(row_of(0, line, lines)), own(row_of(1, line, lines))
                re_j, im_j = others(row_of(0, line, lines)), others(row_of(1, line, lines))
                real.append(re_i * re_j + im_i * im_j)
                imag.append(im_i * re_j - re_i * im_j)
            for part, product in enumerate((real, imag)):
                start = pl.multiple_of((target + part * per) * dates + tile * 16, 16)
                at_rows = pl.ds(start, 16)
                quads = []
                for k in range(out_rows + 1):
                    q = product[STEP * k + 3 : STEP * k + 7]
                    quads.append((q[0] + q[1]) + (q[2] + q[3]))
                for o in range(out_rows):
                    total = quads[o] + quads[o + 1]
                    for k in range(3):
                        total += jnp.where(az[o] <= k, product[STEP * o + k], product[STEP * o + 11 + k])
                    high, low = split(total)
                    left[at_rows, 2 * o * LANES : (2 * o + 1) * LANES] = high
                    left[at_rows, (2 * o + 1) * LANES : (2 * o + 2) * LANES] = low
                for side in range(2):
                    total = jnp.zeros((16, LANES), jnp.float32)
                    for edge in (2 * side, 2 * side + 1):
                        mine = jnp.broadcast_to(own(rows + edge), (16, LANES))
                        if part:
                            mine = swapped(mine)
                        total += jnp.where(edge_on[edge], mine * others(rows + edge), 0.0)
                    high, low = split(total)
                    start_col = depth + 2 * side * LANES
                    left[at_rows, start_col : start_col + LANES] = high
                    left[at_rows, start_col + LANES : start_col + 2 * LANES] = low
        return carry

    for first_date in range(0, dates, group):
        lax.fori_loop(0, group, functools.partial(one_date, first_date), 0)
        sums = jnp.dot(left[...], weights[...], preferred_element_type=jnp.float32)
        send[first_date * 2 * dates : (first_date + group) * 2 * dates, :] = sums
    for date in range(dates):
        at_row = (date // per * 2 * per + date % per) * dates + date
        power[date : date + 1, :] = send[at_row : at_row + 1, :]
    scale = lax.rsqrt(power[...] + epsilon)
    power[...] = scale
    position = iota((dates, wide), 0)
    rank = jnp.zeros((dates, wide), jnp.int32)
    for block in range(blocks):
        rank = jnp.where(position // per == block, order[block] * per + position % per, rank)
    for date in range(dates):
        later = rank > order[date // per] * per + date % per
        factor = jnp.where(later, scale * power[date : date + 1, :], 0.0)
        for part in range(2):
            start = ((date // per * 2 + part) * per + date % per) * dates
            send[start : start + dates, :] = send[start : start + dates, :] * factor


def join_kernel(blocks, count, out_rows, cols, recv, out, halves):
    per_tile = LANES // cols
    lane = iota((8, LANES), 1) // cols
    for start in range(0, count, 8):
        for o_tile in range(out_rows // per_tile):
            for d_tile in range(blocks // per_tile):
                tiles = [
                    recv[d_tile * per_tile + d, start : start + 8, o_tile * LANES : (o_tile + 1) * LANES]
                    for d in range(per_tile)
                ]
                width = 1
                while width < per_tile:
                    swap = [None] * per_tile
                    upper = (lane // width) % 2 == 1
                    for a in range(per_tile):
                        if (a // width) % 2 == 0:
                            b = a + width
                            shift = width * cols
                            swap[a] = jnp.where(upper, pltpu.roll(tiles[b], shift, 1), tiles[a])
                            swap[b] = jnp.where(upper, tiles[b], pltpu.roll(tiles[a], LANES - shift, 1))
                    tiles = swap
                    width *= 2
                for o in range(per_tile):
                    at = start * out_rows + o_tile * per_tile + o
                    halves[d_tile, pl.ds(at, 8, stride=out_rows), :] = tiles[o]
    for d_tile in range(blocks // per_tile):
        out[:, d_tile * LANES : (d_tile + 1) * LANES] = halves[d_tile]


def on_device(slc, block_order, az_offset, rg_offset):
    blocks = lax.axis_size("date")
    strips = lax.axis_size("strip")
    per, lines, span = slc.shape[1:]
    dates = blocks * per
    chunk = span // blocks
    out_rows = lines // STEP
    cols = chunk // STEP
    wide = out_rows * cols
    date_rows = 2 * (lines + 2 * HALO) + EDGE
    group = max(per, 256 // dates)
    me = lax.axis_index("date")

    forward = [(i, i + 1) for i in range(strips - 1)]
    backward = [(target, source) for source, target in forward]
    low = lax.ppermute(slc[:, :, lines - HALO :], "strip", forward)
    high = lax.ppermute(slc[:, :, :HALO], "strip", backward)
    tiled = jnp.tile(lax.dynamic_slice_in_dim(rg_offset, me * cols, cols), out_rows)[None]

    send = pl.pallas_call(
        functools.partial(pack_kernel, blocks, per, lines, chunk),
        out_shape=jax.ShapeDtypeStruct((blocks, per * date_rows, LANES), jnp.bfloat16),
        in_specs=[VMEM] * 3,
        out_specs=VMEM,
        scratch_shapes=[
            pltpu.VMEM((per * date_rows, span), jnp.float32),
            pltpu.VMEM((per * date_rows, LANES), jnp.float32),
        ],
        compiler_params=PARAMS,
        name="pack",
    )(slc, low, high)
    recv = lax.all_to_all(send, "date", 0, 0, tiled=True)
    depth = (out_rows + 2) * 2 * LANES
    pairs = pl.pallas_call(
        functools.partial(pair_kernel, blocks, per, lines, chunk, group),
        out_shape=jax.ShapeDtypeStruct((dates * 2 * dates, wide), jnp.float32),
        in_specs=[VMEM, SMEM, SMEM, SMEM, VMEM],
        out_specs=VMEM,
        scratch_shapes=[
            pltpu.VMEM((date_rows * dates, LANES), jnp.float32),
            pltpu.VMEM((group * 2 * dates, depth), jnp.bfloat16),
            pltpu.VMEM((depth, wide), jnp.bfloat16),
            pltpu.VMEM((dates, wide), jnp.float32),
        ],
        compiler_params=PARAMS,
        name="pairs",
    )(recv, block_order, az_offset, rg_offset, tiled)
    count = 2 * per * dates
    back = lax.all_to_all(pairs.reshape(blocks, count, wide), "date", 0, 0, tiled=True)
    if LANES % cols == 0 and out_rows * cols % LANES == 0 and blocks * cols % LANES == 0:
        out = pl.pallas_call(
            functools.partial(join_kernel, blocks, count, out_rows, cols),
            out_shape=jax.ShapeDtypeStruct((count * out_rows, blocks * cols), jnp.float32),
            in_specs=[VMEM],
            out_specs=VMEM,
            scratch_shapes=[pltpu.VMEM((blocks * cols // LANES, count * out_rows, LANES), jnp.float32)],
            compiler_params=PARAMS,
            name="join",
        )(back)
    else:
        out = back.reshape(blocks, count, out_rows, cols).transpose(1, 2, 0, 3)
    return out.reshape(2, per, dates, out_rows, blocks * cols)


def solution(mesh):
    placed = (P(None, "date", "strip", None), P(), P("strip"), P())
    return jax.shard_map(
        on_device,
        mesh=mesh,
        in_specs=placed,
        out_specs=P(None, "date", None, "strip", None),
        check_vma=False,
    )
```

time: 117 us -> 42.8 us (0.37)
  the two profiles are of different devices: /device:TPU:5 before, /device:TPU:0 now
where the time goes in v1:
time: 42.8 us; the launch traced here: 42.5 us
  blocking collectives  12.2 us (29%)
  starting transfers between devices  11 us (26%)
  waiting for transfers between devices  9.03 us (21%)
  Pallas kernels  8.48 us (20%)
  local copies, waits for them, and re-layouts  1.78 us (4%)
    all_to_all x1, blocking collectives, on_device(): lax.all_to_all(pairs.reshape(blocks, count, wide), 'date', 0, 0, tiled=True)  12.2 us
    all_to_all x1, waiting for transfers between devices, on_device(): recv = lax.all_to_all(send, 'date', 0, 0, tiled=True)  7.15 us
    ppermute x1, starting transfers between devices, on_device(): low = lax.ppermute(slc[:, :, lines - HALO:], 'strip', forward)  5.56 us
    pallas_call x1, Pallas kernels, on_device(): pl.pallas_call(functools.partial(pair_kernel, blocks, per, lines, chunk,...  5.18 us
    all_to_all x1, starting transfers between devices, on_device(): recv = lax.all_to_all(send, 'date', 0, 0, tiled=True)  4.16 us
    pallas_call x1, Pallas kernels, on_device(): pl.pallas_call(functools.partial(join_kernel, blocks, count, out_rows, co...  2.22 us
    ppermute x1, waiting for transfers between devices, on_device(): low = lax.ppermute(slc[:, :, lines - HALO:], 'strip', forward)  1.58 us
    ppermute x1, starting transfers between devices, on_device(): high = lax.ppermute(slc[:, :, :HALO], 'strip', backward)  1.29 us
  transfers between devices with their start and end apart: 3, of which 3 were waited for; matrix products, arithmetic and copies ran while one was open for 0% of the time, Pallas kernels for 0%

profile of v1, /device:TPU:0, one launch (start us, length us, event | category | flops | bytes accessed | tf_op | source)
XLA Modules:
  0.0 42.5 jit_solution(13032120394511137931)
XLA Ops:
  0.0 0.0 copy-start
  0.0 0.9 %fusion = (bf16[2,2,5,1024]{3,2,1,0:T(8,128)(2,1)S(1)}, bf16[2,2,5,1024]{3,2,1,0:T(8,128)(2,1)S(1)}) fusion(bf16[2,2,32,1024]{3,2,1,0:T(8,128)(2,1)} %slc.1), kind=kLoop, calls=%fused_computation | loop fusion | bytes 163840 | tf_op jit(solution)/shard_map/slice | solution.py:232
  0.9 1.3 %collective-permute-start.1 = (bf16[2,2,5,1024]{3,2,1,0:T(8,128)(2,1)S(1)}, bf16[2,2,5,1024]{3,2,1,0:T(8,128)(2,1)S(1)}, u32[]{:S(2)}, u32[]{:S(2)}) collective-permute-start(bf16[2,2,5,1024]{3,2,1,0:T(8,128)(2,1)S(1)} %get-tuple-element.5), channel_id=1, source_target_pairs={{1,0},{2,1},{3,2},{5,4},{6,5},{7,6},{9,8},{10,9},{11,10},{13,12},{... | collective-permute-start | bytes 122888 | tf_op jit(solution)/shard_map/ppermute | solution.py:232
  2.2 5.6 %collective-permute-start = (bf16[2,2,5,1024]{3,2,1,0:T(8,128)(2,1)S(1)}, bf16[2,2,5,1024]{3,2,1,0:T(8,128)(2,1)S(1)}, u32[]{:S(2)}, u32[]{:S(2)}) collective-permute-start(bf16[2,2,5,1024]{3,2,1,0:T(8,128)(2,1)S(1)} %get-tuple-element.6), channel_id=1, source_target_pairs={{0,1},{1,2},{2,3},{4,5},{5,6},{6,7},{8,9},{9,10},{10,11},{12,13},{... | collective-permute-start | bytes 122888 | tf_op jit(solution)/shard_map/ppermute | solution.py:231
  7.8 0.3 collective-permute-done.1.high
  8.1 1.6 %collective-permute-done.low = bf16[2,2,5,1024]{3,2,1,0:T(8,128)(2,1)S(1)} collective-permute-done((bf16[2,2,5,1024]{3,2,1,0:T(8,128)(2,1)S(1)}, bf16[2,2,5,1024]{3,2,1,0:T(8,128)(2,1)S(1)}, u32[]{:S(2)}, u32[]{:S(2)}) %collective-permute-start) | collective-permute-done | bytes 40992 | tf_op jit(solution)/shard_map/ppermute | solution.py:231
  9.7 0.0 copy-done
  9.7 1.1 %pack.1 = bf16[8,176,128]{2,1,0:T(8,128)(2,1)} custom-call(bf16[2,2,32,1024]{3,2,1,0:T(8,128)(2,1)S(1)} %copy-done, bf16[2,2,5,1024]{3,2,1,0:T(8,128)(2,1)S(1)} %collective-permute-done.low, bf16[2,2,5,1024]{3,2,1,0:T(8,128)(2,1)S(1)} %collective-permute-done.1.high), custom_call_target="tpu_custom_call" | custom-call | tf_op jit(solution)/shard_map/pack/pallas_call | solution.py:235
  10.8 4.2 %all-to-all-start = ((bf16[8,176,128]{2,1,0:T(8,128)(2,1)}), bf16[8,176,128]{2,1,0:T(8,128)(2,1)S(1)}, u32[]{:S(2)}, u32[]{:S(2)}) async-start(bf16[8,176,128]{2,1,0:T(8,128)(2,1)} %pack.1), calls=%async_computation | async-start | bytes 720896 | tf_op jit(solution)/shard_map/all_to_all | solution.py:247
  14.9 0.0 copy-start.1
  14.9 0.7 %copy-done.1 = s32[256]{0:T(256)S(1)} copy-done((s32[256]{0:T(256)S(1)}, s32[256]{0:T(256)}, u32[]{:S(2)}) %copy-start.1) | copy-done | bytes 1048
  15.6 0.1 dynamic_slice.3
  15.7 0.0 copy-start.2
  15.7 0.0 copy-start.3
  15.7 0.1 broadcast_in_dim_tile.3.tiled
  15.8 7.1 %all-to-all-done.recv = bf16[8,176,128]{2,1,0:T(8,128)(2,1)S(1)} async-done(((bf16[8,176,128]{2,1,0:T(8,128)(2,1)}), bf16[8,176,128]{2,1,0:T(8,128)(2,1)S(1)}, u32[]{:S(2)}, u32[]{:S(2)}) %all-to-all-start) | async-done | bytes 360480 | tf_op jit(solution)/shard_map/all_to_all | solution.py:247
  22.9 0.0 copy-done.2
  22.9 0.0 copy-done.3
  22.9 5.2 %pairs.1 = f32[512,256]{1,0:T(8,128)S(1)} custom-call(bf16[8,176,128]{2,1,0:T(8,128)(2,1)S(1)} %all-to-all-done.recv, s32[8]{0:T(128)S(1)} %copy-done.2, s32[8]{0:T(128)S(1)} %copy-done.3, s32[256]{0:T(256)S(1)} %copy-done.1, s32[1,256]{1,0:T(1,128)S(1)} %broadcast_in_dim_tile.3.tiled), custom_call_target="tpu_custom_call" | custom-call | tf_op jit(solution)/shard_map/pairs/pallas_call | solution.py:249
  28.1 12.2 %all_to_all.10.recv = f32[8,64,256]{2,1,0:T(8,128)S(1)} all-to-all(f32[8,64,256]{2,1,0:T(8,128)S(1)} %bitcast.2), channel_id=1, replica_groups=mesh['date'=8,'strip'=4] {'date'}, dimensions={0} | all-to-all | bytes 1048576 | tf_op jit(solution)/shard_map/all_to_all | solution.py:264
  40.3 2.2 %join.1 = f32[512,256]{1,0:T(8,128)} custom-call(f32[8,64,256]{2,1,0:T(8,128)S(1)} %all_to_all.10.recv), custom_call_target="tpu_custom_call" | custom-call | tf_op jit(solution)/shard_map/join/pallas_call | solution.py:266
  (1 shorter events, 0.0 us)
Async XLA Ops:
  0.0 9.7 %copy-start = (bf16[2,2,32,1024]{3,2,1,0:T(8,128)(2,1)S(1)}, bf16[2,2,32,1024]{3,2,1,0:T(8,128)(2,1)}, u32[]{:S(2)}) copy-start(bf16[2,2,32,1024]{3,2,1,0:T(8,128)(2,1)} %slc.1) | copy-start | bytes 786436
  0.9 7.2 %collective-permute-start.1 = (bf16[2,2,5,1024]{3,2,1,0:T(8,128)(2,1)S(1)}, bf16[2,2,5,1024]{3,2,1,0:T(8,128)(2,1)S(1)}, u32[]{:S(2)}, u32[]{:S(2)}) collective-permute-start(bf16[2,2,5,1024]{3,2,1,0:T(8,128)(2,1)S(1)} %get-tuple-element.5), channel_id=1, source_target_pairs={{1,0},{2,1},{3,2},{5,4},{6,5},{7,6},{9,8},{10,9},{11,10},{13,12},{... | collective-permute-start | bytes 122888 | tf_op jit(solution)/shard_map/ppermute | solution.py:232
  2.2 7.5 %collective-permute-start = (bf16[2,2,5,1024]{3,2,1,0:T(8,128)(2,1)S(1)}, bf16[2,2,5,1024]{3,2,1,0:T(8,128)(2,1)S(1)}, u32[]{:S(2)}, u32[]{:S(2)}) collective-permute-start(bf16[2,2,5,1024]{3,2,1,0:T(8,128)(2,1)S(1)} %get-tuple-element.6), channel_id=1, source_target_pairs={{0,1},{1,2},{2,3},{4,5},{5,6},{6,7},{8,9},{9,10},{10,11},{12,13},{... | collective-permute-start | bytes 122888 | tf_op jit(solution)/shard_map/ppermute | solution.py:231
  10.8 12.2 %all-to-all-start = ((bf16[8,176,128]{2,1,0:T(8,128)(2,1)}), bf16[8,176,128]{2,1,0:T(8,128)(2,1)S(1)}, u32[]{:S(2)}, u32[]{:S(2)}) async-start(bf16[8,176,128]{2,1,0:T(8,128)(2,1)} %pack.1), calls=%async_computation | async-start | bytes 720896 | tf_op jit(solution)/shard_map/all_to_all | solution.py:247
  14.9 0.7 %copy-start.1 = (s32[256]{0:T(256)S(1)}, s32[256]{0:T(256)}, u32[]{:S(2)}) copy-start(s32[256]{0:T(256)} %rg.1) | copy-start | bytes 3076
  15.7 7.2 %copy-start.2 = (s32[8]{0:T(128)S(1)}, s32[8]{0:T(128)}, u32[]{:S(2)}) copy-start(s32[8]{0:T(128)} %order.1) | copy-start | bytes 100
  15.7 7.2 %copy-start.3 = (s32[8]{0:T(128)S(1)}, s32[8]{0:T(128)}, u32[]{:S(2)}) copy-start(s32[8]{0:T(128)} %az.1) | copy-start | bytes 100

commit v2 on v1

v2 whole, which is shorter than its diff:
```python
import functools

import jax
import jax.numpy as jnp
from jax import lax
from jax.experimental import pallas as pl
from jax.experimental.pallas import tpu as pltpu
from jax.sharding import PartitionSpec as P

STEP = 4
HALO = 5
REACH = 2
EDGE = 4
LANES = 128
GROUP = 16
VMEM = pl.BlockSpec(memory_space=pltpu.VMEM)
SMEM = pl.BlockSpec(memory_space=pltpu.SMEM)
PARAMS = pltpu.CompilerParams(vmem_limit_bytes=48 * 1024 * 1024)

epsilon = 1e-06


def iota(shape, dim):
    return lax.broadcasted_iota(jnp.int32, shape, dim)


def row_of(part, line, lines):
    if line < HALO:
        return part * HALO + line
    if line >= lines - HALO:
        return GROUP + part * HALO + line - (lines - HALO)
    middle = part * (lines - 2 * HALO) + line - HALO
    spare = GROUP - 2 * HALO - EDGE
    if middle < spare:
        return 2 * HALO + EDGE + middle
    if middle < 2 * spare:
        return GROUP + 2 * HALO + EDGE + middle - spare
    return 2 * GROUP + middle - 2 * spare


def place_of(date, row, per, date_rows):
    if row < GROUP:
        return date * GROUP + row
    if row < 2 * GROUP:
        return (per + date - 1) * GROUP + row
    return 2 * per * GROUP + date * (date_rows - 2 * GROUP) + row - 2 * GROUP


def rows_of_date(lines):
    return 2 * GROUP + 2 * (lines - 2 * HALO) - 2 * (GROUP - 2 * HALO - EDGE)


def runs(part, lines):
    found = []
    for line in range(lines):
        row = row_of(part, line, lines)
        if line and row == row_of(part, line - 1, lines) + 1 and row % GROUP:
            found[-1][1] += 1
        else:
            found.append([line, 1])
    return found


def pack_kernel(blocks, per, lines, chunk, slc, send, stage):
    date_rows = rows_of_date(lines)
    span = blocks * chunk
    shape = (EDGE * blocks, span)
    place = iota(shape, 0) % EDGE
    wanted = iota(shape, 0) // EDGE * chunk + jnp.where(place < REACH, place - REACH, place - REACH + chunk)
    picks = (iota(shape, 1) == wanted).astype(jnp.bfloat16)
    lane = iota((EDGE * blocks, LANES), 1)
    edges = []
    for date in range(per):
        mine = jnp.zeros((EDGE * blocks, LANES), jnp.float32)
        for part in range(2):
            samples = slc[part, date]
            for first, count in runs(part, lines):
                at = place_of(date, row_of(part, first, lines), per, date_rows)
                stage[at : at + count, :] = samples[first : first + count].astype(jnp.float32)
            found = lax.dot_general(picks, samples, (((1,), (1,)), ((), ())), preferred_element_type=jnp.float32)
            found = jnp.concatenate([found, jnp.zeros((EDGE * blocks, LANES - lines), jnp.float32)], axis=1)
            mine += pltpu.roll(found, part * (LANES // 2), 1) if part else found
        edges.append(mine)
    for block in range(blocks):
        for date in range(per):
            for group in range(2):
                at = place_of(date, group * GROUP + 2 * HALO, per, date_rows)
                value = edges[date][block * EDGE : (block + 1) * EDGE]
                if chunk == LANES:
                    stage[at : at + EDGE, block * LANES : (block + 1) * LANES] = value
        if chunk == LANES:
            piece = stage[:, block * chunk : (block + 1) * chunk]
        else:
            piece = stage[:, block * chunk : (block + 1) * chunk]
            piece = jnp.concatenate([piece, jnp.zeros((per * date_rows, LANES - chunk), jnp.float32)], axis=1)
            row = iota((per * date_rows, LANES), 0)
            for date in range(per):
                for group in range(2):
                    at = place_of(date, group * GROUP + 2 * HALO, per, date_rows)
                    for k in range(EDGE):
                        value = edges[date][block * EDGE + k : block * EDGE + k + 1]
                        piece = jnp.where(row == at + k, value, piece)
        send[block] = piece.astype(jnp.bfloat16)


def weight_kernel(lines, chunk, az, tiled, weights):
    out_rows = lines // STEP
    cols = chunk // STEP
    wide = out_rows * cols
    depth = out_rows * 2 * LANES
    shape = (LANES, wide)
    col = iota(shape, 1) % cols
    out_row = iota(shape, 1) // cols
    box = jnp.abs(iota(shape, 0) - STEP * col - tiled[...]) <= REACH
    for o in range(out_rows):
        mine = (box & (out_row == o)).astype(jnp.bfloat16)
        weights[2 * o * LANES : (2 * o + 1) * LANES, :] = mine
        weights[(2 * o + 1) * LANES : (2 * o + 2) * LANES, :] = mine
    turn = iota(shape, 0) % (LANES // 2)
    line = jnp.where(turn < lines + HALO, turn + HALO, turn + HALO - LANES // 2)
    lower = jnp.zeros(shape, jnp.int32)
    for o in range(out_rows):
        lower = jnp.where(out_row == o, STEP * o + az[o], lower)
    window = (line >= lower) & (line <= lower + 2 * HALO)
    for side, edge_col in ((0, 0), (1, cols - 1)):
        mine = (window & (col == edge_col)).astype(jnp.bfloat16)
        for term in range(2):
            start = depth + (2 * side + term) * LANES
            weights[start : start + LANES, :] = mine


def to_sublanes(blocks, per, rows, place, source, target):
    dates = blocks * per
    for block in range(blocks):
        value = source[block].astype(jnp.float32)
        for date in range(per):
            for row in range(0, rows, 8):
                at = place(date, row)
                target[pl.ds(row * dates + block * per + date, 8, stride=dates), :] = value[at : at + 8]


def spread_kernel(blocks, per, lines, recv, x):
    date_rows = rows_of_date(lines)
    to_sublanes(blocks, per, date_rows, lambda date, row: place_of(date, row, per, date_rows), recv, x)


def split(value):
    high = value.astype(jnp.bfloat16)
    return high, (value - high.astype(jnp.float32)).astype(jnp.bfloat16)


def pair_kernel(
    blocks, per, lines, chunk, group, x, low, high, order, az, rg, weights, send, below, above, edges, turned, left, power
):
    dates = blocks * per
    out_rows = lines // STEP
    cols = chunk // STEP
    wide = out_rows * cols
    me = lax.axis_index("date")
    depth = out_rows * 2 * LANES

    to_sublanes(blocks, per, GROUP, lambda date, row: date * GROUP + row, low, below)
    to_sublanes(blocks, per, GROUP, lambda date, row: date * GROUP + row, high, above)
    lane = iota((dates, LANES), 1)
    turn = lane % (LANES // 2)
    for k in range(EDGE):
        at = (2 * HALO + k) * dates
        lower_part = pltpu.roll(below[at : at + dates, :], lines, 1)
        upper_part = pltpu.roll(above[at : at + dates, :], lines, 1)
        value = jnp.where(turn < lines, x[at : at + dates, :], jnp.where(turn < lines + HALO, upper_part, lower_part))
        edges[k * dates : (k + 1) * dates, :] = value
        value = pltpu.roll(value, LANES // 2, 1)
        turned[k * dates : (k + 1) * dates, :] = jnp.where(lane < LANES // 2, value, -value)
    first = rg[me * cols]
    last = rg[me * cols + cols - 1]
    edge_on = (first <= 0, first <= 1, last >= 2, last >= 3)

    def where_line(part, line):
        if line < HALO:
            return below, part * HALO + line
        if line >= lines + HALO:
            return above, part * HALO + line - (lines + HALO)
        return x, row_of(part, line - HALO, lines)

    def one_date(first_date, step, carry):
        date = first_date + step
        target = (step // per * 2) * per + step % per
        for tile in range(dates // 16):

            def own(ref, row):
                return ref[pl.ds(row * dates + date, 1), :]

            def others(ref, row):
                return ref[row * dates + tile * 16 : row * dates + tile * 16 + 16, :]

            real, imag = [], []
            for line in range(lines + 2 * HALO):
                at_re, at_im = where_line(0, line), where_line(1, line)
                re_i, im_i = own(*at_re), own(*at_im)
                re_j, im_j = others(*at_re), others(*at_im)
                real.append(re_i * re_j + im_i * im_j)
                imag.append(im_i * re_j - re_i * im_j)
            for part, product in enumerate((real, imag)):
                start = pl.multiple_of((target + part * per) * dates + tile * 16, 16)
                at_rows = pl.ds(start, 16)
                quads = []
                for k in range(out_rows + 1):
                    q = product[STEP * k + 3 : STEP * k + 7]
                    quads.append((q[0] + q[1]) + (q[2] + q[3]))
                for o in range(out_rows):
                    total = quads[o] + quads[o + 1]
                    for k in range(3):
                        total += jnp.where(az[o] <= k, product[STEP * o + k], product[STEP * o + 11 + k])
                    upper, rest = split(total)
                    left[at_rows, 2 * o * LANES : (2 * o + 1) * LANES] = upper
                    left[at_rows, (2 * o + 1) * LANES : (2 * o + 2) * LANES] = rest
                for side in range(2):
                    total = jnp.zeros((16, LANES), jnp.float32)
                    for edge in (2 * side, 2 * side + 1):
                        mine = own(turned if part else edges, edge)
                        total += jnp.where(edge_on[edge], mine * others(edges, edge), 0.0)
                    upper, rest = split(total)
                    start_col = depth + 2 * side * LANES
                    left[at_rows, start_col : start_col + LANES] = upper
                    left[at_rows, start_col + LANES : start_col + 2 * LANES] = rest
        return carry

    for first_date in range(0, dates, group):
        lax.fori_loop(0, group, functools.partial(one_date, first_date), 0)
        sums = jnp.dot(left[...], weights[...], preferred_element_type=jnp.float32)
        send[first_date * 2 * dates : (first_date + group) * 2 * dates, :] = sums
    for date in range(dates):
        at_row = (date // per * 2 * per + date % per) * dates + date
        power[date : date + 1, :] = send[at_row : at_row + 1, :]
    scale = lax.rsqrt(power[...] + epsilon)
    power[...] = scale
    position = iota((dates, wide), 0)
    rank = jnp.zeros((dates, wide), jnp.int32)
    for block in range(blocks):
        rank = jnp.where(position // per == block, order[block] * per + position % per, rank)
    for date in range(dates):
        later = rank > order[date // per] * per + date % per
        factor = jnp.where(later, scale * power[date : date + 1, :], 0.0)
        for part in range(2):
            start = ((date // per * 2 + part) * per + date % per) * dates
            send[start : start + dates, :] = send[start : start + dates, :] * factor


def join_kernel(blocks, count, out_rows, cols, recv, out, halves):
    per_tile = LANES // cols
    lane = iota((8, LANES), 1) // cols
    for start in range(0, count, 8):
        for o_tile in range(out_rows // per_tile):
            for d_tile in range(blocks // per_tile):
                tiles = [
                    recv[d_tile * per_tile + d, start : start + 8, o_tile * LANES : (o_tile + 1) * LANES]
                    for d in range(per_tile)
                ]
                width = 1
                while width < per_tile:
                    swap = [None] * per_tile
                    upper = (lane // width) % 2 == 1
                    for a in range(per_tile):
                        if (a // width) % 2 == 0:
                            b = a + width
                            shift = width * cols
                            swap[a] = jnp.where(upper, pltpu.roll(tiles[b], shift, 1), tiles[a])
                            swap[b] = jnp.where(upper, tiles[b], pltpu.roll(tiles[a], LANES - shift, 1))
                    tiles = swap
                    width *= 2
                for o in range(per_tile):
                    at = start * out_rows + o_tile * per_tile + o
                    halves[d_tile, pl.ds(at, 8, stride=out_rows), :] = tiles[o]
    for d_tile in range(blocks // per_tile):
        out[:, d_tile * LANES : (d_tile + 1) * LANES] = halves[d_tile]


def on_device(slc, block_order, az_offset, rg_offset):
    blocks = lax.axis_size("date")
    strips = lax.axis_size("strip")
    per, lines, span = slc.shape[1:]
    dates = blocks * per
    chunk = span // blocks
    out_rows = lines // STEP
    cols = chunk // STEP
    wide = out_rows * cols
    date_rows = rows_of_date(lines)
    depth = (out_rows + 2) * 2 * LANES
    group = max(per, 256 // dates)
    me = lax.axis_index("date")

    send = pl.pallas_call(
        functools.partial(pack_kernel, blocks, per, lines, chunk),
        out_shape=jax.ShapeDtypeStruct((blocks, per * date_rows, LANES), jnp.bfloat16),
        in_specs=[VMEM],
        out_specs=VMEM,
        scratch_shapes=[pltpu.VMEM((per * date_rows, span), jnp.float32)],
        compiler_params=PARAMS,
        name="pack",
    )(slc)
    recv = lax.all_to_all(send, "date", 0, 0, tiled=True)
    tiled = jnp.tile(lax.dynamic_slice_in_dim(rg_offset, me * cols, cols), out_rows)[None]
    weights = pl.pallas_call(
        functools.partial(weight_kernel, lines, chunk),
        out_shape=jax.ShapeDtypeStruct((depth, wide), jnp.bfloat16),
        in_specs=[SMEM, VMEM],
        out_specs=VMEM,
        compiler_params=PARAMS,
        cost_estimate=pl.CostEstimate(flops=0, bytes_accessed=4 * 1024 * 1024, transcendentals=0),
        name="weights",
    )(az_offset, tiled)

    forward = [(i, i + 1) for i in range(strips - 1)]
    backward = [(target, source) for source, target in forward]
    edge_rows = per * GROUP
    low = lax.ppermute(recv[:, edge_rows : 2 * edge_rows], "strip", forward)
    high = lax.ppermute(recv[:, :edge_rows], "strip", backward)
    x = pl.pallas_call(
        functools.partial(spread_kernel, blocks, per, lines),
        out_shape=jax.ShapeDtypeStruct((date_rows * dates, LANES), jnp.float32),
        in_specs=[VMEM],
        out_specs=VMEM,
        compiler_params=PARAMS,
        cost_estimate=pl.CostEstimate(flops=0, bytes_accessed=4 * 1024 * 1024, transcendentals=0),
        name="spread",
    )(recv)
    pairs = pl.pallas_call(
        functools.partial(pair_kernel, blocks, per, lines, chunk, group),
        out_shape=jax.ShapeDtypeStruct((dates * 2 * dates, wide), jnp.float32),
        in_specs=[VMEM, VMEM, VMEM, SMEM, SMEM, SMEM, VMEM],
        out_specs=VMEM,
        scratch_shapes=[
            pltpu.VMEM((GROUP * dates, LANES), jnp.float32),
            pltpu.VMEM((GROUP * dates, LANES), jnp.float32),
            pltpu.VMEM((EDGE * dates, LANES), jnp.float32),
            pltpu.VMEM((EDGE * dates, LANES), jnp.float32),
            pltpu.VMEM((group * 2 * dates, depth), jnp.bfloat16),
            pltpu.VMEM((dates, wide), jnp.float32),
        ],
        compiler_params=PARAMS,
        name="pairs",
    )(x, low, high, block_order, az_offset, rg_offset, weights)
    count = 2 * per * dates
    back = lax.all_to_all(pairs.reshape(blocks, count, wide), "date", 0, 0, tiled=True)
    if LANES % cols == 0 and out_rows * cols % LANES == 0 and blocks * cols % LANES == 0:
        out = pl.pallas_call(
            functools.partial(join_kernel, blocks, count, out_rows, cols),
            out_shape=jax.ShapeDtypeStruct((count * out_rows, blocks * cols), jnp.float32),
            in_specs=[VMEM],
            out_specs=VMEM,
            scratch_shapes=[pltpu.VMEM((blocks * cols // LANES, count * out_rows, LANES), jnp.float32)],
            compiler_params=PARAMS,
            name="join",
        )(back)
    else:
        out = back.reshape(blocks, count, out_rows, cols).transpose(1, 2, 0, 3)
    return out.reshape(2, per, dates, out_rows, blocks * cols)


def solution(mesh):
    placed = (P(None, "date", "strip", None), P(), P("strip"), P())
    return jax.shard_map(
        on_device,
        mesh=mesh,
        in_specs=placed,
        out_specs=P(None, "date", None, "strip", None),
        check_vma=False,
    )
```

time: 42.8 us -> 40.2 us (0.939)
  blocking collectives: 12.2 us -> 24.4 us
  waiting for transfers between devices: 9.03 us -> 0.72 us
  starting transfers between devices: 11 us -> 5.84 us
  Pallas kernels: 8.48 us -> 7.76 us
  local copies, waits for them, and re-layouts: 1.78 us -> 1.13 us
    all_to_all x0 -> x1, blocking collectives: none -> 12.3 us  [on_device(): recv = lax.all_to_all(send, 'date', 0, 0, tiled=True)]
    all_to_all x1 -> x0, waiting for transfers between devices: 7.15 us -> none  [on_device(): recv = lax.all_to_all(send, 'date', 0, 0, tiled=True)]
    all_to_all x1 -> x0, starting transfers between devices: 4.16 us -> none  [on_device(): recv = lax.all_to_all(send, 'date', 0, 0, tiled=True)]
    ppermute x2, waiting for transfers between devices: 1.88 us -> 0.72 us  [the longest x1 0.72 us: on_device(): low = lax.ppermute(recv[:, edge_rows:2 * edge_rows], 'strip', forward)]
    ppermute x2, starting transfers between devices: 6.85 us -> 5.84 us  [the longest x1 4.55 us: on_device(): low = lax.ppermute(recv[:, edge_rows:2 * edge_rows], 'strip', forward)]
    pallas_call x0 -> x2, Pallas kernels: none -> 0.96 us  [the longest x1 0.68 us: on_device(): pl.pallas_call(functools.partial(weight_kernel, lines, chunk), out_shape=...]
    slice x1, local copies, waits for them, and re-layouts: 0.93 us -> 0.01 us  [on_device(): high = lax.ppermute(recv[:, :edge_rows], 'strip', backward)]
    pallas_call x1, Pallas kernels: 5.18 us -> 4.3 us  [on_device(): pl.pallas_call(functools.partial(pair_kernel, blocks, per, lines, chunk,...]
  transfers between devices with their start and end apart: 3 -> 2, of which waited for: 3 -> 1; matrix products, arithmetic and copies ran while one was open for 0% -> 0% of each run, Pallas kernels for 0% -> 2%
where the time goes in v2:
time: 40.2 us; the launch traced here: 39.9 us
  blocking collectives  24.4 us (61%)
  Pallas kernels  7.76 us (19%)
  starting transfers between devices  5.84 us (15%)
  local copies, waits for them, and re-layouts  1.13 us (3%)
  waiting for transfers between devices  0.72 us (2%)
    all_to_all x1, blocking collectives, on_device(): recv = lax.all_to_all(send, 'date', 0, 0, tiled=True)  12.3 us
    all_to_all x1, blocking collectives, on_device(): lax.all_to_all(pairs.reshape(blocks, count, wide), 'date', 0, 0, tiled=True)  12.2 us
    ppermute x1, starting transfers between devices, on_device(): low = lax.ppermute(recv[:, edge_rows:2 * edge_rows], 'strip', forward)  4.55 us
    pallas_call x1, Pallas kernels, on_device(): pl.pallas_call(functools.partial(pair_kernel, blocks, per, lines, chunk,...  4.3 us
    pallas_call x1, Pallas kernels, on_device(): pl.pallas_call(functools.partial(join_kernel, blocks, count, out_rows, co...  2.22 us
    ppermute x1, starting transfers between devices, on_device(): high = lax.ppermute(recv[:, :edge_rows], 'strip', backward)  1.29 us
    unnamed x8, local copies, waits for them, and re-layouts  0.96 us
  transfers between devices with their start and end apart: 2, of which 1 were waited for; matrix products, arithmetic and copies ran while one was open for 0% of the time, Pallas kernels for 2%

profile of v2, /device:TPU:0, one launch (start us, length us, event | category | flops | bytes accessed | tf_op | source)
XLA Modules:
  0.0 39.9 jit_solution(2508182758786745752)
XLA Ops:
  0.0 0.0 copy-start
  0.0 0.9 %copy-done = bf16[2,2,32,1024]{3,2,1,0:T(8,128)(2,1)S(1)} copy-done((bf16[2,2,32,1024]{3,2,1,0:T(8,128)(2,1)S(1)}, bf16[2,2,32,1024]{3,2,1,0:T(8,128)(2,1)}, u32[]{:S(2)}) %copy-start) | copy-done | bytes 262168
  1.0 0.0 copy-start.2
  1.0 0.0 copy-start.1
  1.0 0.3 pack.1
  1.2 12.3 %all_to_all.10.recv = bf16[8,144,128]{2,1,0:T(8,128)(2,1)S(1)} all-to-all(bf16[8,144,128]{2,1,0:T(8,128)(2,1)S(1)} %pack.1), channel_id=1, replica_groups=mesh['date'=8,'strip'=4] {'date'}, dimensions={0} | all-to-all | bytes 589824 | tf_op jit(solution)/shard_map/all_to_all | solution.py:301
  13.5 0.0 copy-start.3
  13.5 1.3 %collective-permute-start.1 = (bf16[8,32,128]{2,1,0:T(8,128)(2,1)S(1)}, bf16[8,32,128]{2,1,0:T(8,128)(2,1)S(1)}, u32[]{:S(2)}, u32[]{:S(2)}) collective-permute-start(bf16[8,32,128]{2,1,0:T(8,128)(2,1)S(1)} %get-tuple-element.5), channel_id=1, source_target_pairs={{1,0},{2,1},{3,2},{5,4},{6,5},{7,6},{9,8},{10,9},{11,10},{13,12},{... | collective-permute-start | bytes 196616 | tf_op jit(solution)/shard_map/ppermute | solution.py:317
  14.8 4.5 %collective-permute-start = (bf16[8,32,128]{2,1,0:T(8,128)(2,1)S(1)}, bf16[8,32,128]{2,1,0:T(8,128)(2,1)S(1)}, u32[]{:S(2)}, u32[]{:S(2)}) collective-permute-start(bf16[8,32,128]{2,1,0:T(8,128)(2,1)S(1)} %get-tuple-element.6), channel_id=1, source_target_pairs={{0,1},{1,2},{2,3},{4,5},{5,6},{6,7},{8,9},{9,10},{10,11},{12,13},{... | collective-permute-start | bytes 196616 | tf_op jit(solution)/shard_map/ppermute | solution.py:316
  19.4 0.0 copy-done.2
  19.4 0.1 dynamic_slice.3
  19.5 0.1 broadcast_in_dim_tile.3.tiled
  19.6 0.0 copy-done.1
  19.6 0.7 %weights.1 = bf16[2560,256]{1,0:T(8,128)(2,1)S(1)} custom-call(s32[8]{0:T(128)S(1)} %copy-done.1, s32[1,256]{1,0:T(1,128)S(1)} %broadcast_in_dim_tile.3.tiled), custom_call_target="tpu_custom_call" | custom-call | bytes 4194304 | tf_op jit(solution)/shard_map/weights/pallas_call | solution.py:303
  20.2 0.3 spread.1.x
  20.5 0.0 collective-permute-done.1.high
  20.5 0.7 %collective-permute-done.low = bf16[8,32,128]{2,1,0:T(8,128)(2,1)S(1)} collective-permute-done((bf16[8,32,128]{2,1,0:T(8,128)(2,1)S(1)}, bf16[8,32,128]{2,1,0:T(8,128)(2,1)S(1)}, u32[]{:S(2)}, u32[]{:S(2)}) %collective-permute-start) | collective-permute-done | bytes 65568 | tf_op jit(solution)/shard_map/ppermute | solution.py:316
  21.3 0.0 copy-done.3
  21.3 4.3 %pairs.1 = f32[512,256]{1,0:T(8,128)S(1)} custom-call(f32[1152,128]{1,0:T(8,128)S(1)} %spread.1.x, bf16[8,32,128]{2,1,0:T(8,128)(2,1)S(1)} %collective-permute-done.low, bf16[8,32,128]{2,1,0:T(8,128)(2,1)S(1)} %collective-permute-done.1.high, s32[8]{0:T(128)S(1)} %copy-done.3, s32[8]{0:T(128)S(1)} %copy-done.1, s32[256]{0:T(256)S(1)} %copy-done.2, ...), custom_call_target="tpu_custom_call" | custom-call | tf_op jit(solution)/shard_map/pairs/pallas_call | solution.py:327
  25.6 12.2 %all_to_all.11.recv = f32[8,64,256]{2,1,0:T(8,128)S(1)} all-to-all(f32[8,64,256]{2,1,0:T(8,128)S(1)} %bitcast.2), channel_id=1, replica_groups=mesh['date'=8,'strip'=4] {'date'}, dimensions={0} | all-to-all | bytes 1048576 | tf_op jit(solution)/shard_map/all_to_all | solution.py:344
  37.7 2.2 %join.1 = f32[512,256]{1,0:T(8,128)} custom-call(f32[8,64,256]{2,1,0:T(8,128)S(1)} %all_to_all.11.recv), custom_call_target="tpu_custom_call" | custom-call | tf_op jit(solution)/shard_map/join/pallas_call | solution.py:346
  (2 shorter events, 0.0 us)
Async XLA Ops:
  0.0 0.9 %copy-start = (bf16[2,2,32,1024]{3,2,1,0:T(8,128)(2,1)S(1)}, bf16[2,2,32,1024]{3,2,1,0:T(8,128)(2,1)}, u32[]{:S(2)}) copy-start(bf16[2,2,32,1024]{3,2,1,0:T(8,128)(2,1)} %slc.1) | copy-start | bytes 786436
  1.0 18.4 %copy-start.2 = (s32[256]{0:T(256)S(1)}, s32[256]{0:T(256)}, u32[]{:S(2)}) copy-start(s32[256]{0:T(256)} %rg.1) | copy-start | bytes 3076
  1.0 18.6 %copy-start.1 = (s32[8]{0:T(128)S(1)}, s32[8]{0:T(128)}, u32[]{:S(2)}) copy-start(s32[8]{0:T(128)} %az.3) | copy-start | bytes 100
  13.5 7.8 %copy-start.3 = (s32[8]{0:T(128)S(1)}, s32[8]{0:T(128)}, u32[]{:S(2)}) copy-start(s32[8]{0:T(128)} %order.1) | copy-start | bytes 100
  13.5 7.0 %collective-permute-start.1 = (bf16[8,32,128]{2,1,0:T(8,128)(2,1)S(1)}, bf16[8,32,128]{2,1,0:T(8,128)(2,1)S(1)}, u32[]{:S(2)}, u32[]{:S(2)}) collective-permute-start(bf16[8,32,128]{2,1,0:T(8,128)(2,1)S(1)} %get-tuple-element.5), channel_id=1, source_target_pairs={{1,0},{2,1},{3,2},{5,4},{6,5},{7,6},{9,8},{10,9},{11,10},{13,12},{... | collective-permute-start | bytes 196616 | tf_op jit(solution)/shard_map/ppermute | solution.py:317
  14.8 6.4 %collective-permute-start = (bf16[8,32,128]{2,1,0:T(8,128)(2,1)S(1)}, bf16[8,32,128]{2,1,0:T(8,128)(2,1)S(1)}, u32[]{:S(2)}, u32[]{:S(2)}) collective-permute-start(bf16[8,32,128]{2,1,0:T(8,128)(2,1)S(1)} %get-tuple-element.6), channel_id=1, source_target_pairs={{0,1},{1,2},{2,3},{4,5},{5,6},{6,7},{8,9},{9,10},{10,11},{12,13},{... | collective-permute-start | bytes 196616 | tf_op jit(solution)/shard_map/ppermute | solution.py:316

commit v3 on v2

--- a/solution.py
+++ b/solution.py
@@ -18,6 +18,10 @@
 PARAMS = pltpu.CompilerParams(vmem_limit_bytes=48 * 1024 * 1024)
 
 epsilon = 1e-06
+LEVELS = 8.0
+LOWEST, HIGHEST = -880.0, 64.0
+TOP = 32760.0
+LOG_2 = 0.6931471805599453
 
 
 def iota(shape, dim):
@@ -150,7 +154,7 @@
 
 
 def pair_kernel(
-    blocks, per, lines, chunk, group, x, low, high, order, az, rg, weights, send, below, above, edges, turned, left, power
+    blocks, per, lines, chunk, group, x, low, high, order, az, rg, weights, send, sums, below, above, edges, turned, left, power
 ):
     dates = blocks * per
     out_rows = lines // STEP
@@ -227,52 +231,84 @@
 
     for first_date in range(0, dates, group):
         lax.fori_loop(0, group, functools.partial(one_date, first_date), 0)
-        sums = jnp.dot(left[...], weights[...], preferred_element_type=jnp.float32)
-        send[first_date * 2 * dates : (first_date + group) * 2 * dates, :] = sums
+        found = jnp.dot(left[...], weights[...], preferred_element_type=jnp.float32)
+        sums[first_date * 2 * dates : (first_date + group) * 2 * dates, :] = found
     for date in range(dates):
         at_row = (date // per * 2 * per + date % per) * dates + date
-        power[date : date + 1, :] = send[at_row : at_row + 1, :]
+        power[date : date + 1, :] = sums[at_row : at_row + 1, :]
     scale = lax.rsqrt(power[...] + epsilon)
     power[...] = scale
     position = iota((dates, wide), 0)
+    column = iota((dates, wide), 1)
     rank = jnp.zeros((dates, wide), jnp.int32)
     for block in range(blocks):
         rank = jnp.where(position // per == block, order[block] * per + position % per, rank)
     for date in range(dates):
         later = rank > order[date // per] * per + date % per
-        factor = jnp.where(later, scale * power[date : date + 1, :], 0.0)
-        for part in range(2):
-            start = ((date // per * 2 + part) * per + date % per) * dates
-            send[start : start + dates, :] = send[start : start + dates, :] * factor
-
-
-def join_kernel(blocks, count, out_rows, cols, recv, out, halves):
+        factor = scale * power[date : date + 1, :]
+        starts = [((date // per * 2 + part) * per + date % per) * dates for part in range(2)]
+        values = [jnp.where(later, sums[start : start + dates, :] * factor, 0.0) for start in starts]
+        largest = jnp.max(jnp.maximum(jnp.abs(values[0]), jnp.abs(values[1])), axis=1, keepdims=True)
+        level = jnp.floor(jnp.log(largest) * (LEVELS / LOG_2)) + 1.0
+        level = jnp.clip(level, LOWEST, HIGHEST)
+        codes = [jnp.floor(value * (jnp.exp(level * (-LOG_2 / LEVELS)) * TOP) + 0.5) for value in values]
+        header = jnp.sum(jnp.where(position == column, level, 0.0), axis=0, keepdims=True)
+        codes[0] = jnp.where(position == date, header, codes[0])
+        for start, code in zip(starts, codes):
+            send[start : start + dates, :] = code.astype(jnp.int32).astype(jnp.int16)
+
+
+def join_kernel(blocks, per, out_rows, cols, recv, out, halves):
+    dates = blocks * per
+    wide = out_rows * cols
     per_tile = LANES // cols
-    lane = iota((8, LANES), 1) // cols
-    for start in range(0, count, 8):
-        for o_tile in range(out_rows // per_tile):
-            for d_tile in range(blocks // per_tile):
-                tiles = [
-                    recv[d_tile * per_tile + d, start : start + 8, o_tile * LANES : (o_tile + 1) * LANES]
-                    for d in range(per_tile)
-                ]
-                width = 1
-                while width < per_tile:
-                    swap = [None] * per_tile
-                    upper = (lane // width) % 2 == 1
-                    for a in range(per_tile):
-                        if (a // width) % 2 == 0:
-                            b = a + width
-                            shift = width * cols
-                            swap[a] = jnp.where(upper, pltpu.roll(tiles[b], shift, 1), tiles[a])
-                            swap[b] = jnp.where(upper, tiles[b], pltpu.roll(tiles[a], LANES - shift, 1))
-                    tiles = swap
-                    width *= 2
-                for o in range(per_tile):
+    me = lax.axis_index("date")
+    step = pl.program_id(0)
+    part = step // per
+    own = me * per + step % per
+    lane = iota((dates, LANES), 1) // cols
+    position = iota((dates, wide), 0)
+    column = iota((dates, wide), 1)
+    values = []
+    for block in range(blocks):
+        codes = recv[block, pl.ds(pl.multiple_of(step * dates, 16), dates), :].astype(jnp.int32).astype(jnp.float32)
+        heads = recv[block, pl.ds(pl.multiple_of(step % per * dates, 16), dates), :].astype(jnp.int32).astype(jnp.float32)
+        header = jnp.sum(jnp.where(position == own, heads, 0.0), axis=0, keepdims=True)
+        level = jnp.sum(jnp.where(position == column, header, 0.0), axis=1, keepdims=True)
+        factor = jnp.exp(level * (LOG_2 / LEVELS)) * (1.0 / TOP)
+        values.append(jnp.where(position == own, 0.0, codes * factor))
+    for o_tile in range(out_rows // per_tile):
+        for d_tile in range(blocks // per_tile):
+            tiles = [
+                values[d_tile * per_tile + d][:, o_tile * LANES : (o_tile + 1) * LANES] for d in range(per_tile)
+            ]
+            width = 1
+            while width < per_tile:
+                swap = [None] * per_tile
+                upper = (lane // width) % 2 == 1
+                shift = width * cols
+                for a in range(per_tile):
+                    if (a // width) % 2 == 0:
+                        b = a + width
+                        swap[a] = jnp.where(upper, pltpu.roll(tiles[b], shift, 1), tiles[a])
+                        swap[b] = jnp.where(upper, tiles[b], pltpu.roll(tiles[a], LANES - shift, 1))
+                tiles = swap
+                width *= 2
+            for o in range(per_tile):
+                for start in range(0, dates, 8):
                     at = start * out_rows + o_tile * per_tile + o
-                    halves[d_tile, pl.ds(at, 8, stride=out_rows), :] = tiles[o]
+                    halves[d_tile, pl.ds(at, 8, stride=out_rows), :] = tiles[o][start : start + 8]
     for d_tile in range(blocks // per_tile):
         out[:, d_tile * LANES : (d_tile + 1) * LANES] = halves[d_tile]
+
+
+def decode(codes, me, per):
+    values = codes.astype(jnp.float32)
+    dates = codes.shape[3]
+    own = (me * per + jnp.arange(per))[:, None] == jnp.arange(dates)[None]
+    header = jnp.sum(jnp.where(own[None, :, :, None], values[:, 0], 0.0), axis=2)
+    factor = jnp.exp(header[:, :, :dates] * (LOG_2 / LEVELS)) * (1.0 / TOP)
+    return jnp.where(own[None, None, :, :, None], 0.0, values * factor[:, None, :, :, None])
 
 
 def on_device(slc, block_order, az_offset, rg_offset):
@@ -326,10 +362,11 @@
     )(recv)
     pairs = pl.pallas_call(
         functools.partial(pair_kernel, blocks, per, lines, chunk, group),
-        out_shape=jax.ShapeDtypeStruct((dates * 2 * dates, wide), jnp.float32),
+        out_shape=jax.ShapeDtypeStruct((dates * 2 * dates, wide), jnp.int16),
         in_specs=[VMEM, VMEM, VMEM, SMEM, SMEM, SMEM, VMEM],
         out_specs=VMEM,
         scratch_shapes=[
+            pltpu.VMEM((dates * 2 * dates, wide), jnp.float32),
             pltpu.VMEM((GROUP * dates, LANES), jnp.float32),
             pltpu.VMEM((GROUP * dates, LANES), jnp.float32),
             pltpu.VMEM((EDGE * dates, LANES), jnp.float32),
@@ -344,16 +381,18 @@
     back = lax.all_to_all(pairs.reshape(blocks, count, wide), "date", 0, 0, tiled=True)
     if LANES % cols == 0 and out_rows * cols % LANES == 0 and blocks * cols % LANES == 0:
         out = pl.pallas_call(
-            functools.partial(join_kernel, blocks, count, out_rows, cols),
+            functools.partial(join_kernel, blocks, per, out_rows, cols),
+            grid=(2 * per,),
             out_shape=jax.ShapeDtypeStruct((count * out_rows, blocks * cols), jnp.float32),
-            in_specs=[VMEM],
-            out_specs=VMEM,
-            scratch_shapes=[pltpu.VMEM((blocks * cols // LANES, count * out_rows, LANES), jnp.float32)],
+            in_specs=[pl.BlockSpec((blocks, count, wide), lambda step: (0, 0, 0))],
+            out_specs=pl.BlockSpec((dates * out_rows, blocks * cols), lambda step: (step, 0)),
+            scratch_shapes=[pltpu.VMEM((blocks * cols // LANES, dates * out_rows, LANES), jnp.float32)],
             compiler_params=PARAMS,
             name="join",
         )(back)
     else:
-        out = back.reshape(blocks, count, out_rows, cols).transpose(1, 2, 0, 3)
+        values = decode(back.reshape(blocks, 2, per, dates, wide), me, per)
+        out = values.reshape(blocks, count, out_rows, cols).transpose(1, 2, 0, 3)
     return out.reshape(2, per, dates, out_rows, blocks * cols)
 
 

time: 40.2 us -> 37.6 us (0.935)
  blocking collectives: 24.4 us -> 21.6 us
    all_to_all x1, blocking collectives: 12.2 us -> 9.35 us  [on_device(): lax.all_to_all(pairs.reshape(blocks, count, wide), 'date', 0, 0, tiled=True)]
  transfers between devices with their start and end apart: 2 -> 2, of which waited for: 1 -> 1; matrix products, arithmetic and copies ran while one was open for 0% -> 0% of each run, Pallas kernels for 2% -> 3%
where the time goes in v3:
time: 37.6 us; the launch traced here: 37.3 us
  blocking collectives  21.6 us (57%)
  Pallas kernels  7.97 us (21%)
  starting transfers between devices  5.84 us (16%)
  local copies, waits for them, and re-layouts  1.13 us (3%)
  waiting for transfers between devices  0.72 us (2%)
    all_to_all x1, blocking collectives, on_device(): recv = lax.all_to_all(send, 'date', 0, 0, tiled=True)  12.3 us
    all_to_all x1, blocking collectives, on_device(): lax.all_to_all(pairs.reshape(blocks, count, wide), 'date', 0, 0, tiled=True)  9.35 us
    ppermute x1, starting transfers between devices, on_device(): low = lax.ppermute(recv[:, edge_rows:2 * edge_rows], 'strip', forward)  4.55 us
    pallas_call x1, Pallas kernels, on_device(): pl.pallas_call(functools.partial(pair_kernel, blocks, per, lines, chunk,...  4.53 us
    pallas_call x1, Pallas kernels, on_device(): pl.pallas_call(functools.partial(join_kernel, blocks, per, out_rows, cols...  2.2 us
    ppermute x1, starting transfers between devices, on_device(): high = lax.ppermute(recv[:, :edge_rows], 'strip', backward)  1.29 us
    unnamed x8, local copies, waits for them, and re-layouts  0.96 us
  transfers between devices with their start and end apart: 2, of which 1 were waited for; matrix products, arithmetic and copies ran while one was open for 0% of the time, Pallas kernels for 3%

profile of v3, /device:TPU:0, one launch (start us, length us, event | category | flops | bytes accessed | tf_op | source)
XLA Modules:
  0.0 37.3 jit_solution(14028006098805266040)
XLA Ops:
  0.0 0.0 copy-start
  0.0 0.9 %copy-done = bf16[2,2,32,1024]{3,2,1,0:T(8,128)(2,1)S(1)} copy-done((bf16[2,2,32,1024]{3,2,1,0:T(8,128)(2,1)S(1)}, bf16[2,2,32,1024]{3,2,1,0:T(8,128)(2,1)}, u32[]{:S(2)}) %copy-start) | copy-done | bytes 262168
  1.0 0.0 copy-start.2
  1.0 0.0 copy-start.1
  1.0 0.3 pack.1
  1.2 12.3 %all_to_all.10.recv = bf16[8,144,128]{2,1,0:T(8,128)(2,1)S(1)} all-to-all(bf16[8,144,128]{2,1,0:T(8,128)(2,1)S(1)} %pack.1), channel_id=1, replica_groups=mesh['date'=8,'strip'=4] {'date'}, dimensions={0} | all-to-all | bytes 589824 | tf_op jit(solution)/shard_map/all_to_all | solution.py:337
  13.5 0.0 copy-start.3
  13.5 1.3 %collective-permute-start.1 = (bf16[8,32,128]{2,1,0:T(8,128)(2,1)S(1)}, bf16[8,32,128]{2,1,0:T(8,128)(2,1)S(1)}, u32[]{:S(2)}, u32[]{:S(2)}) collective-permute-start(bf16[8,32,128]{2,1,0:T(8,128)(2,1)S(1)} %get-tuple-element.5), channel_id=1, source_target_pairs={{1,0},{2,1},{3,2},{5,4},{6,5},{7,6},{9,8},{10,9},{11,10},{13,12},{... | collective-permute-start | bytes 196616 | tf_op jit(solution)/shard_map/ppermute | solution.py:353
  14.8 4.5 %collective-permute-start = (bf16[8,32,128]{2,1,0:T(8,128)(2,1)S(1)}, bf16[8,32,128]{2,1,0:T(8,128)(2,1)S(1)}, u32[]{:S(2)}, u32[]{:S(2)}) collective-permute-start(bf16[8,32,128]{2,1,0:T(8,128)(2,1)S(1)} %get-tuple-element.6), channel_id=1, source_target_pairs={{0,1},{1,2},{2,3},{4,5},{5,6},{6,7},{8,9},{9,10},{10,11},{12,13},{... | collective-permute-start | bytes 196616 | tf_op jit(solution)/shard_map/ppermute | solution.py:352
  19.4 0.0 copy-done.2
  19.4 0.1 dynamic_slice.3
  19.5 0.1 broadcast_in_dim_tile.3.tiled
  19.6 0.0 copy-done.1
  19.6 0.7 %weights.1 = bf16[2560,256]{1,0:T(8,128)(2,1)S(1)} custom-call(s32[8]{0:T(128)S(1)} %copy-done.1, s32[1,256]{1,0:T(1,128)S(1)} %broadcast_in_dim_tile.3.tiled), custom_call_target="tpu_custom_call" | custom-call | bytes 4194304 | tf_op jit(solution)/shard_map/weights/pallas_call | solution.py:339
  20.2 0.3 spread.1.x
  20.5 0.0 collective-permute-done.1.high
  20.5 0.7 %collective-permute-done.low = bf16[8,32,128]{2,1,0:T(8,128)(2,1)S(1)} collective-permute-done((bf16[8,32,128]{2,1,0:T(8,128)(2,1)S(1)}, bf16[8,32,128]{2,1,0:T(8,128)(2,1)S(1)}, u32[]{:S(2)}, u32[]{:S(2)}) %collective-permute-start) | collective-permute-done | bytes 65568 | tf_op jit(solution)/shard_map/ppermute | solution.py:352
  21.3 0.0 copy-done.3
  21.3 4.5 %pairs.1 = s16[512,256]{1,0:T(8,128)(2,1)S(1)} custom-call(f32[1152,128]{1,0:T(8,128)S(1)} %spread.1.x, bf16[8,32,128]{2,1,0:T(8,128)(2,1)S(1)} %collective-permute-done.low, bf16[8,32,128]{2,1,0:T(8,128)(2,1)S(1)} %collective-permute-done.1.high, s32[8]{0:T(128)S(1)} %copy-done.3, s32[8]{0:T(128)S(1)} %copy-done.1, s32[256]{0:T(256)S(1)} %copy-done.2, ...), custom_call_target="tpu_custom_call" | custom-call | tf_op jit(solution)/shard_map/pairs/pallas_call | solution.py:363
  25.8 9.3 %all_to_all.11.recv = s16[8,64,256]{2,1,0:T(8,128)(2,1)S(1)} all-to-all(s16[8,64,256]{2,1,0:T(8,128)(2,1)S(1)} %bitcast.2), channel_id=1, replica_groups=mesh['date'=8,'strip'=4] {'date'}, dimensions={0} | all-to-all | bytes 524288 | tf_op jit(solution)/shard_map/all_to_all | solution.py:381
  35.1 2.2 %join.1 = f32[512,256]{1,0:T(8,128)} custom-call(s16[8,64,256]{2,1,0:T(8,128)(2,1)S(1)} %all_to_all.11.recv), custom_call_target="tpu_custom_call" | custom-call | tf_op jit(solution)/shard_map/join/pallas_call | solution.py:383
  (2 shorter events, 0.0 us)
Async XLA Ops:
  0.0 0.9 %copy-start = (bf16[2,2,32,1024]{3,2,1,0:T(8,128)(2,1)S(1)}, bf16[2,2,32,1024]{3,2,1,0:T(8,128)(2,1)}, u32[]{:S(2)}) copy-start(bf16[2,2,32,1024]{3,2,1,0:T(8,128)(2,1)} %slc.1) | copy-start | bytes 786436
  1.0 18.4 %copy-start.2 = (s32[256]{0:T(256)S(1)}, s32[256]{0:T(256)}, u32[]{:S(2)}) copy-start(s32[256]{0:T(256)} %rg.1) | copy-start | bytes 3076
  1.0 18.6 %copy-start.1 = (s32[8]{0:T(128)S(1)}, s32[8]{0:T(128)}, u32[]{:S(2)}) copy-start(s32[8]{0:T(128)} %az.3) | copy-start | bytes 100
  13.5 7.8 %copy-start.3 = (s32[8]{0:T(128)S(1)}, s32[8]{0:T(128)}, u32[]{:S(2)}) copy-start(s32[8]{0:T(128)} %order.1) | copy-start | bytes 100
  13.5 7.0 %collective-permute-start.1 = (bf16[8,32,128]{2,1,0:T(8,128)(2,1)S(1)}, bf16[8,32,128]{2,1,0:T(8,128)(2,1)S(1)}, u32[]{:S(2)}, u32[]{:S(2)}) collective-permute-start(bf16[8,32,128]{2,1,0:T(8,128)(2,1)S(1)} %get-tuple-element.5), channel_id=1, source_target_pairs={{1,0},{2,1},{3,2},{5,4},{6,5},{7,6},{9,8},{10,9},{11,10},{13,12},{... | collective-permute-start | bytes 196616 | tf_op jit(solution)/shard_map/ppermute | solution.py:353
  14.8 6.4 %collective-permute-start = (bf16[8,32,128]{2,1,0:T(8,128)(2,1)S(1)}, bf16[8,32,128]{2,1,0:T(8,128)(2,1)S(1)}, u32[]{:S(2)}, u32[]{:S(2)}) collective-permute-start(bf16[8,32,128]{2,1,0:T(8,128)(2,1)S(1)} %get-tuple-element.6), channel_id=1, source_target_pairs={{0,1},{1,2},{2,3},{4,5},{5,6},{6,7},{8,9},{9,10},{10,11},{12,13},{... | collective-permute-start | bytes 196616 | tf_op jit(solution)/shard_map/ppermute | solution.py:352

commit v4 on v3

--- a/solution.py
+++ b/solution.py
@@ -67,6 +67,8 @@
 
 def pack_kernel(blocks, per, lines, chunk, slc, send, stage):
     date_rows = rows_of_date(lines)
+    edge_rows = per * GROUP
+    turn = 1 - lax.axis_index("strip") % 2
     span = blocks * chunk
     shape = (EDGE * blocks, span)
     place = iota(shape, 0) % EDGE
@@ -104,7 +106,10 @@
                     for k in range(EDGE):
                         value = edges[date][block * EDGE + k : block * EDGE + k + 1]
                         piece = jnp.where(row == at + k, value, piece)
-        send[block] = piece.astype(jnp.bfloat16)
+        piece = piece.astype(jnp.bfloat16)
+        send[block, pl.ds(pl.multiple_of(turn * edge_rows, 16), edge_rows), :] = piece[:edge_rows]
+        send[block, pl.ds(pl.multiple_of((1 - turn) * edge_rows, 16), edge_rows), :] = piece[edge_rows : 2 * edge_rows]
+        send[block, 2 * edge_rows :, :] = piece[2 * edge_rows :]
 
 
 def weight_kernel(lines, chunk, az, tiled, weights):
@@ -133,19 +138,27 @@
             weights[start : start + LANES, :] = mine
 
 
-def to_sublanes(blocks, per, rows, place, source, target):
+def to_sublanes(blocks, per, rows, first_row, date_stride, source, target):
     dates = blocks * per
     for block in range(blocks):
-        value = source[block].astype(jnp.float32)
         for date in range(per):
+            at = first_row + date * date_stride
+            if not isinstance(at, int):
+                at = pl.multiple_of(at, 8)
+            value = source[block, pl.ds(at, rows), :].astype(jnp.float32)
             for row in range(0, rows, 8):
-                at = place(date, row)
-                target[pl.ds(row * dates + block * per + date, 8, stride=dates), :] = value[at : at + 8]
+                target[pl.ds(row * dates + block * per + date, 8, stride=dates), :] = value[row : row + 8]
 
 
 def spread_kernel(blocks, per, lines, recv, x):
+    dates = blocks * per
     date_rows = rows_of_date(lines)
-    to_sublanes(blocks, per, date_rows, lambda date, row: place_of(date, row, per, date_rows), recv, x)
+    edge_rows = per * GROUP
+    turn = 1 - lax.axis_index("strip") % 2
+    to_sublanes(blocks, per, GROUP, turn * edge_rows, GROUP, recv, x)
+    to_sublanes(blocks, per, GROUP, (1 - turn) * edge_rows, GROUP, recv, x.at[GROUP * dates :])
+    rest = date_rows - 2 * GROUP
+    to_sublanes(blocks, per, rest, 2 * edge_rows, rest, recv, x.at[2 * GROUP * dates :])
 
 
 def split(value):
@@ -154,7 +167,7 @@
 
 
 def pair_kernel(
-    blocks, per, lines, chunk, group, x, low, high, order, az, rg, weights, send, sums, below, above, edges, turned, left, power
+    blocks, per, lines, chunk, group, x, paired, other, order, az, rg, weights, send, sums, halo, edges, turned, left, power
 ):
     dates = blocks * per
     out_rows = lines // STEP
@@ -163,8 +176,10 @@
     me = lax.axis_index("date")
     depth = out_rows * 2 * LANES
 
-    to_sublanes(blocks, per, GROUP, lambda date, row: date * GROUP + row, low, below)
-    to_sublanes(blocks, per, GROUP, lambda date, row: date * GROUP + row, high, above)
+    odd = lax.axis_index("strip") % 2
+    to_sublanes(blocks, per, GROUP, 0, GROUP, paired, halo.at[1 - odd])
+    to_sublanes(blocks, per, GROUP, 0, GROUP, other, halo.at[odd])
+    below, above = halo.at[0], halo.at[1]
     lane = iota((dates, LANES), 1)
     turn = lane % (LANES // 2)
     for k in range(EDGE):
@@ -258,48 +273,53 @@
             send[start : start + dates, :] = code.astype(jnp.int32).astype(jnp.int16)
 
 
-def join_kernel(blocks, per, out_rows, cols, recv, out, halves):
+def join_kernel(blocks, per, out_rows, cols, recv, out, halves, done):
     dates = blocks * per
     wide = out_rows * cols
     per_tile = LANES // cols
     me = lax.axis_index("date")
-    step = pl.program_id(0)
-    part = step // per
-    own = me * per + step % per
     lane = iota((dates, LANES), 1) // cols
     position = iota((dates, wide), 0)
     column = iota((dates, wide), 1)
-    values = []
-    for block in range(blocks):
-        codes = recv[block, pl.ds(pl.multiple_of(step * dates, 16), dates), :].astype(jnp.int32).astype(jnp.float32)
-        heads = recv[block, pl.ds(pl.multiple_of(step % per * dates, 16), dates), :].astype(jnp.int32).astype(jnp.float32)
-        header = jnp.sum(jnp.where(position == own, heads, 0.0), axis=0, keepdims=True)
-        level = jnp.sum(jnp.where(position == column, header, 0.0), axis=1, keepdims=True)
-        factor = jnp.exp(level * (LOG_2 / LEVELS)) * (1.0 / TOP)
-        values.append(jnp.where(position == own, 0.0, codes * factor))
-    for o_tile in range(out_rows // per_tile):
+    factors = [[None] * blocks for _ in range(per)]
+    copies = []
+    for step in range(2 * per):
+        own = me * per + step % per
+        values = []
+        for block in range(blocks):
+            codes = recv[block, step * dates : (step + 1) * dates, :].astype(jnp.int32).astype(jnp.float32)
+            if step < per:
+                header = jnp.sum(jnp.where(position == own, codes, 0.0), axis=0, keepdims=True)
+                level = jnp.sum(jnp.where(position == column, header, 0.0), axis=1, keepdims=True)
+                factors[step][block] = jnp.exp(level * (LOG_2 / LEVELS)) * (1.0 / TOP)
+            values.append(jnp.where(position == own, 0.0, codes * factors[step % per][block]))
         for d_tile in range(blocks // per_tile):
-            tiles = [
-                values[d_tile * per_tile + d][:, o_tile * LANES : (o_tile + 1) * LANES] for d in range(per_tile)
-            ]
-            width = 1
-            while width < per_tile:
-                swap = [None] * per_tile
-                upper = (lane // width) % 2 == 1
-                shift = width * cols
-                for a in range(per_tile):
-                    if (a // width) % 2 == 0:
-                        b = a + width
-                        swap[a] = jnp.where(upper, pltpu.roll(tiles[b], shift, 1), tiles[a])
-                        swap[b] = jnp.where(upper, tiles[b], pltpu.roll(tiles[a], LANES - shift, 1))
-                tiles = swap
-                width *= 2
-            for o in range(per_tile):
-                for start in range(0, dates, 8):
-                    at = start * out_rows + o_tile * per_tile + o
-                    halves[d_tile, pl.ds(at, 8, stride=out_rows), :] = tiles[o][start : start + 8]
-    for d_tile in range(blocks // per_tile):
-        out[:, d_tile * LANES : (d_tile + 1) * LANES] = halves[d_tile]
+            for o_tile in range(out_rows // per_tile):
+                tiles = [
+                    values[d_tile * per_tile + d][:, o_tile * LANES : (o_tile + 1) * LANES] for d in range(per_tile)
+                ]
+                width = 1
+                while width < per_tile:
+                    swap = [None] * per_tile
+                    upper = (lane // width) % 2 == 1
+                    shift = width * cols
+                    for a in range(per_tile):
+                        if (a // width) % 2 == 0:
+                            b = a + width
+                            swap[a] = jnp.where(upper, pltpu.roll(tiles[b], shift, 1), tiles[a])
+                            swap[b] = jnp.where(upper, tiles[b], pltpu.roll(tiles[a], LANES - shift, 1))
+                    tiles = swap
+                    width *= 2
+                for o in range(per_tile):
+                    for start in range(0, dates, 8):
+                        at = start * out_rows + o_tile * per_tile + o
+                        halves[step, d_tile, pl.ds(at, 8, stride=out_rows), :] = tiles[o][start : start + 8]
+            rows = slice(step * dates * out_rows, (step + 1) * dates * out_rows)
+            target = out.at[rows, d_tile * LANES : (d_tile + 1) * LANES]
+            copies.append(pltpu.make_async_copy(halves.at[step, d_tile], target, done.at[step, d_tile]))
+            copies[-1].start()
+    for copy in copies:
+        copy.wait()
 
 
 def decode(codes, me, per):
@@ -346,11 +366,15 @@
         name="weights",
     )(az_offset, tiled)
 
-    forward = [(i, i + 1) for i in range(strips - 1)]
-    backward = [(target, source) for source, target in forward]
+    recv, weights = lax.optimization_barrier((recv, weights))
     edge_rows = per * GROUP
-    low = lax.ppermute(recv[:, edge_rows : 2 * edge_rows], "strip", forward)
-    high = lax.ppermute(recv[:, :edge_rows], "strip", backward)
+
+    def swaps(first):
+        pairs = [(i, i + 1) for i in range(first, strips - 1, 2)]
+        return pairs + [(target, source) for source, target in pairs]
+
+    paired = lax.ppermute(recv[:, :edge_rows], "strip", swaps(0))
+    other = lax.ppermute(recv[:, edge_rows : 2 * edge_rows], "strip", swaps(1))
     x = pl.pallas_call(
         functools.partial(spread_kernel, blocks, per, lines),
         out_shape=jax.ShapeDtypeStruct((date_rows * dates, LANES), jnp.float32),
@@ -367,8 +391,7 @@
         out_specs=VMEM,
         scratch_shapes=[
             pltpu.VMEM((dates * 2 * dates, wide), jnp.float32),
-            pltpu.VMEM((GROUP * dates, LANES), jnp.float32),
-            pltpu.VMEM((GROUP * dates, LANES), jnp.float32),
+            pltpu.VMEM((2, GROUP * dates, LANES), jnp.float32),
             pltpu.VMEM((EDGE * dates, LANES), jnp.float32),
             pltpu.VMEM((EDGE * dates, LANES), jnp.float32),
             pltpu.VMEM((group * 2 * dates, depth), jnp.bfloat16),
@@ -376,17 +399,19 @@
         ],
         compiler_params=PARAMS,
         name="pairs",
-    )(x, low, high, block_order, az_offset, rg_offset, weights)
+    )(x, paired, other, block_order, az_offset, rg_offset, weights)
     count = 2 * per * dates
     back = lax.all_to_all(pairs.reshape(blocks, count, wide), "date", 0, 0, tiled=True)
     if LANES % cols == 0 and out_rows * cols % LANES == 0 and blocks * cols % LANES == 0:
         out = pl.pallas_call(
             functools.partial(join_kernel, blocks, per, out_rows, cols),
-            grid=(2 * per,),
             out_shape=jax.ShapeDtypeStruct((count * out_rows, blocks * cols), jnp.float32),
-            in_specs=[pl.BlockSpec((blocks, count, wide), lambda step: (0, 0, 0))],
-            out_specs=pl.BlockSpec((dates * out_rows, blocks * cols), lambda step: (step, 0)),
-            scratch_shapes=[pltpu.VMEM((blocks * cols // LANES, dates * out_rows, LANES), jnp.float32)],
+            in_specs=[VMEM],
+            out_specs=pl.BlockSpec(memory_space=pl.ANY),
+            scratch_shapes=[
+                pltpu.VMEM((2 * per, blocks * cols // LANES, dates * out_rows, LANES), jnp.float32),
+                pltpu.SemaphoreType.DMA((2 * per, blocks * cols // LANES)),
+            ],
             compiler_params=PARAMS,
             name="join",
         )(back)

time: 37.6 us -> 37.6 us (level)
  blocking collectives: 21.6 us -> 9.35 us
  waiting for transfers between devices: 0.72 us -> 7.04 us
  starting transfers between devices: 5.84 us -> 10.3 us
  local copies, waits for them, and re-layouts: 1.13 us -> 2.52 us
    all_to_all x1 -> x0, blocking collectives: 12.3 us -> none  [on_device(): recv = lax.all_to_all(send, 'date', 0, 0, tiled=True)]
    all_to_all x0 -> x1, starting transfers between devices: none -> 5.17 us  [on_device(): recv = lax.all_to_all(send, 'date', 0, 0, tiled=True)]
    all_to_all x0 -> x1, waiting for transfers between devices: none -> 5.02 us  [on_device(): recv = lax.all_to_all(send, 'date', 0, 0, tiled=True)]
    ppermute x2, waiting for transfers between devices: 0.72 us -> 2.01 us  [the longest x1 2.01 us: on_device(): paired = lax.ppermute(recv[:, :edge_rows], 'strip', swaps(0))]
    pallas_call x1, Pallas kernels: 0.28 us -> 1.01 us  [on_device(): pl.pallas_call(functools.partial(pack_kernel, blocks, per, lines, chunk),...]
    dynamic_slice x1, local copies, waits for them, and re-layouts: 0.08 us -> 0.8 us  [on_device(): lax.dynamic_slice_in_dim(rg_offset, me * cols, cols)]
    ppermute x2, starting transfers between devices: 5.84 us -> 5.13 us  [the longest x1 4.46 us: on_device(): paired = lax.ppermute(recv[:, :edge_rows], 'strip', swaps(0))]
    pallas_call x1, Pallas kernels: 2.2 us -> 1.52 us  [on_device(): pl.pallas_call(functools.partial(join_kernel, blocks, per, out_rows, cols...]
  transfers between devices with their start and end apart: 2 -> 3, of which waited for: 1 -> 2; matrix products, arithmetic and copies ran while one was open for 0% -> 2% of each run, Pallas kernels for 3% -> 2%
where the time goes in v4:
time: 37.6 us; the launch traced here: 37.2 us
  starting transfers between devices  10.3 us (27%)
  blocking collectives  9.35 us (25%)
  Pallas kernels  7.97 us (21%)
  waiting for transfers between devices  7.04 us (19%)
  local copies, waits for them, and re-layouts  2.52 us (7%)
    all_to_all x1, blocking collectives, on_device(): lax.all_to_all(pairs.reshape(blocks, count, wide), 'date', 0, 0, tiled=True)  9.35 us
    all_to_all x1, starting transfers between devices, on_device(): recv = lax.all_to_all(send, 'date', 0, 0, tiled=True)  5.17 us
    all_to_all x1, waiting for transfers between devices, on_device(): recv = lax.all_to_all(send, 'date', 0, 0, tiled=True)  5.02 us
    pallas_call x1, Pallas kernels, on_device(): pl.pallas_call(functools.partial(pair_kernel, blocks, per, lines, chunk,...  4.54 us
    ppermute x1, starting transfers between devices, on_device(): paired = lax.ppermute(recv[:, :edge_rows], 'strip', swaps(0))  4.46 us
    ppermute x1, waiting for transfers between devices, on_device(): paired = lax.ppermute(recv[:, :edge_rows], 'strip', swaps(0))  2.01 us
    unnamed x10, local copies, waits for them, and re-layouts  1.62 us
    pallas_call x1, Pallas kernels, on_device(): pl.pallas_call(functools.partial(join_kernel, blocks, per, out_rows, cols...  1.52 us
  transfers between devices with their start and end apart: 3, of which 2 were waited for; matrix products, arithmetic and copies ran while one was open for 2% of the time, Pallas kernels for 2%

profile of v4, /device:TPU:0, one launch (start us, length us, event | category | flops | bytes accessed | tf_op | source)
XLA Modules:
  0.0 37.2 jit_solution(10151491579939622133)
XLA Ops:
  0.0 0.0 copy-start
  0.0 0.9 %copy-done = bf16[2,2,32,1024]{3,2,1,0:T(8,128)(2,1)S(1)} copy-done((bf16[2,2,32,1024]{3,2,1,0:T(8,128)(2,1)S(1)}, bf16[2,2,32,1024]{3,2,1,0:T(8,128)(2,1)}, u32[]{:S(2)}) %copy-start) | copy-done | bytes 262168
  1.0 1.0 %pack.1 = bf16[8,144,128]{2,1,0:T(8,128)(2,1)} custom-call(bf16[2,2,32,1024]{3,2,1,0:T(8,128)(2,1)S(1)} %copy-done), custom_call_target="tpu_custom_call" | custom-call | tf_op jit(solution)/shard_map/pack/pallas_call | solution.py:348
  2.0 5.2 %all-to-all-start = ((bf16[8,144,128]{2,1,0:T(8,128)(2,1)}), bf16[8,144,128]{2,1,0:T(8,128)(2,1)S(1)}, u32[]{:S(2)}, u32[]{:S(2)}) async-start(bf16[8,144,128]{2,1,0:T(8,128)(2,1)} %pack.1), calls=%async_computation | async-start | bytes 589824 | tf_op jit(solution)/shard_map/all_to_all | solution.py:357
  7.1 0.0 copy-start.2
  7.1 0.0 copy-start.3
  7.2 0.0 copy-start.4
  7.2 0.8 %dynamic_slice.3 = s32[32]{0:T(128)S(1)} dynamic-slice(s32[256]{0:T(256)} %rg.1, s32[]{:T(128)S(6)} %select_n.3), dynamic_slice_sizes={32} | dynamic-slice | bytes 260 | tf_op jit(solution)/shard_map/dynamic_slice | solution.py:358
  8.0 0.1 broadcast_in_dim_tile.3.tiled
  8.1 0.0 copy-start.1
  8.1 0.7 %copy-done.1 = s32[8]{0:T(128)S(1)} copy-done((s32[8]{0:T(128)S(1)}, s32[8]{0:T(128)}, u32[]{:S(2)}) %copy-start.1) | copy-done | bytes 56
  8.7 0.7 %weights.1 = bf16[2560,256]{1,0:T(8,128)(2,1)S(1)} custom-call(s32[8]{0:T(128)S(1)} %copy-done.1, s32[1,256]{1,0:T(1,128)S(1)} %broadcast_in_dim_tile.3.tiled), custom_call_target="tpu_custom_call" | custom-call | bytes 4194304 | tf_op jit(solution)/shard_map/weights/pallas_call | solution.py:359
  9.4 5.0 %all-to-all-done.recv = bf16[8,144,128]{2,1,0:T(8,128)(2,1)S(1)} async-done(((bf16[8,144,128]{2,1,0:T(8,128)(2,1)}), bf16[8,144,128]{2,1,0:T(8,128)(2,1)S(1)}, u32[]{:S(2)}, u32[]{:S(2)}) %all-to-all-start) | async-done | bytes 294944 | tf_op jit(solution)/shard_map/all_to_all | solution.py:357
  14.4 0.7 %collective-permute-start.1 = (bf16[8,32,128]{2,1,0:T(8,128)(2,1)S(1)}, bf16[8,32,128]{2,1,0:T(8,128)(2,1)S(1)}, u32[]{:S(2)}, u32[]{:S(2)}) collective-permute-start(bf16[8,32,128]{2,1,0:T(8,128)(2,1)S(1)} %get-tuple-element.9), channel_id=1, source_target_pairs={{1,2},{2,1},{5,6},{6,5},{9,10},{10,9},{13,14},{14,13},{17,18},{18,... | collective-permute-start | bytes 196616 | tf_op jit(solution)/shard_map/ppermute | solution.py:377
  15.1 4.5 %collective-permute-start = (bf16[8,32,128]{2,1,0:T(8,128)(2,1)S(1)}, bf16[8,32,128]{2,1,0:T(8,128)(2,1)S(1)}, u32[]{:S(2)}, u32[]{:S(2)}) collective-permute-start(bf16[8,32,128]{2,1,0:T(8,128)(2,1)S(1)} %get-tuple-element.10), channel_id=1, source_target_pairs={{0,1},{2,3},{1,0},{3,2},{4,5},{6,7},{5,4},{7,6},{8,9},{10,11},{9,8... | collective-permute-start | bytes 196616 | tf_op jit(solution)/shard_map/ppermute | solution.py:376
  19.6 0.2 spread.1.x
  19.8 0.0 collective-permute-done.1.other
  19.8 2.0 %collective-permute-done.paired = bf16[8,32,128]{2,1,0:T(8,128)(2,1)S(1)} collective-permute-done((bf16[8,32,128]{2,1,0:T(8,128)(2,1)S(1)}, bf16[8,32,128]{2,1,0:T(8,128)(2,1)S(1)}, u32[]{:S(2)}, u32[]{:S(2)}) %collective-permute-start) | collective-permute-done | bytes 65568 | tf_op jit(solution)/shard_map/ppermute | solution.py:376
  21.8 0.0 copy-done.2
  21.8 0.0 copy-done.3
  21.8 0.0 copy-done.4
  21.8 4.5 %pairs.1 = s16[512,256]{1,0:T(8,128)(2,1)S(1)} custom-call(f32[1152,128]{1,0:T(8,128)S(1)} %spread.1.x, bf16[8,32,128]{2,1,0:T(8,128)(2,1)S(1)} %collective-permute-done.paired, bf16[8,32,128]{2,1,0:T(8,128)(2,1)S(1)} %collective-permute-done.1.other, s32[8]{0:T(128)S(1)} %copy-done.4, s32[8]{0:T(128)S(1)} %copy-done.2, s32[256]{0:T(256)S(1)} %copy-done.3, ...), custom_call_target="tpu_custom_call" | custom-call | tf_op jit(solution)/shard_map/pairs/pallas_call | solution.py:387
  26.4 9.3 %all_to_all.10.recv = s16[8,64,256]{2,1,0:T(8,128)(2,1)S(1)} all-to-all(s16[8,64,256]{2,1,0:T(8,128)(2,1)S(1)} %bitcast.2), channel_id=1, replica_groups=mesh['date'=8,'strip'=4] {'date'}, dimensions={0} | all-to-all | bytes 524288 | tf_op jit(solution)/shard_map/all_to_all | solution.py:404
  35.7 1.5 %join.1 = f32[512,256]{1,0:T(8,128)} custom-call(s16[8,64,256]{2,1,0:T(8,128)(2,1)S(1)} %all_to_all.10.recv), custom_call_target="tpu_custom_call" | custom-call | tf_op jit(solution)/shard_map/join/pallas_call | solution.py:406
  (2 shorter events, 0.0 us)
Async XLA Ops:
  0.0 0.9 %copy-start = (bf16[2,2,32,1024]{3,2,1,0:T(8,128)(2,1)S(1)}, bf16[2,2,32,1024]{3,2,1,0:T(8,128)(2,1)}, u32[]{:S(2)}) copy-start(bf16[2,2,32,1024]{3,2,1,0:T(8,128)(2,1)} %slc.1) | copy-start | bytes 786436
  2.0 12.5 %all-to-all-start = ((bf16[8,144,128]{2,1,0:T(8,128)(2,1)}), bf16[8,144,128]{2,1,0:T(8,128)(2,1)S(1)}, u32[]{:S(2)}, u32[]{:S(2)}) async-start(bf16[8,144,128]{2,1,0:T(8,128)(2,1)} %pack.1), calls=%async_computation | async-start | bytes 589824 | tf_op jit(solution)/shard_map/all_to_all | solution.py:357
  7.1 14.7 %copy-start.2 = (s32[8]{0:T(128)S(1)}, s32[8]{0:T(128)}, u32[]{:S(2)}) copy-start(s32[8]{0:T(128)} %az.3) | copy-start | bytes 100
  7.1 14.7 %copy-start.3 = (s32[256]{0:T(256)S(1)}, s32[256]{0:T(256)}, u32[]{:S(2)}) copy-start(s32[256]{0:T(256)} %rg.1) | copy-start | bytes 3076
  7.2 14.7 %copy-start.4 = (s32[8]{0:T(128)S(1)}, s32[8]{0:T(128)}, u32[]{:S(2)}) copy-start(s32[8]{0:T(128)} %order.1) | copy-start | bytes 100
  8.1 0.7 %copy-start.1 = (s32[8]{0:T(128)S(1)}, s32[8]{0:T(128)}, u32[]{:S(2)}) copy-start(s32[8]{0:T(128)} %az.3) | copy-start | bytes 100
  14.4 5.4 %collective-permute-start.1 = (bf16[8,32,128]{2,1,0:T(8,128)(2,1)S(1)}, bf16[8,32,128]{2,1,0:T(8,128)(2,1)S(1)}, u32[]{:S(2)}, u32[]{:S(2)}) collective-permute-start(bf16[8,32,128]{2,1,0:T(8,128)(2,1)S(1)} %get-tuple-element.9), channel_id=1, source_target_pairs={{1,2},{2,1},{5,6},{6,5},{9,10},{10,9},{13,14},{14,13},{17,18},{18,... | collective-permute-start | bytes 196616 | tf_op jit(solution)/shard_map/ppermute | solution.py:377
  15.1 6.7 %collective-permute-start = (bf16[8,32,128]{2,1,0:T(8,128)(2,1)S(1)}, bf16[8,32,128]{2,1,0:T(8,128)(2,1)S(1)}, u32[]{:S(2)}, u32[]{:S(2)}) collective-permute-start(bf16[8,32,128]{2,1,0:T(8,128)(2,1)S(1)} %get-tuple-element.10), channel_id=1, source_target_pairs={{0,1},{2,3},{1,0},{3,2},{4,5},{6,7},{5,4},{7,6},{8,9},{10,11},{9,8... | collective-permute-start | bytes 196616 | tf_op jit(solution)/shard_map/ppermute | solution.py:376

commit v5 on v4

--- a/solution.py
+++ b/solution.py
@@ -366,15 +366,14 @@
         name="weights",
     )(az_offset, tiled)
 
-    recv, weights = lax.optimization_barrier((recv, weights))
     edge_rows = per * GROUP
 
     def swaps(first):
         pairs = [(i, i + 1) for i in range(first, strips - 1, 2)]
         return pairs + [(target, source) for source, target in pairs]
 
+    other = lax.ppermute(recv[:, edge_rows : 2 * edge_rows], "strip", swaps(1))
     paired = lax.ppermute(recv[:, :edge_rows], "strip", swaps(0))
-    other = lax.ppermute(recv[:, edge_rows : 2 * edge_rows], "strip", swaps(1))
     x = pl.pallas_call(
         functools.partial(spread_kernel, blocks, per, lines),
         out_shape=jax.ShapeDtypeStruct((date_rows * dates, LANES), jnp.float32),

time: 37.6 us -> 36.6 us (0.973)
  blocking collectives: 9.35 us -> 21.6 us
  waiting for transfers between devices: 7.04 us -> 1.16 us
  starting transfers between devices: 10.3 us -> 5.13 us
  local copies, waits for them, and re-layouts: 2.52 us -> 1.13 us
  Pallas kernels: 7.97 us -> 7.25 us
    all_to_all x0 -> x1, blocking collectives: none -> 12.3 us  [on_device(): recv = lax.all_to_all(send, 'date', 0, 0, tiled=True)]
    all_to_all x1 -> x0, starting transfers between devices: 5.17 us -> none  [on_device(): recv = lax.all_to_all(send, 'date', 0, 0, tiled=True)]
    all_to_all x1 -> x0, waiting for transfers between devices: 5.02 us -> none  [on_device(): recv = lax.all_to_all(send, 'date', 0, 0, tiled=True)]
    ppermute x1, waiting for transfers between devices: 2.01 us -> 1.16 us  [on_device(): paired = lax.ppermute(recv[:, :edge_rows], 'strip', swaps(0))]
    dynamic_slice x1, local copies, waits for them, and re-layouts: 0.8 us -> 0.07 us  [on_device(): lax.dynamic_slice_in_dim(rg_offset, me * cols, cols)]
    pallas_call x1, Pallas kernels: 1.01 us -> 0.3 us  [on_device(): pl.pallas_call(functools.partial(pack_kernel, blocks, per, lines, chunk),...]
    unnamed x10 -> x8, local copies, waits for them, and re-layouts: 1.62 us -> 0.96 us
  transfers between devices with their start and end apart: 3 -> 2, of which waited for: 2 -> 1; matrix products, arithmetic and copies ran while one was open for 2% -> 0% of each run, Pallas kernels for 2% -> 2%
where the time goes in v5:
time: 36.6 us; the launch traced here: 36.3 us
  blocking collectives  21.6 us (59%)
  Pallas kernels  7.25 us (20%)
  starting transfers between devices  5.13 us (14%)
  waiting for transfers between devices  1.16 us (3%)
  local copies, waits for them, and re-layouts  1.13 us (3%)
    all_to_all x1, blocking collectives, on_device(): recv = lax.all_to_all(send, 'date', 0, 0, tiled=True)  12.3 us
    all_to_all x1, blocking collectives, on_device(): lax.all_to_all(pairs.reshape(blocks, count, wide), 'date', 0, 0, tiled=True)  9.35 us
    pallas_call x1, Pallas kernels, on_device(): pl.pallas_call(functools.partial(pair_kernel, blocks, per, lines, chunk,...  4.54 us
    ppermute x1, starting transfers between devices, on_device(): paired = lax.ppermute(recv[:, :edge_rows], 'strip', swaps(0))  4.46 us
    pallas_call x1, Pallas kernels, on_device(): pl.pallas_call(functools.partial(join_kernel, blocks, per, out_rows, cols...  1.52 us
    ppermute x1, waiting for transfers between devices, on_device(): paired = lax.ppermute(recv[:, :edge_rows], 'strip', swaps(0))  1.16 us
    unnamed x8, local copies, waits for them, and re-layouts  0.96 us
  transfers between devices with their start and end apart: 2, of which 1 were waited for; matrix products, arithmetic and copies ran while one was open for 0% of the time, Pallas kernels for 2%

profile of v5, /device:TPU:0, one launch (start us, length us, event | category | flops | bytes accessed | tf_op | source)
XLA Modules:
  0.0 36.3 jit_solution(11930022613100652431)
XLA Ops:
  0.0 0.0 copy-start
  0.0 0.9 %copy-done = bf16[2,2,32,1024]{3,2,1,0:T(8,128)(2,1)S(1)} copy-done((bf16[2,2,32,1024]{3,2,1,0:T(8,128)(2,1)S(1)}, bf16[2,2,32,1024]{3,2,1,0:T(8,128)(2,1)}, u32[]{:S(2)}) %copy-start) | copy-done | bytes 262168
  1.0 0.0 copy-start.2
  1.0 0.0 copy-start.1
  1.0 0.3 pack.1
  1.3 12.3 %all_to_all.10.recv = bf16[8,144,128]{2,1,0:T(8,128)(2,1)S(1)} all-to-all(bf16[8,144,128]{2,1,0:T(8,128)(2,1)S(1)} %pack.1), channel_id=1, replica_groups=mesh['date'=8,'strip'=4] {'date'}, dimensions={0} | all-to-all | bytes 589824 | tf_op jit(solution)/shard_map/all_to_all | solution.py:357
  13.5 0.0 copy-start.3
  13.5 0.7 %collective-permute-start.1 = (bf16[8,32,128]{2,1,0:T(8,128)(2,1)S(1)}, bf16[8,32,128]{2,1,0:T(8,128)(2,1)S(1)}, u32[]{:S(2)}, u32[]{:S(2)}) collective-permute-start(bf16[8,32,128]{2,1,0:T(8,128)(2,1)S(1)} %get-tuple-element.5), channel_id=1, source_target_pairs={{1,2},{2,1},{5,6},{6,5},{9,10},{10,9},{13,14},{14,13},{17,18},{18,... | collective-permute-start | bytes 196616 | tf_op jit(solution)/shard_map/ppermute | solution.py:375
  14.2 4.5 %collective-permute-start = (bf16[8,32,128]{2,1,0:T(8,128)(2,1)S(1)}, bf16[8,32,128]{2,1,0:T(8,128)(2,1)S(1)}, u32[]{:S(2)}, u32[]{:S(2)}) collective-permute-start(bf16[8,32,128]{2,1,0:T(8,128)(2,1)S(1)} %get-tuple-element.6), channel_id=1, source_target_pairs={{0,1},{2,3},{1,0},{3,2},{4,5},{6,7},{5,4},{7,6},{8,9},{10,11},{9,8... | collective-permute-start | bytes 196616 | tf_op jit(solution)/shard_map/ppermute | solution.py:376
  18.7 0.0 copy-done.2
  18.7 0.1 dynamic_slice.3
  18.7 0.1 broadcast_in_dim_tile.3.tiled
  18.8 0.0 copy-done.1
  18.8 0.7 %weights.1 = bf16[2560,256]{1,0:T(8,128)(2,1)S(1)} custom-call(s32[8]{0:T(128)S(1)} %copy-done.1, s32[1,256]{1,0:T(1,128)S(1)} %broadcast_in_dim_tile.3.tiled), custom_call_target="tpu_custom_call" | custom-call | bytes 4194304 | tf_op jit(solution)/shard_map/weights/pallas_call | solution.py:359
  19.5 0.2 spread.1.x
  19.7 0.0 collective-permute-done.1.other
  19.8 1.2 %collective-permute-done.paired = bf16[8,32,128]{2,1,0:T(8,128)(2,1)S(1)} collective-permute-done((bf16[8,32,128]{2,1,0:T(8,128)(2,1)S(1)}, bf16[8,32,128]{2,1,0:T(8,128)(2,1)S(1)}, u32[]{:S(2)}, u32[]{:S(2)}) %collective-permute-start) | collective-permute-done | bytes 65568 | tf_op jit(solution)/shard_map/ppermute | solution.py:376
  20.9 0.0 copy-done.3
  20.9 4.5 %pairs.1 = s16[512,256]{1,0:T(8,128)(2,1)S(1)} custom-call(f32[1152,128]{1,0:T(8,128)S(1)} %spread.1.x, bf16[8,32,128]{2,1,0:T(8,128)(2,1)S(1)} %collective-permute-done.paired, bf16[8,32,128]{2,1,0:T(8,128)(2,1)S(1)} %collective-permute-done.1.other, s32[8]{0:T(128)S(1)} %copy-done.3, s32[8]{0:T(128)S(1)} %copy-done.1, s32[256]{0:T(256)S(1)} %copy-done.2, ...), custom_call_target="tpu_custom_call" | custom-call | tf_op jit(solution)/shard_map/pairs/pallas_call | solution.py:386
  25.5 9.3 %all_to_all.11.recv = s16[8,64,256]{2,1,0:T(8,128)(2,1)S(1)} all-to-all(s16[8,64,256]{2,1,0:T(8,128)(2,1)S(1)} %bitcast.2), channel_id=1, replica_groups=mesh['date'=8,'strip'=4] {'date'}, dimensions={0} | all-to-all | bytes 524288 | tf_op jit(solution)/shard_map/all_to_all | solution.py:403
  34.8 1.5 %join.1 = f32[512,256]{1,0:T(8,128)} custom-call(s16[8,64,256]{2,1,0:T(8,128)(2,1)S(1)} %all_to_all.11.recv), custom_call_target="tpu_custom_call" | custom-call | tf_op jit(solution)/shard_map/join/pallas_call | solution.py:405
  (2 shorter events, 0.0 us)
Async XLA Ops:
  0.0 0.9 %copy-start = (bf16[2,2,32,1024]{3,2,1,0:T(8,128)(2,1)S(1)}, bf16[2,2,32,1024]{3,2,1,0:T(8,128)(2,1)}, u32[]{:S(2)}) copy-start(bf16[2,2,32,1024]{3,2,1,0:T(8,128)(2,1)} %slc.1) | copy-start | bytes 786436
  1.0 17.7 %copy-start.2 = (s32[256]{0:T(256)S(1)}, s32[256]{0:T(256)}, u32[]{:S(2)}) copy-start(s32[256]{0:T(256)} %rg.1) | copy-start | bytes 3076
  1.0 17.9 %copy-start.1 = (s32[8]{0:T(128)S(1)}, s32[8]{0:T(128)}, u32[]{:S(2)}) copy-start(s32[8]{0:T(128)} %az.3) | copy-start | bytes 100
  13.5 7.4 %copy-start.3 = (s32[8]{0:T(128)S(1)}, s32[8]{0:T(128)}, u32[]{:S(2)}) copy-start(s32[8]{0:T(128)} %order.1) | copy-start | bytes 100
  13.5 6.2 %collective-permute-start.1 = (bf16[8,32,128]{2,1,0:T(8,128)(2,1)S(1)}, bf16[8,32,128]{2,1,0:T(8,128)(2,1)S(1)}, u32[]{:S(2)}, u32[]{:S(2)}) collective-permute-start(bf16[8,32,128]{2,1,0:T(8,128)(2,1)S(1)} %get-tuple-element.5), channel_id=1, source_target_pairs={{1,2},{2,1},{5,6},{6,5},{9,10},{10,9},{13,14},{14,13},{17,18},{18,... | collective-permute-start | bytes 196616 | tf_op jit(solution)/shard_map/ppermute | solution.py:375
  14.2 6.7 %collective-permute-start = (bf16[8,32,128]{2,1,0:T(8,128)(2,1)S(1)}, bf16[8,32,128]{2,1,0:T(8,128)(2,1)S(1)}, u32[]{:S(2)}, u32[]{:S(2)}) collective-permute-start(bf16[8,32,128]{2,1,0:T(8,128)(2,1)S(1)} %get-tuple-element.6), channel_id=1, source_target_pairs={{0,1},{2,3},{1,0},{3,2},{4,5},{6,7},{5,4},{7,6},{8,9},{10,11},{9,8... | collective-permute-start | bytes 196616 | tf_op jit(solution)/shard_map/ppermute | solution.py:376

commit v6 on v5

--- a/solution.py
+++ b/solution.py
@@ -167,7 +167,7 @@
 
 
 def pair_kernel(
-    blocks, per, lines, chunk, group, x, paired, other, order, az, rg, weights, send, sums, halo, edges, turned, left, power
+    blocks, per, lines, chunk, group, x, other, paired, order, az, rg, weights, send, sums, halo, edges, turned, left, power
 ):
     dates = blocks * per
     out_rows = lines // STEP
@@ -398,7 +398,7 @@
         ],
         compiler_params=PARAMS,
         name="pairs",
-    )(x, paired, other, block_order, az_offset, rg_offset, weights)
+    )(x, other, paired, block_order, az_offset, rg_offset, weights)
     count = 2 * per * dates
     back = lax.all_to_all(pairs.reshape(blocks, count, wide), "date", 0, 0, tiled=True)
     if LANES % cols == 0 and out_rows * cols % LANES == 0 and blocks * cols % LANES == 0:

time: 36.6 us -> 35.5 us (0.970)
  the two profiles are of different devices: /device:TPU:0 before, /device:TPU:16 now
where the time goes in v6:
time: 35.5 us; the launch traced here: 35.3 us
  blocking collectives  20.2 us (57%)
  Pallas kernels  7.25 us (20%)
  starting transfers between devices  3.55 us (10%)
  waiting for transfers between devices  3.13 us (9%)
  local copies, waits for them, and re-layouts  1.13 us (3%)
    all_to_all x1, blocking collectives, on_device(): recv = lax.all_to_all(send, 'date', 0, 0, tiled=True)  10.8 us
    all_to_all x1, blocking collectives, on_device(): lax.all_to_all(pairs.reshape(blocks, count, wide), 'date', 0, 0, tiled=True)  9.35 us
    pallas_call x1, Pallas kernels, on_device(): pl.pallas_call(functools.partial(pair_kernel, blocks, per, lines, chunk,...  4.54 us
    ppermute x1, waiting for transfers between devices, on_device(): other = lax.ppermute(recv[:, edge_rows:2 * edge_rows], 'strip', swaps(1))  3.13 us
    ppermute x1, starting transfers between devices, on_device(): other = lax.ppermute(recv[:, edge_rows:2 * edge_rows], 'strip', swaps(1))  1.91 us
    ppermute x1, starting transfers between devices, on_device(): paired = lax.ppermute(recv[:, :edge_rows], 'strip', swaps(0))  1.64 us
    pallas_call x1, Pallas kernels, on_device(): pl.pallas_call(functools.partial(join_kernel, blocks, per, out_rows, cols...  1.52 us
    unnamed x8, local copies, waits for them, and re-layouts  0.96 us
  transfers between devices with their start and end apart: 2, of which 1 were waited for; matrix products, arithmetic and copies ran while one was open for 0% of the time, Pallas kernels for 3%

profile of v6, /device:TPU:16, one launch (start us, length us, event | category | flops | bytes accessed | tf_op | source)
XLA Modules:
  0.0 35.3 jit_solution(6471535146205862215)
XLA Ops:
  0.0 0.0 copy-start
  0.0 0.9 %copy-done = bf16[2,2,32,1024]{3,2,1,0:T(8,128)(2,1)S(1)} copy-done((bf16[2,2,32,1024]{3,2,1,0:T(8,128)(2,1)S(1)}, bf16[2,2,32,1024]{3,2,1,0:T(8,128)(2,1)}, u32[]{:S(2)}) %copy-start) | copy-done | bytes 262168
  1.0 0.0 copy-start.2
  1.0 0.0 copy-start.1
  1.0 0.3 pack.1
  1.3 10.8 %all_to_all.10.recv = bf16[8,144,128]{2,1,0:T(8,128)(2,1)S(1)} all-to-all(bf16[8,144,128]{2,1,0:T(8,128)(2,1)S(1)} %pack.1), channel_id=1, replica_groups=mesh['date'=8,'strip'=4] {'date'}, dimensions={0} | all-to-all | bytes 589824 | tf_op jit(solution)/shard_map/all_to_all | solution.py:357
  12.1 0.0 copy-start.3
  12.1 1.6 %collective-permute-start.1 = (bf16[8,32,128]{2,1,0:T(8,128)(2,1)S(1)}, bf16[8,32,128]{2,1,0:T(8,128)(2,1)S(1)}, u32[]{:S(2)}, u32[]{:S(2)}) collective-permute-start(bf16[8,32,128]{2,1,0:T(8,128)(2,1)S(1)} %get-tuple-element.5), channel_id=1, source_target_pairs={{0,1},{2,3},{1,0},{3,2},{4,5},{6,7},{5,4},{7,6},{8,9},{10,11},{9,8... | collective-permute-start | bytes 196616 | tf_op jit(solution)/shard_map/ppermute | solution.py:376
  13.7 1.9 %collective-permute-start = (bf16[8,32,128]{2,1,0:T(8,128)(2,1)S(1)}, bf16[8,32,128]{2,1,0:T(8,128)(2,1)S(1)}, u32[]{:S(2)}, u32[]{:S(2)}) collective-permute-start(bf16[8,32,128]{2,1,0:T(8,128)(2,1)S(1)} %get-tuple-element.6), channel_id=1, source_target_pairs={{1,2},{2,1},{5,6},{6,5},{9,10},{10,9},{13,14},{14,13},{17,18},{18,... | collective-permute-start | bytes 196616 | tf_op jit(solution)/shard_map/ppermute | solution.py:375
  15.6 0.0 copy-done.2
  15.7 0.1 dynamic_slice.3
  15.7 0.1 broadcast_in_dim_tile.3.tiled
  15.8 0.0 copy-done.1
  15.8 0.7 %weights.1 = bf16[2560,256]{1,0:T(8,128)(2,1)S(1)} custom-call(s32[8]{0:T(128)S(1)} %copy-done.1, s32[1,256]{1,0:T(1,128)S(1)} %broadcast_in_dim_tile.3.tiled), custom_call_target="tpu_custom_call" | custom-call | bytes 4194304 | tf_op jit(solution)/shard_map/weights/pallas_call | solution.py:359
  16.5 0.2 spread.1.x
  16.7 0.0 collective-permute-done.1.paired
  16.7 3.1 %collective-permute-done.other = bf16[8,32,128]{2,1,0:T(8,128)(2,1)S(1)} collective-permute-done((bf16[8,32,128]{2,1,0:T(8,128)(2,1)S(1)}, bf16[8,32,128]{2,1,0:T(8,128)(2,1)S(1)}, u32[]{:S(2)}, u32[]{:S(2)}) %collective-permute-start) | collective-permute-done | bytes 65568 | tf_op jit(solution)/shard_map/ppermute | solution.py:375
  19.9 0.0 copy-done.3
  19.9 4.5 %pairs.1 = s16[512,256]{1,0:T(8,128)(2,1)S(1)} custom-call(f32[1152,128]{1,0:T(8,128)S(1)} %spread.1.x, bf16[8,32,128]{2,1,0:T(8,128)(2,1)S(1)} %collective-permute-done.other, bf16[8,32,128]{2,1,0:T(8,128)(2,1)S(1)} %collective-permute-done.1.paired, s32[8]{0:T(128)S(1)} %copy-done.3, s32[8]{0:T(128)S(1)} %copy-done.1, s32[256]{0:T(256)S(1)} %copy-done.2, ...), custom_call_target="tpu_custom_call" | custom-call | tf_op jit(solution)/shard_map/pairs/pallas_call | solution.py:386
  24.4 9.3 %all_to_all.11.recv = s16[8,64,256]{2,1,0:T(8,128)(2,1)S(1)} all-to-all(s16[8,64,256]{2,1,0:T(8,128)(2,1)S(1)} %bitcast.2), channel_id=1, replica_groups=mesh['date'=8,'strip'=4] {'date'}, dimensions={0} | all-to-all | bytes 524288 | tf_op jit(solution)/shard_map/all_to_all | solution.py:403
  33.8 1.5 %join.1 = f32[512,256]{1,0:T(8,128)} custom-call(s16[8,64,256]{2,1,0:T(8,128)(2,1)S(1)} %all_to_all.11.recv), custom_call_target="tpu_custom_call" | custom-call | tf_op jit(solution)/shard_map/join/pallas_call | solution.py:405
  (2 shorter events, 0.0 us)
Async XLA Ops:
  0.0 0.9 %copy-start = (bf16[2,2,32,1024]{3,2,1,0:T(8,128)(2,1)S(1)}, bf16[2,2,32,1024]{3,2,1,0:T(8,128)(2,1)}, u32[]{:S(2)}) copy-start(bf16[2,2,32,1024]{3,2,1,0:T(8,128)(2,1)} %slc.1) | copy-start | bytes 786436
  1.0 14.7 %copy-start.2 = (s32[256]{0:T(256)S(1)}, s32[256]{0:T(256)}, u32[]{:S(2)}) copy-start(s32[256]{0:T(256)} %rg.1) | copy-start | bytes 3076
  1.0 14.9 %copy-start.1 = (s32[8]{0:T(128)S(1)}, s32[8]{0:T(128)}, u32[]{:S(2)}) copy-start(s32[8]{0:T(128)} %az.3) | copy-start | bytes 100
  12.1 7.8 %copy-start.3 = (s32[8]{0:T(128)S(1)}, s32[8]{0:T(128)}, u32[]{:S(2)}) copy-start(s32[8]{0:T(128)} %order.1) | copy-start | bytes 100
  12.1 4.7 %collective-permute-start.1 = (bf16[8,32,128]{2,1,0:T(8,128)(2,1)S(1)}, bf16[8,32,128]{2,1,0:T(8,128)(2,1)S(1)}, u32[]{:S(2)}, u32[]{:S(2)}) collective-permute-start(bf16[8,32,128]{2,1,0:T(8,128)(2,1)S(1)} %get-tuple-element.5), channel_id=1, source_target_pairs={{0,1},{2,3},{1,0},{3,2},{4,5},{6,7},{5,4},{7,6},{8,9},{10,11},{9,8... | collective-permute-start | bytes 196616 | tf_op jit(solution)/shard_map/ppermute | solution.py:376
  13.7 6.1 %collective-permute-start = (bf16[8,32,128]{2,1,0:T(8,128)(2,1)S(1)}, bf16[8,32,128]{2,1,0:T(8,128)(2,1)S(1)}, u32[]{:S(2)}, u32[]{:S(2)}) collective-permute-start(bf16[8,32,128]{2,1,0:T(8,128)(2,1)S(1)} %get-tuple-element.6), channel_id=1, source_target_pairs={{1,2},{2,1},{5,6},{6,5},{9,10},{10,9},{13,14},{14,13},{17,18},{18,... | collective-permute-start | bytes 196616 | tf_op jit(solution)/shard_map/ppermute | solution.py:375

commit v7 on v1

v7 whole, which is shorter than its diff:
```python
import functools

import jax
import jax.numpy as jnp
from jax import lax
from jax.experimental import pallas as pl
from jax.experimental.pallas import tpu as pltpu
from jax.sharding import PartitionSpec as P

STEP = 4
HALO = 5
REACH = 2
EDGE = 4
LANES = 128
VMEM = pl.BlockSpec(memory_space=pltpu.VMEM)
SMEM = pl.BlockSpec(memory_space=pltpu.SMEM)
PARAMS = pltpu.CompilerParams(vmem_limit_bytes=48 * 1024 * 1024)

epsilon = 1e-06
LEVELS = 8.0
LOWEST, HIGHEST = -880.0, 64.0
TOP = 32760.0
LOG_2 = 0.6931471805599453


def iota(shape, dim):
    return lax.broadcasted_iota(jnp.int32, shape, dim)


def row_of(part, line, lines):
    if line < HALO:
        return 2 * lines + part * 2 * HALO + line
    if line < HALO + lines:
        return part * lines + line - HALO
    return 2 * lines + part * 2 * HALO + line - lines


def pack_kernel(blocks, per, lines, chunk, slc, other, paired, send, stage, piece):
    rows = 2 * (lines + 2 * HALO)
    date_rows = rows + EDGE
    span = blocks * chunk
    odd = lax.axis_index("strip") % 2 == 1
    for date in range(per):
        base = date * date_rows
        for part in range(2):
            with_pair, with_other = paired[part, date].astype(jnp.float32), other[part, date].astype(jnp.float32)
            edge = base + 2 * lines + part * 2 * HALO
            stage[base + part * lines : base + (part + 1) * lines, :] = slc[part, date].astype(jnp.float32)
            stage[edge : edge + HALO, :] = jnp.where(odd, with_pair, with_other)
            stage[edge + HALO : edge + 2 * HALO, :] = jnp.where(odd, with_other, with_pair)
        stage[base + rows : base + date_rows, :] = jnp.zeros((EDGE, span), jnp.float32)
    samples = stage[...].astype(jnp.bfloat16)
    shape = (EDGE * blocks, span)
    place = iota(shape, 0) % EDGE
    wanted = iota(shape, 0) // EDGE * chunk + jnp.where(place < REACH, place - REACH, place - REACH + chunk)
    picks = (iota(shape, 1) == wanted).astype(jnp.bfloat16)
    edges = lax.dot_general(picks, samples, (((1,), (1,)), ((), ())), preferred_element_type=jnp.float32)
    for block in range(blocks):
        if chunk == LANES:
            piece[...] = stage[:, block * chunk : (block + 1) * chunk]
        else:
            piece[...] = jnp.zeros(piece.shape, jnp.float32)
            piece[:, :chunk] = stage[:, block * chunk : (block + 1) * chunk]
        for date in range(per):
            base = date * date_rows
            mine = edges[block * EDGE : (block + 1) * EDGE, base : base + date_rows]
            piece[base + rows : base + date_rows, :] = jnp.zeros((EDGE, LANES), jnp.float32)
            piece[base + rows : base + date_rows, :date_rows] = mine
        send[block] = piece[...].astype(jnp.bfloat16)


def weight_kernel(lines, chunk, az, tiled, weights):
    out_rows = lines // STEP
    cols = chunk // STEP
    wide = out_rows * cols
    depth = out_rows * 2 * LANES
    shape = (LANES, wide)
    col = iota(shape, 1) % cols
    out_row = iota(shape, 1) // cols
    box = jnp.abs(iota(shape, 0) - STEP * col - tiled[...]) <= REACH
    for o in range(out_rows):
        mine = (box & (out_row == o)).astype(jnp.bfloat16)
        weights[2 * o * LANES : (2 * o + 1) * LANES, :] = mine
        weights[(2 * o + 1) * LANES : (2 * o + 2) * LANES, :] = mine
    rows = 2 * (lines + 2 * HALO)
    at = iota(shape, 0)
    turn = (at - 2 * lines) % (2 * HALO)
    line = jnp.where(at < 2 * lines, at % lines + HALO, jnp.where(turn < HALO, turn, turn + lines))
    line = jnp.where(at < rows, line, -100)
    lower = jnp.zeros(shape, jnp.int32)
    for o in range(out_rows):
        lower = jnp.where(out_row == o, STEP * o + az[o], lower)
    window = (line >= lower) & (line <= lower + 2 * HALO)
    for side, edge_col in ((0, 0), (1, cols - 1)):
        mine = (window & (col == edge_col)).astype(jnp.bfloat16)
        for term in range(2):
            start = depth + (2 * side + term) * LANES
            weights[start : start + LANES, :] = mine


def spread_kernel(blocks, per, date_rows, recv, x):
    dates = blocks * per
    for block in range(blocks):
        value = recv[block].astype(jnp.float32)
        for date in range(per):
            for row in range(0, date_rows, 8):
                part = value[date * date_rows + row : date * date_rows + row + 8]
                x[pl.ds(row * dates + block * per + date, 8, stride=dates), :] = part


def split(value):
    high = value.astype(jnp.bfloat16)
    return high, (value - high.astype(jnp.float32)).astype(jnp.bfloat16)


def pair_kernel(blocks, per, lines, chunk, group, x, order, az, rg, weights, send, sums, turned, left, power):
    dates = blocks * per
    out_rows = lines // STEP
    cols = chunk // STEP
    wide = out_rows * cols
    rows = 2 * (lines + 2 * HALO)
    me = lax.axis_index("date")
    depth = out_rows * 2 * LANES

    lane = iota((dates, LANES), 1)
    real = (lane < lines) | ((lane >= 2 * lines) & (lane < 2 * lines + 2 * HALO))
    for edge in range(EDGE):
        value = x[(rows + edge) * dates : (rows + edge + 1) * dates, :]
        up = jnp.where(lane < lines, pltpu.roll(value, LANES - lines, 1), pltpu.roll(value, LANES - 2 * HALO, 1))
        down = jnp.where(lane < 2 * lines, pltpu.roll(value, lines, 1), pltpu.roll(value, 2 * HALO, 1))
        turned[edge * dates : (edge + 1) * dates, :] = jnp.where(real, up, -down)
    first = rg[me * cols]
    last = rg[me * cols + cols - 1]
    edge_on = (first <= 0, first <= 1, last >= 2, last >= 3)

    def one_date(first_date, step, carry):
        date = first_date + step
        target = (step // per * 2) * per + step % per
        for tile in range(dates // 16):

            def own(row, ref=x):
                return ref[pl.ds(row * dates + date, 1), :]

            def others(row):
                return x[row * dates + tile * 16 : row * dates + tile * 16 + 16, :]

            real, imag = [], []
            for line in range(lines + 2 * HALO):
                at_re, at_im = row_of(0, line, lines), row_of(1, line, lines)
                re_i, im_i = own(at_re), own(at_im)
                re_j, im_j = others(at_re), others(at_im)
                real.append(re_i * re_j + im_i * im_j)
                imag.append(im_i * re_j - re_i * im_j)
            for part, product in enumerate((real, imag)):
                start = pl.multiple_of((target + part * per) * dates + tile * 16, 16)
                at_rows = pl.ds(start, 16)
                quads = []
                for k in range(out_rows + 1):
                    q = product[STEP * k + 3 : STEP * k + 7]
                    quads.append((q[0] + q[1]) + (q[2] + q[3]))
                for o in range(out_rows):
                    total = quads[o] + quads[o + 1]
                    for k in range(3):
                        total += jnp.where(az[o] <= k, product[STEP * o + k], product[STEP * o + 11 + k])
                    upper, rest = split(total)
                    left[at_rows, 2 * o * LANES : (2 * o + 1) * LANES] = upper
                    left[at_rows, (2 * o + 1) * LANES : (2 * o + 2) * LANES] = rest
                for side in range(2):
                    total = jnp.zeros((16, LANES), jnp.float32)
                    for edge in (2 * side, 2 * side + 1):
                        mine = own(edge, turned) if part else own(rows + edge)
                        total += jnp.where(edge_on[edge], mine * others(rows + edge), 0.0)
                    upper, rest = split(total)
                    start_col = depth + 2 * side * LANES
                    left[at_rows, start_col : start_col + LANES] = upper
                    left[at_rows, start_col + LANES : start_col + 2 * LANES] = rest
        return carry

    for first_date in range(0, dates, group):
        lax.fori_loop(0, group, functools.partial(one_date, first_date), 0)
        found = jnp.dot(left[...], weights[...], preferred_element_type=jnp.float32)
        sums[first_date * 2 * dates : (first_date + group) * 2 * dates, :] = found
    for date in range(dates):
        at_row = (date // per * 2 * per + date % per) * dates + date
        power[date : date + 1, :] = sums[at_row : at_row + 1, :]
    scale = lax.rsqrt(power[...] + epsilon)
    power[...] = scale
    position = iota((dates, wide), 0)
    column = iota((dates, wide), 1)
    rank = jnp.zeros((dates, wide), jnp.int32)
    for block in range(blocks):
        rank = jnp.where(position // per == block, order[block] * per + position % per, rank)
    for date in range(dates):
        later = rank > order[date // per] * per + date % per
        factor = scale * power[date : date + 1, :]
        starts = [((date // per * 2 + part) * per + date % per) * dates for part in range(2)]
        values = [jnp.where(later, sums[start : start + dates, :] * factor, 0.0) for start in starts]
        largest = jnp.max(jnp.maximum(jnp.abs(values[0]), jnp.abs(values[1])), axis=1, keepdims=True)
        level = jnp.floor(jnp.log(largest) * (LEVELS / LOG_2)) + 1.0
        level = jnp.clip(level, LOWEST, HIGHEST)
        codes = [jnp.floor(value * (jnp.exp(level * (-LOG_2 / LEVELS)) * TOP) + 0.5) for value in values]
        header = jnp.sum(jnp.where(position == column, level, 0.0), axis=0, keepdims=True)
        codes[0] = jnp.where(position == date, header, codes[0])
        for start, code in zip(starts, codes):
            send[start : start + dates, :] = code.astype(jnp.int32).astype(jnp.int16)


def join_kernel(blocks, per, out_rows, cols, recv, out, halves, done):
    dates = blocks * per
    wide = out_rows * cols
    per_tile = LANES // cols
    me = lax.axis_index("date")
    lane = iota((dates, LANES), 1) // cols
    position = iota((dates, wide), 0)
    column = iota((dates, wide), 1)
    factors = [[None] * blocks for _ in range(per)]
    copies = []
    for step in range(2 * per):
        own = me * per + step % per
        values = []
        for block in range(blocks):
            codes = recv[block, step * dates : (step + 1) * dates, :].astype(jnp.int32).astype(jnp.float32)
            if step < per:
                header = jnp.sum(jnp.where(position == own, codes, 0.0), axis=0, keepdims=True)
                level = jnp.sum(jnp.where(position == column, header, 0.0), axis=1, keepdims=True)
                factors[step][block] = jnp.exp(level * (LOG_2 / LEVELS)) * (1.0 / TOP)
            values.append(jnp.where(position == own, 0.0, codes * factors[step % per][block]))
        for d_tile in range(blocks // per_tile):
            for o_tile in range(out_rows // per_tile):
                tiles = [
                    values[d_tile * per_tile + d][:, o_tile * LANES : (o_tile + 1) * LANES] for d in range(per_tile)
                ]
                width = 1
                while width < per_tile:
                    swap = [None] * per_tile
                    upper = (lane // width) % 2 == 1
                    shift = width * cols
                    for a in range(per_tile):
                        if (a // width) % 2 == 0:
                            b = a + width
                            swap[a] = jnp.where(upper, pltpu.roll(tiles[b], shift, 1), tiles[a])
                            swap[b] = jnp.where(upper, tiles[b], pltpu.roll(tiles[a], LANES - shift, 1))
                    tiles = swap
                    width *= 2
                for o in range(per_tile):
                    for start in range(0, dates, 8):
                        at = start * out_rows + o_tile * per_tile + o
                        halves[step, d_tile, pl.ds(at, 8, stride=out_rows), :] = tiles[o][start : start + 8]
            rows = slice(step * dates * out_rows, (step + 1) * dates * out_rows)
            target = out.at[rows, d_tile * LANES : (d_tile + 1) * LANES]
            copies.append(pltpu.make_async_copy(halves.at[step, d_tile], target, done.at[step, d_tile]))
            copies[-1].start()
    for copy in copies:
        copy.wait()


def decode(codes, me, per):
    values = codes.astype(jnp.float32)
    dates = codes.shape[3]
    own = (me * per + jnp.arange(per))[:, None] == jnp.arange(dates)[None]
    header = jnp.sum(jnp.where(own[None, :, :, None], values[:, 0], 0.0), axis=2)
    factor = jnp.exp(header[:, :, :dates] * (LOG_2 / LEVELS)) * (1.0 / TOP)
    return jnp.where(own[None, None, :, :, None], 0.0, values * factor[:, None, :, :, None])


def on_device(slc, block_order, az_offset, rg_offset):
    blocks = lax.axis_size("date")
    strips = lax.axis_size("strip")
    per, lines, span = slc.shape[1:]
    dates = blocks * per
    chunk = span // blocks
    out_rows = lines // STEP
    cols = chunk // STEP
    wide = out_rows * cols
    date_rows = 2 * (lines + 2 * HALO) + EDGE
    depth = (out_rows + 2) * 2 * LANES
    group = max(per, 256 // dates)
    me = lax.axis_index("date")
    odd = lax.axis_index("strip") % 2

    def swaps(first):
        pairs = [(i, i + 1) for i in range(first, strips - 1, 2)]
        return pairs + [(target, source) for source, target in pairs]

    inner = lines - HALO
    other = lax.ppermute(lax.dynamic_slice_in_dim(slc, inner * odd, HALO, 2), "strip", swaps(1))
    paired = lax.ppermute(lax.dynamic_slice_in_dim(slc, inner * (1 - odd), HALO, 2), "strip", swaps(0))
    tiled = jnp.tile(lax.dynamic_slice_in_dim(rg_offset, me * cols, cols), out_rows)[None]
    weights = pl.pallas_call(
        functools.partial(weight_kernel, lines, chunk),
        out_shape=jax.ShapeDtypeStruct((depth, wide), jnp.bfloat16),
        in_specs=[SMEM, VMEM],
        out_specs=VMEM,
        compiler_params=PARAMS,
        cost_estimate=pl.CostEstimate(flops=0, bytes_accessed=4 * 1024 * 1024, transcendentals=0),
        name="weights",
    )(az_offset, tiled)
    other, paired, weights = lax.optimization_barrier((other, paired, weights))
    send = pl.pallas_call(
        functools.partial(pack_kernel, blocks, per, lines, chunk),
        out_shape=jax.ShapeDtypeStruct((blocks, per * date_rows, LANES), jnp.bfloat16),
        in_specs=[VMEM] * 3,
        out_specs=VMEM,
        scratch_shapes=[
            pltpu.VMEM((per * date_rows, span), jnp.float32),
            pltpu.VMEM((per * date_rows, LANES), jnp.float32),
        ],
        compiler_params=PARAMS,
        name="pack",
    )(slc, other, paired)
    recv = lax.all_to_all(send, "date", 0, 0, tiled=True)
    x = pl.pallas_call(
        functools.partial(spread_kernel, blocks, per, date_rows),
        out_shape=jax.ShapeDtypeStruct((date_rows * dates, LANES), jnp.float32),
        in_specs=[VMEM],
        out_specs=VMEM,
        compiler_params=PARAMS,
        name="spread",
    )(recv)
    pairs = pl.pallas_call(
        functools.partial(pair_kernel, blocks, per, lines, chunk, group),
        out_shape=jax.ShapeDtypeStruct((dates * 2 * dates, wide), jnp.int16),
        in_specs=[VMEM, SMEM, SMEM, SMEM, VMEM],
        out_specs=VMEM,
        scratch_shapes=[
            pltpu.VMEM((dates * 2 * dates, wide), jnp.float32),
            pltpu.VMEM((EDGE * dates, LANES), jnp.float32),
            pltpu.VMEM((group * 2 * dates, depth), jnp.bfloat16),
            pltpu.VMEM((dates, wide), jnp.float32),
        ],
        compiler_params=PARAMS,
        name="pairs",
    )(x, block_order, az_offset, rg_offset, weights)
    count = 2 * per * dates
    back = lax.all_to_all(pairs.reshape(blocks, count, wide), "date", 0, 0, tiled=True)
    if LANES % cols == 0 and out_rows * cols % LANES == 0 and blocks * cols % LANES == 0:
        out = pl.pallas_call(
            functools.partial(join_kernel, blocks, per, out_rows, cols),
            out_shape=jax.ShapeDtypeStruct((count * out_rows, blocks * cols), jnp.float32),
            in_specs=[VMEM],
            out_specs=pl.BlockSpec(memory_space=pl.ANY),
            scratch_shapes=[
                pltpu.VMEM((2 * per, blocks * cols // LANES, dates * out_rows, LANES), jnp.float32),
                pltpu.SemaphoreType.DMA((2 * per, blocks * cols // LANES)),
            ],
            compiler_params=PARAMS,
            name="join",
        )(back)
    else:
        values = decode(back.reshape(blocks, 2, per, dates, wide), me, per)
        out = values.reshape(blocks, count, out_rows, cols).transpose(1, 2, 0, 3)
    return out.reshape(2, per, dates, out_rows, blocks * cols)


def solution(mesh):
    placed = (P(None, "date", "strip", None), P(), P("strip"), P())
    return jax.shard_map(
        on_device,
        mesh=mesh,
        in_specs=placed,
        out_specs=P(None, "date", None, "strip", None),
        check_vma=False,
    )
```

time: 42.8 us -> 36.6 us (0.86)
  the two profiles are of different devices: /device:TPU:0 before, /device:TPU:16 now
where the time goes in v7:
time: 36.6 us; the launch traced here: 36.3 us
  blocking collectives  20.9 us (57%)
  Pallas kernels  7.28 us (20%)
  starting transfers between devices  3.55 us (10%)
  local copies, waits for them, and re-layouts  2.54 us (7%)
  waiting for transfers between devices  2 us (5%)
    all_to_all x1, blocking collectives, on_device(): recv = lax.all_to_all(send, 'date', 0, 0, tiled=True)  11.5 us
    all_to_all x1, blocking collectives, on_device(): lax.all_to_all(pairs.reshape(blocks, count, wide), 'date', 0, 0, tiled=True)  9.35 us
    pallas_call x1, Pallas kernels, on_device(): pl.pallas_call(functools.partial(pair_kernel, blocks, per, lines, chunk,...  4.4 us
    ppermute x1, waiting for transfers between devices, on_device(): lax.ppermute(lax.dynamic_slice_in_dim(slc, inner * odd, HALO, 2), 'strip'...  2 us
    ppermute x1, starting transfers between devices, on_device(): lax.ppermute(lax.dynamic_slice_in_dim(slc, inner * odd, HALO, 2), 'strip'...  1.91 us
    ppermute x1, starting transfers between devices, on_device(): lax.ppermute(lax.dynamic_slice_in_dim(slc, inner * (1 - odd), HALO, 2), '...  1.64 us
    pallas_call x1, Pallas kernels, on_device(): pl.pallas_call(functools.partial(join_kernel, blocks, per, out_rows, cols...  1.52 us
    dynamic_slice x1, local copies, waits for them, and re-layouts, on_device(): lax.dynamic_slice_in_dim(slc, inner * (1 - odd), HALO, 2)  1.02 us
  transfers between devices with their start and end apart: 2, of which 1 were waited for; matrix products, arithmetic and copies ran while one was open for 2% of the time, Pallas kernels for 2%

profile of v7, /device:TPU:16, one launch (start us, length us, event | category | flops | bytes accessed | tf_op | source)
XLA Modules:
  0.0 36.3 jit_solution(10077014828781838129)
XLA Ops:
  0.0 0.0 copy-start
  0.0 1.0 %constant_dynamic-slice_fusion = (bf16[2,2,5,1024]{3,2,1,0:T(8,128)(2,1)S(1)}, bf16[2,2,5,1024]{3,2,1,0:T(8,128)(2,1)S(1)}) fusion(bf16[2,2,32,1024]{3,2,1,0:T(8,128)(2,1)} %slc.1, s32[]{:T(128)S(6)} %select_n.18, s32[]{:T(128)S(6)} %select_n.17), kind=kLoop, calls=%fused_computation | loop fusion | bytes 163848 | tf_op jit(solution)/shard_map/dynamic_slice | solution.py:287
  1.0 1.6 %collective-permute-start.1 = (bf16[2,2,5,1024]{3,2,1,0:T(8,128)(2,1)S(1)}, bf16[2,2,5,1024]{3,2,1,0:T(8,128)(2,1)S(1)}, u32[]{:S(2)}, u32[]{:S(2)}) collective-permute-start(bf16[2,2,5,1024]{3,2,1,0:T(8,128)(2,1)S(1)} %get-tuple-element.11), channel_id=1, source_target_pairs={{0,1},{2,3},{1,0},{3,2},{4,5},{6,7},{5,4},{7,6},{8,9},{10,11},{9,8... | collective-permute-start | bytes 122888 | tf_op jit(solution)/shard_map/ppermute | solution.py:287
  2.7 1.9 %collective-permute-start = (bf16[2,2,5,1024]{3,2,1,0:T(8,128)(2,1)S(1)}, bf16[2,2,5,1024]{3,2,1,0:T(8,128)(2,1)S(1)}, u32[]{:S(2)}, u32[]{:S(2)}) collective-permute-start(bf16[2,2,5,1024]{3,2,1,0:T(8,128)(2,1)S(1)} %get-tuple-element.12), channel_id=1, source_target_pairs={{1,2},{2,1},{5,6},{6,5},{9,10},{10,9},{13,14},{14,13},{17,18},{18,... | collective-permute-start | bytes 122888 | tf_op jit(solution)/shard_map/ppermute | solution.py:286
  4.6 0.8 %dynamic_slice.11 = s32[32]{0:T(128)S(1)} dynamic-slice(s32[256]{0:T(256)} %rg.1, s32[]{:T(128)S(6)} %select_n.19), dynamic_slice_sizes={32} | dynamic-slice | bytes 260 | tf_op jit(solution)/shard_map/dynamic_slice | solution.py:288
  5.4 0.1 broadcast_in_dim_tile.3.tiled
  5.4 0.0 copy-start.1
  5.4 0.7 %copy-done.1 = s32[8]{0:T(128)S(1)} copy-done((s32[8]{0:T(128)S(1)}, s32[8]{0:T(128)}, u32[]{:S(2)}) %copy-start.1) | copy-done | bytes 56
  6.1 0.7 %weights.1 = bf16[2560,256]{1,0:T(8,128)(2,1)S(1)} custom-call(s32[8]{0:T(128)S(1)} %copy-done.1, s32[1,256]{1,0:T(1,128)S(1)} %broadcast_in_dim_tile.3.tiled), custom_call_target="tpu_custom_call" | custom-call | bytes 4194304 | tf_op jit(solution)/shard_map/weights/pallas_call | solution.py:289
  6.8 0.0 copy-start.2
  6.8 0.0 copy-start.3
  6.8 0.0 copy-start.4
  6.8 0.0 collective-permute-done.1.paired
  6.8 2.0 %collective-permute-done.other = bf16[2,2,5,1024]{3,2,1,0:T(8,128)(2,1)S(1)} collective-permute-done((bf16[2,2,5,1024]{3,2,1,0:T(8,128)(2,1)S(1)}, bf16[2,2,5,1024]{3,2,1,0:T(8,128)(2,1)S(1)}, u32[]{:S(2)}, u32[]{:S(2)}) %collective-permute-start) | collective-permute-done | bytes 40992 | tf_op jit(solution)/shard_map/ppermute | solution.py:286
  8.8 0.0 copy-done
  8.8 0.3 pack.1
  9.2 11.5 %all_to_all.10.recv = bf16[8,176,128]{2,1,0:T(8,128)(2,1)S(1)} all-to-all(bf16[8,176,128]{2,1,0:T(8,128)(2,1)S(1)} %pack.1), channel_id=1, replica_groups=mesh['date'=8,'strip'=4] {'date'}, dimensions={0} | all-to-all | bytes 720896 | tf_op jit(solution)/shard_map/all_to_all | solution.py:311
  20.7 0.3 spread.1.x
  21.0 0.0 copy-done.2
  21.0 0.0 copy-done.3
  21.0 0.0 copy-done.4
  21.1 4.4 %pairs.1 = s16[512,256]{1,0:T(8,128)(2,1)S(1)} custom-call(f32[1408,128]{1,0:T(8,128)S(1)} %spread.1.x, s32[8]{0:T(128)S(1)} %copy-done.4, s32[8]{0:T(128)S(1)} %copy-done.2, s32[256]{0:T(256)S(1)} %copy-done.3, bf16[2560,256]{1,0:T(8,128)(2,1)S(1)} %weights.1), custom_call_target="tpu_custom_call" | custom-call | tf_op jit(solution)/shard_map/pairs/pallas_call | solution.py:320
  25.5 9.3 %all_to_all.11.recv = s16[8,64,256]{2,1,0:T(8,128)(2,1)S(1)} all-to-all(s16[8,64,256]{2,1,0:T(8,128)(2,1)S(1)} %bitcast.2), channel_id=1, replica_groups=mesh['date'=8,'strip'=4] {'date'}, dimensions={0} | all-to-all | bytes 524288 | tf_op jit(solution)/shard_map/all_to_all | solution.py:335
  34.8 1.5 %join.1 = f32[512,256]{1,0:T(8,128)} custom-call(s16[8,64,256]{2,1,0:T(8,128)(2,1)S(1)} %all_to_all.11.recv), custom_call_target="tpu_custom_call" | custom-call | tf_op jit(solution)/shard_map/join/pallas_call | solution.py:337
  (1 shorter events, 0.0 us)
Async XLA Ops:
  0.0 8.8 %copy-start = (bf16[2,2,32,1024]{3,2,1,0:T(8,128)(2,1)S(1)}, bf16[2,2,32,1024]{3,2,1,0:T(8,128)(2,1)}, u32[]{:S(2)}) copy-start(bf16[2,2,32,1024]{3,2,1,0:T(8,128)(2,1)} %slc.1) | copy-start | bytes 786436
  1.0 5.8 %collective-permute-start.1 = (bf16[2,2,5,1024]{3,2,1,0:T(8,128)(2,1)S(1)}, bf16[2,2,5,1024]{3,2,1,0:T(8,128)(2,1)S(1)}, u32[]{:S(2)}, u32[]{:S(2)}) collective-permute-start(bf16[2,2,5,1024]{3,2,1,0:T(8,128)(2,1)S(1)} %get-tuple-element.11), channel_id=1, source_target_pairs={{0,1},{2,3},{1,0},{3,2},{4,5},{6,7},{5,4},{7,6},{8,9},{10,11},{9,8... | collective-permute-start | bytes 122888 | tf_op jit(solution)/shard_map/ppermute | solution.py:287
  2.7 6.1 %collective-permute-start = (bf16[2,2,5,1024]{3,2,1,0:T(8,128)(2,1)S(1)}, bf16[2,2,5,1024]{3,2,1,0:T(8,128)(2,1)S(1)}, u32[]{:S(2)}, u32[]{:S(2)}) collective-permute-start(bf16[2,2,5,1024]{3,2,1,0:T(8,128)(2,1)S(1)} %get-tuple-element.12), channel_id=1, source_target_pairs={{1,2},{2,1},{5,6},{6,5},{9,10},{10,9},{13,14},{14,13},{17,18},{18,... | collective-permute-start | bytes 122888 | tf_op jit(solution)/shard_map/ppermute | solution.py:286
  5.4 0.7 %copy-start.1 = (s32[8]{0:T(128)S(1)}, s32[8]{0:T(128)}, u32[]{:S(2)}) copy-start(s32[8]{0:T(128)} %az.3) | copy-start | bytes 100
  6.8 14.3 %copy-start.2 = (s32[8]{0:T(128)S(1)}, s32[8]{0:T(128)}, u32[]{:S(2)}) copy-start(s32[8]{0:T(128)} %az.3) | copy-start | bytes 100
  6.8 14.3 %copy-start.3 = (s32[256]{0:T(256)S(1)}, s32[256]{0:T(256)}, u32[]{:S(2)}) copy-start(s32[256]{0:T(256)} %rg.1) | copy-start | bytes 3076
  6.8 14.2 %copy-start.4 = (s32[8]{0:T(128)S(1)}, s32[8]{0:T(128)}, u32[]{:S(2)}) copy-start(s32[8]{0:T(128)} %order.1) | copy-start | bytes 100

commit v8 on v5

--- a/solution.py
+++ b/solution.py
@@ -65,7 +65,22 @@
     return found
 
 
-def pack_kernel(blocks, per, lines, chunk, slc, send, stage):
+def partners(blocks):
+    return [0] + sorted(range(1, blocks), key=lambda k: (k & 1, -k))
+
+
+def swap_blocks(pieces):
+    blocks = len(pieces)
+    found = list(pieces)
+    for at, k in enumerate(partners(blocks)):
+        if k:
+            found[at] = lax.ppermute(pieces[at], "date", [(i, i ^ k) for i in range(blocks)])
+    return found
+
+
+def pack_kernel(blocks, per, lines, chunk, slc, *refs):
+    pieces, (send, stage) = refs[:blocks], refs[blocks:]
+    me = lax.axis_index("date")
     date_rows = rows_of_date(lines)
     edge_rows = per * GROUP
     turn = 1 - lax.axis_index("strip") % 2
@@ -110,6 +125,8 @@
         send[block, pl.ds(pl.multiple_of(turn * edge_rows, 16), edge_rows), :] = piece[:edge_rows]
         send[block, pl.ds(pl.multiple_of((1 - turn) * edge_rows, 16), edge_rows), :] = piece[edge_rows : 2 * edge_rows]
         send[block, 2 * edge_rows :, :] = piece[2 * edge_rows :]
+    for piece, k in zip(pieces, partners(blocks)):
+        piece[...] = send[me ^ k]
 
 
 def weight_kernel(lines, chunk, az, tiled, weights):
@@ -138,27 +155,31 @@
             weights[start : start + LANES, :] = mine
 
 
-def to_sublanes(blocks, per, rows, first_row, date_stride, source, target):
-    dates = blocks * per
-    for block in range(blocks):
-        for date in range(per):
-            at = first_row + date * date_stride
-            if not isinstance(at, int):
-                at = pl.multiple_of(at, 8)
-            value = source[block, pl.ds(at, rows), :].astype(jnp.float32)
-            for row in range(0, rows, 8):
-                target[pl.ds(row * dates + block * per + date, 8, stride=dates), :] = value[row : row + 8]
-
-
-def spread_kernel(blocks, per, lines, recv, x):
+def to_sublanes(source, first_row, date_stride, rows, block, dates, per, target):
+    for date in range(per):
+        at = first_row + date * date_stride
+        if not isinstance(at, int):
+            at = pl.multiple_of(at, 8)
+        value = source[pl.ds(at, rows), :].astype(jnp.float32)
+        for row in range(0, rows, 8):
+            target[pl.ds(row * dates + block * per + date, 8, stride=dates), :] = value[row : row + 8]
+
+
+def spread_kernel(blocks, per, lines, *refs):
+    recv, (x, paired, other) = refs[:blocks], refs[blocks:]
     dates = blocks * per
     date_rows = rows_of_date(lines)
     edge_rows = per * GROUP
+    me = lax.axis_index("date")
     turn = 1 - lax.axis_index("strip") % 2
-    to_sublanes(blocks, per, GROUP, turn * edge_rows, GROUP, recv, x)
-    to_sublanes(blocks, per, GROUP, (1 - turn) * edge_rows, GROUP, recv, x.at[GROUP * dates :])
     rest = date_rows - 2 * GROUP
-    to_sublanes(blocks, per, rest, 2 * edge_rows, rest, recv, x.at[2 * GROUP * dates :])
+    for piece, k in zip(recv, partners(blocks)):
+        block = me ^ k
+        paired[block] = piece[:edge_rows]
+        other[block] = piece[edge_rows : 2 * edge_rows]
+        to_sublanes(piece, turn * edge_rows, GROUP, GROUP, block, dates, per, x)
+        to_sublanes(piece, (1 - turn) * edge_rows, GROUP, GROUP, block, dates, per, x.at[GROUP * dates :])
+        to_sublanes(piece, 2 * edge_rows, rest, rest, block, dates, per, x.at[2 * GROUP * dates :])
 
 
 def split(value):
@@ -167,8 +188,9 @@
 
 
 def pair_kernel(
-    blocks, per, lines, chunk, group, x, paired, other, order, az, rg, weights, send, sums, halo, edges, turned, left, power
+    blocks, per, lines, chunk, group, x, paired, other, order, az, rg, weights, *refs
 ):
+    pieces, (send, sums, halo, edges, turned, left, power) = refs[:blocks], refs[blocks:]
     dates = blocks * per
     out_rows = lines // STEP
     cols = chunk // STEP
@@ -177,8 +199,9 @@
     depth = out_rows * 2 * LANES
 
     odd = lax.axis_index("strip") % 2
-    to_sublanes(blocks, per, GROUP, 0, GROUP, paired, halo.at[1 - odd])
-    to_sublanes(blocks, per, GROUP, 0, GROUP, other, halo.at[odd])
+    for block in range(blocks):
+        to_sublanes(paired.at[block], 0, GROUP, GROUP, block, dates, per, halo.at[1 - odd])
+        to_sublanes(other.at[block], 0, GROUP, GROUP, block, dates, per, halo.at[odd])
     below, above = halo.at[0], halo.at[1]
     lane = iota((dates, LANES), 1)
     turn = lane % (LANES // 2)
@@ -271,9 +294,13 @@
         codes[0] = jnp.where(position == date, header, codes[0])
         for start, code in zip(starts, codes):
             send[start : start + dates, :] = code.astype(jnp.int32).astype(jnp.int16)
-
-
-def join_kernel(blocks, per, out_rows, cols, recv, out, halves, done):
+    count = 2 * per * dates
+    for piece, k in zip(pieces, partners(blocks)):
+        piece[...] = send[pl.ds(pl.multiple_of((me ^ k) * count, 16), count), :]
+
+
+def join_kernel(blocks, per, out_rows, cols, *refs):
+    pieces, (out, recv, halves, done) = refs[:blocks], refs[blocks:]
     dates = blocks * per
     wide = out_rows * cols
     per_tile = LANES // cols
@@ -281,6 +308,8 @@
     lane = iota((dates, LANES), 1) // cols
     position = iota((dates, wide), 0)
     column = iota((dates, wide), 1)
+    for piece, k in zip(pieces, partners(blocks)):
+        recv[me ^ k] = piece[...]
     factors = [[None] * blocks for _ in range(per)]
     copies = []
     for step in range(2 * per):
@@ -345,16 +374,21 @@
     group = max(per, 256 // dates)
     me = lax.axis_index("date")
 
+    edge_rows = per * GROUP
+    piece = jax.ShapeDtypeStruct((per * date_rows, LANES), jnp.bfloat16)
     send = pl.pallas_call(
         functools.partial(pack_kernel, blocks, per, lines, chunk),
-        out_shape=jax.ShapeDtypeStruct((blocks, per * date_rows, LANES), jnp.bfloat16),
+        out_shape=[piece] * blocks,
         in_specs=[VMEM],
-        out_specs=VMEM,
-        scratch_shapes=[pltpu.VMEM((per * date_rows, span), jnp.float32)],
+        out_specs=[VMEM] * blocks,
+        scratch_shapes=[
+            pltpu.VMEM((blocks, per * date_rows, LANES), jnp.bfloat16),
+            pltpu.VMEM((per * date_rows, span), jnp.float32),
+        ],
         compiler_params=PARAMS,
         name="pack",
     )(slc)
-    recv = lax.all_to_all(send, "date", 0, 0, tiled=True)
+    recv = swap_blocks(send)
     tiled = jnp.tile(lax.dynamic_slice_in_dim(rg_offset, me * cols, cols), out_rows)[None]
     weights = pl.pallas_call(
         functools.partial(weight_kernel, lines, chunk),
@@ -366,29 +400,29 @@
         name="weights",
     )(az_offset, tiled)
 
-    edge_rows = per * GROUP
+    edge = jax.ShapeDtypeStruct((blocks, edge_rows, LANES), jnp.bfloat16)
+    x, to_pair, to_other = pl.pallas_call(
+        functools.partial(spread_kernel, blocks, per, lines),
+        out_shape=[jax.ShapeDtypeStruct((date_rows * dates, LANES), jnp.float32), edge, edge],
+        in_specs=[VMEM] * blocks,
+        out_specs=[VMEM] * 3,
+        compiler_params=PARAMS,
+        name="spread",
+    )(*recv)
 
     def swaps(first):
         pairs = [(i, i + 1) for i in range(first, strips - 1, 2)]
         return pairs + [(target, source) for source, target in pairs]
 
-    other = lax.ppermute(recv[:, edge_rows : 2 * edge_rows], "strip", swaps(1))
-    paired = lax.ppermute(recv[:, :edge_rows], "strip", swaps(0))
-    x = pl.pallas_call(
-        functools.partial(spread_kernel, blocks, per, lines),
-        out_shape=jax.ShapeDtypeStruct((date_rows * dates, LANES), jnp.float32),
-        in_specs=[VMEM],
-        out_specs=VMEM,
-        compiler_params=PARAMS,
-        cost_estimate=pl.CostEstimate(flops=0, bytes_accessed=4 * 1024 * 1024, transcendentals=0),
-        name="spread",
-    )(recv)
+    other = lax.ppermute(to_other, "strip", swaps(1))
+    paired = lax.ppermute(to_pair, "strip", swaps(0))
     pairs = pl.pallas_call(
         functools.partial(pair_kernel, blocks, per, lines, chunk, group),
-        out_shape=jax.ShapeDtypeStruct((dates * 2 * dates, wide), jnp.int16),
+        out_shape=[jax.ShapeDtypeStruct((2 * per * dates, wide), jnp.int16)] * blocks,
         in_specs=[VMEM, VMEM, VMEM, SMEM, SMEM, SMEM, VMEM],
-        out_specs=VMEM,
+        out_specs=[VMEM] * blocks,
         scratch_shapes=[
+            pltpu.VMEM((dates * 2 * dates, wide), jnp.int16),
             pltpu.VMEM((dates * 2 * dates, wide), jnp.float32),
             pltpu.VMEM((2, GROUP * dates, LANES), jnp.float32),
             pltpu.VMEM((EDGE * dates, LANES), jnp.float32),
@@ -400,21 +434,24 @@
         name="pairs",
     )(x, paired, other, block_order, az_offset, rg_offset, weights)
     count = 2 * per * dates
-    back = lax.all_to_all(pairs.reshape(blocks, count, wide), "date", 0, 0, tiled=True)
+    back = swap_blocks(pairs)
     if LANES % cols == 0 and out_rows * cols % LANES == 0 and blocks * cols % LANES == 0:
         out = pl.pallas_call(
             functools.partial(join_kernel, blocks, per, out_rows, cols),
             out_shape=jax.ShapeDtypeStruct((count * out_rows, blocks * cols), jnp.float32),
-            in_specs=[VMEM],
+            in_specs=[VMEM] * blocks,
             out_specs=pl.BlockSpec(memory_space=pl.ANY),
             scratch_shapes=[
+                pltpu.VMEM((blocks, count, wide), jnp.int16),
                 pltpu.VMEM((2 * per, blocks * cols // LANES, dates * out_rows, LANES), jnp.float32),
                 pltpu.SemaphoreType.DMA((2 * per, blocks * cols // LANES)),
             ],
             compiler_params=PARAMS,
             name="join",
-        )(back)
+        )(*back)
     else:
+        place = [partners(blocks).index(k) for k in range(blocks)]
+        back = jnp.stack([back[at] for at in place])[me ^ jnp.arange(blocks)]
         values = decode(back.reshape(blocks, 2, per, dates, wide), me, per)
         out = values.reshape(blocks, count, out_rows, cols).transpose(1, 2, 0, 3)
     return out.reshape(2, per, dates, out_rows, blocks * cols)

time: 36.6 us -> 34.6 us (0.945)
  the two profiles are of different devices: /device:TPU:0 before, /device:TPU:9 now
where the time goes in v8:
time: 34.6 us; the launch traced here: 34 us
  starting transfers between devices  19 us (55%)
  Pallas kernels  7.33 us (21%)
  waiting for transfers between devices  5.11 us (15%)
  local copies, waits for them, and re-layouts  2.46 us (7%)
    ppermute x14, starting transfers between devices, swap_blocks(): lax.ppermute(pieces[at], 'date', [(i, i ^ k) for i in range(blocks)])  14.5 us
    ppermute x14, waiting for transfers between devices, swap_blocks(): lax.ppermute(pieces[at], 'date', [(i, i ^ k) for i in range(blocks)])  5.11 us
    pallas_call x1, Pallas kernels, on_device(): pl.pallas_call(functools.partial(pair_kernel, blocks, per, lines, chunk,...  4.52 us
    ppermute x1, starting transfers between devices, on_device(): other = lax.ppermute(to_other, 'strip', swaps(1))  4.32 us
    unnamed x10, local copies, waits for them, and re-layouts  1.62 us
    pallas_call x1, Pallas kernels, on_device(): pl.pallas_call(functools.partial(join_kernel, blocks, per, out_rows, cols...  1.54 us
    dynamic_slice x1, local copies, waits for them, and re-layouts, on_device(): lax.dynamic_slice_in_dim(rg_offset, me * cols, cols)  0.76 us
  transfers between devices with their start and end apart: 16, of which 6 were waited for; matrix products, arithmetic and copies ran while one was open for 2% of the time, Pallas kernels for 2%

profile of v8, /device:TPU:9, one launch (start us, length us, event | category | flops | bytes accessed | tf_op | source)
XLA Modules:
  0.0 34.0 jit_solution(12230438892838844407)
XLA Ops:
  0.0 0.9 %copy-done = bf16[2,2,32,1024]{3,2,1,0:T(8,128)(2,1)S(1)} copy-done((bf16[2,2,32,1024]{3,2,1,0:T(8,128)(2,1)S(1)}, bf16[2,2,32,1024]{3,2,1,0:T(8,128)(2,1)}, u32[]{:S(2)}) %copy-start) | copy-done | bytes 262168
  1.0 0.3 pack.1
  1.3 2.2 %collective-permute-start = (bf16[144,128]{1,0:T(8,128)(2,1)S(1)}, bf16[144,128]{1,0:T(8,128)(2,1)S(1)}, u32[]{:S(2)}, u32[]{:S(2)}) collective-permute-start(bf16[144,128]{1,0:T(8,128)(2,1)S(1)} %get-tuple-element.25), channel_id=1, source_target_pairs={{0,24},{4,28},{8,16},{12,20},{16,8},{20,12},{24,0},{28,4},{1,25},{... | collective-permute-start | bytes 110600 | tf_op jit(solution)/shard_map/ppermute | solution.py:77
  3.5 0.2 collective-permute-start.1
  3.7 0.3 collective-permute-start.2
  4.0 3.6 %collective-permute-start.3 = (bf16[144,128]{1,0:T(8,128)(2,1)S(1)}, bf16[144,128]{1,0:T(8,128)(2,1)S(1)}, u32[]{:S(2)}, u32[]{:S(2)}) collective-permute-start(bf16[144,128]{1,0:T(8,128)(2,1)S(1)} %get-tuple-element.28), channel_id=1, source_target_pairs={{0,28},{4,24},{8,20},{12,16},{16,12},{20,8},{24,4},{28,0},{1,29},{... | collective-permute-start | bytes 110600 | tf_op jit(solution)/shard_map/ppermute | solution.py:77
  7.6 0.0 collective-permute-done.refs_1_
  7.6 0.8 %collective-permute-start.5 = (bf16[144,128]{1,0:T(8,128)(2,1)S(1)}, bf16[144,128]{1,0:T(8,128)(2,1)S(1)}, u32[]{:S(2)}, u32[]{:S(2)}) collective-permute-start(bf16[144,128]{1,0:T(8,128)(2,1)S(1)} %get-tuple-element.30), channel_id=1, source_target_pairs={{0,12},{4,8},{8,4},{12,0},{16,28},{20,24},{24,20},{28,16},{1,13},{... | collective-permute-start | bytes 110600 | tf_op jit(solution)/shard_map/ppermute | solution.py:77
  8.3 0.0 collective-permute-done.1.refs_2_
  8.3 0.1 collective-permute-start.6
  8.4 0.0 collective-permute-done.2.refs_3_
  8.4 1.5 %collective-permute-done.3.refs_4_ = bf16[144,128]{1,0:T(8,128)(2,1)S(1)} collective-permute-done((bf16[144,128]{1,0:T(8,128)(2,1)S(1)}, bf16[144,128]{1,0:T(8,128)(2,1)S(1)}, u32[]{:S(2)}, u32[]{:S(2)}) %collective-permute-start.3) | collective-permute-done | bytes 36896 | tf_op jit(solution)/shard_map/ppermute | solution.py:77
  9.9 1.3 %collective-permute-done.4.refs_5_ = bf16[144,128]{1,0:T(8,128)(2,1)S(1)} collective-permute-done((bf16[144,128]{1,0:T(8,128)(2,1)S(1)}, bf16[144,128]{1,0:T(8,128)(2,1)S(1)}, u32[]{:S(2)}, u32[]{:S(2)}) %collective-permute-start.4) | collective-permute-done | bytes 36896 | tf_op jit(solution)/shard_map/ppermute | solution.py:77
  11.2 0.3 collective-permute-done.5.refs_6_
  11.5 0.0 collective-permute-done.6.refs_7_
  11.5 0.3 spread.1
  11.8 0.2 collective-permute-start.7
  12.0 4.3 %collective-permute-start.8 = (bf16[8,32,128]{2,1,0:T(8,128)(2,1)S(1)}, bf16[8,32,128]{2,1,0:T(8,128)(2,1)S(1)}, u32[]{:S(2)}, u32[]{:S(2)}) collective-permute-start(bf16[8,32,128]{2,1,0:T(8,128)(2,1)S(1)} %get-tuple-element.34), channel_id=1, source_target_pairs={{1,2},{2,1},{5,6},{6,5},{9,10},{10,9},{13,14},{14,13},{17,18},{18,... | collective-permute-start | bytes 196616 | tf_op jit(solution)/shard_map/ppermute | solution.py:417
  16.3 0.8 %dynamic_slice.3 = s32[32]{0:T(128)S(1)} dynamic-slice(s32[256]{0:T(256)} %rg.1, s32[]{:T(128)S(6)} %select_n.3), dynamic_slice_sizes={32} | dynamic-slice | bytes 260 | tf_op jit(solution)/shard_map/dynamic_slice | solution.py:392
  17.1 0.1 broadcast_in_dim_tile.3.tiled
  17.2 0.7 %copy-done.1 = s32[8]{0:T(128)S(1)} copy-done((s32[8]{0:T(128)S(1)}, s32[8]{0:T(128)}, u32[]{:S(2)}) %copy-start.1) | copy-done | bytes 56
  17.8 0.7 %weights.1 = bf16[2560,256]{1,0:T(8,128)(2,1)S(1)} custom-call(s32[8]{0:T(128)S(1)} %copy-done.1, s32[1,256]{1,0:T(1,128)S(1)} %broadcast_in_dim_tile.3.tiled), custom_call_target="tpu_custom_call" | custom-call | bytes 4194304 | tf_op jit(solution)/shard_map/weights/pallas_call | solution.py:393
  18.6 4.5 %pairs.1 = (s16[64,256]{1,0:T(8,128)(2,1)S(1)}, s16[64,256]{1,0:T(8,128)(2,1)S(1)}, s16[64,256]{1,0:T(8,128)(2,1)S(1)}, s16[64,256]{1,0:T(8,128)(2,1)S(1)}, s16[...) custom-call(f32[1152,128]{1,0:T(8,128)S(1)} %get-tuple-element.32.x,, ...), custom_call_target="tpu_custom_call" | custom-call | tf_op jit(solution)/shard_map/pairs/pallas_call | solution.py:419
  23.1 1.3 %collective-permute-start.9 = (s16[64,256]{1,0:T(8,128)(2,1)S(1)}, s16[64,256]{1,0:T(8,128)(2,1)S(1)}, u32[]{:S(2)}, u32[]{:S(2)}) collective-permute-start(s16[64,256]{1,0:T(8,128)(2,1)S(1)} %get-tuple-element.36), channel_id=1, source_target_pairs={{0,24},{4,28},{8,16},{12,20},{16,8},{20,12},{24,0},{28,4},{1,25},{... | collective-permute-start | bytes 98312 | tf_op jit(solution)/shard_map/ppermute | solution.py:77
  24.4 0.2 collective-permute-start.10
  24.6 1.2 %collective-permute-start.11 = (s16[64,256]{1,0:T(8,128)(2,1)S(1)}, s16[64,256]{1,0:T(8,128)(2,1)S(1)}, u32[]{:S(2)}, u32[]{:S(2)}) collective-permute-start(s16[64,256]{1,0:T(8,128)(2,1)S(1)} %get-tuple-element.38), channel_id=1, source_target_pairs={{0,8},{4,12},{8,0},{12,4},{16,24},{20,28},{24,16},{28,20},{1,9},{5... | collective-permute-start | bytes 98312 | tf_op jit(solution)/shard_map/ppermute | solution.py:77
  25.8 2.9 %collective-permute-start.12 = (s16[64,256]{1,0:T(8,128)(2,1)S(1)}, s16[64,256]{1,0:T(8,128)(2,1)S(1)}, u32[]{:S(2)}, u32[]{:S(2)}) collective-permute-start(s16[64,256]{1,0:T(8,128)(2,1)S(1)} %get-tuple-element.39), channel_id=1, source_target_pairs={{0,28},{4,24},{8,20},{12,16},{16,12},{20,8},{24,4},{28,0},{1,29},{... | collective-permute-start | bytes 98312 | tf_op jit(solution)/shard_map/ppermute | solution.py:77
  28.7 1.7 %collective-permute-start.14 = (s16[64,256]{1,0:T(8,128)(2,1)S(1)}, s16[64,256]{1,0:T(8,128)(2,1)S(1)}, u32[]{:S(2)}, u32[]{:S(2)}) collective-permute-start(s16[64,256]{1,0:T(8,128)(2,1)S(1)} %get-tuple-element.41), channel_id=1, source_target_pairs={{0,12},{4,8},{8,4},{12,0},{16,28},{20,24},{24,20},{28,16},{1,13},{... | collective-permute-start | bytes 98312 | tf_op jit(solution)/shard_map/ppermute | solution.py:77
  30.5 0.2 collective-permute-done.12.refs_4_
  30.7 1.7 %collective-permute-done.13.refs_5_ = s16[64,256]{1,0:T(8,128)(2,1)S(1)} collective-permute-done((s16[64,256]{1,0:T(8,128)(2,1)S(1)}, s16[64,256]{1,0:T(8,128)(2,1)S(1)}, u32[]{:S(2)}, u32[]{:S(2)}) %collective-permute-start.13) | collective-permute-done | bytes 32800 | tf_op jit(solution)/shard_map/ppermute | solution.py:77
  32.4 0.1 collective-permute-done.14.refs_6_
  32.5 1.5 %join.1 = f32[512,256]{1,0:T(8,128)} custom-call(s16[64,256]{1,0:T(8,128)(2,1)S(1)} %get-tuple-element.35.refs_0_, s16[64,256]{1,0:T(8,128)(2,1)S(1)} %collective-permute-done.9.refs_1_, s16[64,256]{1,0:T(8,128)(2,1)S(1)} %collective-permute-done.10.refs_2_, s16[64,256]{1,0:T(8,128)(2,1)S(1)} %collective-permute-done.11.refs_3_, ...), custom_call_target="tpu_custom_call" | custom-call | tf_op jit(solution)/shard_map/join/pallas_call | solution.py:439
  (18 shorter events, 0.0 us)
Async XLA Ops:
  0.0 0.9 %copy-start = (bf16[2,2,32,1024]{3,2,1,0:T(8,128)(2,1)S(1)}, bf16[2,2,32,1024]{3,2,1,0:T(8,128)(2,1)}, u32[]{:S(2)}) copy-start(bf16[2,2,32,1024]{3,2,1,0:T(8,128)(2,1)} %slc.1) | copy-start | bytes 786436
  1.0 17.6 %copy-start.2 = (s32[8]{0:T(128)S(1)}, s32[8]{0:T(128)}, u32[]{:S(2)}) copy-start(s32[8]{0:T(128)} %az.3) | copy-start | bytes 100
  1.0 17.6 %copy-start.3 = (s32[256]{0:T(256)S(1)}, s32[256]{0:T(256)}, u32[]{:S(2)}) copy-start(s32[256]{0:T(256)} %rg.1) | copy-start | bytes 3076
  1.0 17.6 %copy-start.4 = (s32[8]{0:T(128)S(1)}, s32[8]{0:T(128)}, u32[]{:S(2)}) copy-start(s32[8]{0:T(128)} %order.1) | copy-start | bytes 100
  1.3 6.3 %collective-permute-start = (bf16[144,128]{1,0:T(8,128)(2,1)S(1)}, bf16[144,128]{1,0:T(8,128)(2,1)S(1)}, u32[]{:S(2)}, u32[]{:S(2)}) collective-permute-start(bf16[144,128]{1,0:T(8,128)(2,1)S(1)} %get-tuple-element.25), channel_id=1, source_target_pairs={{0,24},{4,28},{8,16},{12,20},{16,8},{20,12},{24,0},{28,4},{1,25},{... | collective-permute-start | bytes 110600 | tf_op jit(solution)/shard_map/ppermute | solution.py:77
  3.5 4.8 %collective-permute-start.1 = (bf16[144,128]{1,0:T(8,128)(2,1)S(1)}, bf16[144,128]{1,0:T(8,128)(2,1)S(1)}, u32[]{:S(2)}, u32[]{:S(2)}) collective-permute-start(bf16[144,128]{1,0:T(8,128)(2,1)S(1)} %get-tuple-element.26), channel_id=1, source_target_pairs={{0,16},{4,20},{8,24},{12,28},{16,0},{20,4},{24,8},{28,12},{1,17},{... | collective-permute-start | bytes 110600 | tf_op jit(solution)/shard_map/ppermute | solution.py:77
  3.7 4.7 %collective-permute-start.2 = (bf16[144,128]{1,0:T(8,128)(2,1)S(1)}, bf16[144,128]{1,0:T(8,128)(2,1)S(1)}, u32[]{:S(2)}, u32[]{:S(2)}) collective-permute-start(bf16[144,128]{1,0:T(8,128)(2,1)S(1)} %get-tuple-element.27), channel_id=1, source_target_pairs={{0,8},{4,12},{8,0},{12,4},{16,24},{20,28},{24,16},{28,20},{1,9},{5... | collective-permute-start | bytes 110600 | tf_op jit(solution)/shard_map/ppermute | solution.py:77
  4.0 5.9 %collective-permute-start.3 = (bf16[144,128]{1,0:T(8,128)(2,1)S(1)}, bf16[144,128]{1,0:T(8,128)(2,1)S(1)}, u32[]{:S(2)}, u32[]{:S(2)}) collective-permute-start(bf16[144,128]{1,0:T(8,128)(2,1)S(1)} %get-tuple-element.28), channel_id=1, source_target_pairs={{0,28},{4,24},{8,20},{12,16},{16,12},{20,8},{24,4},{28,0},{1,29},{... | collective-permute-start | bytes 110600 | tf_op jit(solution)/shard_map/ppermute | solution.py:77
  7.6 3.7 %collective-permute-start.4 = (bf16[144,128]{1,0:T(8,128)(2,1)S(1)}, bf16[144,128]{1,0:T(8,128)(2,1)S(1)}, u32[]{:S(2)}, u32[]{:S(2)}) collective-permute-start(bf16[144,128]{1,0:T(8,128)(2,1)S(1)} %get-tuple-element.29), channel_id=1, source_target_pairs={{0,20},{4,16},{8,28},{12,24},{16,4},{20,0},{24,12},{28,8},{1,21},{... | collective-permute-start | bytes 110600 | tf_op jit(solution)/shard_map/ppermute | solution.py:77
  7.6 3.9 %collective-permute-start.5 = (bf16[144,128]{1,0:T(8,128)(2,1)S(1)}, bf16[144,128]{1,0:T(8,128)(2,1)S(1)}, u32[]{:S(2)}, u32[]{:S(2)}) collective-permute-start(bf16[144,128]{1,0:T(8,128)(2,1)S(1)} %get-tuple-element.30), channel_id=1, source_target_pairs={{0,12},{4,8},{8,4},{12,0},{16,28},{20,24},{24,20},{28,16},{1,13},{... | collective-permute-start | bytes 110600 | tf_op jit(solution)/shard_map/ppermute | solution.py:77
  8.3 3.2 %collective-permute-start.6 = (bf16[144,128]{1,0:T(8,128)(2,1)S(1)}, bf16[144,128]{1,0:T(8,128)(2,1)S(1)}, u32[]{:S(2)}, u32[]{:S(2)}) collective-permute-start(bf16[144,128]{1,0:T(8,128)(2,1)S(1)} %get-tuple-element.31), channel_id=1, source_target_pairs={{0,4},{4,0},{8,12},{12,8},{16,20},{20,16},{24,28},{28,24},{1,5},{5... | collective-permute-start | bytes 110600 | tf_op jit(solution)/shard_map/ppermute | solution.py:77
  11.8 6.8 %collective-permute-start.7 = (bf16[8,32,128]{2,1,0:T(8,128)(2,1)S(1)}, bf16[8,32,128]{2,1,0:T(8,128)(2,1)S(1)}, u32[]{:S(2)}, u32[]{:S(2)}) collective-permute-start(bf16[8,32,128]{2,1,0:T(8,128)(2,1)S(1)} %get-tuple-element.33), channel_id=1, source_target_pairs={{0,1},{2,3},{1,0},{3,2},{4,5},{6,7},{5,4},{7,6},{8,9},{10,11},{9,8... | collective-permute-start | bytes 196616 | tf_op jit(solution)/shard_map/ppermute | solution.py:418
  12.0 6.5 %collective-permute-start.8 = (bf16[8,32,128]{2,1,0:T(8,128)(2,1)S(1)}, bf16[8,32,128]{2,1,0:T(8,128)(2,1)S(1)}, u32[]{:S(2)}, u32[]{:S(2)}) collective-permute-start(bf16[8,32,128]{2,1,0:T(8,128)(2,1)S(1)} %get-tuple-element.34), channel_id=1, source_target_pairs={{1,2},{2,1},{5,6},{6,5},{9,10},{10,9},{13,14},{14,13},{17,18},{18,... | collective-permute-start | bytes 196616 | tf_op jit(solution)/shard_map/ppermute | solution.py:417
  17.2 0.7 %copy-start.1 = (s32[8]{0:T(128)S(1)}, s32[8]{0:T(128)}, u32[]{:S(2)}) copy-start(s32[8]{0:T(128)} %az.3) | copy-start | bytes 100
  23.1 5.6 %collective-permute-start.9 = (s16[64,256]{1,0:T(8,128)(2,1)S(1)}, s16[64,256]{1,0:T(8,128)(2,1)S(1)}, u32[]{:S(2)}, u32[]{:S(2)}) collective-permute-start(s16[64,256]{1,0:T(8,128)(2,1)S(1)} %get-tuple-element.36), channel_id=1, source_target_pairs={{0,24},{4,28},{8,16},{12,20},{16,8},{20,12},{24,0},{28,4},{1,25},{... | collective-permute-start | bytes 98312 | tf_op jit(solution)/shard_map/ppermute | solution.py:77
  24.4 6.0 %collective-permute-start.10 = (s16[64,256]{1,0:T(8,128)(2,1)S(1)}, s16[64,256]{1,0:T(8,128)(2,1)S(1)}, u32[]{:S(2)}, u32[]{:S(2)}) collective-permute-start(s16[64,256]{1,0:T(8,128)(2,1)S(1)} %get-tuple-element.37), channel_id=1, source_target_pairs={{0,16},{4,20},{8,24},{12,28},{16,0},{20,4},{24,8},{28,12},{1,17},{... | collective-permute-start | bytes 98312 | tf_op jit(solution)/shard_map/ppermute | solution.py:77
  24.6 5.9 %collective-permute-start.11 = (s16[64,256]{1,0:T(8,128)(2,1)S(1)}, s16[64,256]{1,0:T(8,128)(2,1)S(1)}, u32[]{:S(2)}, u32[]{:S(2)}) collective-permute-start(s16[64,256]{1,0:T(8,128)(2,1)S(1)} %get-tuple-element.38), channel_id=1, source_target_pairs={{0,8},{4,12},{8,0},{12,4},{16,24},{20,28},{24,16},{28,20},{1,9},{5... | collective-permute-start | bytes 98312 | tf_op jit(solution)/shard_map/ppermute | solution.py:77
  25.8 4.9 %collective-permute-start.12 = (s16[64,256]{1,0:T(8,128)(2,1)S(1)}, s16[64,256]{1,0:T(8,128)(2,1)S(1)}, u32[]{:S(2)}, u32[]{:S(2)}) collective-permute-start(s16[64,256]{1,0:T(8,128)(2,1)S(1)} %get-tuple-element.39), channel_id=1, source_target_pairs={{0,28},{4,24},{8,20},{12,16},{16,12},{20,8},{24,4},{28,0},{1,29},{... | collective-permute-start | bytes 98312 | tf_op jit(solution)/shard_map/ppermute | solution.py:77
  28.7 3.6 %collective-permute-start.13 = (s16[64,256]{1,0:T(8,128)(2,1)S(1)}, s16[64,256]{1,0:T(8,128)(2,1)S(1)}, u32[]{:S(2)}, u32[]{:S(2)}) collective-permute-start(s16[64,256]{1,0:T(8,128)(2,1)S(1)} %get-tuple-element.40), channel_id=1, source_target_pairs={{0,20},{4,16},{8,28},{12,24},{16,4},{20,0},{24,12},{28,8},{1,21},{... | collective-permute-start | bytes 98312 | tf_op jit(solution)/shard_map/ppermute | solution.py:77
  28.7 3.7 %collective-permute-start.14 = (s16[64,256]{1,0:T(8,128)(2,1)S(1)}, s16[64,256]{1,0:T(8,128)(2,1)S(1)}, u32[]{:S(2)}, u32[]{:S(2)}) collective-permute-start(s16[64,256]{1,0:T(8,128)(2,1)S(1)} %get-tuple-element.41), channel_id=1, source_target_pairs={{0,12},{4,8},{8,4},{12,0},{16,28},{20,24},{24,20},{28,16},{1,13},{... | collective-permute-start | bytes 98312 | tf_op jit(solution)/shard_map/ppermute | solution.py:77
  30.4 2.0 %collective-permute-start.15 = (s16[64,256]{1,0:T(8,128)(2,1)S(1)}, s16[64,256]{1,0:T(8,128)(2,1)S(1)}, u32[]{:S(2)}, u32[]{:S(2)}) collective-permute-start(s16[64,256]{1,0:T(8,128)(2,1)S(1)} %get-tuple-element.42), channel_id=1, source_target_pairs={{0,4},{4,0},{8,12},{12,8},{16,20},{20,16},{24,28},{28,24},{1,5},{5... | collective-permute-start | bytes 98312 | tf_op jit(solution)/shard_map/ppermute | solution.py:77

commit v9 on v8

--- a/solution.py
+++ b/solution.py
@@ -129,30 +129,34 @@
         piece[...] = send[me ^ k]
 
 
-def weight_kernel(lines, chunk, az, tiled, weights):
-    out_rows = lines // STEP
+def kinds_of_rows(out_rows):
+    return list(range(2, out_rows - 2)), [0, 1, out_rows - 2, out_rows - 1]
+
+
+def weight_kernel(lines, chunk, az, tiled, *weights):
     cols = chunk // STEP
-    wide = out_rows * cols
-    depth = out_rows * 2 * LANES
-    shape = (LANES, wide)
-    col = iota(shape, 1) % cols
-    out_row = iota(shape, 1) // cols
-    box = jnp.abs(iota(shape, 0) - STEP * col - tiled[...]) <= REACH
-    for o in range(out_rows):
-        mine = (box & (out_row == o)).astype(jnp.bfloat16)
-        weights[2 * o * LANES : (2 * o + 1) * LANES, :] = mine
-        weights[(2 * o + 1) * LANES : (2 * o + 2) * LANES, :] = mine
-    turn = iota(shape, 0) % (LANES // 2)
-    line = jnp.where(turn < lines + HALO, turn + HALO, turn + HALO - LANES // 2)
-    lower = jnp.zeros(shape, jnp.int32)
-    for o in range(out_rows):
-        lower = jnp.where(out_row == o, STEP * o + az[o], lower)
-    window = (line >= lower) & (line <= lower + 2 * HALO)
-    for side, edge_col in ((0, 0), (1, cols - 1)):
-        mine = (window & (col == edge_col)).astype(jnp.bfloat16)
-        for term in range(2):
-            start = depth + (2 * side + term) * LANES
-            weights[start : start + LANES, :] = mine
+    for rows, target in zip(kinds_of_rows(lines // STEP), weights):
+        count = len(rows)
+        depth = count * 2 * LANES
+        shape = (LANES, count * cols)
+        col = iota(shape, 1) % cols
+        slot = iota(shape, 1) // cols
+        box = jnp.abs(iota(shape, 0) - STEP * col - tiled[:, : count * cols]) <= REACH
+        for o in range(count):
+            mine = (box & (slot == o)).astype(jnp.bfloat16)
+            target[2 * o * LANES : (2 * o + 1) * LANES, :] = mine
+            target[(2 * o + 1) * LANES : (2 * o + 2) * LANES, :] = mine
+        turn = iota(shape, 0) % (LANES // 2)
+        line = jnp.where(turn < lines + HALO, turn + HALO, turn + HALO - LANES // 2)
+        lower = jnp.zeros(shape, jnp.int32)
+        for place, o in enumerate(rows):
+            lower = jnp.where(slot == place, STEP * o + az[o], lower)
+        window = (line >= lower) & (line <= lower + 2 * HALO)
+        for side, edge_col in ((0, 0), (1, cols - 1)):
+            mine = (window & (col == edge_col)).astype(jnp.bfloat16)
+            for term in range(2):
+                start = depth + (2 * side + term) * LANES
+                target[start : start + LANES, :] = mine
 
 
 def to_sublanes(source, first_row, date_stride, rows, block, dates, per, target):
@@ -187,8 +191,114 @@
     return high, (value - high.astype(jnp.float32)).astype(jnp.bfloat16)
 
 
-def pair_kernel(
-    blocks, per, lines, chunk, group, x, paired, other, order, az, rg, weights, *refs
+def plus(total, value):
+    return value if total is None else total + value
+
+
+def window_sums(product, rows, out_rows, az):
+    quads = [None] * (out_rows + 1)
+    for k in range(out_rows + 1):
+        for line in range(STEP * k + 3, STEP * k + 7):
+            if product[line] is not None:
+                quads[k] = plus(quads[k], product[line])
+    sums = []
+    for o in rows:
+        total = None
+        for quad in (quads[o], quads[o + 1]):
+            if quad is not None:
+                total = plus(total, quad)
+        for k in range(3):
+            early, late = product[STEP * o + k], product[STEP * o + 11 + k]
+            if early is None and late is None:
+                continue
+            early = jnp.zeros_like(late) if early is None else early
+            late = jnp.zeros_like(early) if late is None else late
+            total = plus(total, jnp.where(az[o] <= k, early, late))
+        sums.append(total)
+    return sums
+
+
+def products(places, date, tile, dates):
+    real, imag = [], []
+    for line in places:
+        if line is None:
+            real.append(None)
+            imag.append(None)
+            continue
+        (ref, at_re), (_, at_im) = line
+        re_i, im_i = (ref[pl.ds(row * dates + date, 1), :] for row in (at_re, at_im))
+        re_j, im_j = (ref[row * dates + tile * 16 : row * dates + tile * 16 + 16, :] for row in (at_re, at_im))
+        real.append(re_i * re_j + im_i * im_j)
+        imag.append(im_i * re_j - re_i * im_j)
+    return real, imag
+
+
+def store_split(target, rows, start, value):
+    upper, rest = split(value)
+    target[rows, start : start + LANES] = upper
+    target[rows, start + LANES : start + 2 * LANES] = rest
+
+
+def store_edges(target, rows, depth, edges, turned, part, date, tile, dates, edge_on):
+    for side in range(2):
+        total = jnp.zeros((16, LANES), jnp.float32)
+        for edge in (2 * side, 2 * side + 1):
+            mine = (turned if part else edges)[pl.ds(edge * dates + date, 1), :]
+            others = edges[edge * dates + tile * 16 : edge * dates + tile * 16 + 16, :]
+            total += jnp.where(edge_on[edge], mine * others, 0.0)
+        store_split(target, rows, depth + 2 * side * LANES, total)
+
+
+def turn_edges(edges, turned, dates):
+    lane = iota((dates, LANES), 1)
+    for k in range(EDGE):
+        value = pltpu.roll(edges[k * dates : (k + 1) * dates, :], LANES // 2, 1)
+        turned[k * dates : (k + 1) * dates, :] = jnp.where(lane < LANES // 2, value, -value)
+
+
+def edges_in_use(rg, cols):
+    me = lax.axis_index("date")
+    first = rg[me * cols]
+    last = rg[me * cols + cols - 1]
+    return first <= 0, first <= 1, last >= 2, last >= 3
+
+
+def inner_kernel(blocks, per, lines, chunk, group, x, order, az, rg, weights, found, partial, turned, left):
+    dates = blocks * per
+    out_rows = lines // STEP
+    inner, outer = kinds_of_rows(out_rows)
+    depth = len(inner) * 2 * LANES
+    edge_on = edges_in_use(rg, chunk // STEP)
+    edges = x.at[2 * HALO * dates : (2 * HALO + EDGE) * dates]
+    turn_edges(edges, turned, dates)
+    places = [None] * HALO
+    places += [[(x, row_of(part, line, lines)) for part in range(2)] for line in range(lines)]
+    places += [None] * HALO
+
+    def one_date(first_date, step, carry):
+        date = first_date + step
+        target = (step // per * 2) * per + step % per
+        for tile in range(dates // 16):
+            for part, product in enumerate(products(places, date, tile, dates)):
+                start = pl.multiple_of((target + part * per) * dates + tile * 16, 16)
+                at_rows = pl.ds(start, 16)
+                sums = window_sums(product, range(out_rows), out_rows, az)
+                for slot, o in enumerate(inner):
+                    store_split(left, at_rows, 2 * slot * LANES, sums[o])
+                whole = pl.ds(pl.multiple_of(first_date * 2 * dates + start, 16), 16)
+                for slot, o in enumerate(outer):
+                    partial[whole, slot * LANES : (slot + 1) * LANES] = sums[o]
+                store_edges(left, at_rows, depth, edges, turned, part, date, tile, dates, edge_on)
+        return carry
+
+    for first_date in range(0, dates, group):
+        lax.fori_loop(0, group, functools.partial(one_date, first_date), 0)
+        result = jnp.dot(left[...], weights[...], preferred_element_type=jnp.float32)
+        found[first_date * 2 * dates : (first_date + group) * 2 * dates, :] = result
+
+
+def outer_kernel(
+    blocks, per, lines, chunk, group, x, paired, other, partial, found, order, az, rg, weights, *refs
 ):
     pieces, (send, sums, halo, edges, turned, left, power) = refs[:blocks], refs[blocks:]
     dates = blocks * per
@@ -196,7 +306,9 @@
     cols = chunk // STEP
     wide = out_rows * cols
     me = lax.axis_index("date")
-    depth = out_rows * 2 * LANES
+    inner, outer = kinds_of_rows(out_rows)
+    depth = len(outer) * 2 * LANES
+    edge_on = edges_in_use(rg, cols)
 
     odd = lax.axis_index("strip") % 2
     for block in range(blocks):
@@ -211,66 +323,30 @@
         upper_part = pltpu.roll(above[at : at + dates, :], lines, 1)
         value = jnp.where(turn < lines, x[at : at + dates, :], jnp.where(turn < lines + HALO, upper_part, lower_part))
         edges[k * dates : (k + 1) * dates, :] = value
-        value = pltpu.roll(value, LANES // 2, 1)
-        turned[k * dates : (k + 1) * dates, :] = jnp.where(lane < LANES // 2, value, -value)
-    first = rg[me * cols]
-    last = rg[me * cols + cols - 1]
-    edge_on = (first <= 0, first <= 1, last >= 2, last >= 3)
-
-    def where_line(part, line):
-        if line < HALO:
-            return below, part * HALO + line
-        if line >= lines + HALO:
-            return above, part * HALO + line - (lines + HALO)
-        return x, row_of(part, line - HALO, lines)
+    turn_edges(edges, turned, dates)
+    places = [[(below, part * HALO + line) for part in range(2)] for line in range(HALO)]
+    places += [None] * lines
+    places += [[(above, part * HALO + line) for part in range(2)] for line in range(HALO)]
 
     def one_date(first_date, step, carry):
         date = first_date + step
         target = (step // per * 2) * per + step % per
         for tile in range(dates // 16):
-
-            def own(ref, row):
-                return ref[pl.ds(row * dates + date, 1), :]
-
-            def others(ref, row):
-                return ref[row * dates + tile * 16 : row * dates + tile * 16 + 16, :]
-
-            real, imag = [], []
-            for line in range(lines + 2 * HALO):
-                at_re, at_im = where_line(0, line), where_line(1, line)
-                re_i, im_i = own(*at_re), own(*at_im)
-                re_j, im_j = others(*at_re), others(*at_im)
-                real.append(re_i * re_j + im_i * im_j)
-                imag.append(im_i * re_j - re_i * im_j)
-            for part, product in enumerate((real, imag)):
+            for part, product in enumerate(products(places, date, tile, dates)):
                 start = pl.multiple_of((target + part * per) * dates + tile * 16, 16)
                 at_rows = pl.ds(start, 16)
-                quads = []
-                for k in range(out_rows + 1):
-                    q = product[STEP * k + 3 : STEP * k + 7]
-                    quads.append((q[0] + q[1]) + (q[2] + q[3]))
-                for o in range(out_rows):
-                    total = quads[o] + quads[o + 1]
-                    for k in range(3):
-                        total += jnp.where(az[o] <= k, product[STEP * o + k], product[STEP * o + 11 + k])
-                    upper, rest = split(total)
-                    left[at_rows, 2 * o * LANES : (2 * o + 1) * LANES] = upper
-                    left[at_rows, (2 * o + 1) * LANES : (2 * o + 2) * LANES] = rest
-                for side in range(2):
-                    total = jnp.zeros((16, LANES), jnp.float32)
-                    for edge in (2 * side, 2 * side + 1):
-                        mine = own(turned if part else edges, edge)
-                        total += jnp.where(edge_on[edge], mine * others(edges, edge), 0.0)
-                    upper, rest = split(total)
-                    start_col = depth + 2 * side * LANES
-                    left[at_rows, start_col : start_col + LANES] = upper
-                    left[at_rows, start_col + LANES : start_col + 2 * LANES] = rest
+                whole = pl.ds(pl.multiple_of(first_date * 2 * dates + start, 16), 16)
+                for slot, total in enumerate(window_sums(product, outer, out_rows, az)):
+                    total += partial[whole, slot * LANES : (slot + 1) * LANES]
+                    store_split(left, at_rows, 2 * slot * LANES, total)
+                store_edges(left, at_rows, depth, edges, turned, part, date, tile, dates, edge_on)
         return carry
 
+    sums[:, : len(inner) * cols] = found[...]
     for first_date in range(0, dates, group):
         lax.fori_loop(0, group, functools.partial(one_date, first_date), 0)
-        found = jnp.dot(left[...], weights[...], preferred_element_type=jnp.float32)
-        sums[first_date * 2 * dates : (first_date + group) * 2 * dates, :] = found
+        result = jnp.dot(left[...], weights[...], preferred_element_type=jnp.float32)
+        sums[first_date * 2 * dates : (first_date + group) * 2 * dates, len(inner) * cols :] = result
     for date in range(dates):
         at_row = (date // per * 2 * per + date % per) * dates + date
         power[date : date + 1, :] = sums[at_row : at_row + 1, :]
@@ -308,6 +384,7 @@
     lane = iota((dates, LANES), 1) // cols
     position = iota((dates, wide), 0)
     column = iota((dates, wide), 1)
+    row_order = sum(kinds_of_rows(out_rows), [])
     for piece, k in zip(pieces, partners(blocks)):
         recv[me ^ k] = piece[...]
     factors = [[None] * blocks for _ in range(per)]
@@ -341,7 +418,7 @@
                     width *= 2
                 for o in range(per_tile):
                     for start in range(0, dates, 8):
-                        at = start * out_rows + o_tile * per_tile + o
+                        at = start * out_rows + row_order[o_tile * per_tile + o]
                         halves[step, d_tile, pl.ds(at, 8, stride=out_rows), :] = tiles[o][start : start + 8]
             rows = slice(step * dates * out_rows, (step + 1) * dates * out_rows)
             target = out.at[rows, d_tile * LANES : (d_tile + 1) * LANES]
@@ -370,7 +447,6 @@
     cols = chunk // STEP
     wide = out_rows * cols
     date_rows = rows_of_date(lines)
-    depth = (out_rows + 2) * 2 * LANES
     group = max(per, 256 // dates)
     me = lax.axis_index("date")
 
@@ -390,15 +466,20 @@
     )(slc)
     recv = swap_blocks(send)
     tiled = jnp.tile(lax.dynamic_slice_in_dim(rg_offset, me * cols, cols), out_rows)[None]
+    kinds = kinds_of_rows(out_rows)
+    depths = [(len(rows) + 2) * 2 * LANES for rows in kinds]
     weights = pl.pallas_call(
         functools.partial(weight_kernel, lines, chunk),
-        out_shape=jax.ShapeDtypeStruct((depth, wide), jnp.bfloat16),
+        out_shape=[
+            jax.ShapeDtypeStruct((depth, len(rows) * cols), jnp.bfloat16) for depth, rows in zip(depths, kinds)
+        ],
         in_specs=[SMEM, VMEM],
-        out_specs=VMEM,
+        out_specs=[VMEM] * 2,
         compiler_params=PARAMS,
         cost_estimate=pl.CostEstimate(flops=0, bytes_accessed=4 * 1024 * 1024, transcendentals=0),
         name="weights",
     )(az_offset, tiled)
+    recv, weights = lax.optimization_barrier((recv, weights))
 
     edge = jax.ShapeDtypeStruct((blocks, edge_rows, LANES), jnp.bfloat16)
     x, to_pair, to_other = pl.pallas_call(
@@ -416,23 +497,40 @@
 
     other = lax.ppermute(to_other, "strip", swaps(1))
     paired = lax.ppermute(to_pair, "strip", swaps(0))
+    count = dates * 2 * dates
+    found, partial = pl.pallas_call(
+        functools.partial(inner_kernel, blocks, per, lines, chunk, group),
+        out_shape=[
+            jax.ShapeDtypeStruct((count, len(kinds[0]) * cols), jnp.float32),
+            jax.ShapeDtypeStruct((count, len(kinds[1]) * LANES), jnp.float32),
+        ],
+        in_specs=[VMEM, SMEM, SMEM, SMEM, VMEM],
+        out_specs=[VMEM] * 2,
+        scratch_shapes=[
+            pltpu.VMEM((EDGE * dates, LANES), jnp.float32),
+            pltpu.VMEM((group * 2 * dates, depths[0]), jnp.bfloat16),
+        ],
+        compiler_params=PARAMS,
+        cost_estimate=pl.CostEstimate(flops=0, bytes_accessed=12 * 1024 * 1024, transcendentals=0),
+        name="inner",
+    )(x, block_order, az_offset, rg_offset, weights[0])
     pairs = pl.pallas_call(
-        functools.partial(pair_kernel, blocks, per, lines, chunk, group),
+        functools.partial(outer_kernel, blocks, per, lines, chunk, group),
         out_shape=[jax.ShapeDtypeStruct((2 * per * dates, wide), jnp.int16)] * blocks,
-        in_specs=[VMEM, VMEM, VMEM, SMEM, SMEM, SMEM, VMEM],
+        in_specs=[VMEM] * 5 + [SMEM] * 3 + [VMEM],
         out_specs=[VMEM] * blocks,
         scratch_shapes=[
-            pltpu.VMEM((dates * 2 * dates, wide), jnp.int16),
-            pltpu.VMEM((dates * 2 * dates, wide), jnp.float32),
+            pltpu.VMEM((count, wide), jnp.int16),
+            pltpu.VMEM((count, wide), jnp.float32),
             pltpu.VMEM((2, GROUP * dates, LANES), jnp.float32),
             pltpu.VMEM((EDGE * dates, LANES), jnp.float32),
             pltpu.VMEM((EDGE * dates, LANES), jnp.float32),
-            pltpu.VMEM((group * 2 * dates, depth), jnp.bfloat16),
+            pltpu.VMEM((group * 2 * dates, depths[1]), jnp.bfloat16),
             pltpu.VMEM((dates, wide), jnp.float32),
         ],
         compiler_params=PARAMS,
-        name="pairs",
-    )(x, paired, other, block_order, az_offset, rg_offset, weights)
+        name="outer",
+    )(x, paired, other, partial, found, block_order, az_offset, rg_offset, weights[1])
     count = 2 * per * dates
     back = swap_blocks(pairs)
     if LANES % cols == 0 and out_rows * cols % LANES == 0 and blocks * cols % LANES == 0:
@@ -453,7 +551,9 @@
         place = [partners(blocks).index(k) for k in range(blocks)]
         back = jnp.stack([back[at] for at in place])[me ^ jnp.arange(blocks)]
         values = decode(back.reshape(blocks, 2, per, dates, wide), me, per)
-        out = values.reshape(blocks, count, out_rows, cols).transpose(1, 2, 0, 3)
+        values = values.reshape(blocks, count, out_rows, cols).transpose(1, 2, 0, 3)
+        row_order = sum(kinds_of_rows(out_rows), [])
+        out = jnp.stack([values[:, row_order.index(o)] for o in range(out_rows)], axis=1)
     return out.reshape(2, per, dates, out_rows, blocks * cols)
 
 

time: 34.6 us -> 33.6 us (0.971); the launches traced: 34 us -> 33.5 us
  waiting for transfers between devices: 5.11 us -> 3.13 us
  Pallas kernels: 7.33 us -> 8.71 us
    ppermute x14, waiting for transfers between devices: 5.11 us -> 3.12 us  [swap_blocks(): lax.ppermute(pieces[at], 'date', [(i, i ^ k) for i in range(blocks)])]
    pallas_call x1 -> x2, Pallas kernels: 4.52 us -> 5.96 us  [the longest x1 3.39 us: on_device(): pl.pallas_call(functools.partial(inner_kernel, blocks, per, lines, chunk,...]
    dynamic_slice x1, local copies, waits for them, and re-layouts: 0.76 us -> 0.07 us  [on_device(): lax.dynamic_slice_in_dim(rg_offset, me * cols, cols)]
    unnamed x10 -> x8, local copies, waits for them, and re-layouts: 1.62 us -> 2.21 us
  transfers between devices with their start and end apart: 16 -> 16, of which waited for: 6 -> 5; matrix products, arithmetic and copies ran while one was open for 2% -> 0% of each run, Pallas kernels for 2% -> 12%
where the time goes in v9:
time: 33.6 us; the launch traced here: 33.5 us
  starting transfers between devices  19.1 us (57%)
  Pallas kernels  8.71 us (26%)
  waiting for transfers between devices  3.13 us (9%)
  local copies, waits for them, and re-layouts  2.36 us (7%)
    ppermute x14, starting transfers between devices, swap_blocks(): lax.ppermute(pieces[at], 'date', [(i, i ^ k) for i in range(blocks)])  14.5 us
    ppermute x1, starting transfers between devices, on_device(): other = lax.ppermute(to_other, 'strip', swaps(1))  4.45 us
    pallas_call x1, Pallas kernels, on_device(): pl.pallas_call(functools.partial(inner_kernel, blocks, per, lines, chunk,...  3.39 us
    ppermute x14, waiting for transfers between devices, swap_blocks(): lax.ppermute(pieces[at], 'date', [(i, i ^ k) for i in range(blocks)])  3.12 us
    pallas_call x1, Pallas kernels, on_device(): pl.pallas_call(functools.partial(outer_kernel, blocks, per, lines, chunk,...  2.57 us
    unnamed x8, local copies, waits for them, and re-layouts  2.21 us
    pallas_call x1, Pallas kernels, on_device(): pl.pallas_call(functools.partial(join_kernel, blocks, per, out_rows, cols...  1.54 us
  transfers between devices with their start and end apart: 16, of which 5 were waited for; matrix products, arithmetic and copies ran while one was open for 0% of the time, Pallas kernels for 12%

profile of v9, /device:TPU:9, one launch (start us, length us, event | category | flops | bytes accessed | tf_op | source)
XLA Modules:
  0.0 33.5 jit_solution(10019916459634416118)
XLA Ops:
  0.0 0.9 %copy-done = bf16[2,2,32,1024]{3,2,1,0:T(8,128)(2,1)S(1)} copy-done((bf16[2,2,32,1024]{3,2,1,0:T(8,128)(2,1)S(1)}, bf16[2,2,32,1024]{3,2,1,0:T(8,128)(2,1)}, u32[]{:S(2)}) %copy-start) | copy-done | bytes 262168
  1.0 0.3 pack.1
  1.3 2.2 %collective-permute-start = (bf16[144,128]{1,0:T(8,128)(2,1)S(1)}, bf16[144,128]{1,0:T(8,128)(2,1)S(1)}, u32[]{:S(2)}, u32[]{:S(2)}) collective-permute-start(bf16[144,128]{1,0:T(8,128)(2,1)S(1)} %get-tuple-element.39), channel_id=1, source_target_pairs={{0,24},{4,28},{8,16},{12,20},{16,8},{20,12},{24,0},{28,4},{1,25},{... | collective-permute-start | bytes 110600 | tf_op jit(solution)/shard_map/ppermute | solution.py:77
  3.5 0.2 collective-permute-start.1
  3.7 0.3 collective-permute-start.2
  4.0 3.6 %collective-permute-start.3 = (bf16[144,128]{1,0:T(8,128)(2,1)S(1)}, bf16[144,128]{1,0:T(8,128)(2,1)S(1)}, u32[]{:S(2)}, u32[]{:S(2)}) collective-permute-start(bf16[144,128]{1,0:T(8,128)(2,1)S(1)} %get-tuple-element.42), channel_id=1, source_target_pairs={{0,28},{4,24},{8,20},{12,16},{16,12},{20,8},{24,4},{28,0},{1,29},{... | collective-permute-start | bytes 110600 | tf_op jit(solution)/shard_map/ppermute | solution.py:77
  7.6 0.0 collective-permute-start.4
  7.6 0.8 %collective-permute-start.5 = (bf16[144,128]{1,0:T(8,128)(2,1)S(1)}, bf16[144,128]{1,0:T(8,128)(2,1)S(1)}, u32[]{:S(2)}, u32[]{:S(2)}) collective-permute-start(bf16[144,128]{1,0:T(8,128)(2,1)S(1)} %get-tuple-element.44), channel_id=1, source_target_pairs={{0,12},{4,8},{8,4},{12,0},{16,28},{20,24},{24,20},{28,16},{1,13},{... | collective-permute-start | bytes 110600 | tf_op jit(solution)/shard_map/ppermute | solution.py:77
  8.3 0.0 collective-permute-done.1.refs_2_
  8.3 0.1 collective-permute-start.6
  8.4 0.7 %copy-done.1 = s32[256]{0:T(256)S(1)} copy-done((s32[256]{0:T(256)S(1)}, s32[256]{0:T(256)}, u32[]{:S(2)}) %copy-start.1) | copy-done | bytes 1048
  9.1 0.1 dynamic_slice.3
  9.2 0.1 broadcast_in_dim_tile.3.tiled
  9.3 0.6 %copy-done.3 = s32[8]{0:T(128)S(1)} copy-done((s32[8]{0:T(128)S(1)}, s32[8]{0:T(128)}, u32[]{:S(2)}) %copy-start.3) | copy-done | bytes 56
  9.8 0.6 %weights.1 = (bf16[1536,128]{1,0:T(8,128)(2,1)S(1)}, bf16[1536,128]{1,0:T(8,128)(2,1)S(1)}) custom-call(s32[8]{0:T(128)S(1)} %copy-done.3, s32[1,256]{1,0:T(1,128)S(1)} %broadcast_in_dim_tile.3.tiled), custom_call_target="tpu_custom_call" | custom-call | bytes 4194304 | tf_op jit(solution)/shard_map/weights/pallas_call | solution.py:471
  10.5 0.0 collective-permute-done.3.refs_4_
  10.5 0.7 %collective-permute-done.4.refs_5_ = bf16[144,128]{1,0:T(8,128)(2,1)S(1)} collective-permute-done((bf16[144,128]{1,0:T(8,128)(2,1)S(1)}, bf16[144,128]{1,0:T(8,128)(2,1)S(1)}, u32[]{:S(2)}, u32[]{:S(2)}) %collective-permute-start.4) | collective-permute-done | bytes 36896 | tf_op jit(solution)/shard_map/ppermute | solution.py:77
  11.2 0.3 collective-permute-done.5.refs_6_
  11.5 0.3 spread.1
  11.8 0.2 collective-permute-start.7
  12.0 4.5 %collective-permute-start.8 = (bf16[8,32,128]{2,1,0:T(8,128)(2,1)S(1)}, bf16[8,32,128]{2,1,0:T(8,128)(2,1)S(1)}, u32[]{:S(2)}, u32[]{:S(2)}) collective-permute-start(bf16[8,32,128]{2,1,0:T(8,128)(2,1)S(1)} %get-tuple-element.58), channel_id=1, source_target_pairs={{1,2},{2,1},{5,6},{6,5},{9,10},{10,9},{13,14},{14,13},{17,18},{18,... | collective-permute-start | bytes 196616 | tf_op jit(solution)/shard_map/ppermute | solution.py:498
  16.5 3.4 %inner.1 = (f32[512,128]{1,0:T(8,128)S(1)}, f32[512,512]{1,0:T(8,128)S(1)}) custom-call(f32[1152,128]{1,0:T(8,128)S(1)} %get-tuple-element.56.x, s32[8]{0:T(128)S(1)} %copy-done.2, s32[8]{0:T(128)S(1)} %copy-done.3, s32[256]{0:T(256)S(1)} %copy-done.1, bf16[1536,128]{1,0:T(8,128)(2,1)S(1)} %get-tuple-element.59.weights), custom_call_target="tpu_custom_call" | custom-call | bytes 12582912 | tf_op jit(solution)/shard_map/inner/pallas_call | solution.py:501
  19.9 2.6 %outer.1 = (s16[64,256]{1,0:T(8,128)(2,1)S(1)}, s16[64,256]{1,0:T(8,128)(2,1)S(1)}, s16[64,256]{1,0:T(8,128)(2,1)S(1)}, s16[64,256]{1,0:T(8,128)(2,1)S(1)}, s16[...) custom-call(f32[1152,128]{1,0:T(8,128)S(1)} %get-tuple-element.56.x,, ...), custom_call_target="tpu_custom_call" | custom-call | tf_op jit(solution)/shard_map/outer/pallas_call | solution.py:517
  22.5 1.3 %collective-permute-start.9 = (s16[64,256]{1,0:T(8,128)(2,1)S(1)}, s16[64,256]{1,0:T(8,128)(2,1)S(1)}, u32[]{:S(2)}, u32[]{:S(2)}) collective-permute-start(s16[64,256]{1,0:T(8,128)(2,1)S(1)} %get-tuple-element.64), channel_id=1, source_target_pairs={{0,24},{4,28},{8,16},{12,20},{16,8},{20,12},{24,0},{28,4},{1,25},{... | collective-permute-start | bytes 98312 | tf_op jit(solution)/shard_map/ppermute | solution.py:77
  23.8 0.2 collective-permute-start.10
  23.9 1.2 %collective-permute-start.11 = (s16[64,256]{1,0:T(8,128)(2,1)S(1)}, s16[64,256]{1,0:T(8,128)(2,1)S(1)}, u32[]{:S(2)}, u32[]{:S(2)}) collective-permute-start(s16[64,256]{1,0:T(8,128)(2,1)S(1)} %get-tuple-element.66), channel_id=1, source_target_pairs={{0,8},{4,12},{8,0},{12,4},{16,24},{20,28},{24,16},{28,20},{1,9},{5... | collective-permute-start | bytes 98312 | tf_op jit(solution)/shard_map/ppermute | solution.py:77
  25.2 2.9 %collective-permute-start.12 = (s16[64,256]{1,0:T(8,128)(2,1)S(1)}, s16[64,256]{1,0:T(8,128)(2,1)S(1)}, u32[]{:S(2)}, u32[]{:S(2)}) collective-permute-start(s16[64,256]{1,0:T(8,128)(2,1)S(1)} %get-tuple-element.67), channel_id=1, source_target_pairs={{0,28},{4,24},{8,20},{12,16},{16,12},{20,8},{24,4},{28,0},{1,29},{... | collective-permute-start | bytes 98312 | tf_op jit(solution)/shard_map/ppermute | solution.py:77
  28.1 1.7 %collective-permute-start.14 = (s16[64,256]{1,0:T(8,128)(2,1)S(1)}, s16[64,256]{1,0:T(8,128)(2,1)S(1)}, u32[]{:S(2)}, u32[]{:S(2)}) collective-permute-start(s16[64,256]{1,0:T(8,128)(2,1)S(1)} %get-tuple-element.69), channel_id=1, source_target_pairs={{0,12},{4,8},{8,4},{12,0},{16,28},{20,24},{24,20},{28,16},{1,13},{... | collective-permute-start | bytes 98312 | tf_op jit(solution)/shard_map/ppermute | solution.py:77
  29.8 0.2 collective-permute-done.12.refs_4_
  30.0 1.7 %collective-permute-done.13.refs_5_ = s16[64,256]{1,0:T(8,128)(2,1)S(1)} collective-permute-done((s16[64,256]{1,0:T(8,128)(2,1)S(1)}, s16[64,256]{1,0:T(8,128)(2,1)S(1)}, u32[]{:S(2)}, u32[]{:S(2)}) %collective-permute-start.13) | collective-permute-done | bytes 32800 | tf_op jit(solution)/shard_map/ppermute | solution.py:77
  31.7 0.2 collective-permute-done.14.refs_6_
  31.9 1.5 %join.1 = f32[512,256]{1,0:T(8,128)} custom-call(s16[64,256]{1,0:T(8,128)(2,1)S(1)} %get-tuple-element.63.refs_0_, s16[64,256]{1,0:T(8,128)(2,1)S(1)} %collective-permute-done.9.refs_1_, s16[64,256]{1,0:T(8,128)(2,1)S(1)} %collective-permute-done.10.refs_2_, s16[64,256]{1,0:T(8,128)(2,1)S(1)} %collective-permute-done.11.refs_3_, ...), custom_call_target="tpu_custom_call" | custom-call | tf_op jit(solution)/shard_map/join/pallas_call | solution.py:537
  (17 shorter events, 0.0 us)
Async XLA Ops:
  0.0 0.9 %copy-start = (bf16[2,2,32,1024]{3,2,1,0:T(8,128)(2,1)S(1)}, bf16[2,2,32,1024]{3,2,1,0:T(8,128)(2,1)}, u32[]{:S(2)}) copy-start(bf16[2,2,32,1024]{3,2,1,0:T(8,128)(2,1)} %slc.1) | copy-start | bytes 786436
  1.3 6.3 %collective-permute-start = (bf16[144,128]{1,0:T(8,128)(2,1)S(1)}, bf16[144,128]{1,0:T(8,128)(2,1)S(1)}, u32[]{:S(2)}, u32[]{:S(2)}) collective-permute-start(bf16[144,128]{1,0:T(8,128)(2,1)S(1)} %get-tuple-element.39), channel_id=1, source_target_pairs={{0,24},{4,28},{8,16},{12,20},{16,8},{20,12},{24,0},{28,4},{1,25},{... | collective-permute-start | bytes 110600 | tf_op jit(solution)/shard_map/ppermute | solution.py:77
  3.5 4.8 %collective-permute-start.1 = (bf16[144,128]{1,0:T(8,128)(2,1)S(1)}, bf16[144,128]{1,0:T(8,128)(2,1)S(1)}, u32[]{:S(2)}, u32[]{:S(2)}) collective-permute-start(bf16[144,128]{1,0:T(8,128)(2,1)S(1)} %get-tuple-element.40), channel_id=1, source_target_pairs={{0,16},{4,20},{8,24},{12,28},{16,0},{20,4},{24,8},{28,12},{1,17},{... | collective-permute-start | bytes 110600 | tf_op jit(solution)/shard_map/ppermute | solution.py:77
  3.7 6.7 %collective-permute-start.2 = (bf16[144,128]{1,0:T(8,128)(2,1)S(1)}, bf16[144,128]{1,0:T(8,128)(2,1)S(1)}, u32[]{:S(2)}, u32[]{:S(2)}) collective-permute-start(bf16[144,128]{1,0:T(8,128)(2,1)S(1)} %get-tuple-element.41), channel_id=1, source_target_pairs={{0,8},{4,12},{8,0},{12,4},{16,24},{20,28},{24,16},{28,20},{1,9},{5... | collective-permute-start | bytes 110600 | tf_op jit(solution)/shard_map/ppermute | solution.py:77
  4.0 6.5 %collective-permute-start.3 = (bf16[144,128]{1,0:T(8,128)(2,1)S(1)}, bf16[144,128]{1,0:T(8,128)(2,1)S(1)}, u32[]{:S(2)}, u32[]{:S(2)}) collective-permute-start(bf16[144,128]{1,0:T(8,128)(2,1)S(1)} %get-tuple-element.42), channel_id=1, source_target_pairs={{0,28},{4,24},{8,20},{12,16},{16,12},{20,8},{24,4},{28,0},{1,29},{... | collective-permute-start | bytes 110600 | tf_op jit(solution)/shard_map/ppermute | solution.py:77
  7.6 3.7 %collective-permute-start.4 = (bf16[144,128]{1,0:T(8,128)(2,1)S(1)}, bf16[144,128]{1,0:T(8,128)(2,1)S(1)}, u32[]{:S(2)}, u32[]{:S(2)}) collective-permute-start(bf16[144,128]{1,0:T(8,128)(2,1)S(1)} %get-tuple-element.43), channel_id=1, source_target_pairs={{0,20},{4,16},{8,28},{12,24},{16,4},{20,0},{24,12},{28,8},{1,21},{... | collective-permute-start | bytes 110600 | tf_op jit(solution)/shard_map/ppermute | solution.py:77
  7.6 3.9 %collective-permute-start.5 = (bf16[144,128]{1,0:T(8,128)(2,1)S(1)}, bf16[144,128]{1,0:T(8,128)(2,1)S(1)}, u32[]{:S(2)}, u32[]{:S(2)}) collective-permute-start(bf16[144,128]{1,0:T(8,128)(2,1)S(1)} %get-tuple-element.44), channel_id=1, source_target_pairs={{0,12},{4,8},{8,4},{12,0},{16,28},{20,24},{24,20},{28,16},{1,13},{... | collective-permute-start | bytes 110600 | tf_op jit(solution)/shard_map/ppermute | solution.py:77
  8.3 3.2 %collective-permute-start.6 = (bf16[144,128]{1,0:T(8,128)(2,1)S(1)}, bf16[144,128]{1,0:T(8,128)(2,1)S(1)}, u32[]{:S(2)}, u32[]{:S(2)}) collective-permute-start(bf16[144,128]{1,0:T(8,128)(2,1)S(1)} %get-tuple-element.45), channel_id=1, source_target_pairs={{0,4},{4,0},{8,12},{12,8},{16,20},{20,16},{24,28},{28,24},{1,5},{5... | collective-permute-start | bytes 110600 | tf_op jit(solution)/shard_map/ppermute | solution.py:77
  8.4 0.7 %copy-start.1 = (s32[256]{0:T(256)S(1)}, s32[256]{0:T(256)}, u32[]{:S(2)}) copy-start(s32[256]{0:T(256)} %rg.3) | copy-start | bytes 3076
  9.2 0.7 %copy-start.3 = (s32[8]{0:T(128)S(1)}, s32[8]{0:T(128)}, u32[]{:S(2)}) copy-start(s32[8]{0:T(128)} %az.5) | copy-start | bytes 100
  11.8 8.1 %collective-permute-start.7 = (bf16[8,32,128]{2,1,0:T(8,128)(2,1)S(1)}, bf16[8,32,128]{2,1,0:T(8,128)(2,1)S(1)}, u32[]{:S(2)}, u32[]{:S(2)}) collective-permute-start(bf16[8,32,128]{2,1,0:T(8,128)(2,1)S(1)} %get-tuple-element.57), channel_id=1, source_target_pairs={{0,1},{2,3},{1,0},{3,2},{4,5},{6,7},{5,4},{7,6},{8,9},{10,11},{9,8... | collective-permute-start | bytes 196616 | tf_op jit(solution)/shard_map/ppermute | solution.py:499
  12.0 4.5 %copy-start.2 = (s32[8]{0:T(128)S(1)}, s32[8]{0:T(128)}, u32[]{:S(2)}) copy-start(s32[8]{0:T(128)} %order.3) | copy-start | bytes 100
  12.0 7.9 %collective-permute-start.8 = (bf16[8,32,128]{2,1,0:T(8,128)(2,1)S(1)}, bf16[8,32,128]{2,1,0:T(8,128)(2,1)S(1)}, u32[]{:S(2)}, u32[]{:S(2)}) collective-permute-start(bf16[8,32,128]{2,1,0:T(8,128)(2,1)S(1)} %get-tuple-element.58), channel_id=1, source_target_pairs={{1,2},{2,1},{5,6},{6,5},{9,10},{10,9},{13,14},{14,13},{17,18},{18,... | collective-permute-start | bytes 196616 | tf_op jit(solution)/shard_map/ppermute | solution.py:498
  22.5 5.6 %collective-permute-start.9 = (s16[64,256]{1,0:T(8,128)(2,1)S(1)}, s16[64,256]{1,0:T(8,128)(2,1)S(1)}, u32[]{:S(2)}, u32[]{:S(2)}) collective-permute-start(s16[64,256]{1,0:T(8,128)(2,1)S(1)} %get-tuple-element.64), channel_id=1, source_target_pairs={{0,24},{4,28},{8,16},{12,20},{16,8},{20,12},{24,0},{28,4},{1,25},{... | collective-permute-start | bytes 98312 | tf_op jit(solution)/shard_map/ppermute | solution.py:77
  23.8 6.0 %collective-permute-start.10 = (s16[64,256]{1,0:T(8,128)(2,1)S(1)}, s16[64,256]{1,0:T(8,128)(2,1)S(1)}, u32[]{:S(2)}, u32[]{:S(2)}) collective-permute-start(s16[64,256]{1,0:T(8,128)(2,1)S(1)} %get-tuple-element.65), channel_id=1, source_target_pairs={{0,16},{4,20},{8,24},{12,28},{16,0},{20,4},{24,8},{28,12},{1,17},{... | collective-permute-start | bytes 98312 | tf_op jit(solution)/shard_map/ppermute | solution.py:77
  23.9 5.9 %collective-permute-start.11 = (s16[64,256]{1,0:T(8,128)(2,1)S(1)}, s16[64,256]{1,0:T(8,128)(2,1)S(1)}, u32[]{:S(2)}, u32[]{:S(2)}) collective-permute-start(s16[64,256]{1,0:T(8,128)(2,1)S(1)} %get-tuple-element.66), channel_id=1, source_target_pairs={{0,8},{4,12},{8,0},{12,4},{16,24},{20,28},{24,16},{28,20},{1,9},{5... | collective-permute-start | bytes 98312 | tf_op jit(solution)/shard_map/ppermute | solution.py:77
  25.2 4.9 %collective-permute-start.12 = (s16[64,256]{1,0:T(8,128)(2,1)S(1)}, s16[64,256]{1,0:T(8,128)(2,1)S(1)}, u32[]{:S(2)}, u32[]{:S(2)}) collective-permute-start(s16[64,256]{1,0:T(8,128)(2,1)S(1)} %get-tuple-element.67), channel_id=1, source_target_pairs={{0,28},{4,24},{8,20},{12,16},{16,12},{20,8},{24,4},{28,0},{1,29},{... | collective-permute-start | bytes 98312 | tf_op jit(solution)/shard_map/ppermute | solution.py:77
  28.1 3.6 %collective-permute-start.13 = (s16[64,256]{1,0:T(8,128)(2,1)S(1)}, s16[64,256]{1,0:T(8,128)(2,1)S(1)}, u32[]{:S(2)}, u32[]{:S(2)}) collective-permute-start(s16[64,256]{1,0:T(8,128)(2,1)S(1)} %get-tuple-element.68), channel_id=1, source_target_pairs={{0,20},{4,16},{8,28},{12,24},{16,4},{20,0},{24,12},{28,8},{1,21},{... | collective-permute-start | bytes 98312 | tf_op jit(solution)/shard_map/ppermute | solution.py:77
  28.1 3.8 %collective-permute-start.14 = (s16[64,256]{1,0:T(8,128)(2,1)S(1)}, s16[64,256]{1,0:T(8,128)(2,1)S(1)}, u32[]{:S(2)}, u32[]{:S(2)}) collective-permute-start(s16[64,256]{1,0:T(8,128)(2,1)S(1)} %get-tuple-element.69), channel_id=1, source_target_pairs={{0,12},{4,8},{8,4},{12,0},{16,28},{20,24},{24,20},{28,16},{1,13},{... | collective-permute-start | bytes 98312 | tf_op jit(solution)/shard_map/ppermute | solution.py:77
  29.8 2.1 %collective-permute-start.15 = (s16[64,256]{1,0:T(8,128)(2,1)S(1)}, s16[64,256]{1,0:T(8,128)(2,1)S(1)}, u32[]{:S(2)}, u32[]{:S(2)}) collective-permute-start(s16[64,256]{1,0:T(8,128)(2,1)S(1)} %get-tuple-element.70), channel_id=1, source_target_pairs={{0,4},{4,0},{8,12},{12,8},{16,20},{20,16},{24,28},{28,24},{1,5},{5... | collective-permute-start | bytes 98312 | tf_op jit(solution)/shard_map/ppermute | solution.py:77

commit v10 on v9

--- a/solution.py
+++ b/solution.py
@@ -169,7 +169,7 @@
             target[pl.ds(row * dates + block * per + date, 8, stride=dates), :] = value[row : row + 8]
 
 
-def spread_kernel(blocks, per, lines, *refs):
+def spread_kernel(blocks, per, lines, order, *refs):
     recv, (x, paired, other) = refs[:blocks], refs[blocks:]
     dates = blocks * per
     date_rows = rows_of_date(lines)
@@ -181,6 +181,7 @@
         block = me ^ k
         paired[block] = piece[:edge_rows]
         other[block] = piece[edge_rows : 2 * edge_rows]
+        block = order[block]
         to_sublanes(piece, turn * edge_rows, GROUP, GROUP, block, dates, per, x)
         to_sublanes(piece, (1 - turn) * edge_rows, GROUP, GROUP, block, dates, per, x.at[GROUP * dates :])
         to_sublanes(piece, 2 * edge_rows, rest, rest, block, dates, per, x.at[2 * GROUP * dates :])
@@ -218,7 +219,7 @@
     return sums
 
 
-def products(places, date, tile, dates):
+def products(places, date, first, count, dates):
     real, imag = [], []
     for line in places:
         if line is None:
@@ -227,7 +228,7 @@
             continue
         (ref, at_re), (_, at_im) = line
         re_i, im_i = (ref[pl.ds(row * dates + date, 1), :] for row in (at_re, at_im))
-        re_j, im_j = (ref[row * dates + tile * 16 : row * dates + tile * 16 + 16, :] for row in (at_re, at_im))
+        re_j, im_j = (ref[row * dates + first : row * dates + first + count, :] for row in (at_re, at_im))
         real.append(re_i * re_j + im_i * im_j)
         imag.append(im_i * re_j - re_i * im_j)
     return real, imag
@@ -239,14 +240,46 @@
     target[rows, start + LANES : start + 2 * LANES] = rest
 
 
-def store_edges(target, rows, depth, edges, turned, part, date, tile, dates, edge_on):
+def edge_sums(edges, own, date, first, count, dates, edge_on):
+    sums = []
     for side in range(2):
-        total = jnp.zeros((16, LANES), jnp.float32)
+        total = jnp.zeros((count, LANES), jnp.float32)
         for edge in (2 * side, 2 * side + 1):
-            mine = (turned if part else edges)[pl.ds(edge * dates + date, 1), :]
-            others = edges[edge * dates + tile * 16 : edge * dates + tile * 16 + 16, :]
-            total += jnp.where(edge_on[edge], mine * others, 0.0)
-        store_split(target, rows, depth + 2 * side * LANES, total)
+            others = edges[edge * dates + first : edge * dates + first + count, :]
+            total += jnp.where(edge_on[edge], own[pl.ds(edge * dates + date, 1), :] * others, 0.0)
+        sums.append(total)
+    return sums
+
+
+def all_dates(dates, group, places, rows, out_rows, az, edges, turned, edge_on, store, finish):
+    half = dates // 2
+    group = min(group, half)
+
+    def sums_of(date, first, count):
+        found = []
+        for part, product in enumerate(products(places, date, first, count, dates)):
+            sums = window_sums(product, rows, out_rows, az)
+            found.append(sums + edge_sums(edges, turned if part else edges, date, first, count, dates, edge_on))
+        return found
+
+    def early(first_date, step, carry):
+        for tile in range(dates // 16):
+            for part, sums in enumerate(sums_of(first_date + step, tile * 16, 16)):
+                store(first_date * 2 * dates, step * 2 * dates + part * dates + tile * 16, sums)
+        return carry
+
+    def late(first_date, step, carry):
+        for tile in range(half // 8):
+            real, imag = sums_of(half + first_date + step, half + tile * 8, 8)
+            both = [jnp.concatenate([re, im], axis=0) for re, im in zip(real, imag)]
+            store((dates + first_date) * dates, step * dates + tile * 16, both)
+        return carry
+
+    for body, width in ((early, 2 * dates), (late, dates)):
+        for first_date in range(0, half, group):
+            lax.fori_loop(0, group, functools.partial(body, first_date), 0)
+            start = first_date * width + (half * 2 * dates if body is late else 0)
+            finish(start, group * width)
 
 
 def turn_edges(edges, turned, dates):
@@ -267,34 +300,26 @@
     dates = blocks * per
     out_rows = lines // STEP
     inner, outer = kinds_of_rows(out_rows)
-    depth = len(inner) * 2 * LANES
-    edge_on = edges_in_use(rg, chunk // STEP)
     edges = x.at[2 * HALO * dates : (2 * HALO + EDGE) * dates]
     turn_edges(edges, turned, dates)
     places = [None] * HALO
     places += [[(x, row_of(part, line, lines)) for part in range(2)] for line in range(lines)]
     places += [None] * HALO
-
-    def one_date(first_date, step, carry):
-        date = first_date + step
-        target = (step // per * 2) * per + step % per
-        for tile in range(dates // 16):
-            for part, product in enumerate(products(places, date, tile, dates)):
-                start = pl.multiple_of((target + part * per) * dates + tile * 16, 16)
-                at_rows = pl.ds(start, 16)
-                sums = window_sums(product, range(out_rows), out_rows, az)
-                for slot, o in enumerate(inner):
-                    store_split(left, at_rows, 2 * slot * LANES, sums[o])
-                whole = pl.ds(pl.multiple_of(first_date * 2 * dates + start, 16), 16)
-                for slot, o in enumerate(outer):
-                    partial[whole, slot * LANES : (slot + 1) * LANES] = sums[o]
-                store_edges(left, at_rows, depth, edges, turned, part, date, tile, dates, edge_on)
-        return carry
-
-    for first_date in range(0, dates, group):
-        lax.fori_loop(0, group, functools.partial(one_date, first_date), 0)
-        result = jnp.dot(left[...], weights[...], preferred_element_type=jnp.float32)
-        found[first_date * 2 * dates : (first_date + group) * 2 * dates, :] = result
+    rows = inner + outer
+
+    def store(base, start, sums):
+        at_rows = pl.ds(pl.multiple_of(start, 16), 16)
+        whole = pl.ds(pl.multiple_of(base + start, 16), 16)
+        for slot, total in enumerate(sums[: len(inner)] + sums[len(rows) :]):
+            store_split(left, at_rows, 2 * slot * LANES, total)
+        for slot, total in enumerate(sums[len(inner) : len(rows)]):
+            partial[whole, slot * LANES : (slot + 1) * LANES] = total
+
+    def finish(start, count):
+        found[start : start + count, :] = jnp.dot(left[:count, :], weights[...], preferred_element_type=jnp.float32)
+
+    edge_on = edges_in_use(rg, chunk // STEP)
+    all_dates(dates, group, places, rows, out_rows, az, edges, turned, edge_on, store, finish)
 
 
 def outer_kernel(
@@ -302,18 +327,18 @@
 ):
     pieces, (send, sums, halo, edges, turned, left, power) = refs[:blocks], refs[blocks:]
     dates = blocks * per
+    half = dates // 2
     out_rows = lines // STEP
     cols = chunk // STEP
     wide = out_rows * cols
     me = lax.axis_index("date")
     inner, outer = kinds_of_rows(out_rows)
-    depth = len(outer) * 2 * LANES
-    edge_on = edges_in_use(rg, cols)
+    split_at = len(inner) * cols
 
     odd = lax.axis_index("strip") % 2
     for block in range(blocks):
-        to_sublanes(paired.at[block], 0, GROUP, GROUP, block, dates, per, halo.at[1 - odd])
-        to_sublanes(other.at[block], 0, GROUP, GROUP, block, dates, per, halo.at[odd])
+        to_sublanes(paired.at[block], 0, GROUP, GROUP, order[block], dates, per, halo.at[1 - odd])
+        to_sublanes(other.at[block], 0, GROUP, GROUP, order[block], dates, per, halo.at[odd])
     below, above = halo.at[0], halo.at[1]
     lane = iota((dates, LANES), 1)
     turn = lane % (LANES // 2)
@@ -328,55 +353,62 @@
     places += [None] * lines
     places += [[(above, part * HALO + line) for part in range(2)] for line in range(HALO)]
 
-    def one_date(first_date, step, carry):
-        date = first_date + step
-        target = (step // per * 2) * per + step % per
-        for tile in range(dates // 16):
-            for part, product in enumerate(products(places, date, tile, dates)):
-                start = pl.multiple_of((target + part * per) * dates + tile * 16, 16)
-                at_rows = pl.ds(start, 16)
-                whole = pl.ds(pl.multiple_of(first_date * 2 * dates + start, 16), 16)
-                for slot, total in enumerate(window_sums(product, outer, out_rows, az)):
-                    total += partial[whole, slot * LANES : (slot + 1) * LANES]
-                    store_split(left, at_rows, 2 * slot * LANES, total)
-                store_edges(left, at_rows, depth, edges, turned, part, date, tile, dates, edge_on)
-        return carry
-
-    sums[:, : len(inner) * cols] = found[...]
-    for first_date in range(0, dates, group):
-        lax.fori_loop(0, group, functools.partial(one_date, first_date), 0)
-        result = jnp.dot(left[...], weights[...], preferred_element_type=jnp.float32)
-        sums[first_date * 2 * dates : (first_date + group) * 2 * dates, len(inner) * cols :] = result
+    def store(base, start, totals):
+        at_rows = pl.ds(pl.multiple_of(start, 16), 16)
+        whole = pl.ds(pl.multiple_of(base + start, 16), 16)
+        for slot, total in enumerate(totals):
+            if slot < len(outer):
+                total += partial[whole, slot * LANES : (slot + 1) * LANES]
+            store_split(left, at_rows, 2 * slot * LANES, total)
+
+    def finish(start, count):
+        rows = slice(start, start + count)
+        sums[rows, split_at:] = jnp.dot(left[:count, :], weights[...], preferred_element_type=jnp.float32)
+
+    sums[:, :split_at] = found[...]
+    edge_on = edges_in_use(rg, cols)
+    all_dates(dates, group, places, outer, out_rows, az, edges, turned, edge_on, store, finish)
+
+    def row_at(date, part, later):
+        if date < half:
+            return (date * 2 + part) * dates + later
+        later -= half
+        return (dates + date - half) * dates + later // 8 * 16 + part * 8 + later % 8
+
     for date in range(dates):
-        at_row = (date // per * 2 * per + date % per) * dates + date
+        at_row = row_at(date, 0, date)
         power[date : date + 1, :] = sums[at_row : at_row + 1, :]
     scale = lax.rsqrt(power[...] + epsilon)
     power[...] = scale
     position = iota((dates, wide), 0)
     column = iota((dates, wide), 1)
-    rank = jnp.zeros((dates, wide), jnp.int32)
-    for block in range(blocks):
-        rank = jnp.where(position // per == block, order[block] * per + position % per, rank)
     for date in range(dates):
-        later = rank > order[date // per] * per + date % per
         factor = scale * power[date : date + 1, :]
-        starts = [((date // per * 2 + part) * per + date % per) * dates for part in range(2)]
-        values = [jnp.where(later, sums[start : start + dates, :] * factor, 0.0) for start in starts]
+        values = []
+        for part in range(2):
+            if date < half:
+                value = sums[row_at(date, part, 0) : row_at(date, part, 0) + dates, :]
+            else:
+                tiles = [row_at(date, part, half + tile) for tile in range(0, half, 8)]
+                value = [jnp.zeros((half, wide), jnp.float32)] + [sums[row : row + 8, :] for row in tiles]
+                value = jnp.concatenate(value, axis=0)
+            values.append(jnp.where(position > date, value * factor, 0.0))
         largest = jnp.max(jnp.maximum(jnp.abs(values[0]), jnp.abs(values[1])), axis=1, keepdims=True)
         level = jnp.floor(jnp.log(largest) * (LEVELS / LOG_2)) + 1.0
         level = jnp.clip(level, LOWEST, HIGHEST)
         codes = [jnp.floor(value * (jnp.exp(level * (-LOG_2 / LEVELS)) * TOP) + 0.5) for value in values]
         header = jnp.sum(jnp.where(position == column, level, 0.0), axis=0, keepdims=True)
         codes[0] = jnp.where(position == date, header, codes[0])
-        for start, code in zip(starts, codes):
+        for part, code in enumerate(codes):
+            start = ((date // per * 2 + part) * per + date % per) * dates
             send[start : start + dates, :] = code.astype(jnp.int32).astype(jnp.int16)
     count = 2 * per * dates
     for piece, k in zip(pieces, partners(blocks)):
-        piece[...] = send[pl.ds(pl.multiple_of((me ^ k) * count, 16), count), :]
-
-
-def join_kernel(blocks, per, out_rows, cols, *refs):
-    pieces, (out, recv, halves, done) = refs[:blocks], refs[blocks:]
+        piece[...] = send[pl.ds(pl.multiple_of(order[me ^ k] * count, 16), count), :]
+
+
+def join_kernel(blocks, per, out_rows, cols, order, *refs):
+    pieces, (out, recv, halves, placed, done) = refs[:blocks], refs[blocks:]
     dates = blocks * per
     wide = out_rows * cols
     per_tile = LANES // cols
@@ -390,7 +422,7 @@
     factors = [[None] * blocks for _ in range(per)]
     copies = []
     for step in range(2 * per):
-        own = me * per + step % per
+        own = order[me] * per + step % per
         values = []
         for block in range(blocks):
             codes = recv[block, step * dates : (step + 1) * dates, :].astype(jnp.int32).astype(jnp.float32)
@@ -420,9 +452,13 @@
                     for start in range(0, dates, 8):
                         at = start * out_rows + row_order[o_tile * per_tile + o]
                         halves[step, d_tile, pl.ds(at, 8, stride=out_rows), :] = tiles[o][start : start + 8]
+            own_rows = per * out_rows
+            for block in range(blocks):
+                found = halves[step, d_tile, pl.ds(pl.multiple_of(order[block] * own_rows, 8), own_rows), :]
+                placed[step, d_tile, block * own_rows : (block + 1) * own_rows, :] = found
             rows = slice(step * dates * out_rows, (step + 1) * dates * out_rows)
             target = out.at[rows, d_tile * LANES : (d_tile + 1) * LANES]
-            copies.append(pltpu.make_async_copy(halves.at[step, d_tile], target, done.at[step, d_tile]))
+            copies.append(pltpu.make_async_copy(placed.at[step, d_tile], target, done.at[step, d_tile]))
             copies[-1].start()
     for copy in copies:
         copy.wait()
@@ -485,11 +521,11 @@
     x, to_pair, to_other = pl.pallas_call(
         functools.partial(spread_kernel, blocks, per, lines),
         out_shape=[jax.ShapeDtypeStruct((date_rows * dates, LANES), jnp.float32), edge, edge],
-        in_specs=[VMEM] * blocks,
+        in_specs=[SMEM] + [VMEM] * blocks,
         out_specs=[VMEM] * 3,
         compiler_params=PARAMS,
         name="spread",
-    )(*recv)
+    )(block_order, *recv)
 
     def swaps(first):
         pairs = [(i, i + 1) for i in range(first, strips - 1, 2)]
@@ -497,7 +533,8 @@
 
     other = lax.ppermute(to_other, "strip", swaps(1))
     paired = lax.ppermute(to_pair, "strip", swaps(0))
-    count = dates * 2 * dates
+    count = dates * dates * 3 // 2
+    half_group = min(group, dates // 2)
     found, partial = pl.pallas_call(
         functools.partial(inner_kernel, blocks, per, lines, chunk, group),
         out_shape=[
@@ -508,7 +545,7 @@
         out_specs=[VMEM] * 2,
         scratch_shapes=[
             pltpu.VMEM((EDGE * dates, LANES), jnp.float32),
-            pltpu.VMEM((group * 2 * dates, depths[0]), jnp.bfloat16),
+            pltpu.VMEM((half_group * 2 * dates, depths[0]), jnp.bfloat16),
         ],
         compiler_params=PARAMS,
         cost_estimate=pl.CostEstimate(flops=0, bytes_accessed=12 * 1024 * 1024, transcendentals=0),
@@ -520,12 +557,12 @@
         in_specs=[VMEM] * 5 + [SMEM] * 3 + [VMEM],
         out_specs=[VMEM] * blocks,
         scratch_shapes=[
-            pltpu.VMEM((count, wide), jnp.int16),
+            pltpu.VMEM((dates * 2 * dates, wide), jnp.int16),
             pltpu.VMEM((count, wide), jnp.float32),
             pltpu.VMEM((2, GROUP * dates, LANES), jnp.float32),
             pltpu.VMEM((EDGE * dates, LANES), jnp.float32),
             pltpu.VMEM((EDGE * dates, LANES), jnp.float32),
-            pltpu.VMEM((group * 2 * dates, depths[1]), jnp.bfloat16),
+            pltpu.VMEM((half_group * 2 * dates, depths[1]), jnp.bfloat16),
             pltpu.VMEM((dates, wide), jnp.float32),
         ],
         compiler_params=PARAMS,
@@ -537,20 +574,22 @@
         out = pl.pallas_call(
             functools.partial(join_kernel, blocks, per, out_rows, cols),
             out_shape=jax.ShapeDtypeStruct((count * out_rows, blocks * cols), jnp.float32),
-            in_specs=[VMEM] * blocks,
+            in_specs=[SMEM] + [VMEM] * blocks,
             out_specs=pl.BlockSpec(memory_space=pl.ANY),
             scratch_shapes=[
                 pltpu.VMEM((blocks, count, wide), jnp.int16),
+                pltpu.VMEM((2 * per, blocks * cols // LANES, dates * out_rows, LANES), jnp.float32),
                 pltpu.VMEM((2 * per, blocks * cols // LANES, dates * out_rows, LANES), jnp.float32),
                 pltpu.SemaphoreType.DMA((2 * per, blocks * cols // LANES)),
             ],
             compiler_params=PARAMS,
             name="join",
-        )(*back)
+        )(block_order, *back)
     else:
         place = [partners(blocks).index(k) for k in range(blocks)]
         back = jnp.stack([back[at] for at in place])[me ^ jnp.arange(blocks)]
-        values = decode(back.reshape(blocks, 2, per, dates, wide), me, per)
+        values = decode(back.reshape(blocks, 2, per, dates, wide), block_order[me], per)
+        values = values.reshape(blocks, 2, per, blocks, per, wide)[:, :, :, block_order]
         values = values.reshape(blocks, count, out_rows, cols).transpose(1, 2, 0, 3)
         row_order = sum(kinds_of_rows(out_rows), [])
         out = jnp.stack([values[:, row_order.index(o)] for o in range(out_rows)], axis=1)

time: 33.6 us -> 34.5 us (1.027)
  local copies, waits for them, and re-layouts: 2.36 us -> 3.02 us
    unnamed x8, local copies, waits for them, and re-layouts: 2.21 us -> 2.86 us
    pallas_call x1, Pallas kernels: 0.27 us -> 0.8 us  [on_device(): pl.pallas_call(functools.partial(spread_kernel, blocks, per, lines), out_...]
    pallas_call x1, Pallas kernels: 3.39 us -> 2.88 us  [on_device(): pl.pallas_call(functools.partial(inner_kernel, blocks, per, lines, chunk,...]
    pallas_call x1, Pallas kernels: 1.54 us -> 2.04 us  [on_device(): pl.pallas_call(functools.partial(join_kernel, blocks, per, out_rows, cols...]
  transfers between devices with their start and end apart: 16 -> 16, of which waited for: 5 -> 5; matrix products, arithmetic and copies ran while one was open for 0% -> 0% of each run, Pallas kernels for 12% -> 10%
where the time goes in v10:
time: 34.5 us; the launch traced here: 34.3 us
  starting transfers between devices  19 us (55%)
  Pallas kernels  9.01 us (26%)
  waiting for transfers between devices  3.13 us (9%)
  local copies, waits for them, and re-layouts  3.02 us (9%)
    ppermute x14, starting transfers between devices, swap_blocks(): lax.ppermute(pieces[at], 'date', [(i, i ^ k) for i in range(blocks)])  14.5 us
    ppermute x1, starting transfers between devices, on_device(): other = lax.ppermute(to_other, 'strip', swaps(1))  4.32 us
    ppermute x14, waiting for transfers between devices, swap_blocks(): lax.ppermute(pieces[at], 'date', [(i, i ^ k) for i in range(blocks)])  3.12 us
    pallas_call x1, Pallas kernels, on_device(): pl.pallas_call(functools.partial(inner_kernel, blocks, per, lines, chunk,...  2.88 us
    unnamed x8, local copies, waits for them, and re-layouts  2.86 us
    pallas_call x1, Pallas kernels, on_device(): pl.pallas_call(functools.partial(outer_kernel, blocks, per, lines, chunk,...  2.35 us
    pallas_call x1, Pallas kernels, on_device(): pl.pallas_call(functools.partial(join_kernel, blocks, per, out_rows, cols...  2.04 us
    pallas_call x1, Pallas kernels, on_device(): pl.pallas_call(functools.partial(spread_kernel, blocks, per, lines), out_...  0.8 us
  transfers between devices with their start and end apart: 16, of which 5 were waited for; matrix products, arithmetic and copies ran while one was open for 0% of the time, Pallas kernels for 10%

profile of v10, /device:TPU:9, one launch (start us, length us, event | category | flops | bytes accessed | tf_op | source)
XLA Modules:
  0.0 34.3 jit_solution(7531346597649793071)
XLA Ops:
  0.0 0.9 %copy-done = bf16[2,2,32,1024]{3,2,1,0:T(8,128)(2,1)S(1)} copy-done((bf16[2,2,32,1024]{3,2,1,0:T(8,128)(2,1)S(1)}, bf16[2,2,32,1024]{3,2,1,0:T(8,128)(2,1)}, u32[]{:S(2)}) %copy-start) | copy-done | bytes 262168
  1.0 0.3 pack.1
  1.3 2.2 %collective-permute-start = (bf16[144,128]{1,0:T(8,128)(2,1)S(1)}, bf16[144,128]{1,0:T(8,128)(2,1)S(1)}, u32[]{:S(2)}, u32[]{:S(2)}) collective-permute-start(bf16[144,128]{1,0:T(8,128)(2,1)S(1)} %get-tuple-element.39), channel_id=1, source_target_pairs={{0,24},{4,28},{8,16},{12,20},{16,8},{20,12},{24,0},{28,4},{1,25},{... | collective-permute-start | bytes 110600 | tf_op jit(solution)/shard_map/ppermute | solution.py:77
  3.5 0.2 collective-permute-start.1
  3.7 0.3 collective-permute-start.2
  4.0 3.6 %collective-permute-start.3 = (bf16[144,128]{1,0:T(8,128)(2,1)S(1)}, bf16[144,128]{1,0:T(8,128)(2,1)S(1)}, u32[]{:S(2)}, u32[]{:S(2)}) collective-permute-start(bf16[144,128]{1,0:T(8,128)(2,1)S(1)} %get-tuple-element.42), channel_id=1, source_target_pairs={{0,28},{4,24},{8,20},{12,16},{16,12},{20,8},{24,4},{28,0},{1,29},{... | collective-permute-start | bytes 110600 | tf_op jit(solution)/shard_map/ppermute | solution.py:77
  7.6 0.8 %collective-permute-start.5 = (bf16[144,128]{1,0:T(8,128)(2,1)S(1)}, bf16[144,128]{1,0:T(8,128)(2,1)S(1)}, u32[]{:S(2)}, u32[]{:S(2)}) collective-permute-start(bf16[144,128]{1,0:T(8,128)(2,1)S(1)} %get-tuple-element.44), channel_id=1, source_target_pairs={{0,12},{4,8},{8,4},{12,0},{16,28},{20,24},{24,20},{28,16},{1,13},{... | collective-permute-start | bytes 110600 | tf_op jit(solution)/shard_map/ppermute | solution.py:77
  8.3 0.0 collective-permute-done.1.refs_2_
  8.3 0.1 collective-permute-start.6
  8.4 0.7 %copy-done.2 = s32[256]{0:T(256)S(1)} copy-done((s32[256]{0:T(256)S(1)}, s32[256]{0:T(256)}, u32[]{:S(2)}) %copy-start.2) | copy-done | bytes 1048
  9.1 0.1 dynamic_slice.3
  9.2 0.1 broadcast_in_dim_tile.3.tiled
  9.3 0.6 %copy-done.3 = s32[8]{0:T(128)S(1)} copy-done((s32[8]{0:T(128)S(1)}, s32[8]{0:T(128)}, u32[]{:S(2)}) %copy-start.3) | copy-done | bytes 56
  9.8 0.6 %weights.1 = (bf16[1536,128]{1,0:T(8,128)(2,1)S(1)}, bf16[1536,128]{1,0:T(8,128)(2,1)S(1)}) custom-call(s32[8]{0:T(128)S(1)} %copy-done.3, s32[1,256]{1,0:T(1,128)S(1)} %broadcast_in_dim_tile.3.tiled), custom_call_target="tpu_custom_call" | custom-call | bytes 4194304 | tf_op jit(solution)/shard_map/weights/pallas_call | solution.py:507
  10.5 0.0 collective-permute-done.3.refs_4_
  10.5 0.7 %collective-permute-done.4.refs_5_ = bf16[144,128]{1,0:T(8,128)(2,1)S(1)} collective-permute-done((bf16[144,128]{1,0:T(8,128)(2,1)S(1)}, bf16[144,128]{1,0:T(8,128)(2,1)S(1)}, u32[]{:S(2)}, u32[]{:S(2)}) %collective-permute-start.4) | collective-permute-done | bytes 36896 | tf_op jit(solution)/shard_map/ppermute | solution.py:77
  11.2 0.3 collective-permute-done.5.refs_6_
  11.5 0.7 %copy-done.1 = s32[8]{0:T(128)S(1)} copy-done((s32[8]{0:T(128)S(1)}, s32[8]{0:T(128)}, u32[]{:S(2)}) %copy-start.1) | copy-done | bytes 56
  12.1 0.8 %spread.1 = (f32[1152,128]{1,0:T(8,128)S(1)}, bf16[8,32,128]{2,1,0:T(8,128)(2,1)S(1)}, bf16[8,32,128]{2,1,0:T(8,128)(2,1)S(1)}) custom-call(s32[8]{0:T(128)S(1)} %copy-done.1, bf16[144,128]{1,0:T(8,128)(2,1)S(1)} %get-tuple-element.48.refs_0_, bf16[144,128]{1,0:T(8,128)(2,1)S(1)} %collective-permute-done.refs_1_, ...), custom_call_target="tpu_custom_call" | custom-call | tf_op jit(solution)/shard_map/spread/pallas_call | solution.py:521
  13.0 0.2 collective-permute-start.7
  13.2 4.3 %collective-permute-start.8 = (bf16[8,32,128]{2,1,0:T(8,128)(2,1)S(1)}, bf16[8,32,128]{2,1,0:T(8,128)(2,1)S(1)}, u32[]{:S(2)}, u32[]{:S(2)}) collective-permute-start(bf16[8,32,128]{2,1,0:T(8,128)(2,1)S(1)} %get-tuple-element.58), channel_id=1, source_target_pairs={{1,2},{2,1},{5,6},{6,5},{9,10},{10,9},{13,14},{14,13},{17,18},{18,... | collective-permute-start | bytes 196616 | tf_op jit(solution)/shard_map/ppermute | solution.py:534
  17.5 2.9 %inner.1 = (f32[384,128]{1,0:T(8,128)S(1)}, f32[384,512]{1,0:T(8,128)S(1)}) custom-call(f32[1152,128]{1,0:T(8,128)S(1)} %get-tuple-element.56.x, s32[8]{0:T(128)S(1)} %copy-done.1, s32[8]{0:T(128)S(1)} %copy-done.3, s32[256]{0:T(256)S(1)} %copy-done.2, bf16[1536,128]{1,0:T(8,128)(2,1)S(1)} %get-tuple-element.59.weights), custom_call_target="tpu_custom_call" | custom-call | bytes 12582912 | tf_op jit(solution)/shard_map/inner/pallas_call | solution.py:538
  20.4 2.4 %outer.1 = (s16[64,256]{1,0:T(8,128)(2,1)S(1)}, s16[64,256]{1,0:T(8,128)(2,1)S(1)}, s16[64,256]{1,0:T(8,128)(2,1)S(1)}, s16[64,256]{1,0:T(8,128)(2,1)S(1)}, s16[...) custom-call(f32[1152,128]{1,0:T(8,128)S(1)} %get-tuple-element.56.x,, ...), custom_call_target="tpu_custom_call" | custom-call | tf_op jit(solution)/shard_map/outer/pallas_call | solution.py:554
  22.8 1.3 %collective-permute-start.9 = (s16[64,256]{1,0:T(8,128)(2,1)S(1)}, s16[64,256]{1,0:T(8,128)(2,1)S(1)}, u32[]{:S(2)}, u32[]{:S(2)}) collective-permute-start(s16[64,256]{1,0:T(8,128)(2,1)S(1)} %get-tuple-element.64), channel_id=1, source_target_pairs={{0,24},{4,28},{8,16},{12,20},{16,8},{20,12},{24,0},{28,4},{1,25},{... | collective-permute-start | bytes 98312 | tf_op jit(solution)/shard_map/ppermute | solution.py:77
  24.1 0.2 collective-permute-start.10
  24.3 1.2 %collective-permute-start.11 = (s16[64,256]{1,0:T(8,128)(2,1)S(1)}, s16[64,256]{1,0:T(8,128)(2,1)S(1)}, u32[]{:S(2)}, u32[]{:S(2)}) collective-permute-start(s16[64,256]{1,0:T(8,128)(2,1)S(1)} %get-tuple-element.66), channel_id=1, source_target_pairs={{0,8},{4,12},{8,0},{12,4},{16,24},{20,28},{24,16},{28,20},{1,9},{5... | collective-permute-start | bytes 98312 | tf_op jit(solution)/shard_map/ppermute | solution.py:77
  25.5 2.9 %collective-permute-start.12 = (s16[64,256]{1,0:T(8,128)(2,1)S(1)}, s16[64,256]{1,0:T(8,128)(2,1)S(1)}, u32[]{:S(2)}, u32[]{:S(2)}) collective-permute-start(s16[64,256]{1,0:T(8,128)(2,1)S(1)} %get-tuple-element.67), channel_id=1, source_target_pairs={{0,28},{4,24},{8,20},{12,16},{16,12},{20,8},{24,4},{28,0},{1,29},{... | collective-permute-start | bytes 98312 | tf_op jit(solution)/shard_map/ppermute | solution.py:77
  28.4 1.7 %collective-permute-start.14 = (s16[64,256]{1,0:T(8,128)(2,1)S(1)}, s16[64,256]{1,0:T(8,128)(2,1)S(1)}, u32[]{:S(2)}, u32[]{:S(2)}) collective-permute-start(s16[64,256]{1,0:T(8,128)(2,1)S(1)} %get-tuple-element.69), channel_id=1, source_target_pairs={{0,12},{4,8},{8,4},{12,0},{16,28},{20,24},{24,20},{28,16},{1,13},{... | collective-permute-start | bytes 98312 | tf_op jit(solution)/shard_map/ppermute | solution.py:77
  30.1 0.2 collective-permute-done.12.refs_4_
  30.4 1.7 %collective-permute-done.13.refs_5_ = s16[64,256]{1,0:T(8,128)(2,1)S(1)} collective-permute-done((s16[64,256]{1,0:T(8,128)(2,1)S(1)}, s16[64,256]{1,0:T(8,128)(2,1)S(1)}, u32[]{:S(2)}, u32[]{:S(2)}) %collective-permute-start.13) | collective-permute-done | bytes 32800 | tf_op jit(solution)/shard_map/ppermute | solution.py:77
  32.1 0.2 collective-permute-done.14.refs_6_
  32.2 2.0 %join.1 = f32[512,256]{1,0:T(8,128)} custom-call(s32[8]{0:T(128)S(1)} %copy-done.1, s16[64,256]{1,0:T(8,128)(2,1)S(1)} %get-tuple-element.63.refs_0_, s16[64,256]{1,0:T(8,128)(2,1)S(1)} %collective-permute-done.9.refs_1_, s16[64,256]{1,0:T(8,128)(2,1)S(1)} %collective-permute-done.10.refs_2_, s16[64,256]{1,0:T(8,128)(2,1)S(1)} %collective-permute-done.11.refs_3_, ...), custom_call_target="tpu_custom_call" | custom-call | tf_op jit(solution)/shard_map/join/pallas_call | solution.py:574
  (17 shorter events, 0.0 us)
Async XLA Ops:
  0.0 0.9 %copy-start = (bf16[2,2,32,1024]{3,2,1,0:T(8,128)(2,1)S(1)}, bf16[2,2,32,1024]{3,2,1,0:T(8,128)(2,1)}, u32[]{:S(2)}) copy-start(bf16[2,2,32,1024]{3,2,1,0:T(8,128)(2,1)} %slc.1) | copy-start | bytes 786436
  1.3 6.3 %collective-permute-start = (bf16[144,128]{1,0:T(8,128)(2,1)S(1)}, bf16[144,128]{1,0:T(8,128)(2,1)S(1)}, u32[]{:S(2)}, u32[]{:S(2)}) collective-permute-start(bf16[144,128]{1,0:T(8,128)(2,1)S(1)} %get-tuple-element.39), channel_id=1, source_target_pairs={{0,24},{4,28},{8,16},{12,20},{16,8},{20,12},{24,0},{28,4},{1,25},{... | collective-permute-start | bytes 110600 | tf_op jit(solution)/shard_map/ppermute | solution.py:77
  3.5 4.8 %collective-permute-start.1 = (bf16[144,128]{1,0:T(8,128)(2,1)S(1)}, bf16[144,128]{1,0:T(8,128)(2,1)S(1)}, u32[]{:S(2)}, u32[]{:S(2)}) collective-permute-start(bf16[144,128]{1,0:T(8,128)(2,1)S(1)} %get-tuple-element.40), channel_id=1, source_target_pairs={{0,16},{4,20},{8,24},{12,28},{16,0},{20,4},{24,8},{28,12},{1,17},{... | collective-permute-start | bytes 110600 | tf_op jit(solution)/shard_map/ppermute | solution.py:77
  3.7 6.7 %collective-permute-start.2 = (bf16[144,128]{1,0:T(8,128)(2,1)S(1)}, bf16[144,128]{1,0:T(8,128)(2,1)S(1)}, u32[]{:S(2)}, u32[]{:S(2)}) collective-permute-start(bf16[144,128]{1,0:T(8,128)(2,1)S(1)} %get-tuple-element.41), channel_id=1, source_target_pairs={{0,8},{4,12},{8,0},{12,4},{16,24},{20,28},{24,16},{28,20},{1,9},{5... | collective-permute-start | bytes 110600 | tf_op jit(solution)/shard_map/ppermute | solution.py:77
  4.0 6.5 %collective-permute-start.3 = (bf16[144,128]{1,0:T(8,128)(2,1)S(1)}, bf16[144,128]{1,0:T(8,128)(2,1)S(1)}, u32[]{:S(2)}, u32[]{:S(2)}) collective-permute-start(bf16[144,128]{1,0:T(8,128)(2,1)S(1)} %get-tuple-element.42), channel_id=1, source_target_pairs={{0,28},{4,24},{8,20},{12,16},{16,12},{20,8},{24,4},{28,0},{1,29},{... | collective-permute-start | bytes 110600 | tf_op jit(solution)/shard_map/ppermute | solution.py:77
  7.6 3.7 %collective-permute-start.4 = (bf16[144,128]{1,0:T(8,128)(2,1)S(1)}, bf16[144,128]{1,0:T(8,128)(2,1)S(1)}, u32[]{:S(2)}, u32[]{:S(2)}) collective-permute-start(bf16[144,128]{1,0:T(8,128)(2,1)S(1)} %get-tuple-element.43), channel_id=1, source_target_pairs={{0,20},{4,16},{8,28},{12,24},{16,4},{20,0},{24,12},{28,8},{1,21},{... | collective-permute-start | bytes 110600 | tf_op jit(solution)/shard_map/ppermute | solution.py:77
  7.6 3.9 %collective-permute-start.5 = (bf16[144,128]{1,0:T(8,128)(2,1)S(1)}, bf16[144,128]{1,0:T(8,128)(2,1)S(1)}, u32[]{:S(2)}, u32[]{:S(2)}) collective-permute-start(bf16[144,128]{1,0:T(8,128)(2,1)S(1)} %get-tuple-element.44), channel_id=1, source_target_pairs={{0,12},{4,8},{8,4},{12,0},{16,28},{20,24},{24,20},{28,16},{1,13},{... | collective-permute-start | bytes 110600 | tf_op jit(solution)/shard_map/ppermute | solution.py:77
  8.3 3.2 %collective-permute-start.6 = (bf16[144,128]{1,0:T(8,128)(2,1)S(1)}, bf16[144,128]{1,0:T(8,128)(2,1)S(1)}, u32[]{:S(2)}, u32[]{:S(2)}) collective-permute-start(bf16[144,128]{1,0:T(8,128)(2,1)S(1)} %get-tuple-element.45), channel_id=1, source_target_pairs={{0,4},{4,0},{8,12},{12,8},{16,20},{20,16},{24,28},{28,24},{1,5},{5... | collective-permute-start | bytes 110600 | tf_op jit(solution)/shard_map/ppermute | solution.py:77
  8.4 0.7 %copy-start.2 = (s32[256]{0:T(256)S(1)}, s32[256]{0:T(256)}, u32[]{:S(2)}) copy-start(s32[256]{0:T(256)} %rg.3) | copy-start | bytes 3076
  9.2 0.7 %copy-start.3 = (s32[8]{0:T(128)S(1)}, s32[8]{0:T(128)}, u32[]{:S(2)}) copy-start(s32[8]{0:T(128)} %az.5) | copy-start | bytes 100
  11.5 0.7 %copy-start.1 = (s32[8]{0:T(128)S(1)}, s32[8]{0:T(128)}, u32[]{:S(2)}) copy-start(s32[8]{0:T(128)} %order.7) | copy-start | bytes 100
  13.0 7.5 %collective-permute-start.7 = (bf16[8,32,128]{2,1,0:T(8,128)(2,1)S(1)}, bf16[8,32,128]{2,1,0:T(8,128)(2,1)S(1)}, u32[]{:S(2)}, u32[]{:S(2)}) collective-permute-start(bf16[8,32,128]{2,1,0:T(8,128)(2,1)S(1)} %get-tuple-element.57), channel_id=1, source_target_pairs={{0,1},{2,3},{1,0},{3,2},{4,5},{6,7},{5,4},{7,6},{8,9},{10,11},{9,8... | collective-permute-start | bytes 196616 | tf_op jit(solution)/shard_map/ppermute | solution.py:535
  13.2 7.2 %collective-permute-start.8 = (bf16[8,32,128]{2,1,0:T(8,128)(2,1)S(1)}, bf16[8,32,128]{2,1,0:T(8,128)(2,1)S(1)}, u32[]{:S(2)}, u32[]{:S(2)}) collective-permute-start(bf16[8,32,128]{2,1,0:T(8,128)(2,1)S(1)} %get-tuple-element.58), channel_id=1, source_target_pairs={{1,2},{2,1},{5,6},{6,5},{9,10},{10,9},{13,14},{14,13},{17,18},{18,... | collective-permute-start | bytes 196616 | tf_op jit(solution)/shard_map/ppermute | solution.py:534
  22.8 5.6 %collective-permute-start.9 = (s16[64,256]{1,0:T(8,128)(2,1)S(1)}, s16[64,256]{1,0:T(8,128)(2,1)S(1)}, u32[]{:S(2)}, u32[]{:S(2)}) collective-permute-start(s16[64,256]{1,0:T(8,128)(2,1)S(1)} %get-tuple-element.64), channel_id=1, source_target_pairs={{0,24},{4,28},{8,16},{12,20},{16,8},{20,12},{24,0},{28,4},{1,25},{... | collective-permute-start | bytes 98312 | tf_op jit(solution)/shard_map/ppermute | solution.py:77
  24.1 6.0 %collective-permute-start.10 = (s16[64,256]{1,0:T(8,128)(2,1)S(1)}, s16[64,256]{1,0:T(8,128)(2,1)S(1)}, u32[]{:S(2)}, u32[]{:S(2)}) collective-permute-start(s16[64,256]{1,0:T(8,128)(2,1)S(1)} %get-tuple-element.65), channel_id=1, source_target_pairs={{0,16},{4,20},{8,24},{12,28},{16,0},{20,4},{24,8},{28,12},{1,17},{... | collective-permute-start | bytes 98312 | tf_op jit(solution)/shard_map/ppermute | solution.py:77
  24.3 5.9 %collective-permute-start.11 = (s16[64,256]{1,0:T(8,128)(2,1)S(1)}, s16[64,256]{1,0:T(8,128)(2,1)S(1)}, u32[]{:S(2)}, u32[]{:S(2)}) collective-permute-start(s16[64,256]{1,0:T(8,128)(2,1)S(1)} %get-tuple-element.66), channel_id=1, source_target_pairs={{0,8},{4,12},{8,0},{12,4},{16,24},{20,28},{24,16},{28,20},{1,9},{5... | collective-permute-start | bytes 98312 | tf_op jit(solution)/shard_map/ppermute | solution.py:77
  25.5 4.9 %collective-permute-start.12 = (s16[64,256]{1,0:T(8,128)(2,1)S(1)}, s16[64,256]{1,0:T(8,128)(2,1)S(1)}, u32[]{:S(2)}, u32[]{:S(2)}) collective-permute-start(s16[64,256]{1,0:T(8,128)(2,1)S(1)} %get-tuple-element.67), channel_id=1, source_target_pairs={{0,28},{4,24},{8,20},{12,16},{16,12},{20,8},{24,4},{28,0},{1,29},{... | collective-permute-start | bytes 98312 | tf_op jit(solution)/shard_map/ppermute | solution.py:77
  28.4 3.6 %collective-permute-start.13 = (s16[64,256]{1,0:T(8,128)(2,1)S(1)}, s16[64,256]{1,0:T(8,128)(2,1)S(1)}, u32[]{:S(2)}, u32[]{:S(2)}) collective-permute-start(s16[64,256]{1,0:T(8,128)(2,1)S(1)} %get-tuple-element.68), channel_id=1, source_target_pairs={{0,20},{4,16},{8,28},{12,24},{16,4},{20,0},{24,12},{28,8},{1,21},{... | collective-permute-start | bytes 98312 | tf_op jit(solution)/shard_map/ppermute | solution.py:77
  28.4 3.8 %collective-permute-start.14 = (s16[64,256]{1,0:T(8,128)(2,1)S(1)}, s16[64,256]{1,0:T(8,128)(2,1)S(1)}, u32[]{:S(2)}, u32[]{:S(2)}) collective-permute-start(s16[64,256]{1,0:T(8,128)(2,1)S(1)} %get-tuple-element.69), channel_id=1, source_target_pairs={{0,12},{4,8},{8,4},{12,0},{16,28},{20,24},{24,20},{28,16},{1,13},{... | collective-permute-start | bytes 98312 | tf_op jit(solution)/shard_map/ppermute | solution.py:77
  30.1 2.1 %collective-permute-start.15 = (s16[64,256]{1,0:T(8,128)(2,1)S(1)}, s16[64,256]{1,0:T(8,128)(2,1)S(1)}, u32[]{:S(2)}, u32[]{:S(2)}) collective-permute-start(s16[64,256]{1,0:T(8,128)(2,1)S(1)} %get-tuple-element.70), channel_id=1, source_target_pairs={{0,4},{4,0},{8,12},{12,8},{16,20},{20,16},{24,28},{28,24},{1,5},{5... | collective-permute-start | bytes 98312 | tf_op jit(solution)/shard_map/ppermute | solution.py:77

commit v11 on v10

--- a/solution.py
+++ b/solution.py
@@ -169,22 +169,39 @@
             target[pl.ds(row * dates + block * per + date, 8, stride=dates), :] = value[row : row + 8]
 
 
-def spread_kernel(blocks, per, lines, order, *refs):
-    recv, (x, paired, other) = refs[:blocks], refs[blocks:]
-    dates = blocks * per
-    date_rows = rows_of_date(lines)
-    edge_rows = per * GROUP
+def halo_rows(per):
+    return per * 2 * HALO + EDGE
+
+
+def gather_kernel(blocks, per, lines, *refs):
+    recv, (paired, other, stage) = refs[:blocks], refs[blocks:]
     me = lax.axis_index("date")
-    turn = 1 - lax.axis_index("strip") % 2
-    rest = date_rows - 2 * GROUP
+    tail = 2 * HALO - 8
     for piece, k in zip(recv, partners(blocks)):
-        block = me ^ k
-        paired[block] = piece[:edge_rows]
-        other[block] = piece[edge_rows : 2 * edge_rows]
-        block = order[block]
-        to_sublanes(piece, turn * edge_rows, GROUP, GROUP, block, dates, per, x)
-        to_sublanes(piece, (1 - turn) * edge_rows, GROUP, GROUP, block, dates, per, x.at[GROUP * dates :])
-        to_sublanes(piece, 2 * edge_rows, rest, rest, block, dates, per, x.at[2 * GROUP * dates :])
+        for group, target in enumerate((paired, other)):
+            edges = jnp.zeros((EDGE, LANES), jnp.float32)
+            for date in range(per):
+                at = (group * per + date) * GROUP
+                value = piece[at : at + GROUP].astype(jnp.float32)
+                stage[date * 8 : date * 8 + 8, :] = value[:8]
+                stage[per * 8 + date * tail : per * 8 + (date + 1) * tail, :] = value[8 : 2 * HALO]
+                mine = value[2 * HALO : 2 * HALO + EDGE]
+                edges += pltpu.roll(mine, date * lines, 1) if date else mine
+            stage[per * 2 * HALO :, :] = edges
+            target[me ^ k] = stage[...].astype(jnp.bfloat16)
+
+
+def scatter_halo(source, block, lines, dates, per, target):
+    value = source.astype(jnp.float32)
+    tail = 2 * HALO - 8
+    for date in range(per):
+        place = block * per + date
+        target[pl.ds(place, 8, stride=dates), :] = value[date * 8 : date * 8 + 8]
+        rest = value[per * 8 + date * tail : per * 8 + (date + 1) * tail]
+        target[pl.ds(8 * dates + place, tail, stride=dates), :] = rest
+        mine = value[per * 2 * HALO :]
+        mine = pltpu.roll(mine, LANES - date * lines, 1) if date else mine
+        target[pl.ds(2 * HALO * dates + place, EDGE, stride=dates), :] = mine
 
 
 def split(value):
@@ -296,8 +313,20 @@
     return first <= 0, first <= 1, last >= 2, last >= 3
 
 
-def inner_kernel(blocks, per, lines, chunk, group, x, order, az, rg, weights, found, partial, turned, left):
+def inner_kernel(blocks, per, lines, chunk, group, order, az, rg, weights, *refs):
+    recv, (found, partial, own_edges, x, turned, left) = refs[:blocks], refs[blocks:]
     dates = blocks * per
+    date_rows = rows_of_date(lines)
+    edge_rows = per * GROUP
+    me = lax.axis_index("date")
+    swap = 1 - lax.axis_index("strip") % 2
+    rest = date_rows - 2 * GROUP
+    for piece, k in zip(recv, partners(blocks)):
+        block = order[me ^ k]
+        to_sublanes(piece, swap * edge_rows, GROUP, GROUP, block, dates, per, x)
+        to_sublanes(piece, (1 - swap) * edge_rows, GROUP, GROUP, block, dates, per, x.at[GROUP * dates :])
+        to_sublanes(piece, 2 * edge_rows, rest, rest, block, dates, per, x.at[2 * GROUP * dates :])
+    own_edges[...] = x[2 * HALO * dates : (2 * HALO + EDGE) * dates, :]
     out_rows = lines // STEP
     inner, outer = kinds_of_rows(out_rows)
     edges = x.at[2 * HALO * dates : (2 * HALO + EDGE) * dates]
@@ -323,7 +352,7 @@
 
 
 def outer_kernel(
-    blocks, per, lines, chunk, group, x, paired, other, partial, found, order, az, rg, weights, *refs
+    blocks, per, lines, chunk, group, own_edges, paired, other, partial, found, order, az, rg, weights, *refs
 ):
     pieces, (send, sums, halo, edges, turned, left, power) = refs[:blocks], refs[blocks:]
     dates = blocks * per
@@ -337,8 +366,8 @@
 
     odd = lax.axis_index("strip") % 2
     for block in range(blocks):
-        to_sublanes(paired.at[block], 0, GROUP, GROUP, order[block], dates, per, halo.at[1 - odd])
-        to_sublanes(other.at[block], 0, GROUP, GROUP, order[block], dates, per, halo.at[odd])
+        scatter_halo(paired[block], order[block], lines, dates, per, halo.at[1 - odd])
+        scatter_halo(other[block], order[block], lines, dates, per, halo.at[odd])
     below, above = halo.at[0], halo.at[1]
     lane = iota((dates, LANES), 1)
     turn = lane % (LANES // 2)
@@ -346,7 +375,8 @@
         at = (2 * HALO + k) * dates
         lower_part = pltpu.roll(below[at : at + dates, :], lines, 1)
         upper_part = pltpu.roll(above[at : at + dates, :], lines, 1)
-        value = jnp.where(turn < lines, x[at : at + dates, :], jnp.where(turn < lines + HALO, upper_part, lower_part))
+        mine = own_edges[k * dates : (k + 1) * dates, :]
+        value = jnp.where(turn < lines, mine, jnp.where(turn < lines + HALO, upper_part, lower_part))
         edges[k * dates : (k + 1) * dates, :] = value
     turn_edges(edges, turned, dates)
     places = [[(below, part * HALO + line) for part in range(2)] for line in range(HALO)]
@@ -398,7 +428,7 @@
         level = jnp.clip(level, LOWEST, HIGHEST)
         codes = [jnp.floor(value * (jnp.exp(level * (-LOG_2 / LEVELS)) * TOP) + 0.5) for value in values]
         header = jnp.sum(jnp.where(position == column, level, 0.0), axis=0, keepdims=True)
-        codes[0] = jnp.where(position == date, header, codes[0])
+        codes[0] = jnp.where(position == 0, header, codes[0])
         for part, code in enumerate(codes):
             start = ((date // per * 2 + part) * per + date % per) * dates
             send[start : start + dates, :] = code.astype(jnp.int32).astype(jnp.int16)
@@ -410,6 +440,8 @@
 def join_kernel(blocks, per, out_rows, cols, order, *refs):
     pieces, (out, recv, halves, placed, done) = refs[:blocks], refs[blocks:]
     dates = blocks * per
+    own_rows = per * out_rows
+    chosen = [[jnp.broadcast_to(order[b : b + 1, :] == r, (own_rows, LANES)) for r in range(blocks)] for b in range(blocks)]
     wide = out_rows * cols
     per_tile = LANES // cols
     me = lax.axis_index("date")
@@ -422,15 +454,14 @@
     factors = [[None] * blocks for _ in range(per)]
     copies = []
     for step in range(2 * per):
-        own = order[me] * per + step % per
         values = []
         for block in range(blocks):
             codes = recv[block, step * dates : (step + 1) * dates, :].astype(jnp.int32).astype(jnp.float32)
             if step < per:
-                header = jnp.sum(jnp.where(position == own, codes, 0.0), axis=0, keepdims=True)
+                header = codes[:1]
                 level = jnp.sum(jnp.where(position == column, header, 0.0), axis=1, keepdims=True)
                 factors[step][block] = jnp.exp(level * (LOG_2 / LEVELS)) * (1.0 / TOP)
-            values.append(jnp.where(position == own, 0.0, codes * factors[step % per][block]))
+            values.append(jnp.where(position == 0, 0.0, codes * factors[step % per][block]))
         for d_tile in range(blocks // per_tile):
             for o_tile in range(out_rows // per_tile):
                 tiles = [
@@ -452,9 +483,11 @@
                     for start in range(0, dates, 8):
                         at = start * out_rows + row_order[o_tile * per_tile + o]
                         halves[step, d_tile, pl.ds(at, 8, stride=out_rows), :] = tiles[o][start : start + 8]
-            own_rows = per * out_rows
+            ranked = [halves[step, d_tile, r * own_rows : (r + 1) * own_rows, :] for r in range(blocks)]
             for block in range(blocks):
-                found = halves[step, d_tile, pl.ds(pl.multiple_of(order[block] * own_rows, 8), own_rows), :]
+                found = ranked[0]
+                for r in range(1, blocks):
+                    found = jnp.where(chosen[block][r], ranked[r], found)
                 placed[step, d_tile, block * own_rows : (block + 1) * own_rows, :] = found
             rows = slice(step * dates * out_rows, (step + 1) * dates * out_rows)
             target = out.at[rows, d_tile * LANES : (d_tile + 1) * LANES]
@@ -464,13 +497,11 @@
         copy.wait()
 
 
-def decode(codes, me, per):
+def decode(codes):
     values = codes.astype(jnp.float32)
     dates = codes.shape[3]
-    own = (me * per + jnp.arange(per))[:, None] == jnp.arange(dates)[None]
-    header = jnp.sum(jnp.where(own[None, :, :, None], values[:, 0], 0.0), axis=2)
-    factor = jnp.exp(header[:, :, :dates] * (LOG_2 / LEVELS)) * (1.0 / TOP)
-    return jnp.where(own[None, None, :, :, None], 0.0, values * factor[:, None, :, :, None])
+    factor = jnp.exp(values[:, 0, :, 0, :dates] * (LOG_2 / LEVELS)) * (1.0 / TOP)
+    return (values * factor[:, None, :, :, None]).at[:, :, :, 0].set(0.0)
 
 
 def on_device(slc, block_order, az_offset, rg_offset):
@@ -517,15 +548,16 @@
     )(az_offset, tiled)
     recv, weights = lax.optimization_barrier((recv, weights))
 
-    edge = jax.ShapeDtypeStruct((blocks, edge_rows, LANES), jnp.bfloat16)
-    x, to_pair, to_other = pl.pallas_call(
-        functools.partial(spread_kernel, blocks, per, lines),
-        out_shape=[jax.ShapeDtypeStruct((date_rows * dates, LANES), jnp.float32), edge, edge],
-        in_specs=[SMEM] + [VMEM] * blocks,
-        out_specs=[VMEM] * 3,
+    edge = jax.ShapeDtypeStruct((blocks, halo_rows(per), LANES), jnp.bfloat16)
+    to_pair, to_other = pl.pallas_call(
+        functools.partial(gather_kernel, blocks, per, lines),
+        out_shape=[edge] * 2,
+        in_specs=[VMEM] * blocks,
+        out_specs=[VMEM] * 2,
+        scratch_shapes=[pltpu.VMEM((halo_rows(per), LANES), jnp.float32)],
         compiler_params=PARAMS,
-        name="spread",
-    )(block_order, *recv)
+        name="gather",
+    )(*recv)
 
     def swaps(first):
         pairs = [(i, i + 1) for i in range(first, strips - 1, 2)]
@@ -535,22 +567,24 @@
     paired = lax.ppermute(to_pair, "strip", swaps(0))
     count = dates * dates * 3 // 2
     half_group = min(group, dates // 2)
-    found, partial = pl.pallas_call(
+    found, partial, own_edges = pl.pallas_call(
         functools.partial(inner_kernel, blocks, per, lines, chunk, group),
         out_shape=[
             jax.ShapeDtypeStruct((count, len(kinds[0]) * cols), jnp.float32),
             jax.ShapeDtypeStruct((count, len(kinds[1]) * LANES), jnp.float32),
+            jax.ShapeDtypeStruct((EDGE * dates, LANES), jnp.float32),
         ],
-        in_specs=[VMEM, SMEM, SMEM, SMEM, VMEM],
-        out_specs=[VMEM] * 2,
+        in_specs=[SMEM] * 3 + [VMEM] * (1 + blocks),
+        out_specs=[VMEM] * 3,
         scratch_shapes=[
+            pltpu.VMEM((date_rows * dates, LANES), jnp.float32),
             pltpu.VMEM((EDGE * dates, LANES), jnp.float32),
             pltpu.VMEM((half_group * 2 * dates, depths[0]), jnp.bfloat16),
         ],
         compiler_params=PARAMS,
         cost_estimate=pl.CostEstimate(flops=0, bytes_accessed=12 * 1024 * 1024, transcendentals=0),
         name="inner",
-    )(x, block_order, az_offset, rg_offset, weights[0])
+    )(block_order, az_offset, rg_offset, weights[0], *recv)
     pairs = pl.pallas_call(
         functools.partial(outer_kernel, blocks, per, lines, chunk, group),
         out_shape=[jax.ShapeDtypeStruct((2 * per * dates, wide), jnp.int16)] * blocks,
@@ -567,14 +601,14 @@
         ],
         compiler_params=PARAMS,
         name="outer",
-    )(x, paired, other, partial, found, block_order, az_offset, rg_offset, weights[1])
+    )(own_edges, paired, other, partial, found, block_order, az_offset, rg_offset, weights[1])
     count = 2 * per * dates
     back = swap_blocks(pairs)
     if LANES % cols == 0 and out_rows * cols % LANES == 0 and blocks * cols % LANES == 0:
         out = pl.pallas_call(
             functools.partial(join_kernel, blocks, per, out_rows, cols),
             out_shape=jax.ShapeDtypeStruct((count * out_rows, blocks * cols), jnp.float32),
-            in_specs=[SMEM] + [VMEM] * blocks,
+            in_specs=[VMEM] * (1 + blocks),
             out_specs=pl.BlockSpec(memory_space=pl.ANY),
             scratch_shapes=[
                 pltpu.VMEM((blocks, count, wide), jnp.int16),
@@ -584,11 +618,11 @@
             ],
             compiler_params=PARAMS,
             name="join",
-        )(block_order, *back)
+        )(jnp.broadcast_to(block_order[:, None], (blocks, LANES)), *back)
     else:
         place = [partners(blocks).index(k) for k in range(blocks)]
         back = jnp.stack([back[at] for at in place])[me ^ jnp.arange(blocks)]
-        values = decode(back.reshape(blocks, 2, per, dates, wide), block_order[me], per)
+        values = decode(back.reshape(blocks, 2, per, dates, wide))
         values = values.reshape(blocks, 2, per, blocks, per, wide)[:, :, :, block_order]
         values = values.reshape(blocks, count, out_rows, cols).transpose(1, 2, 0, 3)
         row_order = sum(kinds_of_rows(out_rows), [])

time: 34.5 us -> 33.1 us (0.959)
  Pallas kernels: 9.01 us -> 8.26 us
  local copies, waits for them, and re-layouts: 3.02 us -> 2.43 us
    unnamed x8, local copies, waits for them, and re-layouts: 2.86 us -> 2.21 us
    pallas_call x1, Pallas kernels: 0.8 us -> 0.17 us  [on_device(): pl.pallas_call(functools.partial(gather_kernel, blocks, per, lines), out_...]
    pallas_call x1, Pallas kernels: 2.04 us -> 1.69 us  [on_device(): pl.pallas_call(functools.partial(join_kernel, blocks, per, out_rows, cols...]
  transfers between devices with their start and end apart: 16 -> 16, of which waited for: 5 -> 5; matrix products, arithmetic and copies ran while one was open for 0% -> 0% of each run, Pallas kernels for 10% -> 11%
where the time goes in v11:
time: 33.1 us; the launch traced here: 32.9 us
  starting transfers between devices  19 us (57%)
  Pallas kernels  8.26 us (25%)
  waiting for transfers between devices  3.14 us (9%)
  local copies, waits for them, and re-layouts  2.43 us (7%)
    ppermute x14, starting transfers between devices, swap_blocks(): lax.ppermute(pieces[at], 'date', [(i, i ^ k) for i in range(blocks)])  14.5 us
    ppermute x1, starting transfers between devices, on_device(): other = lax.ppermute(to_other, 'strip', swaps(1))  4.32 us
    ppermute x14, waiting for transfers between devices, swap_blocks(): lax.ppermute(pieces[at], 'date', [(i, i ^ k) for i in range(blocks)])  3.13 us
    pallas_call x1, Pallas kernels, on_device(): pl.pallas_call(functools.partial(inner_kernel, blocks, per, lines, chunk,...  3.06 us
    pallas_call x1, Pallas kernels, on_device(): pl.pallas_call(functools.partial(outer_kernel, blocks, per, lines, chunk,...  2.4 us
    unnamed x8, local copies, waits for them, and re-layouts  2.21 us
    pallas_call x1, Pallas kernels, on_device(): pl.pallas_call(functools.partial(join_kernel, blocks, per, out_rows, cols...  1.69 us
  transfers between devices with their start and end apart: 16, of which 5 were waited for; matrix products, arithmetic and copies ran while one was open for 0% of the time, Pallas kernels for 11%

profile of v11, /device:TPU:9, one launch (start us, length us, event | category | flops | bytes accessed | tf_op | source)
XLA Modules:
  0.0 32.9 jit_solution(12650265691451385689)
XLA Ops:
  0.0 0.9 %copy-done = bf16[2,2,32,1024]{3,2,1,0:T(8,128)(2,1)S(1)} copy-done((bf16[2,2,32,1024]{3,2,1,0:T(8,128)(2,1)S(1)}, bf16[2,2,32,1024]{3,2,1,0:T(8,128)(2,1)}, u32[]{:S(2)}) %copy-start) | copy-done | bytes 262168
  1.0 0.3 pack.1
  1.3 2.2 %collective-permute-start = (bf16[144,128]{1,0:T(8,128)(2,1)S(1)}, bf16[144,128]{1,0:T(8,128)(2,1)S(1)}, u32[]{:S(2)}, u32[]{:S(2)}) collective-permute-start(bf16[144,128]{1,0:T(8,128)(2,1)S(1)} %get-tuple-element.39), channel_id=1, source_target_pairs={{0,24},{4,28},{8,16},{12,20},{16,8},{20,12},{24,0},{28,4},{1,25},{... | collective-permute-start | bytes 110600 | tf_op jit(solution)/shard_map/ppermute | solution.py:77
  3.5 0.2 collective-permute-start.1
  3.7 0.3 collective-permute-start.2
  4.0 3.6 %collective-permute-start.3 = (bf16[144,128]{1,0:T(8,128)(2,1)S(1)}, bf16[144,128]{1,0:T(8,128)(2,1)S(1)}, u32[]{:S(2)}, u32[]{:S(2)}) collective-permute-start(bf16[144,128]{1,0:T(8,128)(2,1)S(1)} %get-tuple-element.42), channel_id=1, source_target_pairs={{0,28},{4,24},{8,20},{12,16},{16,12},{20,8},{24,4},{28,0},{1,29},{... | collective-permute-start | bytes 110600 | tf_op jit(solution)/shard_map/ppermute | solution.py:77
  7.6 0.8 %collective-permute-start.5 = (bf16[144,128]{1,0:T(8,128)(2,1)S(1)}, bf16[144,128]{1,0:T(8,128)(2,1)S(1)}, u32[]{:S(2)}, u32[]{:S(2)}) collective-permute-start(bf16[144,128]{1,0:T(8,128)(2,1)S(1)} %get-tuple-element.44), channel_id=1, source_target_pairs={{0,12},{4,8},{8,4},{12,0},{16,28},{20,24},{24,20},{28,16},{1,13},{... | collective-permute-start | bytes 110600 | tf_op jit(solution)/shard_map/ppermute | solution.py:77
  8.3 0.0 collective-permute-done.1.refs_2_
  8.3 0.1 collective-permute-start.6
  8.4 0.7 %copy-done.2 = s32[256]{0:T(256)S(1)} copy-done((s32[256]{0:T(256)S(1)}, s32[256]{0:T(256)}, u32[]{:S(2)}) %copy-start.2) | copy-done | bytes 1048
  9.1 0.1 dynamic_slice.3
  9.2 0.1 broadcast_in_dim_tile.3.tiled
  9.3 0.6 %copy-done.3 = s32[8]{0:T(128)S(1)} copy-done((s32[8]{0:T(128)S(1)}, s32[8]{0:T(128)}, u32[]{:S(2)}) %copy-start.3) | copy-done | bytes 56
  9.8 0.6 %weights.1 = (bf16[1536,128]{1,0:T(8,128)(2,1)S(1)}, bf16[1536,128]{1,0:T(8,128)(2,1)S(1)}) custom-call(s32[8]{0:T(128)S(1)} %copy-done.3, s32[1,256]{1,0:T(1,128)S(1)} %broadcast_in_dim_tile.3.tiled), custom_call_target="tpu_custom_call" | custom-call | bytes 4194304 | tf_op jit(solution)/shard_map/weights/pallas_call | solution.py:538
  10.5 0.0 collective-permute-done.3.refs_4_
  10.5 0.7 %collective-permute-done.4.refs_5_ = bf16[144,128]{1,0:T(8,128)(2,1)S(1)} collective-permute-done((bf16[144,128]{1,0:T(8,128)(2,1)S(1)}, bf16[144,128]{1,0:T(8,128)(2,1)S(1)}, u32[]{:S(2)}, u32[]{:S(2)}) %collective-permute-start.4) | collective-permute-done | bytes 36896 | tf_op jit(solution)/shard_map/ppermute | solution.py:77
  11.2 0.3 collective-permute-done.5.refs_6_
  11.5 0.2 gather.1
  11.7 0.2 collective-permute-start.7
  11.9 4.3 %collective-permute-start.8 = (bf16[8,24,128]{2,1,0:T(8,128)(2,1)S(1)}, bf16[8,24,128]{2,1,0:T(8,128)(2,1)S(1)}, u32[]{:S(2)}, u32[]{:S(2)}) collective-permute-start(bf16[8,24,128]{2,1,0:T(8,128)(2,1)S(1)} %get-tuple-element.59), channel_id=1, source_target_pairs={{1,2},{2,1},{5,6},{6,5},{9,10},{10,9},{13,14},{14,13},{17,18},{18,... | collective-permute-start | bytes 147464 | tf_op jit(solution)/shard_map/ppermute | solution.py:566
  16.2 3.1 %inner.1 = (f32[384,128]{1,0:T(8,128)S(1)}, f32[384,512]{1,0:T(8,128)S(1)}, f32[64,128]{1,0:T(8,128)S(1)}) custom-call(s32[8]{0:T(128)S(1)} %copy-done.1, s32[8]{0:T(128)S(1)} %copy-done.3, s32[256]{0:T(256)S(1)} %copy-done.2, bf16[1536,128]{1,0:T(8,128)(2,1)S(1)} %get-tuple-element.48.weights, bf16[144,128]{1,0:T(8,128)(2,1)S(1)} %get-tuple-element.49.refs_0_, ...), custom_call_target="tpu_custom_call" | custom-call | bytes 12582912 | tf_op jit(solution)/shard_map/inner/pallas_call | solution.py:570
  19.3 2.4 %outer.1 = (s16[64,256]{1,0:T(8,128)(2,1)S(1)}, s16[64,256]{1,0:T(8,128)(2,1)S(1)}, s16[64,256]{1,0:T(8,128)(2,1)S(1)}, s16[64,256]{1,0:T(8,128)(2,1)S(1)}, s16[...) custom-call(f32[64,128]{1,0:T(8,128)S(1)} %get-tuple-element.57.own_, ...), custom_call_target="tpu_custom_call" | custom-call | tf_op jit(solution)/shard_map/outer/pallas_call | solution.py:588
  21.7 1.3 %collective-permute-start.9 = (s16[64,256]{1,0:T(8,128)(2,1)S(1)}, s16[64,256]{1,0:T(8,128)(2,1)S(1)}, u32[]{:S(2)}, u32[]{:S(2)}) collective-permute-start(s16[64,256]{1,0:T(8,128)(2,1)S(1)} %get-tuple-element.64), channel_id=1, source_target_pairs={{0,24},{4,28},{8,16},{12,20},{16,8},{20,12},{24,0},{28,4},{1,25},{... | collective-permute-start | bytes 98312 | tf_op jit(solution)/shard_map/ppermute | solution.py:77
  23.0 0.2 collective-permute-start.10
  23.2 1.2 %collective-permute-start.11 = (s16[64,256]{1,0:T(8,128)(2,1)S(1)}, s16[64,256]{1,0:T(8,128)(2,1)S(1)}, u32[]{:S(2)}, u32[]{:S(2)}) collective-permute-start(s16[64,256]{1,0:T(8,128)(2,1)S(1)} %get-tuple-element.66), channel_id=1, source_target_pairs={{0,8},{4,12},{8,0},{12,4},{16,24},{20,28},{24,16},{28,20},{1,9},{5... | collective-permute-start | bytes 98312 | tf_op jit(solution)/shard_map/ppermute | solution.py:77
  24.5 2.9 %collective-permute-start.12 = (s16[64,256]{1,0:T(8,128)(2,1)S(1)}, s16[64,256]{1,0:T(8,128)(2,1)S(1)}, u32[]{:S(2)}, u32[]{:S(2)}) collective-permute-start(s16[64,256]{1,0:T(8,128)(2,1)S(1)} %get-tuple-element.67), channel_id=1, source_target_pairs={{0,28},{4,24},{8,20},{12,16},{16,12},{20,8},{24,4},{28,0},{1,29},{... | collective-permute-start | bytes 98312 | tf_op jit(solution)/shard_map/ppermute | solution.py:77
  27.4 1.7 %collective-permute-start.14 = (s16[64,256]{1,0:T(8,128)(2,1)S(1)}, s16[64,256]{1,0:T(8,128)(2,1)S(1)}, u32[]{:S(2)}, u32[]{:S(2)}) collective-permute-start(s16[64,256]{1,0:T(8,128)(2,1)S(1)} %get-tuple-element.69), channel_id=1, source_target_pairs={{0,12},{4,8},{8,4},{12,0},{16,28},{20,24},{24,20},{28,16},{1,13},{... | collective-permute-start | bytes 98312 | tf_op jit(solution)/shard_map/ppermute | solution.py:77
  29.1 0.2 collective-permute-done.12.refs_4_
  29.3 1.7 %collective-permute-done.13.refs_5_ = s16[64,256]{1,0:T(8,128)(2,1)S(1)} collective-permute-done((s16[64,256]{1,0:T(8,128)(2,1)S(1)}, s16[64,256]{1,0:T(8,128)(2,1)S(1)}, u32[]{:S(2)}, u32[]{:S(2)}) %collective-permute-start.13) | collective-permute-done | bytes 32800 | tf_op jit(solution)/shard_map/ppermute | solution.py:77
  31.0 0.2 collective-permute-done.14.refs_6_
  31.2 0.1 broadcast_in_dim.2.order
  31.3 1.7 %join.1 = f32[512,256]{1,0:T(8,128)} custom-call(s32[8,128]{1,0:T(8,128)S(1)} %broadcast_in_dim.2.order, s16[64,256]{1,0:T(8,128)(2,1)S(1)} %get-tuple-element.63.refs_0_, s16[64,256]{1,0:T(8,128)(2,1)S(1)} %collective-permute-done.9.refs_1_, s16[64,256]{1,0:T(8,128)(2,1)S(1)} %collective-permute-done.10.refs_2_, ...), custom_call_target="tpu_custom_call" | custom-call | tf_op jit(solution)/shard_map/join/pallas_call | solution.py:608
  (18 shorter events, 0.0 us)
Async XLA Ops:
  0.0 0.9 %copy-start = (bf16[2,2,32,1024]{3,2,1,0:T(8,128)(2,1)S(1)}, bf16[2,2,32,1024]{3,2,1,0:T(8,128)(2,1)}, u32[]{:S(2)}) copy-start(bf16[2,2,32,1024]{3,2,1,0:T(8,128)(2,1)} %slc.1) | copy-start | bytes 786436
  1.3 6.3 %collective-permute-start = (bf16[144,128]{1,0:T(8,128)(2,1)S(1)}, bf16[144,128]{1,0:T(8,128)(2,1)S(1)}, u32[]{:S(2)}, u32[]{:S(2)}) collective-permute-start(bf16[144,128]{1,0:T(8,128)(2,1)S(1)} %get-tuple-element.39), channel_id=1, source_target_pairs={{0,24},{4,28},{8,16},{12,20},{16,8},{20,12},{24,0},{28,4},{1,25},{... | collective-permute-start | bytes 110600 | tf_op jit(solution)/shard_map/ppermute | solution.py:77
  3.5 4.8 %collective-permute-start.1 = (bf16[144,128]{1,0:T(8,128)(2,1)S(1)}, bf16[144,128]{1,0:T(8,128)(2,1)S(1)}, u32[]{:S(2)}, u32[]{:S(2)}) collective-permute-start(bf16[144,128]{1,0:T(8,128)(2,1)S(1)} %get-tuple-element.40), channel_id=1, source_target_pairs={{0,16},{4,20},{8,24},{12,28},{16,0},{20,4},{24,8},{28,12},{1,17},{... | collective-permute-start | bytes 110600 | tf_op jit(solution)/shard_map/ppermute | solution.py:77
  3.7 6.7 %collective-permute-start.2 = (bf16[144,128]{1,0:T(8,128)(2,1)S(1)}, bf16[144,128]{1,0:T(8,128)(2,1)S(1)}, u32[]{:S(2)}, u32[]{:S(2)}) collective-permute-start(bf16[144,128]{1,0:T(8,128)(2,1)S(1)} %get-tuple-element.41), channel_id=1, source_target_pairs={{0,8},{4,12},{8,0},{12,4},{16,24},{20,28},{24,16},{28,20},{1,9},{5... | collective-permute-start | bytes 110600 | tf_op jit(solution)/shard_map/ppermute | solution.py:77
  4.0 6.5 %collective-permute-start.3 = (bf16[144,128]{1,0:T(8,128)(2,1)S(1)}, bf16[144,128]{1,0:T(8,128)(2,1)S(1)}, u32[]{:S(2)}, u32[]{:S(2)}) collective-permute-start(bf16[144,128]{1,0:T(8,128)(2,1)S(1)} %get-tuple-element.42), channel_id=1, source_target_pairs={{0,28},{4,24},{8,20},{12,16},{16,12},{20,8},{24,4},{28,0},{1,29},{... | collective-permute-start | bytes 110600 | tf_op jit(solution)/shard_map/ppermute | solution.py:77
  7.6 3.7 %collective-permute-start.4 = (bf16[144,128]{1,0:T(8,128)(2,1)S(1)}, bf16[144,128]{1,0:T(8,128)(2,1)S(1)}, u32[]{:S(2)}, u32[]{:S(2)}) collective-permute-start(bf16[144,128]{1,0:T(8,128)(2,1)S(1)} %get-tuple-element.43), channel_id=1, source_target_pairs={{0,20},{4,16},{8,28},{12,24},{16,4},{20,0},{24,12},{28,8},{1,21},{... | collective-permute-start | bytes 110600 | tf_op jit(solution)/shard_map/ppermute | solution.py:77
  7.6 3.9 %collective-permute-start.5 = (bf16[144,128]{1,0:T(8,128)(2,1)S(1)}, bf16[144,128]{1,0:T(8,128)(2,1)S(1)}, u32[]{:S(2)}, u32[]{:S(2)}) collective-permute-start(bf16[144,128]{1,0:T(8,128)(2,1)S(1)} %get-tuple-element.44), channel_id=1, source_target_pairs={{0,12},{4,8},{8,4},{12,0},{16,28},{20,24},{24,20},{28,16},{1,13},{... | collective-permute-start | bytes 110600 | tf_op jit(solution)/shard_map/ppermute | solution.py:77
  8.3 3.2 %collective-permute-start.6 = (bf16[144,128]{1,0:T(8,128)(2,1)S(1)}, bf16[144,128]{1,0:T(8,128)(2,1)S(1)}, u32[]{:S(2)}, u32[]{:S(2)}) collective-permute-start(bf16[144,128]{1,0:T(8,128)(2,1)S(1)} %get-tuple-element.45), channel_id=1, source_target_pairs={{0,4},{4,0},{8,12},{12,8},{16,20},{20,16},{24,28},{28,24},{1,5},{5... | collective-permute-start | bytes 110600 | tf_op jit(solution)/shard_map/ppermute | solution.py:77
  8.4 0.7 %copy-start.2 = (s32[256]{0:T(256)S(1)}, s32[256]{0:T(256)}, u32[]{:S(2)}) copy-start(s32[256]{0:T(256)} %rg.3) | copy-start | bytes 3076
  9.2 0.7 %copy-start.3 = (s32[8]{0:T(128)S(1)}, s32[8]{0:T(128)}, u32[]{:S(2)}) copy-start(s32[8]{0:T(128)} %az.5) | copy-start | bytes 100
  11.7 4.6 %copy-start.1 = (s32[8]{0:T(128)S(1)}, s32[8]{0:T(128)}, u32[]{:S(2)}) copy-start(s32[8]{0:T(128)} %order.3) | copy-start | bytes 100
  11.7 7.6 %collective-permute-start.7 = (bf16[8,24,128]{2,1,0:T(8,128)(2,1)S(1)}, bf16[8,24,128]{2,1,0:T(8,128)(2,1)S(1)}, u32[]{:S(2)}, u32[]{:S(2)}) collective-permute-start(bf16[8,24,128]{2,1,0:T(8,128)(2,1)S(1)} %get-tuple-element.58), channel_id=1, source_target_pairs={{0,1},{2,3},{1,0},{3,2},{4,5},{6,7},{5,4},{7,6},{8,9},{10,11},{9,8... | collective-permute-start | bytes 147464 | tf_op jit(solution)/shard_map/ppermute | solution.py:567
  11.9 7.4 %collective-permute-start.8 = (bf16[8,24,128]{2,1,0:T(8,128)(2,1)S(1)}, bf16[8,24,128]{2,1,0:T(8,128)(2,1)S(1)}, u32[]{:S(2)}, u32[]{:S(2)}) collective-permute-start(bf16[8,24,128]{2,1,0:T(8,128)(2,1)S(1)} %get-tuple-element.59), channel_id=1, source_target_pairs={{1,2},{2,1},{5,6},{6,5},{9,10},{10,9},{13,14},{14,13},{17,18},{18,... | collective-permute-start | bytes 147464 | tf_op jit(solution)/shard_map/ppermute | solution.py:566
  21.7 5.6 %collective-permute-start.9 = (s16[64,256]{1,0:T(8,128)(2,1)S(1)}, s16[64,256]{1,0:T(8,128)(2,1)S(1)}, u32[]{:S(2)}, u32[]{:S(2)}) collective-permute-start(s16[64,256]{1,0:T(8,128)(2,1)S(1)} %get-tuple-element.64), channel_id=1, source_target_pairs={{0,24},{4,28},{8,16},{12,20},{16,8},{20,12},{24,0},{28,4},{1,25},{... | collective-permute-start | bytes 98312 | tf_op jit(solution)/shard_map/ppermute | solution.py:77
  23.0 6.0 %collective-permute-start.10 = (s16[64,256]{1,0:T(8,128)(2,1)S(1)}, s16[64,256]{1,0:T(8,128)(2,1)S(1)}, u32[]{:S(2)}, u32[]{:S(2)}) collective-permute-start(s16[64,256]{1,0:T(8,128)(2,1)S(1)} %get-tuple-element.65), channel_id=1, source_target_pairs={{0,16},{4,20},{8,24},{12,28},{16,0},{20,4},{24,8},{28,12},{1,17},{... | collective-permute-start | bytes 98312 | tf_op jit(solution)/shard_map/ppermute | solution.py:77
  23.2 5.9 %collective-permute-start.11 = (s16[64,256]{1,0:T(8,128)(2,1)S(1)}, s16[64,256]{1,0:T(8,128)(2,1)S(1)}, u32[]{:S(2)}, u32[]{:S(2)}) collective-permute-start(s16[64,256]{1,0:T(8,128)(2,1)S(1)} %get-tuple-element.66), channel_id=1, source_target_pairs={{0,8},{4,12},{8,0},{12,4},{16,24},{20,28},{24,16},{28,20},{1,9},{5... | collective-permute-start | bytes 98312 | tf_op jit(solution)/shard_map/ppermute | solution.py:77
  24.5 4.9 %collective-permute-start.12 = (s16[64,256]{1,0:T(8,128)(2,1)S(1)}, s16[64,256]{1,0:T(8,128)(2,1)S(1)}, u32[]{:S(2)}, u32[]{:S(2)}) collective-permute-start(s16[64,256]{1,0:T(8,128)(2,1)S(1)} %get-tuple-element.67), channel_id=1, source_target_pairs={{0,28},{4,24},{8,20},{12,16},{16,12},{20,8},{24,4},{28,0},{1,29},{... | collective-permute-start | bytes 98312 | tf_op jit(solution)/shard_map/ppermute | solution.py:77
  27.4 3.6 %collective-permute-start.13 = (s16[64,256]{1,0:T(8,128)(2,1)S(1)}, s16[64,256]{1,0:T(8,128)(2,1)S(1)}, u32[]{:S(2)}, u32[]{:S(2)}) collective-permute-start(s16[64,256]{1,0:T(8,128)(2,1)S(1)} %get-tuple-element.68), channel_id=1, source_target_pairs={{0,20},{4,16},{8,28},{12,24},{16,4},{20,0},{24,12},{28,8},{1,21},{... | collective-permute-start | bytes 98312 | tf_op jit(solution)/shard_map/ppermute | solution.py:77
  27.4 3.8 %collective-permute-start.14 = (s16[64,256]{1,0:T(8,128)(2,1)S(1)}, s16[64,256]{1,0:T(8,128)(2,1)S(1)}, u32[]{:S(2)}, u32[]{:S(2)}) collective-permute-start(s16[64,256]{1,0:T(8,128)(2,1)S(1)} %get-tuple-element.69), channel_id=1, source_target_pairs={{0,12},{4,8},{8,4},{12,0},{16,28},{20,24},{24,20},{28,16},{1,13},{... | collective-permute-start | bytes 98312 | tf_op jit(solution)/shard_map/ppermute | solution.py:77
  29.1 2.1 %collective-permute-start.15 = (s16[64,256]{1,0:T(8,128)(2,1)S(1)}, s16[64,256]{1,0:T(8,128)(2,1)S(1)}, u32[]{:S(2)}, u32[]{:S(2)}) collective-permute-start(s16[64,256]{1,0:T(8,128)(2,1)S(1)} %get-tuple-element.70), channel_id=1, source_target_pairs={{0,4},{4,0},{8,12},{12,8},{16,20},{20,16},{24,28},{28,24},{1,5},{5... | collective-permute-start | bytes 98312 | tf_op jit(solution)/shard_map/ppermute | solution.py:77

commit v12 on v11

--- a/solution.py
+++ b/solution.py
@@ -173,22 +173,25 @@
     return per * 2 * HALO + EDGE
 
 
-def gather_kernel(blocks, per, lines, *refs):
-    recv, (paired, other, stage) = refs[:blocks], refs[blocks:]
+def gather_rows(recv, group, per, lines, target, stage):
     me = lax.axis_index("date")
     tail = 2 * HALO - 8
-    for piece, k in zip(recv, partners(blocks)):
-        for group, target in enumerate((paired, other)):
-            edges = jnp.zeros((EDGE, LANES), jnp.float32)
-            for date in range(per):
-                at = (group * per + date) * GROUP
-                value = piece[at : at + GROUP].astype(jnp.float32)
-                stage[date * 8 : date * 8 + 8, :] = value[:8]
-                stage[per * 8 + date * tail : per * 8 + (date + 1) * tail, :] = value[8 : 2 * HALO]
-                mine = value[2 * HALO : 2 * HALO + EDGE]
-                edges += pltpu.roll(mine, date * lines, 1) if date else mine
-            stage[per * 2 * HALO :, :] = edges
-            target[me ^ k] = stage[...].astype(jnp.bfloat16)
+    for piece, k in zip(recv, partners(len(recv))):
+        edges = jnp.zeros((EDGE, LANES), jnp.float32)
+        for date in range(per):
+            at = (group * per + date) * GROUP
+            value = piece[at : at + GROUP].astype(jnp.float32)
+            stage[date * 8 : date * 8 + 8, :] = value[:8]
+            stage[per * 8 + date * tail : per * 8 + (date + 1) * tail, :] = value[8 : 2 * HALO]
+            mine = value[2 * HALO : 2 * HALO + EDGE]
+            edges += pltpu.roll(mine, date * lines, 1) if date else mine
+        stage[per * 2 * HALO :, :] = edges
+        target[me ^ k] = stage[...].astype(jnp.bfloat16)
+
+
+def gather_kernel(blocks, per, lines, *refs):
+    recv, (paired, stage) = refs[:blocks], refs[blocks:]
+    gather_rows(recv, 0, per, lines, paired, stage)
 
 
 def scatter_halo(source, block, lines, dates, per, target):
@@ -268,7 +271,7 @@
     return sums
 
 
-def all_dates(dates, group, places, rows, out_rows, az, edges, turned, edge_on, store, finish):
+def half_of_dates(late_half, dates, group, places, rows, out_rows, az, edges, turned, edge_on, store, finish):
     half = dates // 2
     group = min(group, half)
 
@@ -289,14 +292,13 @@
         for tile in range(half // 8):
             real, imag = sums_of(half + first_date + step, half + tile * 8, 8)
             both = [jnp.concatenate([re, im], axis=0) for re, im in zip(real, imag)]
-            store((dates + first_date) * dates, step * dates + tile * 16, both)
+            store(first_date * dates, step * dates + tile * 16, both)
         return carry
 
-    for body, width in ((early, 2 * dates), (late, dates)):
-        for first_date in range(0, half, group):
-            lax.fori_loop(0, group, functools.partial(body, first_date), 0)
-            start = first_date * width + (half * 2 * dates if body is late else 0)
-            finish(start, group * width)
+    body, width = (late, dates) if late_half else (early, 2 * dates)
+    for first_date in range(0, half, group):
+        lax.fori_loop(0, group, functools.partial(body, first_date), 0)
+        finish(first_date * width, group * width)
 
 
 def turn_edges(edges, turned, dates):
@@ -313,20 +315,8 @@
     return first <= 0, first <= 1, last >= 2, last >= 3
 
 
-def inner_kernel(blocks, per, lines, chunk, group, order, az, rg, weights, *refs):
-    recv, (found, partial, own_edges, x, turned, left) = refs[:blocks], refs[blocks:]
+def own_sums(late_half, blocks, per, lines, chunk, group, az, rg, weights, x, found, partial, turned, left):
     dates = blocks * per
-    date_rows = rows_of_date(lines)
-    edge_rows = per * GROUP
-    me = lax.axis_index("date")
-    swap = 1 - lax.axis_index("strip") % 2
-    rest = date_rows - 2 * GROUP
-    for piece, k in zip(recv, partners(blocks)):
-        block = order[me ^ k]
-        to_sublanes(piece, swap * edge_rows, GROUP, GROUP, block, dates, per, x)
-        to_sublanes(piece, (1 - swap) * edge_rows, GROUP, GROUP, block, dates, per, x.at[GROUP * dates :])
-        to_sublanes(piece, 2 * edge_rows, rest, rest, block, dates, per, x.at[2 * GROUP * dates :])
-    own_edges[...] = x[2 * HALO * dates : (2 * HALO + EDGE) * dates, :]
     out_rows = lines // STEP
     inner, outer = kinds_of_rows(out_rows)
     edges = x.at[2 * HALO * dates : (2 * HALO + EDGE) * dates]
@@ -348,11 +338,32 @@
         found[start : start + count, :] = jnp.dot(left[:count, :], weights[...], preferred_element_type=jnp.float32)
 
     edge_on = edges_in_use(rg, chunk // STEP)
-    all_dates(dates, group, places, rows, out_rows, az, edges, turned, edge_on, store, finish)
+    half_of_dates(late_half, dates, group, places, rows, out_rows, az, edges, turned, edge_on, store, finish)
+
+
+def late_kernel(blocks, per, lines, chunk, group, order, az, rg, weights, *refs):
+    recv, (x, other, found, partial, stage, turned, left) = refs[:blocks], refs[blocks:]
+    dates = blocks * per
+    date_rows = rows_of_date(lines)
+    edge_rows = per * GROUP
+    me = lax.axis_index("date")
+    swap = 1 - lax.axis_index("strip") % 2
+    rest = date_rows - 2 * GROUP
+    gather_rows(recv, 1, per, lines, other, stage)
+    for piece, k in zip(recv, partners(blocks)):
+        block = order[me ^ k]
+        to_sublanes(piece, swap * edge_rows, GROUP, GROUP, block, dates, per, x)
+        to_sublanes(piece, (1 - swap) * edge_rows, GROUP, GROUP, block, dates, per, x.at[GROUP * dates :])
+        to_sublanes(piece, 2 * edge_rows, rest, rest, block, dates, per, x.at[2 * GROUP * dates :])
+    own_sums(True, blocks, per, lines, chunk, group, az, rg, weights, x, found, partial, turned, left)
+
+
+def early_kernel(blocks, per, lines, chunk, group, az, rg, weights, x, found, partial, turned, left):
+    own_sums(False, blocks, per, lines, chunk, group, az, rg, weights, x, found, partial, turned, left)
 
 
 def outer_kernel(
-    blocks, per, lines, chunk, group, own_edges, paired, other, partial, found, order, az, rg, weights, *refs
+    blocks, per, lines, chunk, group, x, paired, other, early, late, early_found, late_found, order, az, rg, weights, *refs
 ):
     pieces, (send, sums, halo, edges, turned, left, power) = refs[:blocks], refs[blocks:]
     dates = blocks * per
@@ -375,29 +386,31 @@
         at = (2 * HALO + k) * dates
         lower_part = pltpu.roll(below[at : at + dates, :], lines, 1)
         upper_part = pltpu.roll(above[at : at + dates, :], lines, 1)
-        mine = own_edges[k * dates : (k + 1) * dates, :]
-        value = jnp.where(turn < lines, mine, jnp.where(turn < lines + HALO, upper_part, lower_part))
+        value = jnp.where(turn < lines, x[at : at + dates, :], jnp.where(turn < lines + HALO, upper_part, lower_part))
         edges[k * dates : (k + 1) * dates, :] = value
     turn_edges(edges, turned, dates)
     places = [[(below, part * HALO + line) for part in range(2)] for line in range(HALO)]
     places += [None] * lines
     places += [[(above, part * HALO + line) for part in range(2)] for line in range(HALO)]
 
-    def store(base, start, totals):
-        at_rows = pl.ds(pl.multiple_of(start, 16), 16)
-        whole = pl.ds(pl.multiple_of(base + start, 16), 16)
-        for slot, total in enumerate(totals):
-            if slot < len(outer):
-                total += partial[whole, slot * LANES : (slot + 1) * LANES]
-            store_split(left, at_rows, 2 * slot * LANES, total)
-
-    def finish(start, count):
-        rows = slice(start, start + count)
-        sums[rows, split_at:] = jnp.dot(left[:count, :], weights[...], preferred_element_type=jnp.float32)
-
-    sums[:, :split_at] = found[...]
     edge_on = edges_in_use(rg, cols)
-    all_dates(dates, group, places, outer, out_rows, az, edges, turned, edge_on, store, finish)
+    for late_half, partial, found in ((False, early, early_found), (True, late, late_found)):
+        offset = dates * dates * late_half
+
+        def store(base, start, totals):
+            at_rows = pl.ds(pl.multiple_of(start, 16), 16)
+            whole = pl.ds(pl.multiple_of(base + start, 16), 16)
+            for slot, total in enumerate(totals):
+                if slot < len(outer):
+                    total += partial[whole, slot * LANES : (slot + 1) * LANES]
+                store_split(left, at_rows, 2 * slot * LANES, total)
+
+        def finish(start, count):
+            rows = slice(offset + start, offset + start + count)
+            sums[rows, :split_at] = found[start : start + count, :]
+            sums[rows, split_at:] = jnp.dot(left[:count, :], weights[...], preferred_element_type=jnp.float32)
+
+        half_of_dates(late_half, dates, group, places, outer, out_rows, az, edges, turned, edge_on, store, finish)
 
     def row_at(date, part, later):
         if date < half:
@@ -549,11 +562,11 @@
     recv, weights = lax.optimization_barrier((recv, weights))
 
     edge = jax.ShapeDtypeStruct((blocks, halo_rows(per), LANES), jnp.bfloat16)
-    to_pair, to_other = pl.pallas_call(
+    to_pair = pl.pallas_call(
         functools.partial(gather_kernel, blocks, per, lines),
-        out_shape=[edge] * 2,
+        out_shape=edge,
         in_specs=[VMEM] * blocks,
-        out_specs=[VMEM] * 2,
+        out_specs=VMEM,
         scratch_shapes=[pltpu.VMEM((halo_rows(per), LANES), jnp.float32)],
         compiler_params=PARAMS,
         name="gather",
@@ -563,32 +576,47 @@
         pairs = [(i, i + 1) for i in range(first, strips - 1, 2)]
         return pairs + [(target, source) for source, target in pairs]
 
-    other = lax.ppermute(to_other, "strip", swaps(1))
     paired = lax.ppermute(to_pair, "strip", swaps(0))
-    count = dates * dates * 3 // 2
     half_group = min(group, dates // 2)
-    found, partial, own_edges = pl.pallas_call(
-        functools.partial(inner_kernel, blocks, per, lines, chunk, group),
-        out_shape=[
+
+    def sums_of(count):
+        return [
             jax.ShapeDtypeStruct((count, len(kinds[0]) * cols), jnp.float32),
             jax.ShapeDtypeStruct((count, len(kinds[1]) * LANES), jnp.float32),
-            jax.ShapeDtypeStruct((EDGE * dates, LANES), jnp.float32),
-        ],
+        ]
+
+    def scratch(width):
+        return [
+            pltpu.VMEM((EDGE * dates, LANES), jnp.float32),
+            pltpu.VMEM((half_group * width * dates, depths[0]), jnp.bfloat16),
+        ]
+
+    x, to_other, late_found, late = pl.pallas_call(
+        functools.partial(late_kernel, blocks, per, lines, chunk, group),
+        out_shape=[jax.ShapeDtypeStruct((date_rows * dates, LANES), jnp.float32), edge] + sums_of(dates * dates // 2),
         in_specs=[SMEM] * 3 + [VMEM] * (1 + blocks),
-        out_specs=[VMEM] * 3,
-        scratch_shapes=[
-            pltpu.VMEM((date_rows * dates, LANES), jnp.float32),
-            pltpu.VMEM((EDGE * dates, LANES), jnp.float32),
-            pltpu.VMEM((half_group * 2 * dates, depths[0]), jnp.bfloat16),
-        ],
+        out_specs=[VMEM] * 4,
+        scratch_shapes=[pltpu.VMEM((halo_rows(per), LANES), jnp.float32)] + scratch(1),
         compiler_params=PARAMS,
-        cost_estimate=pl.CostEstimate(flops=0, bytes_accessed=12 * 1024 * 1024, transcendentals=0),
-        name="inner",
+        cost_estimate=pl.CostEstimate(flops=0, bytes_accessed=6 * 1024 * 1024, transcendentals=0),
+        name="late",
     )(block_order, az_offset, rg_offset, weights[0], *recv)
+    other = lax.ppermute(to_other, "strip", swaps(1))
+    early_found, early = pl.pallas_call(
+        functools.partial(early_kernel, blocks, per, lines, chunk, group),
+        out_shape=sums_of(dates * dates),
+        in_specs=[SMEM] * 2 + [VMEM] * 2,
+        out_specs=[VMEM] * 2,
+        scratch_shapes=scratch(2),
+        compiler_params=PARAMS,
+        cost_estimate=pl.CostEstimate(flops=0, bytes_accessed=8 * 1024 * 1024, transcendentals=0),
+        name="early",
+    )(az_offset, rg_offset, weights[0], x)
+    count = dates * dates * 3 // 2
     pairs = pl.pallas_call(
         functools.partial(outer_kernel, blocks, per, lines, chunk, group),
         out_shape=[jax.ShapeDtypeStruct((2 * per * dates, wide), jnp.int16)] * blocks,
-        in_specs=[VMEM] * 5 + [SMEM] * 3 + [VMEM],
+        in_specs=[VMEM] * 7 + [SMEM] * 3 + [VMEM],
         out_specs=[VMEM] * blocks,
         scratch_shapes=[
             pltpu.VMEM((dates * 2 * dates, wide), jnp.int16),
@@ -601,7 +629,7 @@
         ],
         compiler_params=PARAMS,
         name="outer",
-    )(own_edges, paired, other, partial, found, block_order, az_offset, rg_offset, weights[1])
+    )(x, paired, other, early, late, early_found, late_found, block_order, az_offset, rg_offset, weights[1])
     count = 2 * per * dates
     back = swap_blocks(pairs)
     if LANES % cols == 0 and out_rows * cols % LANES == 0 and blocks * cols % LANES == 0:

time: 33.1 us -> 34.2 us (1.033); the launches traced: 32.9 us -> 33.6 us
  Pallas kernels: 8.26 us -> 8.9 us
    pallas_call x1 -> x2, Pallas kernels: 3.06 us -> 3.75 us  [the longest x1 2.05 us: on_device(): pl.pallas_call(functools.partial(early_kernel, blocks, per, lines, chunk,...]
  transfers between devices with their start and end apart: 16 -> 16, of which waited for: 5 -> 5; matrix products, arithmetic and copies ran while one was open for 0% -> 0% of each run, Pallas kernels for 11% -> 13%
where the time goes in v12:
time: 34.2 us; the launch traced here: 33.6 us
  starting transfers between devices  18.7 us (55%)
  Pallas kernels  8.9 us (26%)
  waiting for transfers between devices  3.14 us (9%)
  local copies, waits for them, and re-layouts  2.73 us (8%)
    ppermute x14, starting transfers between devices, swap_blocks(): lax.ppermute(pieces[at], 'date', [(i, i ^ k) for i in range(blocks)])  14.5 us
    ppermute x1, starting transfers between devices, on_device(): other = lax.ppermute(to_other, 'strip', swaps(1))  4.03 us
    ppermute x14, waiting for transfers between devices, swap_blocks(): lax.ppermute(pieces[at], 'date', [(i, i ^ k) for i in range(blocks)])  3.14 us
    unnamed x8, local copies, waits for them, and re-layouts  2.51 us
    pallas_call x1, Pallas kernels, on_device(): pl.pallas_call(functools.partial(outer_kernel, blocks, per, lines, chunk,...  2.4 us
    pallas_call x1, Pallas kernels, on_device(): pl.pallas_call(functools.partial(early_kernel, blocks, per, lines, chunk,...  2.05 us
    pallas_call x1, Pallas kernels, on_device(): pl.pallas_call(functools.partial(late_kernel, blocks, per, lines, chunk,...  1.69 us
    pallas_call x1, Pallas kernels, on_device(): pl.pallas_call(functools.partial(join_kernel, blocks, per, out_rows, cols...  1.69 us
  transfers between devices with their start and end apart: 16, of which 5 were waited for; matrix products, arithmetic and copies ran while one was open for 0% of the time, Pallas kernels for 13%

profile of v12, /device:TPU:9, one launch (start us, length us, event | category | flops | bytes accessed | tf_op | source)
XLA Modules:
  0.0 33.6 jit_solution(6763666279111221315)
XLA Ops:
  0.0 0.9 %copy-done = bf16[2,2,32,1024]{3,2,1,0:T(8,128)(2,1)S(1)} copy-done((bf16[2,2,32,1024]{3,2,1,0:T(8,128)(2,1)S(1)}, bf16[2,2,32,1024]{3,2,1,0:T(8,128)(2,1)}, u32[]{:S(2)}) %copy-start) | copy-done | bytes 262168
  1.0 0.3 pack.1
  1.3 2.2 %collective-permute-start = (bf16[144,128]{1,0:T(8,128)(2,1)S(1)}, bf16[144,128]{1,0:T(8,128)(2,1)S(1)}, u32[]{:S(2)}, u32[]{:S(2)}) collective-permute-start(bf16[144,128]{1,0:T(8,128)(2,1)S(1)} %get-tuple-element.40), channel_id=1, source_target_pairs={{0,24},{4,28},{8,16},{12,20},{16,8},{20,12},{24,0},{28,4},{1,25},{... | collective-permute-start | bytes 110600 | tf_op jit(solution)/shard_map/ppermute | solution.py:77
  3.5 0.2 collective-permute-start.1
  3.7 0.3 collective-permute-start.2
  4.0 3.6 %collective-permute-start.3 = (bf16[144,128]{1,0:T(8,128)(2,1)S(1)}, bf16[144,128]{1,0:T(8,128)(2,1)S(1)}, u32[]{:S(2)}, u32[]{:S(2)}) collective-permute-start(bf16[144,128]{1,0:T(8,128)(2,1)S(1)} %get-tuple-element.43), channel_id=1, source_target_pairs={{0,28},{4,24},{8,20},{12,16},{16,12},{20,8},{24,4},{28,0},{1,29},{... | collective-permute-start | bytes 110600 | tf_op jit(solution)/shard_map/ppermute | solution.py:77
  7.6 0.8 %collective-permute-start.5 = (bf16[144,128]{1,0:T(8,128)(2,1)S(1)}, bf16[144,128]{1,0:T(8,128)(2,1)S(1)}, u32[]{:S(2)}, u32[]{:S(2)}) collective-permute-start(bf16[144,128]{1,0:T(8,128)(2,1)S(1)} %get-tuple-element.45), channel_id=1, source_target_pairs={{0,12},{4,8},{8,4},{12,0},{16,28},{20,24},{24,20},{28,16},{1,13},{... | collective-permute-start | bytes 110600 | tf_op jit(solution)/shard_map/ppermute | solution.py:77
  8.3 0.1 collective-permute-start.6
  8.4 0.7 %copy-done.1 = s32[256]{0:T(256)S(1)} copy-done((s32[256]{0:T(256)S(1)}, s32[256]{0:T(256)}, u32[]{:S(2)}) %copy-start.1) | copy-done | bytes 1048
  9.1 0.1 dynamic_slice.3
  9.2 0.1 broadcast_in_dim_tile.3.tiled
  9.3 0.6 %copy-done.2 = s32[8]{0:T(128)S(1)} copy-done((s32[8]{0:T(128)S(1)}, s32[8]{0:T(128)}, u32[]{:S(2)}) %copy-start.2) | copy-done | bytes 56
  9.8 0.6 %weights.1 = (bf16[1536,128]{1,0:T(8,128)(2,1)S(1)}, bf16[1536,128]{1,0:T(8,128)(2,1)S(1)}) custom-call(s32[8]{0:T(128)S(1)} %copy-done.2, s32[1,256]{1,0:T(1,128)S(1)} %broadcast_in_dim_tile.3.tiled), custom_call_target="tpu_custom_call" | custom-call | bytes 4194304 | tf_op jit(solution)/shard_map/weights/pallas_call | solution.py:551
  10.5 0.7 %collective-permute-done.4.refs_5_ = bf16[144,128]{1,0:T(8,128)(2,1)S(1)} collective-permute-done((bf16[144,128]{1,0:T(8,128)(2,1)S(1)}, bf16[144,128]{1,0:T(8,128)(2,1)S(1)}, u32[]{:S(2)}, u32[]{:S(2)}) %collective-permute-start.4) | collective-permute-done | bytes 36896 | tf_op jit(solution)/shard_map/ppermute | solution.py:77
  11.2 0.3 collective-permute-done.5.refs_6_
  11.5 0.1 gather.1
  11.6 0.2 collective-permute-start.7
  11.8 0.3 copy-done.3
  12.1 1.7 %late.1 = (f32[1152,128]{1,0:T(8,128)S(1)}, bf16[8,24,128]{2,1,0:T(8,128)(2,1)S(1)}, f32[128,128]{1,0:T(8,128)S(1)}, f32[128,512]{1,0:T(8,128)S(1)}) custom-call(s32[8]{0:T(128)S(1)} %copy-done.3, s32[8]{0:T(128)S(1)} %copy-done.2, s32[256]{0:T(256)S(1)} %copy-done.1, bf16[1536,128]{1,0:T(8,128)(2,1)S(1)} %get-tuple-element.49.weights, ...), custom_call_target="tpu_custom_call" | custom-call | bytes 6291456 | tf_op jit(solution)/shard_map/late/pallas_call | solution.py:594
  13.8 4.0 %collective-permute-start.8 = (bf16[8,24,128]{2,1,0:T(8,128)(2,1)S(1)}, bf16[8,24,128]{2,1,0:T(8,128)(2,1)S(1)}, u32[]{:S(2)}, u32[]{:S(2)}) collective-permute-start(bf16[8,24,128]{2,1,0:T(8,128)(2,1)S(1)} %get-tuple-element.59), channel_id=1, source_target_pairs={{1,2},{2,1},{5,6},{6,5},{9,10},{10,9},{13,14},{14,13},{17,18},{18,... | collective-permute-start | bytes 147464 | tf_op jit(solution)/shard_map/ppermute | solution.py:604
  17.9 2.1 %early.1 = (f32[256,128]{1,0:T(8,128)S(1)}, f32[256,512]{1,0:T(8,128)S(1)}) custom-call(s32[8]{0:T(128)S(1)} %copy-done.2, s32[256]{0:T(256)S(1)} %copy-done.1, bf16[1536,128]{1,0:T(8,128)(2,1)S(1)} %get-tuple-element.49.weights, f32[1152,128]{1,0:T(8,128)S(1)} %get-tuple-element.58.x), custom_call_target="tpu_custom_call" | custom-call | bytes 8388608 | tf_op jit(solution)/shard_map/early/pallas_call | solution.py:605
  20.0 2.4 %outer.1 = (s16[64,256]{1,0:T(8,128)(2,1)S(1)}, s16[64,256]{1,0:T(8,128)(2,1)S(1)}, s16[64,256]{1,0:T(8,128)(2,1)S(1)}, s16[64,256]{1,0:T(8,128)(2,1)S(1)}, s16[...) custom-call(f32[1152,128]{1,0:T(8,128)S(1)} %get-tuple-element.58.x,, ...), custom_call_target="tpu_custom_call" | custom-call | tf_op jit(solution)/shard_map/outer/pallas_call | solution.py:616
  22.4 1.3 %collective-permute-start.9 = (s16[64,256]{1,0:T(8,128)(2,1)S(1)}, s16[64,256]{1,0:T(8,128)(2,1)S(1)}, u32[]{:S(2)}, u32[]{:S(2)}) collective-permute-start(s16[64,256]{1,0:T(8,128)(2,1)S(1)} %get-tuple-element.66), channel_id=1, source_target_pairs={{0,24},{4,28},{8,16},{12,20},{16,8},{20,12},{24,0},{28,4},{1,25},{... | collective-permute-start | bytes 98312 | tf_op jit(solution)/shard_map/ppermute | solution.py:77
  23.7 0.2 collective-permute-start.10
  23.9 1.2 %collective-permute-start.11 = (s16[64,256]{1,0:T(8,128)(2,1)S(1)}, s16[64,256]{1,0:T(8,128)(2,1)S(1)}, u32[]{:S(2)}, u32[]{:S(2)}) collective-permute-start(s16[64,256]{1,0:T(8,128)(2,1)S(1)} %get-tuple-element.68), channel_id=1, source_target_pairs={{0,8},{4,12},{8,0},{12,4},{16,24},{20,28},{24,16},{28,20},{1,9},{5... | collective-permute-start | bytes 98312 | tf_op jit(solution)/shard_map/ppermute | solution.py:77
  25.1 2.9 %collective-permute-start.12 = (s16[64,256]{1,0:T(8,128)(2,1)S(1)}, s16[64,256]{1,0:T(8,128)(2,1)S(1)}, u32[]{:S(2)}, u32[]{:S(2)}) collective-permute-start(s16[64,256]{1,0:T(8,128)(2,1)S(1)} %get-tuple-element.69), channel_id=1, source_target_pairs={{0,28},{4,24},{8,20},{12,16},{16,12},{20,8},{24,4},{28,0},{1,29},{... | collective-permute-start | bytes 98312 | tf_op jit(solution)/shard_map/ppermute | solution.py:77
  28.0 1.7 %collective-permute-start.14 = (s16[64,256]{1,0:T(8,128)(2,1)S(1)}, s16[64,256]{1,0:T(8,128)(2,1)S(1)}, u32[]{:S(2)}, u32[]{:S(2)}) collective-permute-start(s16[64,256]{1,0:T(8,128)(2,1)S(1)} %get-tuple-element.71), channel_id=1, source_target_pairs={{0,12},{4,8},{8,4},{12,0},{16,28},{20,24},{24,20},{28,16},{1,13},{... | collective-permute-start | bytes 98312 | tf_op jit(solution)/shard_map/ppermute | solution.py:77
  29.7 0.2 collective-permute-done.12.refs_4_
  30.0 1.7 %collective-permute-done.13.refs_5_ = s16[64,256]{1,0:T(8,128)(2,1)S(1)} collective-permute-done((s16[64,256]{1,0:T(8,128)(2,1)S(1)}, s16[64,256]{1,0:T(8,128)(2,1)S(1)}, u32[]{:S(2)}, u32[]{:S(2)}) %collective-permute-start.13) | collective-permute-done | bytes 32800 | tf_op jit(solution)/shard_map/ppermute | solution.py:77
  31.6 0.2 collective-permute-done.14.refs_6_
  31.8 0.1 broadcast_in_dim.2.order
  31.9 1.7 %join.1 = f32[512,256]{1,0:T(8,128)} custom-call(s32[8,128]{1,0:T(8,128)S(1)} %broadcast_in_dim.2.order, s16[64,256]{1,0:T(8,128)(2,1)S(1)} %get-tuple-element.65.refs_0_, s16[64,256]{1,0:T(8,128)(2,1)S(1)} %collective-permute-done.9.refs_1_, s16[64,256]{1,0:T(8,128)(2,1)S(1)} %collective-permute-done.10.refs_2_, ...), custom_call_target="tpu_custom_call" | custom-call | tf_op jit(solution)/shard_map/join/pallas_call | solution.py:636
  (19 shorter events, 0.0 us)
Async XLA Ops:
  0.0 0.9 %copy-start = (bf16[2,2,32,1024]{3,2,1,0:T(8,128)(2,1)S(1)}, bf16[2,2,32,1024]{3,2,1,0:T(8,128)(2,1)}, u32[]{:S(2)}) copy-start(bf16[2,2,32,1024]{3,2,1,0:T(8,128)(2,1)} %slc.1) | copy-start | bytes 786436
  1.3 6.3 %collective-permute-start = (bf16[144,128]{1,0:T(8,128)(2,1)S(1)}, bf16[144,128]{1,0:T(8,128)(2,1)S(1)}, u32[]{:S(2)}, u32[]{:S(2)}) collective-permute-start(bf16[144,128]{1,0:T(8,128)(2,1)S(1)} %get-tuple-element.40), channel_id=1, source_target_pairs={{0,24},{4,28},{8,16},{12,20},{16,8},{20,12},{24,0},{28,4},{1,25},{... | collective-permute-start | bytes 110600 | tf_op jit(solution)/shard_map/ppermute | solution.py:77
  3.5 4.8 %collective-permute-start.1 = (bf16[144,128]{1,0:T(8,128)(2,1)S(1)}, bf16[144,128]{1,0:T(8,128)(2,1)S(1)}, u32[]{:S(2)}, u32[]{:S(2)}) collective-permute-start(bf16[144,128]{1,0:T(8,128)(2,1)S(1)} %get-tuple-element.41), channel_id=1, source_target_pairs={{0,16},{4,20},{8,24},{12,28},{16,0},{20,4},{24,8},{28,12},{1,17},{... | collective-permute-start | bytes 110600 | tf_op jit(solution)/shard_map/ppermute | solution.py:77
  3.7 6.7 %collective-permute-start.2 = (bf16[144,128]{1,0:T(8,128)(2,1)S(1)}, bf16[144,128]{1,0:T(8,128)(2,1)S(1)}, u32[]{:S(2)}, u32[]{:S(2)}) collective-permute-start(bf16[144,128]{1,0:T(8,128)(2,1)S(1)} %get-tuple-element.42), channel_id=1, source_target_pairs={{0,8},{4,12},{8,0},{12,4},{16,24},{20,28},{24,16},{28,20},{1,9},{5... | collective-permute-start | bytes 110600 | tf_op jit(solution)/shard_map/ppermute | solution.py:77
  4.0 6.5 %collective-permute-start.3 = (bf16[144,128]{1,0:T(8,128)(2,1)S(1)}, bf16[144,128]{1,0:T(8,128)(2,1)S(1)}, u32[]{:S(2)}, u32[]{:S(2)}) collective-permute-start(bf16[144,128]{1,0:T(8,128)(2,1)S(1)} %get-tuple-element.43), channel_id=1, source_target_pairs={{0,28},{4,24},{8,20},{12,16},{16,12},{20,8},{24,4},{28,0},{1,29},{... | collective-permute-start | bytes 110600 | tf_op jit(solution)/shard_map/ppermute | solution.py:77
  7.6 3.7 %collective-permute-start.4 = (bf16[144,128]{1,0:T(8,128)(2,1)S(1)}, bf16[144,128]{1,0:T(8,128)(2,1)S(1)}, u32[]{:S(2)}, u32[]{:S(2)}) collective-permute-start(bf16[144,128]{1,0:T(8,128)(2,1)S(1)} %get-tuple-element.44), channel_id=1, source_target_pairs={{0,20},{4,16},{8,28},{12,24},{16,4},{20,0},{24,12},{28,8},{1,21},{... | collective-permute-start | bytes 110600 | tf_op jit(solution)/shard_map/ppermute | solution.py:77
  7.6 3.9 %collective-permute-start.5 = (bf16[144,128]{1,0:T(8,128)(2,1)S(1)}, bf16[144,128]{1,0:T(8,128)(2,1)S(1)}, u32[]{:S(2)}, u32[]{:S(2)}) collective-permute-start(bf16[144,128]{1,0:T(8,128)(2,1)S(1)} %get-tuple-element.45), channel_id=1, source_target_pairs={{0,12},{4,8},{8,4},{12,0},{16,28},{20,24},{24,20},{28,16},{1,13},{... | collective-permute-start | bytes 110600 | tf_op jit(solution)/shard_map/ppermute | solution.py:77
  8.3 3.2 %collective-permute-start.6 = (bf16[144,128]{1,0:T(8,128)(2,1)S(1)}, bf16[144,128]{1,0:T(8,128)(2,1)S(1)}, u32[]{:S(2)}, u32[]{:S(2)}) collective-permute-start(bf16[144,128]{1,0:T(8,128)(2,1)S(1)} %get-tuple-element.46), channel_id=1, source_target_pairs={{0,4},{4,0},{8,12},{12,8},{16,20},{20,16},{24,28},{28,24},{1,5},{5... | collective-permute-start | bytes 110600 | tf_op jit(solution)/shard_map/ppermute | solution.py:77
  8.4 0.7 %copy-start.1 = (s32[256]{0:T(256)S(1)}, s32[256]{0:T(256)}, u32[]{:S(2)}) copy-start(s32[256]{0:T(256)} %rg.5) | copy-start | bytes 3076
  9.2 0.7 %copy-start.2 = (s32[8]{0:T(128)S(1)}, s32[8]{0:T(128)}, u32[]{:S(2)}) copy-start(s32[8]{0:T(128)} %az.7) | copy-start | bytes 100
  11.5 0.7 %copy-start.3 = (s32[8]{0:T(128)S(1)}, s32[8]{0:T(128)}, u32[]{:S(2)}) copy-start(s32[8]{0:T(128)} %order.3) | copy-start | bytes 100
  11.6 8.3 %collective-permute-start.7 = (bf16[8,24,128]{2,1,0:T(8,128)(2,1)S(1)}, bf16[8,24,128]{2,1,0:T(8,128)(2,1)S(1)}, u32[]{:S(2)}, u32[]{:S(2)}) collective-permute-start(bf16[8,24,128]{2,1,0:T(8,128)(2,1)S(1)} %gather.1), channel_id=1, source_target_pairs={{0,1},{2,3},{1,0},{3,2},{4,5},{6,7},{5,4},{7,6},{8,9},{10,11},{9,8... | collective-permute-start | bytes 147464 | tf_op jit(solution)/shard_map/ppermute | solution.py:579
  13.8 6.1 %collective-permute-start.8 = (bf16[8,24,128]{2,1,0:T(8,128)(2,1)S(1)}, bf16[8,24,128]{2,1,0:T(8,128)(2,1)S(1)}, u32[]{:S(2)}, u32[]{:S(2)}) collective-permute-start(bf16[8,24,128]{2,1,0:T(8,128)(2,1)S(1)} %get-tuple-element.59), channel_id=1, source_target_pairs={{1,2},{2,1},{5,6},{6,5},{9,10},{10,9},{13,14},{14,13},{17,18},{18,... | collective-permute-start | bytes 147464 | tf_op jit(solution)/shard_map/ppermute | solution.py:604
  22.4 5.6 %collective-permute-start.9 = (s16[64,256]{1,0:T(8,128)(2,1)S(1)}, s16[64,256]{1,0:T(8,128)(2,1)S(1)}, u32[]{:S(2)}, u32[]{:S(2)}) collective-permute-start(s16[64,256]{1,0:T(8,128)(2,1)S(1)} %get-tuple-element.66), channel_id=1, source_target_pairs={{0,24},{4,28},{8,16},{12,20},{16,8},{20,12},{24,0},{28,4},{1,25},{... | collective-permute-start | bytes 98312 | tf_op jit(solution)/shard_map/ppermute | solution.py:77
  23.7 6.0 %collective-permute-start.10 = (s16[64,256]{1,0:T(8,128)(2,1)S(1)}, s16[64,256]{1,0:T(8,128)(2,1)S(1)}, u32[]{:S(2)}, u32[]{:S(2)}) collective-permute-start(s16[64,256]{1,0:T(8,128)(2,1)S(1)} %get-tuple-element.67), channel_id=1, source_target_pairs={{0,16},{4,20},{8,24},{12,28},{16,0},{20,4},{24,8},{28,12},{1,17},{... | collective-permute-start | bytes 98312 | tf_op jit(solution)/shard_map/ppermute | solution.py:77
  23.9 5.9 %collective-permute-start.11 = (s16[64,256]{1,0:T(8,128)(2,1)S(1)}, s16[64,256]{1,0:T(8,128)(2,1)S(1)}, u32[]{:S(2)}, u32[]{:S(2)}) collective-permute-start(s16[64,256]{1,0:T(8,128)(2,1)S(1)} %get-tuple-element.68), channel_id=1, source_target_pairs={{0,8},{4,12},{8,0},{12,4},{16,24},{20,28},{24,16},{28,20},{1,9},{5... | collective-permute-start | bytes 98312 | tf_op jit(solution)/shard_map/ppermute | solution.py:77
  25.1 4.9 %collective-permute-start.12 = (s16[64,256]{1,0:T(8,128)(2,1)S(1)}, s16[64,256]{1,0:T(8,128)(2,1)S(1)}, u32[]{:S(2)}, u32[]{:S(2)}) collective-permute-start(s16[64,256]{1,0:T(8,128)(2,1)S(1)} %get-tuple-element.69), channel_id=1, source_target_pairs={{0,28},{4,24},{8,20},{12,16},{16,12},{20,8},{24,4},{28,0},{1,29},{... | collective-permute-start | bytes 98312 | tf_op jit(solution)/shard_map/ppermute | solution.py:77
  28.0 3.6 %collective-permute-start.13 = (s16[64,256]{1,0:T(8,128)(2,1)S(1)}, s16[64,256]{1,0:T(8,128)(2,1)S(1)}, u32[]{:S(2)}, u32[]{:S(2)}) collective-permute-start(s16[64,256]{1,0:T(8,128)(2,1)S(1)} %get-tuple-element.70), channel_id=1, source_target_pairs={{0,20},{4,16},{8,28},{12,24},{16,4},{20,0},{24,12},{28,8},{1,21},{... | collective-permute-start | bytes 98312 | tf_op jit(solution)/shard_map/ppermute | solution.py:77
  28.0 3.8 %collective-permute-start.14 = (s16[64,256]{1,0:T(8,128)(2,1)S(1)}, s16[64,256]{1,0:T(8,128)(2,1)S(1)}, u32[]{:S(2)}, u32[]{:S(2)}) collective-permute-start(s16[64,256]{1,0:T(8,128)(2,1)S(1)} %get-tuple-element.71), channel_id=1, source_target_pairs={{0,12},{4,8},{8,4},{12,0},{16,28},{20,24},{24,20},{28,16},{1,13},{... | collective-permute-start | bytes 98312 | tf_op jit(solution)/shard_map/ppermute | solution.py:77
  29.7 2.1 %collective-permute-start.15 = (s16[64,256]{1,0:T(8,128)(2,1)S(1)}, s16[64,256]{1,0:T(8,128)(2,1)S(1)}, u32[]{:S(2)}, u32[]{:S(2)}) collective-permute-start(s16[64,256]{1,0:T(8,128)(2,1)S(1)} %get-tuple-element.72), channel_id=1, source_target_pairs={{0,4},{4,0},{8,12},{12,8},{16,20},{20,16},{24,28},{28,24},{1,5},{5... | collective-permute-start | bytes 98312 | tf_op jit(solution)/shard_map/ppermute | solution.py:77

commit v13 on v11

--- a/solution.py
+++ b/solution.py
@@ -66,7 +66,9 @@
 
 
 def partners(blocks):
-    return [0] + sorted(range(1, blocks), key=lambda k: (k & 1, -k))
+    even = sorted(range(2, blocks, 2), key=lambda k: (bin(k).count("1"), -k))
+    odd = sorted(range(3, blocks, 2), key=lambda k: (-bin(k).count("1"), -k))
+    return [0] + even + [1] + odd
 
 
 def swap_blocks(pieces):

time: 33.1 us -> 33.6 us (1.015)
  waiting for transfers between devices: 3.14 us -> 3.7 us
    ppermute x14, waiting for transfers between devices: 3.13 us -> 3.7 us  [swap_blocks(): lax.ppermute(pieces[at], 'date', [(i, i ^ k) for i in range(blocks)])]
where the time goes in v13:
time: 33.6 us; the launch traced here: 33.4 us
  starting transfers between devices  18.9 us (56%)
  Pallas kernels  8.25 us (25%)
  waiting for transfers between devices  3.7 us (11%)
  local copies, waits for them, and re-layouts  2.43 us (7%)
    ppermute x14, starting transfers between devices, swap_blocks(): lax.ppermute(pieces[at], 'date', [(i, i ^ k) for i in range(blocks)])  14.3 us
    ppermute x1, starting transfers between devices, on_device(): other = lax.ppermute(to_other, 'strip', swaps(1))  4.32 us
    ppermute x14, waiting for transfers between devices, swap_blocks(): lax.ppermute(pieces[at], 'date', [(i, i ^ k) for i in range(blocks)])  3.7 us
    pallas_call x1, Pallas kernels, on_device(): pl.pallas_call(functools.partial(inner_kernel, blocks, per, lines, chunk,...  3.06 us
    pallas_call x1, Pallas kernels, on_device(): pl.pallas_call(functools.partial(outer_kernel, blocks, per, lines, chunk,...  2.39 us
    unnamed x8, local copies, waits for them, and re-layouts  2.21 us
    pallas_call x1, Pallas kernels, on_device(): pl.pallas_call(functools.partial(join_kernel, blocks, per, out_rows, cols...  1.68 us
  transfers between devices with their start and end apart: 16, of which 5 were waited for; matrix products, arithmetic and copies ran while one was open for 0% of the time, Pallas kernels for 11%

profile of v13, /device:TPU:9, one launch (start us, length us, event | category | flops | bytes accessed | tf_op | source)
XLA Modules:
  0.0 33.4 jit_solution(13181946703352311640)
XLA Ops:
  0.0 0.9 %copy-done = bf16[2,2,32,1024]{3,2,1,0:T(8,128)(2,1)S(1)} copy-done((bf16[2,2,32,1024]{3,2,1,0:T(8,128)(2,1)S(1)}, bf16[2,2,32,1024]{3,2,1,0:T(8,128)(2,1)}, u32[]{:S(2)}) %copy-start) | copy-done | bytes 262168
  1.0 0.3 pack.1
  1.3 1.3 %collective-permute-start = (bf16[144,128]{1,0:T(8,128)(2,1)S(1)}, bf16[144,128]{1,0:T(8,128)(2,1)S(1)}, u32[]{:S(2)}, u32[]{:S(2)}) collective-permute-start(bf16[144,128]{1,0:T(8,128)(2,1)S(1)} %get-tuple-element.39), channel_id=1, source_target_pairs={{0,16},{4,20},{8,24},{12,28},{16,0},{20,4},{24,8},{28,12},{1,17},{... | collective-permute-start | bytes 110600 | tf_op jit(solution)/shard_map/ppermute | solution.py:79
  2.6 1.2 %collective-permute-start.1 = (bf16[144,128]{1,0:T(8,128)(2,1)S(1)}, bf16[144,128]{1,0:T(8,128)(2,1)S(1)}, u32[]{:S(2)}, u32[]{:S(2)}) collective-permute-start(bf16[144,128]{1,0:T(8,128)(2,1)S(1)} %get-tuple-element.40), channel_id=1, source_target_pairs={{0,8},{4,12},{8,0},{12,4},{16,24},{20,28},{24,16},{28,20},{1,9},{5... | collective-permute-start | bytes 110600 | tf_op jit(solution)/shard_map/ppermute | solution.py:79
  3.8 0.2 collective-permute-start.2
  4.0 1.5 %collective-permute-start.3 = (bf16[144,128]{1,0:T(8,128)(2,1)S(1)}, bf16[144,128]{1,0:T(8,128)(2,1)S(1)}, u32[]{:S(2)}, u32[]{:S(2)}) collective-permute-start(bf16[144,128]{1,0:T(8,128)(2,1)S(1)} %get-tuple-element.42), channel_id=1, source_target_pairs={{0,4},{4,0},{8,12},{12,8},{16,20},{20,16},{24,28},{28,24},{1,5},{5... | collective-permute-start | bytes 110600 | tf_op jit(solution)/shard_map/ppermute | solution.py:79
  5.5 2.1 %collective-permute-start.4 = (bf16[144,128]{1,0:T(8,128)(2,1)S(1)}, bf16[144,128]{1,0:T(8,128)(2,1)S(1)}, u32[]{:S(2)}, u32[]{:S(2)}) collective-permute-start(bf16[144,128]{1,0:T(8,128)(2,1)S(1)} %get-tuple-element.43), channel_id=1, source_target_pairs={{0,28},{4,24},{8,20},{12,16},{16,12},{20,8},{24,4},{28,0},{1,29},{... | collective-permute-start | bytes 110600 | tf_op jit(solution)/shard_map/ppermute | solution.py:79
  7.6 0.6 %collective-permute-start.5 = (bf16[144,128]{1,0:T(8,128)(2,1)S(1)}, bf16[144,128]{1,0:T(8,128)(2,1)S(1)}, u32[]{:S(2)}, u32[]{:S(2)}) collective-permute-start(bf16[144,128]{1,0:T(8,128)(2,1)S(1)} %get-tuple-element.44), channel_id=1, source_target_pairs={{0,20},{4,16},{8,28},{12,24},{16,4},{20,0},{24,12},{28,8},{1,21},{... | collective-permute-start | bytes 110600 | tf_op jit(solution)/shard_map/ppermute | solution.py:79
  8.2 0.4 %collective-permute-start.6 = (bf16[144,128]{1,0:T(8,128)(2,1)S(1)}, bf16[144,128]{1,0:T(8,128)(2,1)S(1)}, u32[]{:S(2)}, u32[]{:S(2)}) collective-permute-start(bf16[144,128]{1,0:T(8,128)(2,1)S(1)} %get-tuple-element.45), channel_id=1, source_target_pairs={{0,12},{4,8},{8,4},{12,0},{16,28},{20,24},{24,20},{28,16},{1,13},{... | collective-permute-start | bytes 110600 | tf_op jit(solution)/shard_map/ppermute | solution.py:79
  8.6 0.7 %copy-done.2 = s32[256]{0:T(256)S(1)} copy-done((s32[256]{0:T(256)S(1)}, s32[256]{0:T(256)}, u32[]{:S(2)}) %copy-start.2) | copy-done | bytes 1048
  9.3 0.1 dynamic_slice.3
  9.4 0.1 broadcast_in_dim_tile.3.tiled
  9.4 0.6 %copy-done.3 = s32[8]{0:T(128)S(1)} copy-done((s32[8]{0:T(128)S(1)}, s32[8]{0:T(128)}, u32[]{:S(2)}) %copy-start.3) | copy-done | bytes 56
  10.0 0.6 %weights.1 = (bf16[1536,128]{1,0:T(8,128)(2,1)S(1)}, bf16[1536,128]{1,0:T(8,128)(2,1)S(1)}) custom-call(s32[8]{0:T(128)S(1)} %copy-done.3, s32[1,256]{1,0:T(1,128)S(1)} %broadcast_in_dim_tile.3.tiled), custom_call_target="tpu_custom_call" | custom-call | bytes 4194304 | tf_op jit(solution)/shard_map/weights/pallas_call | solution.py:540
  10.7 0.6 %collective-permute-done.5.refs_6_ = bf16[144,128]{1,0:T(8,128)(2,1)S(1)} collective-permute-done((bf16[144,128]{1,0:T(8,128)(2,1)S(1)}, bf16[144,128]{1,0:T(8,128)(2,1)S(1)}, u32[]{:S(2)}, u32[]{:S(2)}) %collective-permute-start.5) | collective-permute-done | bytes 36896 | tf_op jit(solution)/shard_map/ppermute | solution.py:79
  11.3 0.3 collective-permute-done.6.refs_7_
  11.6 0.2 gather.1
  11.7 0.3 collective-permute-start.7
  12.0 4.3 %collective-permute-start.8 = (bf16[8,24,128]{2,1,0:T(8,128)(2,1)S(1)}, bf16[8,24,128]{2,1,0:T(8,128)(2,1)S(1)}, u32[]{:S(2)}, u32[]{:S(2)}) collective-permute-start(bf16[8,24,128]{2,1,0:T(8,128)(2,1)S(1)} %get-tuple-element.59), channel_id=1, source_target_pairs={{1,2},{2,1},{5,6},{6,5},{9,10},{10,9},{13,14},{14,13},{17,18},{18,... | collective-permute-start | bytes 147464 | tf_op jit(solution)/shard_map/ppermute | solution.py:568
  16.3 3.1 %inner.1 = (f32[384,128]{1,0:T(8,128)S(1)}, f32[384,512]{1,0:T(8,128)S(1)}, f32[64,128]{1,0:T(8,128)S(1)}) custom-call(s32[8]{0:T(128)S(1)} %copy-done.1, s32[8]{0:T(128)S(1)} %copy-done.3, s32[256]{0:T(256)S(1)} %copy-done.2, bf16[1536,128]{1,0:T(8,128)(2,1)S(1)} %get-tuple-element.48.weights, bf16[144,128]{1,0:T(8,128)(2,1)S(1)} %get-tuple-element.49.refs_0_, ...), custom_call_target="tpu_custom_call" | custom-call | bytes 12582912 | tf_op jit(solution)/shard_map/inner/pallas_call | solution.py:572
  19.4 2.4 %outer.1 = (s16[64,256]{1,0:T(8,128)(2,1)S(1)}, s16[64,256]{1,0:T(8,128)(2,1)S(1)}, s16[64,256]{1,0:T(8,128)(2,1)S(1)}, s16[64,256]{1,0:T(8,128)(2,1)S(1)}, s16[...) custom-call(f32[64,128]{1,0:T(8,128)S(1)} %get-tuple-element.57.own_, ...), custom_call_target="tpu_custom_call" | custom-call | tf_op jit(solution)/shard_map/outer/pallas_call | solution.py:590
  21.8 1.3 %collective-permute-start.9 = (s16[64,256]{1,0:T(8,128)(2,1)S(1)}, s16[64,256]{1,0:T(8,128)(2,1)S(1)}, u32[]{:S(2)}, u32[]{:S(2)}) collective-permute-start(s16[64,256]{1,0:T(8,128)(2,1)S(1)} %get-tuple-element.64), channel_id=1, source_target_pairs={{0,16},{4,20},{8,24},{12,28},{16,0},{20,4},{24,8},{28,12},{1,17},{... | collective-permute-start | bytes 98312 | tf_op jit(solution)/shard_map/ppermute | solution.py:79
  23.1 0.3 collective-permute-start.10
  23.4 1.2 %collective-permute-start.11 = (s16[64,256]{1,0:T(8,128)(2,1)S(1)}, s16[64,256]{1,0:T(8,128)(2,1)S(1)}, u32[]{:S(2)}, u32[]{:S(2)}) collective-permute-start(s16[64,256]{1,0:T(8,128)(2,1)S(1)} %get-tuple-element.66), channel_id=1, source_target_pairs={{0,24},{4,28},{8,16},{12,20},{16,8},{20,12},{24,0},{28,4},{1,25},{... | collective-permute-start | bytes 98312 | tf_op jit(solution)/shard_map/ppermute | solution.py:79
  24.5 1.5 %collective-permute-start.12 = (s16[64,256]{1,0:T(8,128)(2,1)S(1)}, s16[64,256]{1,0:T(8,128)(2,1)S(1)}, u32[]{:S(2)}, u32[]{:S(2)}) collective-permute-start(s16[64,256]{1,0:T(8,128)(2,1)S(1)} %get-tuple-element.67), channel_id=1, source_target_pairs={{0,4},{4,0},{8,12},{12,8},{16,20},{20,16},{24,28},{28,24},{1,5},{5... | collective-permute-start | bytes 98312 | tf_op jit(solution)/shard_map/ppermute | solution.py:79
  26.0 1.3 %collective-permute-start.13 = (s16[64,256]{1,0:T(8,128)(2,1)S(1)}, s16[64,256]{1,0:T(8,128)(2,1)S(1)}, u32[]{:S(2)}, u32[]{:S(2)}) collective-permute-start(s16[64,256]{1,0:T(8,128)(2,1)S(1)} %get-tuple-element.68), channel_id=1, source_target_pairs={{0,28},{4,24},{8,20},{12,16},{16,12},{20,8},{24,4},{28,0},{1,29},{... | collective-permute-start | bytes 98312 | tf_op jit(solution)/shard_map/ppermute | solution.py:79
  27.4 0.9 %collective-permute-start.14 = (s16[64,256]{1,0:T(8,128)(2,1)S(1)}, s16[64,256]{1,0:T(8,128)(2,1)S(1)}, u32[]{:S(2)}, u32[]{:S(2)}) collective-permute-start(s16[64,256]{1,0:T(8,128)(2,1)S(1)} %get-tuple-element.69), channel_id=1, source_target_pairs={{0,20},{4,16},{8,28},{12,24},{16,4},{20,0},{24,12},{28,8},{1,21},{... | collective-permute-start | bytes 98312 | tf_op jit(solution)/shard_map/ppermute | solution.py:79
  28.3 0.6 %collective-permute-start.15 = (s16[64,256]{1,0:T(8,128)(2,1)S(1)}, s16[64,256]{1,0:T(8,128)(2,1)S(1)}, u32[]{:S(2)}, u32[]{:S(2)}) collective-permute-start(s16[64,256]{1,0:T(8,128)(2,1)S(1)} %get-tuple-element.70), channel_id=1, source_target_pairs={{0,12},{4,8},{8,4},{12,0},{16,28},{20,24},{24,20},{28,16},{1,13},{... | collective-permute-start | bytes 98312 | tf_op jit(solution)/shard_map/ppermute | solution.py:79
  28.9 1.4 %collective-permute-done.13.refs_5_ = s16[64,256]{1,0:T(8,128)(2,1)S(1)} collective-permute-done((s16[64,256]{1,0:T(8,128)(2,1)S(1)}, s16[64,256]{1,0:T(8,128)(2,1)S(1)}, u32[]{:S(2)}, u32[]{:S(2)}) %collective-permute-start.13) | collective-permute-done | bytes 32800 | tf_op jit(solution)/shard_map/ppermute | solution.py:79
  30.3 1.0 %collective-permute-done.14.refs_6_ = s16[64,256]{1,0:T(8,128)(2,1)S(1)} collective-permute-done((s16[64,256]{1,0:T(8,128)(2,1)S(1)}, s16[64,256]{1,0:T(8,128)(2,1)S(1)}, u32[]{:S(2)}, u32[]{:S(2)}) %collective-permute-start.14) | collective-permute-done | bytes 32800 | tf_op jit(solution)/shard_map/ppermute | solution.py:79
  31.2 0.4 %collective-permute-done.15.refs_7_ = s16[64,256]{1,0:T(8,128)(2,1)S(1)} collective-permute-done((s16[64,256]{1,0:T(8,128)(2,1)S(1)}, s16[64,256]{1,0:T(8,128)(2,1)S(1)}, u32[]{:S(2)}, u32[]{:S(2)}) %collective-permute-start.15) | collective-permute-done | bytes 32800 | tf_op jit(solution)/shard_map/ppermute | solution.py:79
  31.7 1.7 %join.1 = f32[512,256]{1,0:T(8,128)} custom-call(s32[8,128]{1,0:T(8,128)S(1)} %broadcast_in_dim.2.order, s16[64,256]{1,0:T(8,128)(2,1)S(1)} %get-tuple-element.63.refs_0_, s16[64,256]{1,0:T(8,128)(2,1)S(1)} %collective-permute-done.9.refs_1_, s16[64,256]{1,0:T(8,128)(2,1)S(1)} %collective-permute-done.10.refs_2_, ...), custom_call_target="tpu_custom_call" | custom-call | tf_op jit(solution)/shard_map/join/pallas_call | solution.py:610
  (18 shorter events, 0.1 us)
Async XLA Ops:
  0.0 0.9 %copy-start = (bf16[2,2,32,1024]{3,2,1,0:T(8,128)(2,1)S(1)}, bf16[2,2,32,1024]{3,2,1,0:T(8,128)(2,1)}, u32[]{:S(2)}) copy-start(bf16[2,2,32,1024]{3,2,1,0:T(8,128)(2,1)} %slc.1) | copy-start | bytes 786436
  1.3 6.3 %collective-permute-start = (bf16[144,128]{1,0:T(8,128)(2,1)S(1)}, bf16[144,128]{1,0:T(8,128)(2,1)S(1)}, u32[]{:S(2)}, u32[]{:S(2)}) collective-permute-start(bf16[144,128]{1,0:T(8,128)(2,1)S(1)} %get-tuple-element.39), channel_id=1, source_target_pairs={{0,16},{4,20},{8,24},{12,28},{16,0},{20,4},{24,8},{28,12},{1,17},{... | collective-permute-start | bytes 110600 | tf_op jit(solution)/shard_map/ppermute | solution.py:79
  2.6 5.6 %collective-permute-start.1 = (bf16[144,128]{1,0:T(8,128)(2,1)S(1)}, bf16[144,128]{1,0:T(8,128)(2,1)S(1)}, u32[]{:S(2)}, u32[]{:S(2)}) collective-permute-start(bf16[144,128]{1,0:T(8,128)(2,1)S(1)} %get-tuple-element.40), channel_id=1, source_target_pairs={{0,8},{4,12},{8,0},{12,4},{16,24},{20,28},{24,16},{28,20},{1,9},{5... | collective-permute-start | bytes 110600 | tf_op jit(solution)/shard_map/ppermute | solution.py:79
  3.8 6.8 %collective-permute-start.2 = (bf16[144,128]{1,0:T(8,128)(2,1)S(1)}, bf16[144,128]{1,0:T(8,128)(2,1)S(1)}, u32[]{:S(2)}, u32[]{:S(2)}) collective-permute-start(bf16[144,128]{1,0:T(8,128)(2,1)S(1)} %get-tuple-element.41), channel_id=1, source_target_pairs={{0,24},{4,28},{8,16},{12,20},{16,8},{20,12},{24,0},{28,4},{1,25},{... | collective-permute-start | bytes 110600 | tf_op jit(solution)/shard_map/ppermute | solution.py:79
  4.0 6.7 %collective-permute-start.3 = (bf16[144,128]{1,0:T(8,128)(2,1)S(1)}, bf16[144,128]{1,0:T(8,128)(2,1)S(1)}, u32[]{:S(2)}, u32[]{:S(2)}) collective-permute-start(bf16[144,128]{1,0:T(8,128)(2,1)S(1)} %get-tuple-element.42), channel_id=1, source_target_pairs={{0,4},{4,0},{8,12},{12,8},{16,20},{20,16},{24,28},{28,24},{1,5},{5... | collective-permute-start | bytes 110600 | tf_op jit(solution)/shard_map/ppermute | solution.py:79
  5.5 5.2 %collective-permute-start.4 = (bf16[144,128]{1,0:T(8,128)(2,1)S(1)}, bf16[144,128]{1,0:T(8,128)(2,1)S(1)}, u32[]{:S(2)}, u32[]{:S(2)}) collective-permute-start(bf16[144,128]{1,0:T(8,128)(2,1)S(1)} %get-tuple-element.43), channel_id=1, source_target_pairs={{0,28},{4,24},{8,20},{12,16},{16,12},{20,8},{24,4},{28,0},{1,29},{... | collective-permute-start | bytes 110600 | tf_op jit(solution)/shard_map/ppermute | solution.py:79
  7.6 3.7 %collective-permute-start.5 = (bf16[144,128]{1,0:T(8,128)(2,1)S(1)}, bf16[144,128]{1,0:T(8,128)(2,1)S(1)}, u32[]{:S(2)}, u32[]{:S(2)}) collective-permute-start(bf16[144,128]{1,0:T(8,128)(2,1)S(1)} %get-tuple-element.44), channel_id=1, source_target_pairs={{0,20},{4,16},{8,28},{12,24},{16,4},{20,0},{24,12},{28,8},{1,21},{... | collective-permute-start | bytes 110600 | tf_op jit(solution)/shard_map/ppermute | solution.py:79
  8.2 3.4 %collective-permute-start.6 = (bf16[144,128]{1,0:T(8,128)(2,1)S(1)}, bf16[144,128]{1,0:T(8,128)(2,1)S(1)}, u32[]{:S(2)}, u32[]{:S(2)}) collective-permute-start(bf16[144,128]{1,0:T(8,128)(2,1)S(1)} %get-tuple-element.45), channel_id=1, source_target_pairs={{0,12},{4,8},{8,4},{12,0},{16,28},{20,24},{24,20},{28,16},{1,13},{... | collective-permute-start | bytes 110600 | tf_op jit(solution)/shard_map/ppermute | solution.py:79
  8.6 0.7 %copy-start.2 = (s32[256]{0:T(256)S(1)}, s32[256]{0:T(256)}, u32[]{:S(2)}) copy-start(s32[256]{0:T(256)} %rg.3) | copy-start | bytes 3076
  9.4 0.7 %copy-start.3 = (s32[8]{0:T(128)S(1)}, s32[8]{0:T(128)}, u32[]{:S(2)}) copy-start(s32[8]{0:T(128)} %az.5) | copy-start | bytes 100
  11.7 4.6 %copy-start.1 = (s32[8]{0:T(128)S(1)}, s32[8]{0:T(128)}, u32[]{:S(2)}) copy-start(s32[8]{0:T(128)} %order.3) | copy-start | bytes 100
  11.7 7.7 %collective-permute-start.7 = (bf16[8,24,128]{2,1,0:T(8,128)(2,1)S(1)}, bf16[8,24,128]{2,1,0:T(8,128)(2,1)S(1)}, u32[]{:S(2)}, u32[]{:S(2)}) collective-permute-start(bf16[8,24,128]{2,1,0:T(8,128)(2,1)S(1)} %get-tuple-element.58), channel_id=1, source_target_pairs={{0,1},{2,3},{1,0},{3,2},{4,5},{6,7},{5,4},{7,6},{8,9},{10,11},{9,8... | collective-permute-start | bytes 147464 | tf_op jit(solution)/shard_map/ppermute | solution.py:569
  12.0 7.4 %collective-permute-start.8 = (bf16[8,24,128]{2,1,0:T(8,128)(2,1)S(1)}, bf16[8,24,128]{2,1,0:T(8,128)(2,1)S(1)}, u32[]{:S(2)}, u32[]{:S(2)}) collective-permute-start(bf16[8,24,128]{2,1,0:T(8,128)(2,1)S(1)} %get-tuple-element.59), channel_id=1, source_target_pairs={{1,2},{2,1},{5,6},{6,5},{9,10},{10,9},{13,14},{14,13},{17,18},{18,... | collective-permute-start | bytes 147464 | tf_op jit(solution)/shard_map/ppermute | solution.py:568
  21.8 5.5 %collective-permute-start.9 = (s16[64,256]{1,0:T(8,128)(2,1)S(1)}, s16[64,256]{1,0:T(8,128)(2,1)S(1)}, u32[]{:S(2)}, u32[]{:S(2)}) collective-permute-start(s16[64,256]{1,0:T(8,128)(2,1)S(1)} %get-tuple-element.64), channel_id=1, source_target_pairs={{0,16},{4,20},{8,24},{12,28},{16,0},{20,4},{24,8},{28,12},{1,17},{... | collective-permute-start | bytes 98312 | tf_op jit(solution)/shard_map/ppermute | solution.py:79
  23.1 5.2 %collective-permute-start.10 = (s16[64,256]{1,0:T(8,128)(2,1)S(1)}, s16[64,256]{1,0:T(8,128)(2,1)S(1)}, u32[]{:S(2)}, u32[]{:S(2)}) collective-permute-start(s16[64,256]{1,0:T(8,128)(2,1)S(1)} %get-tuple-element.65), channel_id=1, source_target_pairs={{0,8},{4,12},{8,0},{12,4},{16,24},{20,28},{24,16},{28,20},{1,9},{5... | collective-permute-start | bytes 98312 | tf_op jit(solution)/shard_map/ppermute | solution.py:79
  23.4 5.5 %collective-permute-start.11 = (s16[64,256]{1,0:T(8,128)(2,1)S(1)}, s16[64,256]{1,0:T(8,128)(2,1)S(1)}, u32[]{:S(2)}, u32[]{:S(2)}) collective-permute-start(s16[64,256]{1,0:T(8,128)(2,1)S(1)} %get-tuple-element.66), channel_id=1, source_target_pairs={{0,24},{4,28},{8,16},{12,20},{16,8},{20,12},{24,0},{28,4},{1,25},{... | collective-permute-start | bytes 98312 | tf_op jit(solution)/shard_map/ppermute | solution.py:79
  24.5 4.3 %collective-permute-start.12 = (s16[64,256]{1,0:T(8,128)(2,1)S(1)}, s16[64,256]{1,0:T(8,128)(2,1)S(1)}, u32[]{:S(2)}, u32[]{:S(2)}) collective-permute-start(s16[64,256]{1,0:T(8,128)(2,1)S(1)} %get-tuple-element.67), channel_id=1, source_target_pairs={{0,4},{4,0},{8,12},{12,8},{16,20},{20,16},{24,28},{28,24},{1,5},{5... | collective-permute-start | bytes 98312 | tf_op jit(solution)/shard_map/ppermute | solution.py:79
  26.0 4.2 %collective-permute-start.13 = (s16[64,256]{1,0:T(8,128)(2,1)S(1)}, s16[64,256]{1,0:T(8,128)(2,1)S(1)}, u32[]{:S(2)}, u32[]{:S(2)}) collective-permute-start(s16[64,256]{1,0:T(8,128)(2,1)S(1)} %get-tuple-element.68), channel_id=1, source_target_pairs={{0,28},{4,24},{8,20},{12,16},{16,12},{20,8},{24,4},{28,0},{1,29},{... | collective-permute-start | bytes 98312 | tf_op jit(solution)/shard_map/ppermute | solution.py:79
  27.4 3.9 %collective-permute-start.14 = (s16[64,256]{1,0:T(8,128)(2,1)S(1)}, s16[64,256]{1,0:T(8,128)(2,1)S(1)}, u32[]{:S(2)}, u32[]{:S(2)}) collective-permute-start(s16[64,256]{1,0:T(8,128)(2,1)S(1)} %get-tuple-element.69), channel_id=1, source_target_pairs={{0,20},{4,16},{8,28},{12,24},{16,4},{20,0},{24,12},{28,8},{1,21},{... | collective-permute-start | bytes 98312 | tf_op jit(solution)/shard_map/ppermute | solution.py:79
  28.3 3.3 %collective-permute-start.15 = (s16[64,256]{1,0:T(8,128)(2,1)S(1)}, s16[64,256]{1,0:T(8,128)(2,1)S(1)}, u32[]{:S(2)}, u32[]{:S(2)}) collective-permute-start(s16[64,256]{1,0:T(8,128)(2,1)S(1)} %get-tuple-element.70), channel_id=1, source_target_pairs={{0,12},{4,8},{8,4},{12,0},{16,28},{20,24},{24,20},{28,16},{1,13},{... | collective-permute-start | bytes 98312 | tf_op jit(solution)/shard_map/ppermute | solution.py:79

commit v14 on v11

--- a/solution.py
+++ b/solution.py
@@ -66,7 +66,7 @@
 
 
 def partners(blocks):
-    return [0] + sorted(range(1, blocks), key=lambda k: (k & 1, -k))
+    return [0, 1] + sorted(range(2, blocks), key=lambda k: (k & 1, -k))
 
 
 def swap_blocks(pieces):

time: 33.1 us -> 33.2 us (level)
  transfers between devices with their start and end apart: 16 -> 16, of which waited for: 5 -> 4; matrix products, arithmetic and copies ran while one was open for 0% -> 0% of each run, Pallas kernels for 11% -> 11%
where the time goes in v14:
time: 33.2 us; the launch traced here: 32.9 us
  starting transfers between devices  19.1 us (58%)
  Pallas kernels  8.26 us (25%)
  waiting for transfers between devices  3 us (9%)
  local copies, waits for them, and re-layouts  2.43 us (7%)
    ppermute x14, starting transfers between devices, swap_blocks(): lax.ppermute(pieces[at], 'date', [(i, i ^ k) for i in range(blocks)])  14.5 us
    ppermute x1, starting transfers between devices, on_device(): other = lax.ppermute(to_other, 'strip', swaps(1))  4.32 us
    pallas_call x1, Pallas kernels, on_device(): pl.pallas_call(functools.partial(inner_kernel, blocks, per, lines, chunk,...  3.06 us
    ppermute x14, waiting for transfers between devices, swap_blocks(): lax.ppermute(pieces[at], 'date', [(i, i ^ k) for i in range(blocks)])  2.99 us
    pallas_call x1, Pallas kernels, on_device(): pl.pallas_call(functools.partial(outer_kernel, blocks, per, lines, chunk,...  2.4 us
    unnamed x8, local copies, waits for them, and re-layouts  2.21 us
    pallas_call x1, Pallas kernels, on_device(): pl.pallas_call(functools.partial(join_kernel, blocks, per, out_rows, cols...  1.68 us
  transfers between devices with their start and end apart: 16, of which 4 were waited for; matrix products, arithmetic and copies ran while one was open for 0% of the time, Pallas kernels for 11%

profile of v14, /device:TPU:9, one launch (start us, length us, event | category | flops | bytes accessed | tf_op | source)
XLA Modules:
  0.0 32.9 jit_solution(5823519552677534866)
XLA Ops:
  0.0 0.9 %copy-done = bf16[2,2,32,1024]{3,2,1,0:T(8,128)(2,1)S(1)} copy-done((bf16[2,2,32,1024]{3,2,1,0:T(8,128)(2,1)S(1)}, bf16[2,2,32,1024]{3,2,1,0:T(8,128)(2,1)}, u32[]{:S(2)}) %copy-start) | copy-done | bytes 262168
  1.0 0.3 pack.1
  1.3 0.7 %collective-permute-start = (bf16[144,128]{1,0:T(8,128)(2,1)S(1)}, bf16[144,128]{1,0:T(8,128)(2,1)S(1)}, u32[]{:S(2)}, u32[]{:S(2)}) collective-permute-start(bf16[144,128]{1,0:T(8,128)(2,1)S(1)} %get-tuple-element.39), channel_id=1, source_target_pairs={{0,4},{4,0},{8,12},{12,8},{16,20},{20,16},{24,28},{28,24},{1,5},{5... | collective-permute-start | bytes 110600 | tf_op jit(solution)/shard_map/ppermute | solution.py:77
  2.0 2.2 %collective-permute-start.1 = (bf16[144,128]{1,0:T(8,128)(2,1)S(1)}, bf16[144,128]{1,0:T(8,128)(2,1)S(1)}, u32[]{:S(2)}, u32[]{:S(2)}) collective-permute-start(bf16[144,128]{1,0:T(8,128)(2,1)S(1)} %get-tuple-element.40), channel_id=1, source_target_pairs={{0,24},{4,28},{8,16},{12,20},{16,8},{20,12},{24,0},{28,4},{1,25},{... | collective-permute-start | bytes 110600 | tf_op jit(solution)/shard_map/ppermute | solution.py:77
  4.2 0.2 collective-permute-start.2
  4.4 0.3 collective-permute-start.3
  4.7 3.0 %collective-permute-start.4 = (bf16[144,128]{1,0:T(8,128)(2,1)S(1)}, bf16[144,128]{1,0:T(8,128)(2,1)S(1)}, u32[]{:S(2)}, u32[]{:S(2)}) collective-permute-start(bf16[144,128]{1,0:T(8,128)(2,1)S(1)} %get-tuple-element.43), channel_id=1, source_target_pairs={{0,28},{4,24},{8,20},{12,16},{16,12},{20,8},{24,4},{28,0},{1,29},{... | collective-permute-start | bytes 110600 | tf_op jit(solution)/shard_map/ppermute | solution.py:77
  7.6 0.0 collective-permute-done.1.refs_2_
  7.6 0.8 %collective-permute-start.6 = (bf16[144,128]{1,0:T(8,128)(2,1)S(1)}, bf16[144,128]{1,0:T(8,128)(2,1)S(1)}, u32[]{:S(2)}, u32[]{:S(2)}) collective-permute-start(bf16[144,128]{1,0:T(8,128)(2,1)S(1)} %get-tuple-element.45), channel_id=1, source_target_pairs={{0,12},{4,8},{8,4},{12,0},{16,28},{20,24},{24,20},{28,16},{1,13},{... | collective-permute-start | bytes 110600 | tf_op jit(solution)/shard_map/ppermute | solution.py:77
  8.4 0.7 %copy-done.2 = s32[256]{0:T(256)S(1)} copy-done((s32[256]{0:T(256)S(1)}, s32[256]{0:T(256)}, u32[]{:S(2)}) %copy-start.2) | copy-done | bytes 1048
  9.1 0.1 dynamic_slice.3
  9.2 0.1 broadcast_in_dim_tile.3.tiled
  9.2 0.6 %copy-done.3 = s32[8]{0:T(128)S(1)} copy-done((s32[8]{0:T(128)S(1)}, s32[8]{0:T(128)}, u32[]{:S(2)}) %copy-start.3) | copy-done | bytes 56
  9.8 0.6 %weights.1 = (bf16[1536,128]{1,0:T(8,128)(2,1)S(1)}, bf16[1536,128]{1,0:T(8,128)(2,1)S(1)}) custom-call(s32[8]{0:T(128)S(1)} %copy-done.3, s32[1,256]{1,0:T(1,128)S(1)} %broadcast_in_dim_tile.3.tiled), custom_call_target="tpu_custom_call" | custom-call | bytes 4194304 | tf_op jit(solution)/shard_map/weights/pallas_call | solution.py:538
  10.5 0.0 collective-permute-done.2.refs_3_
  10.5 0.8 %collective-permute-done.5.refs_6_ = bf16[144,128]{1,0:T(8,128)(2,1)S(1)} collective-permute-done((bf16[144,128]{1,0:T(8,128)(2,1)S(1)}, bf16[144,128]{1,0:T(8,128)(2,1)S(1)}, u32[]{:S(2)}, u32[]{:S(2)}) %collective-permute-start.5) | collective-permute-done | bytes 36896 | tf_op jit(solution)/shard_map/ppermute | solution.py:77
  11.3 0.2 collective-permute-done.6.refs_7_
  11.5 0.2 gather.1
  11.7 0.2 collective-permute-start.7
  11.9 4.3 %collective-permute-start.8 = (bf16[8,24,128]{2,1,0:T(8,128)(2,1)S(1)}, bf16[8,24,128]{2,1,0:T(8,128)(2,1)S(1)}, u32[]{:S(2)}, u32[]{:S(2)}) collective-permute-start(bf16[8,24,128]{2,1,0:T(8,128)(2,1)S(1)} %get-tuple-element.59), channel_id=1, source_target_pairs={{1,2},{2,1},{5,6},{6,5},{9,10},{10,9},{13,14},{14,13},{17,18},{18,... | collective-permute-start | bytes 147464 | tf_op jit(solution)/shard_map/ppermute | solution.py:566
  16.3 3.1 %inner.1 = (f32[384,128]{1,0:T(8,128)S(1)}, f32[384,512]{1,0:T(8,128)S(1)}, f32[64,128]{1,0:T(8,128)S(1)}) custom-call(s32[8]{0:T(128)S(1)} %copy-done.1, s32[8]{0:T(128)S(1)} %copy-done.3, s32[256]{0:T(256)S(1)} %copy-done.2, bf16[1536,128]{1,0:T(8,128)(2,1)S(1)} %get-tuple-element.48.weights, bf16[144,128]{1,0:T(8,128)(2,1)S(1)} %get-tuple-element.49.refs_0_, ...), custom_call_target="tpu_custom_call" | custom-call | bytes 12582912 | tf_op jit(solution)/shard_map/inner/pallas_call | solution.py:570
  19.3 2.4 %outer.1 = (s16[64,256]{1,0:T(8,128)(2,1)S(1)}, s16[64,256]{1,0:T(8,128)(2,1)S(1)}, s16[64,256]{1,0:T(8,128)(2,1)S(1)}, s16[64,256]{1,0:T(8,128)(2,1)S(1)}, s16[...) custom-call(f32[64,128]{1,0:T(8,128)S(1)} %get-tuple-element.57.own_, ...), custom_call_target="tpu_custom_call" | custom-call | tf_op jit(solution)/shard_map/outer/pallas_call | solution.py:588
  21.8 1.0 %collective-permute-start.9 = (s16[64,256]{1,0:T(8,128)(2,1)S(1)}, s16[64,256]{1,0:T(8,128)(2,1)S(1)}, u32[]{:S(2)}, u32[]{:S(2)}) collective-permute-start(s16[64,256]{1,0:T(8,128)(2,1)S(1)} %get-tuple-element.64), channel_id=1, source_target_pairs={{0,4},{4,0},{8,12},{12,8},{16,20},{20,16},{24,28},{28,24},{1,5},{5... | collective-permute-start | bytes 98312 | tf_op jit(solution)/shard_map/ppermute | solution.py:77
  22.8 1.3 %collective-permute-start.10 = (s16[64,256]{1,0:T(8,128)(2,1)S(1)}, s16[64,256]{1,0:T(8,128)(2,1)S(1)}, u32[]{:S(2)}, u32[]{:S(2)}) collective-permute-start(s16[64,256]{1,0:T(8,128)(2,1)S(1)} %get-tuple-element.65), channel_id=1, source_target_pairs={{0,24},{4,28},{8,16},{12,20},{16,8},{20,12},{24,0},{28,4},{1,25},{... | collective-permute-start | bytes 98312 | tf_op jit(solution)/shard_map/ppermute | solution.py:77
  24.1 0.1 collective-permute-start.11
  24.2 1.2 %collective-permute-start.12 = (s16[64,256]{1,0:T(8,128)(2,1)S(1)}, s16[64,256]{1,0:T(8,128)(2,1)S(1)}, u32[]{:S(2)}, u32[]{:S(2)}) collective-permute-start(s16[64,256]{1,0:T(8,128)(2,1)S(1)} %get-tuple-element.67), channel_id=1, source_target_pairs={{0,8},{4,12},{8,0},{12,4},{16,24},{20,28},{24,16},{28,20},{1,9},{5... | collective-permute-start | bytes 98312 | tf_op jit(solution)/shard_map/ppermute | solution.py:77
  25.4 2.1 %collective-permute-start.13 = (s16[64,256]{1,0:T(8,128)(2,1)S(1)}, s16[64,256]{1,0:T(8,128)(2,1)S(1)}, u32[]{:S(2)}, u32[]{:S(2)}) collective-permute-start(s16[64,256]{1,0:T(8,128)(2,1)S(1)} %get-tuple-element.68), channel_id=1, source_target_pairs={{0,28},{4,24},{8,20},{12,16},{16,12},{20,8},{24,4},{28,0},{1,29},{... | collective-permute-start | bytes 98312 | tf_op jit(solution)/shard_map/ppermute | solution.py:77
  27.5 1.6 %collective-permute-start.15 = (s16[64,256]{1,0:T(8,128)(2,1)S(1)}, s16[64,256]{1,0:T(8,128)(2,1)S(1)}, u32[]{:S(2)}, u32[]{:S(2)}) collective-permute-start(s16[64,256]{1,0:T(8,128)(2,1)S(1)} %get-tuple-element.70), channel_id=1, source_target_pairs={{0,12},{4,8},{8,4},{12,0},{16,28},{20,24},{24,20},{28,16},{1,13},{... | collective-permute-start | bytes 98312 | tf_op jit(solution)/shard_map/ppermute | solution.py:77
  29.2 0.9 %collective-permute-done.13.refs_5_ = s16[64,256]{1,0:T(8,128)(2,1)S(1)} collective-permute-done((s16[64,256]{1,0:T(8,128)(2,1)S(1)}, s16[64,256]{1,0:T(8,128)(2,1)S(1)}, u32[]{:S(2)}, u32[]{:S(2)}) %collective-permute-start.13) | collective-permute-done | bytes 32800 | tf_op jit(solution)/shard_map/ppermute | solution.py:77
  30.1 1.0 %collective-permute-done.14.refs_6_ = s16[64,256]{1,0:T(8,128)(2,1)S(1)} collective-permute-done((s16[64,256]{1,0:T(8,128)(2,1)S(1)}, s16[64,256]{1,0:T(8,128)(2,1)S(1)}, u32[]{:S(2)}, u32[]{:S(2)}) %collective-permute-start.14) | collective-permute-done | bytes 32800 | tf_op jit(solution)/shard_map/ppermute | solution.py:77
  31.1 0.1 broadcast_in_dim.2.order
  31.2 1.7 %join.1 = f32[512,256]{1,0:T(8,128)} custom-call(s32[8,128]{1,0:T(8,128)S(1)} %broadcast_in_dim.2.order, s16[64,256]{1,0:T(8,128)(2,1)S(1)} %get-tuple-element.63.refs_0_, s16[64,256]{1,0:T(8,128)(2,1)S(1)} %collective-permute-done.9.refs_1_, s16[64,256]{1,0:T(8,128)(2,1)S(1)} %collective-permute-done.10.refs_2_, ...), custom_call_target="tpu_custom_call" | custom-call | tf_op jit(solution)/shard_map/join/pallas_call | solution.py:608
  (18 shorter events, 0.0 us)
Async XLA Ops:
  0.0 0.9 %copy-start = (bf16[2,2,32,1024]{3,2,1,0:T(8,128)(2,1)S(1)}, bf16[2,2,32,1024]{3,2,1,0:T(8,128)(2,1)}, u32[]{:S(2)}) copy-start(bf16[2,2,32,1024]{3,2,1,0:T(8,128)(2,1)} %slc.1) | copy-start | bytes 786436
  1.3 6.4 %collective-permute-start = (bf16[144,128]{1,0:T(8,128)(2,1)S(1)}, bf16[144,128]{1,0:T(8,128)(2,1)S(1)}, u32[]{:S(2)}, u32[]{:S(2)}) collective-permute-start(bf16[144,128]{1,0:T(8,128)(2,1)S(1)} %get-tuple-element.39), channel_id=1, source_target_pairs={{0,4},{4,0},{8,12},{12,8},{16,20},{20,16},{24,28},{28,24},{1,5},{5... | collective-permute-start | bytes 110600 | tf_op jit(solution)/shard_map/ppermute | solution.py:77
  2.0 5.6 %collective-permute-start.1 = (bf16[144,128]{1,0:T(8,128)(2,1)S(1)}, bf16[144,128]{1,0:T(8,128)(2,1)S(1)}, u32[]{:S(2)}, u32[]{:S(2)}) collective-permute-start(bf16[144,128]{1,0:T(8,128)(2,1)S(1)} %get-tuple-element.40), channel_id=1, source_target_pairs={{0,24},{4,28},{8,16},{12,20},{16,8},{20,12},{24,0},{28,4},{1,25},{... | collective-permute-start | bytes 110600 | tf_op jit(solution)/shard_map/ppermute | solution.py:77
  4.2 6.3 %collective-permute-start.2 = (bf16[144,128]{1,0:T(8,128)(2,1)S(1)}, bf16[144,128]{1,0:T(8,128)(2,1)S(1)}, u32[]{:S(2)}, u32[]{:S(2)}) collective-permute-start(bf16[144,128]{1,0:T(8,128)(2,1)S(1)} %get-tuple-element.41), channel_id=1, source_target_pairs={{0,16},{4,20},{8,24},{12,28},{16,0},{20,4},{24,8},{28,12},{1,17},{... | collective-permute-start | bytes 110600 | tf_op jit(solution)/shard_map/ppermute | solution.py:77
  4.4 6.0 %collective-permute-start.3 = (bf16[144,128]{1,0:T(8,128)(2,1)S(1)}, bf16[144,128]{1,0:T(8,128)(2,1)S(1)}, u32[]{:S(2)}, u32[]{:S(2)}) collective-permute-start(bf16[144,128]{1,0:T(8,128)(2,1)S(1)} %get-tuple-element.42), channel_id=1, source_target_pairs={{0,8},{4,12},{8,0},{12,4},{16,24},{20,28},{24,16},{28,20},{1,9},{5... | collective-permute-start | bytes 110600 | tf_op jit(solution)/shard_map/ppermute | solution.py:77
  4.7 5.8 %collective-permute-start.4 = (bf16[144,128]{1,0:T(8,128)(2,1)S(1)}, bf16[144,128]{1,0:T(8,128)(2,1)S(1)}, u32[]{:S(2)}, u32[]{:S(2)}) collective-permute-start(bf16[144,128]{1,0:T(8,128)(2,1)S(1)} %get-tuple-element.43), channel_id=1, source_target_pairs={{0,28},{4,24},{8,20},{12,16},{16,12},{20,8},{24,4},{28,0},{1,29},{... | collective-permute-start | bytes 110600 | tf_op jit(solution)/shard_map/ppermute | solution.py:77
  7.6 3.7 %collective-permute-start.5 = (bf16[144,128]{1,0:T(8,128)(2,1)S(1)}, bf16[144,128]{1,0:T(8,128)(2,1)S(1)}, u32[]{:S(2)}, u32[]{:S(2)}) collective-permute-start(bf16[144,128]{1,0:T(8,128)(2,1)S(1)} %get-tuple-element.44), channel_id=1, source_target_pairs={{0,20},{4,16},{8,28},{12,24},{16,4},{20,0},{24,12},{28,8},{1,21},{... | collective-permute-start | bytes 110600 | tf_op jit(solution)/shard_map/ppermute | solution.py:77
  7.6 3.9 %collective-permute-start.6 = (bf16[144,128]{1,0:T(8,128)(2,1)S(1)}, bf16[144,128]{1,0:T(8,128)(2,1)S(1)}, u32[]{:S(2)}, u32[]{:S(2)}) collective-permute-start(bf16[144,128]{1,0:T(8,128)(2,1)S(1)} %get-tuple-element.45), channel_id=1, source_target_pairs={{0,12},{4,8},{8,4},{12,0},{16,28},{20,24},{24,20},{28,16},{1,13},{... | collective-permute-start | bytes 110600 | tf_op jit(solution)/shard_map/ppermute | solution.py:77
  8.4 0.7 %copy-start.2 = (s32[256]{0:T(256)S(1)}, s32[256]{0:T(256)}, u32[]{:S(2)}) copy-start(s32[256]{0:T(256)} %rg.3) | copy-start | bytes 3076
  9.2 0.7 %copy-start.3 = (s32[8]{0:T(128)S(1)}, s32[8]{0:T(128)}, u32[]{:S(2)}) copy-start(s32[8]{0:T(128)} %az.5) | copy-start | bytes 100
  11.7 4.6 %copy-start.1 = (s32[8]{0:T(128)S(1)}, s32[8]{0:T(128)}, u32[]{:S(2)}) copy-start(s32[8]{0:T(128)} %order.3) | copy-start | bytes 100
  11.7 7.6 %collective-permute-start.7 = (bf16[8,24,128]{2,1,0:T(8,128)(2,1)S(1)}, bf16[8,24,128]{2,1,0:T(8,128)(2,1)S(1)}, u32[]{:S(2)}, u32[]{:S(2)}) collective-permute-start(bf16[8,24,128]{2,1,0:T(8,128)(2,1)S(1)} %get-tuple-element.58), channel_id=1, source_target_pairs={{0,1},{2,3},{1,0},{3,2},{4,5},{6,7},{5,4},{7,6},{8,9},{10,11},{9,8... | collective-permute-start | bytes 147464 | tf_op jit(solution)/shard_map/ppermute | solution.py:567
  11.9 7.4 %collective-permute-start.8 = (bf16[8,24,128]{2,1,0:T(8,128)(2,1)S(1)}, bf16[8,24,128]{2,1,0:T(8,128)(2,1)S(1)}, u32[]{:S(2)}, u32[]{:S(2)}) collective-permute-start(bf16[8,24,128]{2,1,0:T(8,128)(2,1)S(1)} %get-tuple-element.59), channel_id=1, source_target_pairs={{1,2},{2,1},{5,6},{6,5},{9,10},{10,9},{13,14},{14,13},{17,18},{18,... | collective-permute-start | bytes 147464 | tf_op jit(solution)/shard_map/ppermute | solution.py:566
  21.8 5.8 %collective-permute-start.9 = (s16[64,256]{1,0:T(8,128)(2,1)S(1)}, s16[64,256]{1,0:T(8,128)(2,1)S(1)}, u32[]{:S(2)}, u32[]{:S(2)}) collective-permute-start(s16[64,256]{1,0:T(8,128)(2,1)S(1)} %get-tuple-element.64), channel_id=1, source_target_pairs={{0,4},{4,0},{8,12},{12,8},{16,20},{20,16},{24,28},{28,24},{1,5},{5... | collective-permute-start | bytes 98312 | tf_op jit(solution)/shard_map/ppermute | solution.py:77
  22.8 4.8 %collective-permute-start.10 = (s16[64,256]{1,0:T(8,128)(2,1)S(1)}, s16[64,256]{1,0:T(8,128)(2,1)S(1)}, u32[]{:S(2)}, u32[]{:S(2)}) collective-permute-start(s16[64,256]{1,0:T(8,128)(2,1)S(1)} %get-tuple-element.65), channel_id=1, source_target_pairs={{0,24},{4,28},{8,16},{12,20},{16,8},{20,12},{24,0},{28,4},{1,25},{... | collective-permute-start | bytes 98312 | tf_op jit(solution)/shard_map/ppermute | solution.py:77
  24.1 5.1 %collective-permute-start.11 = (s16[64,256]{1,0:T(8,128)(2,1)S(1)}, s16[64,256]{1,0:T(8,128)(2,1)S(1)}, u32[]{:S(2)}, u32[]{:S(2)}) collective-permute-start(s16[64,256]{1,0:T(8,128)(2,1)S(1)} %get-tuple-element.66), channel_id=1, source_target_pairs={{0,16},{4,20},{8,24},{12,28},{16,0},{20,4},{24,8},{28,12},{1,17},{... | collective-permute-start | bytes 98312 | tf_op jit(solution)/shard_map/ppermute | solution.py:77
  24.2 4.9 %collective-permute-start.12 = (s16[64,256]{1,0:T(8,128)(2,1)S(1)}, s16[64,256]{1,0:T(8,128)(2,1)S(1)}, u32[]{:S(2)}, u32[]{:S(2)}) collective-permute-start(s16[64,256]{1,0:T(8,128)(2,1)S(1)} %get-tuple-element.67), channel_id=1, source_target_pairs={{0,8},{4,12},{8,0},{12,4},{16,24},{20,28},{24,16},{28,20},{1,9},{5... | collective-permute-start | bytes 98312 | tf_op jit(solution)/shard_map/ppermute | solution.py:77
  25.4 4.7 %collective-permute-start.13 = (s16[64,256]{1,0:T(8,128)(2,1)S(1)}, s16[64,256]{1,0:T(8,128)(2,1)S(1)}, u32[]{:S(2)}, u32[]{:S(2)}) collective-permute-start(s16[64,256]{1,0:T(8,128)(2,1)S(1)} %get-tuple-element.68), channel_id=1, source_target_pairs={{0,28},{4,24},{8,20},{12,16},{16,12},{20,8},{24,4},{28,0},{1,29},{... | collective-permute-start | bytes 98312 | tf_op jit(solution)/shard_map/ppermute | solution.py:77
  27.5 3.6 %collective-permute-start.14 = (s16[64,256]{1,0:T(8,128)(2,1)S(1)}, s16[64,256]{1,0:T(8,128)(2,1)S(1)}, u32[]{:S(2)}, u32[]{:S(2)}) collective-permute-start(s16[64,256]{1,0:T(8,128)(2,1)S(1)} %get-tuple-element.69), channel_id=1, source_target_pairs={{0,20},{4,16},{8,28},{12,24},{16,4},{20,0},{24,12},{28,8},{1,21},{... | collective-permute-start | bytes 98312 | tf_op jit(solution)/shard_map/ppermute | solution.py:77
  27.5 3.6 %collective-permute-start.15 = (s16[64,256]{1,0:T(8,128)(2,1)S(1)}, s16[64,256]{1,0:T(8,128)(2,1)S(1)}, u32[]{:S(2)}, u32[]{:S(2)}) collective-permute-start(s16[64,256]{1,0:T(8,128)(2,1)S(1)} %get-tuple-element.70), channel_id=1, source_target_pairs={{0,12},{4,8},{8,4},{12,0},{16,28},{20,24},{24,20},{28,16},{1,13},{... | collective-permute-start | bytes 98312 | tf_op jit(solution)/shard_map/ppermute | solution.py:77
